TPU v7x, 32 devices: a whole 2x2x4 slice. The times are simulated.
32 devices in a mesh: dp: 8 (over z, core), fsdp: 4 (over y, x).
Axes of the slice: x: 2, y: 2, z: 4, core: 2. Of those that a mesh axis runs over, the one named last changes fastest.
Arguments:
- tokens: bfloat16 [32, 512, 2048], P(('dp', 'fsdp')), may hold values from -6 to 6
- cotangent: bfloat16 [32, 512, 2048], P(('dp', 'fsdp')), may hold values from -6 to 6
- doc_starts: int32 [32, 4], P(('dp', 'fsdp')), may hold values from 0 to 511, as said below
- valid_len: int32 [32], P(('dp', 'fsdp')), may hold values from 257 to 512, as said below
- w_in: float32 [2048, 8512], P('fsdp', 'dp'), may hold values from -0.125 to 0.125
- w_out: float32 [4096, 2048], P('fsdp', 'dp'), may hold values from -0.09375 to 0.09375
- norm_gain: float32 [2048], P('fsdp'), may hold values from 0.5 to 1.5
- gate_gain: float32 [4096], P('fsdp'), may hold values from 0.5 to 1.5
- conv_w: float32 [4, 4352], P(None, 'fsdp'), may hold values from -3 to 3
- conv_b: float32 [4352], P('fsdp'), may hold values from -3 to 3
- dt_bias: float32 [64], P('fsdp'), may hold values from -6.9 to -2.25
- a_log: float32 [64], P('fsdp'), may hold values from 0 to 2.77
- d_skip: float32 [64], P('fsdp'), may hold values from 0.5 to 1.5
- first_w_in: float32 [2048, 8512], P('fsdp', 'dp'), may hold values from -0.625 to 0.625
- second_w_in: float32 [2048, 8512], P('fsdp', 'dp'), may hold values from 0.01 to 0.3
- first_w_out: float32 [4096, 2048], P('fsdp', 'dp'), may hold values from -0.625 to 0.625
- second_w_out: float32 [4096, 2048], P('fsdp', 'dp'), may hold values from 0.01 to 0.3
- first_norm_gain: float32 [2048], P('fsdp'), may hold values from -0.625 to 0.625
- second_norm_gain: float32 [2048], P('fsdp'), may hold values from 0.01 to 0.3
- first_gate_gain: float32 [4096], P('fsdp'), may hold values from -0.625 to 0.625
- second_gate_gain: float32 [4096], P('fsdp'), may hold values from 0.01 to 0.3
- first_conv_w: float32 [4, 4352], P(None, 'fsdp'), may hold values from -0.625 to 0.625
- second_conv_w: float32 [4, 4352], P(None, 'fsdp'), may hold values from 0.01 to 0.3
- first_conv_b: float32 [4352], P('fsdp'), may hold values from -0.625 to 0.625
- second_conv_b: float32 [4352], P('fsdp'), may hold values from 0.01 to 0.3
- first_dt_bias: float32 [64], P('fsdp'), may hold values from -0.625 to 0.625
- second_dt_bias: float32 [64], P('fsdp'), may hold values from 0.01 to 0.3
- first_a_log: float32 [64], P('fsdp'), may hold values from -0.625 to 0.625
- second_a_log: float32 [64], P('fsdp'), may hold values from 0.01 to 0.3
- first_d_skip: float32 [64], P('fsdp'), may hold values from -0.625 to 0.625
- second_d_skip: float32 [64], P('fsdp'), may hold values from 0.01 to 0.3
Outputs:
- out_tokens: bfloat16 [32, 512, 2048], P(('dp', 'fsdp'))
- grad_tokens: float32 [32, 512, 2048], P(('dp', 'fsdp'))
- new_w_in: float32 [2048, 8512], P('fsdp', 'dp')
- new_first_w_in: float32 [2048, 8512], P('fsdp', 'dp')
- new_second_w_in: float32 [2048, 8512], P('fsdp', 'dp')
- new_w_out: float32 [4096, 2048], P('fsdp', 'dp')
- new_first_w_out: float32 [4096, 2048], P('fsdp', 'dp')
- new_second_w_out: float32 [4096, 2048], P('fsdp', 'dp')
- step_norm_gain: float32 [2048], P('fsdp')
- new_first_norm_gain: float32 [2048], P('fsdp')
- new_second_norm_gain: float32 [2048], P('fsdp')
- step_gate_gain: float32 [4096], P('fsdp')
- new_first_gate_gain: float32 [4096], P('fsdp')
- new_second_gate_gain: float32 [4096], P('fsdp')
- step_conv_w: float32 [4, 4352], P(None, 'fsdp')
- new_first_conv_w: float32 [4, 4352], P(None, 'fsdp')
- new_second_conv_w: float32 [4, 4352], P(None, 'fsdp')
- step_conv_b: float32 [4352], P('fsdp')
- new_first_conv_b: float32 [4352], P('fsdp')
- new_second_conv_b: float32 [4352], P('fsdp')
- step_dt_bias: float32 [64], P('fsdp')
- new_first_dt_bias: float32 [64], P('fsdp')
- new_second_dt_bias: float32 [64], P('fsdp')
- step_a_log: float32 [64], P('fsdp')
- new_first_a_log: float32 [64], P('fsdp')
- new_second_a_log: float32 [64], P('fsdp')
- step_d_skip: float32 [64], P('fsdp')
- new_first_d_skip: float32 [64], P('fsdp')
- new_second_d_skip: float32 [64], P('fsdp')
Inputs may be any that keep to these rules, and one draw needn't show every extreme that they name: `doc_starts`: in every row the first start is 0 and the starts rise strictly; a document runs from its start to the next start or to the row's end. Tokens of a row at positions from valid_len on are padding. Some row is full and some row has the least length in every draw.
All inputs are finite; a program needn't handle non-finite values.
Results may differ from a plain program's by a relative error of at most 0.024.
The roundings to bfloat16 on the way count: a program that leaves them out, or rounds other values in their place, can miss the bound.
Values may be sent and summed in bfloat16 or wider, within the bound.
No kernel may reach another device: no remote copies, remote signals or barrier semaphores. Data moves between devices by JAX's collectives and lax.ppermute only.
A program may use at most 320 MiB of HBM per device.

v0:
```python
import math

import jax
import jax.numpy as jnp
from jax import lax
from jax.sharding import PartitionSpec as P

NH = 64
HP = 64
NS = 128
CONVW = 4
SPAN = 256
DI = 4096
CONV = 4352


EPSILON = 1e-05
BETA_ONE = 0.9
BETA_TWO = 0.95
ADAM_EPS = 1e-08
LEARN_RATE = 0.01
DECAY_RATE = 0.1
adam_step = 10
highest = lax.Precision.HIGHEST


def block_state(carry, inputs):
    carried_state, prev_segment = carry
    x_block, b_block, c_block, rate_block, step_block, seg_block = inputs
    block_len = seg_block.shape[0]
    row_index = jnp.arange(block_len, dtype=jnp.int32)
    lower_mask = row_index[:, None] >= row_index[None, :]
    cumulated = jnp.dot(lower_mask.astype(jnp.float32), rate_block, precision=highest)
    scores = jnp.dot(c_block, b_block.T, precision=highest)
    keep_mask = lower_mask & (seg_block[:, None] == seg_block[None, :])
    spread = cumulated[:, None, :] - cumulated[None, :, :]
    keep_float = keep_mask.astype(jnp.float32)[:, :, None]
    decay_table = jnp.exp(jnp.where(keep_mask[:, :, None], spread, 0.0)) * keep_float
    weights = scores[:, :, None] * decay_table * step_block[None, :, :]
    inside_part = jnp.einsum("tsh,shp->thp", weights, x_block, precision=highest)
    entering = (seg_block == prev_segment).astype(jnp.float32)
    reach = jnp.exp(cumulated) * entering[:, None]
    outside_part = (
        jnp.einsum("tn,hpn->thp", c_block, carried_state, precision=highest) * reach[:, :, None]
    )
    last_seg = seg_block[block_len - 1]
    same_last = (seg_block == last_seg).astype(jnp.float32)
    tail_weight = (
        jnp.exp(cumulated[block_len - 1][None, :] - cumulated) * same_last[:, None] * step_block
    )
    carried = jnp.exp(cumulated[block_len - 1]) * (last_seg == prev_segment).astype(jnp.float32)
    new_state = carried[:, None, None] * carried_state + jnp.einsum(
        "sh,shp,sn->hpn", tail_weight, x_block, b_block, precision=highest
    )
    return ((new_state, last_seg), inside_part + outside_part)


def mixer(projected, starts, gate_g, conv_weight, conv_bias, dt_shift, log_decay, skip_gain):
    length = projected.shape[0]
    gate_part = projected[:, :DI]
    conv_in = projected[:, DI : DI + CONV]
    raw_dt = projected[:, DI + CONV :]
    position = jnp.arange(length, dtype=jnp.int32)
    counted = jnp.sum((starts[None, :] <= position[:, None]).astype(jnp.int32), axis=1)
    segment = counted - 1
    convolved = jnp.zeros_like(conv_in) + conv_bias[None, :]
    for offset_k in range(CONVW):
        lag_rows = CONVW - 1 - offset_k
        moved = jnp.pad(conv_in, ((lag_rows, 0), (0, 0)))[:length]
        moved_seg = jnp.pad(segment, (lag_rows, 0), constant_values=-1)[:length]
        same_doc = (moved_seg == segment).astype(jnp.float32)
        convolved = convolved + conv_weight[offset_k][None, :] * moved * same_doc[:, None]
    activated = jax.nn.silu(convolved)
    x_heads = activated[:, :DI].reshape(length, NH, HP)
    b_input = activated[:, DI : DI + NS]
    c_input = activated[:, DI + NS :]
    step_size = jax.nn.softplus(raw_dt + dt_shift[None, :])
    decay_rates = step_size * (-jnp.exp(log_decay))[None, :]
    blocks = length // SPAN
    start_carry = (jnp.zeros((NH, HP, NS), jnp.float32), jnp.array(-1, dtype=jnp.int32))
    scan_inputs = (
        x_heads.reshape(blocks, SPAN, NH, HP),
        b_input.reshape(blocks, SPAN, NS),
        c_input.reshape(blocks, SPAN, NS),
        decay_rates.reshape(blocks, SPAN, NH),
        step_size.reshape(blocks, SPAN, NH),
        segment.reshape(blocks, SPAN),
    )
    unused, outputs = lax.scan(jax.checkpoint(block_state), start_carry, scan_inputs)
    scanned = outputs.reshape(length, NH, HP) + skip_gain[None, :, None] * x_heads
    gated_out = scanned.reshape(length, DI) * jax.nn.silu(gate_part)
    return (
        gated_out
        * lax.rsqrt(jnp.mean(gated_out * gated_out, axis=-1, keepdims=True) + EPSILON)
        * gate_g[None, :]
    )


def rms_scale(values, gain):
    return values * lax.rsqrt(jnp.mean(values * values, axis=-1, keepdims=True) + EPSILON) * gain


def adam_direction(weight, gradient, first, second, decayed):
    first_new = BETA_ONE * first + (1.0 - BETA_ONE) * gradient
    second_new = BETA_TWO * second + (1.0 - BETA_TWO) * gradient * gradient
    first_hat = first_new / (1.0 - BETA_ONE**adam_step)
    second_hat = second_new / (1.0 - BETA_TWO**adam_step)
    direction = first_hat / (jnp.sqrt(second_hat) + ADAM_EPS)
    if decayed:
        direction = direction + DECAY_RATE * weight
    return (direction, first_new, second_new)


def shards(
    tokens,
    cotangent,
    doc_starts,
    valid_len,
    w_in,
    w_out,
    norm_gain,
    gate_gain,
    conv_w,
    conv_b,
    dt_bias,
    a_log,
    d_skip,
    first_w_in,
    second_w_in,
    first_w_out,
    second_w_out,
    first_norm_gain,
    second_norm_gain,
    first_gate_gain,
    second_gate_gain,
    first_conv_w,
    second_conv_w,
    first_conv_b,
    second_conv_b,
    first_dt_bias,
    second_dt_bias,
    first_a_log,
    second_a_log,
    first_d_skip,
    second_d_skip,
):
    hidden = tokens.astype(jnp.float32)
    row_total = hidden.shape[0]
    length = hidden.shape[1]
    in_rows, out_rows = (
        lax.all_gather(w_in.astype(jnp.bfloat16), "dp", axis=1, tiled=True),
        lax.all_gather(w_out.astype(jnp.bfloat16), "dp", axis=1, tiled=True),
    )
    gathered = (
        lax.all_gather(norm_gain.astype(jnp.bfloat16), "fsdp", axis=0, tiled=True),
        lax.all_gather(gate_gain.astype(jnp.bfloat16), "fsdp", axis=0, tiled=True),
        lax.all_gather(conv_w.astype(jnp.bfloat16), "fsdp", axis=1, tiled=True),
        lax.all_gather(conv_b.astype(jnp.bfloat16), "fsdp", axis=0, tiled=True),
        lax.all_gather(dt_bias.astype(jnp.bfloat16), "fsdp", axis=0, tiled=True),
        lax.all_gather(a_log.astype(jnp.bfloat16), "fsdp", axis=0, tiled=True),
        lax.all_gather(d_skip.astype(jnp.bfloat16), "fsdp", axis=0, tiled=True),
    )
    norm_full, gate_full, convw_full, convb_full, shift_full, logd_full, skip_full = [
        part_value.astype(jnp.float32) for part_value in gathered
    ]
    normed_f, norm_pull = jax.vjp(rms_scale, hidden, norm_full)
    normed = normed_f.astype(jnp.bfloat16)
    columns = normed
    projected = jnp.einsum(
        "rld,de->rle",
        columns,
        lax.all_gather(in_rows, "fsdp", axis=0, tiled=True),
        preferred_element_type=jnp.float32,
    )

    def mix_rows(values, gate_g, conv_weight, conv_bias, dt_shift, log_decay, skip_gain):
        return jax.vmap(mixer, in_axes=(0, 0, None, None, None, None, None, None))(
            values, doc_starts, gate_g, conv_weight, conv_bias, dt_shift, log_decay, skip_gain
        )

    mixed_f, mix_pull = jax.vjp(
        mix_rows, projected, gate_full, convw_full, convb_full, shift_full, logd_full, skip_full
    )
    mixed = mixed_f.astype(jnp.bfloat16)
    columns = mixed
    branch = jnp.einsum(
        "rli,id->rld",
        columns,
        lax.all_gather(out_rows, "fsdp", axis=0, tiled=True),
        preferred_element_type=jnp.float32,
    )
    position = jnp.arange(length, dtype=jnp.int32)
    live = (position[None, :] < valid_len[:, None]).astype(jnp.float32)[:, :, None]
    out_tokens = (hidden + branch * live).astype(jnp.bfloat16)
    upstream = cotangent.astype(jnp.float32)
    d_branch = (upstream * live).astype(jnp.bfloat16)
    d_mixed = jnp.einsum(
        "rld,id->rli",
        d_branch,
        lax.all_gather(out_rows, "fsdp", axis=0, tiled=True),
        preferred_element_type=jnp.float32,
    )
    d_project, d_gate, d_convw, d_convb, d_shift, d_logd, d_skip_g = mix_pull(d_mixed)
    d_low = d_project.astype(jnp.bfloat16)
    d_normed = jnp.einsum(
        "rle,de->rld",
        d_low,
        lax.all_gather(in_rows, "fsdp", axis=0, tiled=True),
        preferred_element_type=jnp.float32,
    )
    d_hidden, d_norm = norm_pull(d_normed)
    grad_tokens = upstream + d_hidden
    columns = mixed
    out_summed = lax.psum_scatter(
        jnp.einsum("rli,rld->id", columns, d_branch, preferred_element_type=jnp.float32).astype(
            jnp.bfloat16
        ),
        "fsdp",
        scatter_dimension=0,
        tiled=True,
    )
    columns = normed
    in_summed = lax.psum_scatter(
        jnp.einsum("rld,rle->de", columns, d_low, preferred_element_type=jnp.float32).astype(
            jnp.bfloat16
        ),
        "fsdp",
        scatter_dimension=0,
        tiled=True,
    )
    grad_in_shard, grad_out_shard = (
        lax.psum_scatter(in_summed, "dp", scatter_dimension=1, tiled=True).astype(jnp.float32),
        lax.psum_scatter(out_summed, "dp", scatter_dimension=1, tiled=True).astype(jnp.float32),
    )
    part_norm, part_gate, part_convw, part_convb, part_shift, part_logd, part_skip = (
        lax.psum_scatter(d_norm, "fsdp", scatter_dimension=0, tiled=True),
        lax.psum_scatter(d_gate, "fsdp", scatter_dimension=0, tiled=True),
        lax.psum_scatter(d_convw, "fsdp", scatter_dimension=1, tiled=True),
        lax.psum_scatter(d_convb, "fsdp", scatter_dimension=0, tiled=True),
        lax.psum_scatter(d_shift, "fsdp", scatter_dimension=0, tiled=True),
        lax.psum_scatter(d_logd, "fsdp", scatter_dimension=0, tiled=True),
        lax.psum_scatter(d_skip_g, "fsdp", scatter_dimension=0, tiled=True),
    )
    small_grads = lax.psum(
        (part_norm, part_gate, part_convw, part_convb, part_shift, part_logd, part_skip), "dp"
    )
    factor = 1.0 / math.sqrt(row_total * length * lax.axis_size("dp") * lax.axis_size("fsdp"))
    weight_list = (w_in, w_out, norm_gain, gate_gain, conv_w, conv_b, dt_bias, a_log, d_skip)
    grad_list = (grad_in_shard, grad_out_shard) + tuple(small_grads)
    first_list = (
        first_w_in,
        first_w_out,
        first_norm_gain,
        first_gate_gain,
        first_conv_w,
        first_conv_b,
        first_dt_bias,
        first_a_log,
        first_d_skip,
    )
    second_list = (
        second_w_in,
        second_w_out,
        second_norm_gain,
        second_gate_gain,
        second_conv_w,
        second_conv_b,
        second_dt_bias,
        second_a_log,
        second_d_skip,
    )
    decay_flags = (True, True, False, False, True, True, False, False, False)
    moved_flags = (True, True, False, False, False, False, False, False, False)
    results = []
    for weight, gradient, first, second, decayed, moved in zip(
        weight_list, grad_list, first_list, second_list, decay_flags, moved_flags
    ):
        direction, first_new, second_new = adam_direction(
            weight, gradient * factor, first, second, decayed
        )
        if moved:
            results.extend((weight - LEARN_RATE * direction, first_new, second_new))
        else:
            results.extend((direction, first_new, second_new))
    return (out_tokens, grad_tokens) + tuple(results)


def solution(mesh):
    placed = (
        P(("dp", "fsdp"), None, None),
        P(("dp", "fsdp"), None, None),
        P(("dp", "fsdp"), None),
        P(("dp", "fsdp")),
        P("fsdp", "dp"),
        P("fsdp", "dp"),
        P("fsdp"),
        P("fsdp"),
        P(None, "fsdp"),
        P("fsdp"),
        P("fsdp"),
        P("fsdp"),
        P("fsdp"),
        P("fsdp", "dp"),
        P("fsdp", "dp"),
        P("fsdp", "dp"),
        P("fsdp", "dp"),
        P("fsdp"),
        P("fsdp"),
        P("fsdp"),
        P("fsdp"),
        P(None, "fsdp"),
        P(None, "fsdp"),
        P("fsdp"),
        P("fsdp"),
        P("fsdp"),
        P("fsdp"),
        P("fsdp"),
        P("fsdp"),
        P("fsdp"),
        P("fsdp"),
    )
    return jax.shard_map(
        shards,
        mesh=mesh,
        in_specs=placed,
        out_specs=(
            P(("dp", "fsdp"), None, None),
            P(("dp", "fsdp"), None, None),
            P("fsdp", "dp"),
            P("fsdp", "dp"),
            P("fsdp", "dp"),
            P("fsdp", "dp"),
            P("fsdp", "dp"),
            P("fsdp", "dp"),
            P("fsdp"),
            P("fsdp"),
            P("fsdp"),
            P("fsdp"),
            P("fsdp"),
            P("fsdp"),
            P(None, "fsdp"),
            P(None, "fsdp"),
            P(None, "fsdp"),
            P("fsdp"),
            P("fsdp"),
            P("fsdp"),
            P("fsdp"),
            P("fsdp"),
            P("fsdp"),
            P("fsdp"),
            P("fsdp"),
            P("fsdp"),
            P("fsdp"),
            P("fsdp"),
            P("fsdp"),
        ),
        check_vma=False,
    )
```

profile of v0, /device:TPU:0, one launch (start us, length us, event | category | flops | bytes accessed | tf_op | source)
XLA Modules:
  0.0 2249.9 jit_solution(14524336943867327583)
XLA Ops:
  10.2 87.7 %all-gather.7.cloned.1.call-done = bf16[512,8512]{0,1:T(8,128)(2,1)} async-done(((bf16[512,1064]{0,1:T(8,128)(2,1)}), bf16[512,8512]{0,1:T(8,128)(2,1)}) %all-gather.7.cloned.1.call-update) | async-done | bytes 8716304 | tf_op jit(solution)/shard_map/all_gather | solution.py:151
  100.7 8.1 all-gather
  108.8 8.0 all_gather.43
  118.3 15.6 all-reduce.33
  134.6 7.6 all-gather.1
  146.1 261.8 %all-gather.9.cloned.1.call-done = bf16[2048,8512]{0,1:T(8,128)(2,1)} async-done(((bf16[512,8512]{0,1:T(8,128)(2,1)}), bf16[2048,8512]{0,1:T(8,128)(2,1)}) %all-gather.9.cloned.1.call-update) | async-done | bytes 34865168 | tf_op jit(solution)/shard_map/all_gather | solution.py:172
  407.9 25.8 %convolution_bitcast_fusion.3 = f32[1,512,8512]{1,2,0:T(8,128)} fusion(bf16[2048,8512]{0,1:T(8,128)(2,1)} %all-gather.9.cloned.1.call-done, bf16[1,512,2048]{2,1,0:T(8,128)(2,1)} %param.35, f32[2048]{0:T(1024)S(1)} %bitcast.587, f32[512]{0:T(512)S(1)} %fusion.182), kind=kOutput, calls=%fused_computation.185 | convolution fusion | flops 17855152128 | bytes 54405120 | tf_op jit(solution)/shard_map/rld,de->rle/dot_general | solution.py:169
  438.3 13.1 fusion.147
  459.5 10.5 reshape.1322
  470.1 7.9 copy.141
  478.0 7.3 broadcast.870.clone2
  485.3 265.1 %while.45 = (s32[]{:T(128)}, f32[1,64,64,128]{3,2,1,0:T(8,128)S(1)}, s32[1]{0:T(128)}, f32[2,1,256,64,64]{2,0,4,3,1:T(2,128)}, f32[2,1,64,64,128]{4,3,2,1,0:T(8,...) while((s32[]{:T(128)}, ...), condition=%wide.region_3.4_spmd.clone, body=%wide.region_2.3_spmd.clone.sunk | while | flops 6620644352 | bytes 50804972 | solution.py:89
  490.6 21.0 fusion.269
  511.7 5.3 fusion.270
  517.0 9.0 copy.225
  526.0 84.4 %dynamic_update_slice.84 = f32[2,1,256,64,64]{2,0,4,3,1:T(2,128)} dynamic-update-slice(f32[2,1,256,64,64]{2,0,4,3,1:T(2,128)} %get-tuple-element.1139, f32[1,1,256,64,64]{2,0,4,3,1:T(1,128)} %copy.225, s32[]{:T(128)S(6)} %copy.251, s32[]{:T(128)} %constant.218.clone.1..sunk, s32[]{:T(128)} %constant.218.clone.1..sunk, s32[]{:T(128)} %constant.218.clone.1..sunk, s32[]{:T(128)} %constant.218.clone.1..sunk) | dynamic-update-slice | bytes 8388612 | tf_op jit(solution)/shard_map/jvp(vmap())/while/body/jit(dynamic_update_index_in_dim)/dynamic_update_slice | solution.py:89
  622.9 21.0 fusion.269
  644.0 5.3 fusion.270
  649.3 9.0 copy.225
  658.3 84.4 %dynamic_update_slice.84 = f32[2,1,256,64,64]{2,0,4,3,1:T(2,128)} dynamic-update-slice(f32[2,1,256,64,64]{2,0,4,3,1:T(2,128)} %get-tuple-element.1139, f32[1,1,256,64,64]{2,0,4,3,1:T(1,128)} %copy.225, s32[]{:T(128)S(6)} %copy.251, s32[]{:T(128)} %constant.218.clone.1..sunk, s32[]{:T(128)} %constant.218.clone.1..sunk, s32[]{:T(128)} %constant.218.clone.1..sunk, s32[]{:T(128)} %constant.218.clone.1..sunk) | dynamic-update-slice | bytes 8388612 | tf_op jit(solution)/shard_map/jvp(vmap())/while/body/jit(dynamic_update_index_in_dim)/dynamic_update_slice | solution.py:89
  750.4 11.5 transpose.159
  762.0 13.6 multiply_reduce_fusion.9
  775.7 16.3 convolution_convert_fusion.1
  792.0 153.9 %reduce-scatter.12.cloned.1.call-done = bf16[1024,2048]{1,0:T(8,128)(2,1)} async-done(((bf16[4096,2048]{1,0:T(8,128)(2,1)}), bf16[1024,2048]{1,0:T(8,128)(2,1)}) %reduce-scatter.12.cloned.1.call-update) | async-done | bytes 4194320 | tf_op jit(solution)/shard_map/reduce_scatter | solution.py:214
  946.0 52.1 %reduce-scatter.14.cloned.1.call-done = bf16[1024,256]{1,0:T(8,128)(2,1)} async-done(((bf16[1024,2048]{1,0:T(8,128)(2,1)}), bf16[1024,256]{1,0:T(8,128)(2,1)}) %reduce-scatter.14.cloned.1.call-update) | async-done | bytes 524304 | tf_op jit(solution)/shard_map/reduce_scatter | solution.py:233
  1002.9 46.1 %all-gather.11.cloned.1.call-done = bf16[1024,2048]{1,0:T(8,128)(2,1)} async-done(((bf16[1024,256]{1,0:T(8,128)(2,1)}), bf16[1024,2048]{1,0:T(8,128)(2,1)}) %all-gather.11.cloned.1.call-update) | async-done | bytes 4194320 | tf_op jit(solution)/shard_map/all_gather | solution.py:152
  1049.1 157.3 %all-gather.13.cloned.1.call-done = bf16[4096,2048]{1,0:T(8,128)(2,1)} async-done(((bf16[1024,2048]{1,0:T(8,128)(2,1)}), bf16[4096,2048]{1,0:T(8,128)(2,1)}) %all-gather.13.cloned.1.call-update) | async-done | bytes 16777232 | tf_op jit(solution)/shard_map/all_gather | solution.py:189
  1206.4 15.9 fusion.151
  1222.3 18.2 multiply_reduce_fusion.8
  1240.5 10.5 reshape.1327
  1253.9 7.4 broadcast.870.clone
  1261.4 427.8 %while.46 = (s32[]{:T(128)}, f32[1,64,64,128]{3,2,1,0:T(8,128)}, f32[2,1,256,64,64]{2,0,4,3,1:T(2,128)}, f32[2,1,256,128]{2,0,3,1:T(2,128)}, f32[2,1,256,128]{3,...) while((s32[]{:T(128)}, f32[1,64,64,128]{3,2,1,0:T(8,128)}, ...), condition=%wide.region_14.15_spmd.clone, body=%wide.region_6.14_spmd.clone.sunk | while | flops 14994834432 | bytes 196890240 | solution.py:89
  1267.0 9.7 constant_dynamic-slice_fusion.9
  1276.8 7.9 copy_bitcast_fusion.3
  1290.2 6.9 fusion.299
  1298.3 29.7 %fusion.292 = (f32[256,64]{0,1:T(8,128)}, f32[256,64]{0,1:T(8,128)}, f32[256,64]{0,1:T(8,128)S(1)}, f32[256,256]{1,0:T(8,128)S(1)}) fusion(f32[256,256]{1,0:T(8,128)S(1)} %fusion.289, f32[256,256]{1,0:T(8,128)S(1)} %get-tuple-element.1100, f32[256,64]{0,1:T(8,128)S(1)} %fusion.291, f32[256,64]{0,1:T(8,128)S(1)} %bitcast.559, ...), kind=kOutput, calls=%fused_computation.78.clone.1 | convolution fusion | flops 3284025344 | bytes 9568256 | tf_op jit(solution)/shard_map/transpose(jvp(vmap()))/while/body/eval_jaxpr/checkpoint/tsh,shp->thp/dot_general | solution.py:40
  1333.8 6.7 fusion.297
  1344.7 5.9 fusion.296
  1350.6 18.2 fusion.295
  1373.6 9.1 copy.228
  1386.0 84.4 %dynamic_update_slice.87 = f32[2,1,256,64,64]{2,0,4,3,1:T(2,128)} dynamic-update-slice(f32[2,1,256,64,64]{2,0,4,3,1:T(2,128)} %get-tuple-element.1184, f32[1,1,256,64,64]{2,0,4,3,1:T(1,128)} %copy.228, s32[]{:T(128)S(6)} %sub.294, s32[]{:T(128)} %constant.218.clone.1..sunk.1, s32[]{:T(128)} %constant.218.clone.1..sunk.1, s32[]{:T(128)} %constant.218.clone.1..sunk.1, s32[]{:T(128)} %constant.218.clone.1..sunk.1) | dynamic-update-slice | bytes 8388612 | tf_op jit(solution)/shard_map/transpose(jvp(vmap()))/while/body/jit(dynamic_update_index_in_dim)/dynamic_update_slice | solution.py:89
  1477.9 9.7 constant_dynamic-slice_fusion.9
  1487.7 7.9 copy_bitcast_fusion.3
  1501.1 6.9 fusion.299
  1509.2 29.4 %fusion.292 = (f32[256,64]{0,1:T(8,128)}, f32[256,64]{0,1:T(8,128)}, f32[256,64]{0,1:T(8,128)S(1)}, f32[256,256]{1,0:T(8,128)S(1)}) fusion(f32[256,256]{1,0:T(8,128)S(1)} %fusion.289, f32[256,256]{1,0:T(8,128)S(1)} %get-tuple-element.1100, f32[256,64]{0,1:T(8,128)S(1)} %fusion.291, f32[256,64]{0,1:T(8,128)S(1)} %bitcast.559, ...), kind=kOutput, calls=%fused_computation.78.clone.1 | convolution fusion | flops 3284025344 | bytes 9568256 | tf_op jit(solution)/shard_map/transpose(jvp(vmap()))/while/body/eval_jaxpr/checkpoint/tsh,shp->thp/dot_general | solution.py:40
  1544.4 6.7 fusion.297
  1555.3 5.9 fusion.296
  1561.2 18.4 fusion.295
  1584.4 9.1 copy.228
  1596.9 84.4 %dynamic_update_slice.87 = f32[2,1,256,64,64]{2,0,4,3,1:T(2,128)} dynamic-update-slice(f32[2,1,256,64,64]{2,0,4,3,1:T(2,128)} %get-tuple-element.1184, f32[1,1,256,64,64]{2,0,4,3,1:T(1,128)} %copy.228, s32[]{:T(128)S(6)} %sub.294, s32[]{:T(128)} %constant.218.clone.1..sunk.1, s32[]{:T(128)} %constant.218.clone.1..sunk.1, s32[]{:T(128)} %constant.218.clone.1..sunk.1, s32[]{:T(128)} %constant.218.clone.1..sunk.1) | dynamic-update-slice | bytes 8388612 | tf_op jit(solution)/shard_map/transpose(jvp(vmap()))/while/body/jit(dynamic_update_index_in_dim)/dynamic_update_slice | solution.py:89
  1693.4 11.5 transpose.164
  1705.0 9.9 multiply_add_fusion.1
  1714.9 28.4 %multiply_reduce_fusion.6 = (f32[4352]{0:T(1024)S(1)}, f32[4352]{0:T(1024)S(1)}, f32[4352]{0:T(1024)S(1)}, f32[4352]{0:T(1024)S(1)}, f32[4352]{0:T(1024)S(1)}, /*index=5*/f32[1,512,4352]{1,2,0:T(8,128)}) fusion(f32[1,512,4352]{1,2,0:T(8,128)} %copy-done.6, f32[512]{0:T(512)S(1)} %bitcast.585, f32[512]{0:T(512)S(1)} %bitcast.582, f32[512]{0:T(512)S(1)} %bitcast.579, ...), kind=kLoop, calls=%fused_computation.202 | loop fusion | flops 51227392 | bytes 44657664 | tf_op jit(solution)/shard_map/transpose(jvp(vmap()))/reduce_sum | solution.py:72
  1743.4 13.4 multiply_multiply_fusion.1
  1757.9 14.0 fusion.144
  1772.0 29.3 %convolution_convert_fusion = bf16[2048,8512]{0,1:T(8,128)(2,1)} fusion(bf16[1,512,2048]{2,1,0:T(8,128)(2,1)S(1)} %copy-done.9, f32[2048]{0:T(1024)S(1)} %bitcast.588, f32[512]{0:T(512)S(1)} %copy-done.60, f32[1,512,4096]{1,2,0:T(8,128)} %get-tuple-element.854, f32[1,512,4352]{1,2,0:T(8,128)} %fusion.144, f32[1,512,64]{1,2,0:T(8,128)S(1)} %get-tuple-element.820), kind=kOutput, calls=%fused_computation.182 | convolution fusion | flops 17885659136 | bytes 54405120 | tf_op jit(solution)/shard_map/rld,rle->de/dot_general | solution.py:224
  1803.6 297.0 %reduce-scatter.8.cloned.1.call-done = bf16[512,8512]{0,1:T(8,128)(2,1)} async-done(((bf16[2048,8512]{0,1:T(8,128)(2,1)}), bf16[512,8512]{0,1:T(8,128)(2,1)}) %reduce-scatter.8.cloned.1.call-update) | async-done | bytes 8716304 | tf_op jit(solution)/shard_map/reduce_scatter | solution.py:223
  2103.5 33.5 %fusion.157 = (f32[2048]{0:T(1024)S(1)}, f32[512]{0:T(512)S(1)}, f32[512,2048]{1,0:T(8,128)}) fusion(bf16[1,512,2048]{2,1,0:T(8,128)(2,1)S(1)} %copy-done.9, f32[512]{0:T(512)S(1)} %copy-done.60, f32[2048]{0:T(1024)S(1)} %bitcast.589, bf16[2048,8512]{0,1:T(8,128)(2,1)} %all-gather.9.cloned.1.call-done, f32[1,512,4096]{1,2,0:T(8,128)} %get-tuple-element.854, ...), kind=kOutput, calls=%fused_computation.235 | convolution fusion | flops 17871370240 | bytes 58609664 | tf_op jit(solution)/shard_map/rle,de->rld/dot_general | solution.py:205
  2137.0 16.1 all-reduce.32
  2153.6 6.3 convert_add_fusion.1
  2160.1 16.3 fusion.160
  2177.6 28.9 %all-reduce.31 = (f32[512]{0:T(512)S(1)}, f32[1024]{0:T(1024)S(1)}, f32[4,1088]{1,0:T(4,128)S(1)}, f32[1088]{0:T(1024)S(1)}, f32[16]{0:T(128)S(1)}, /*index=5*/f32[16]{0:T(128)S(1)}, f32[16]{0:T(128)S(1)}) all-reduce(f32[512]{0:T(512)S(1)} %dynamic-slice.5, f32[1024]{0:T(1024)S(1)} %dynamic-slice.7, ...), channel_id=1, replica_groups=mesh['dp'=8,'fsdp'=4] {'dp'}, use_global_device_ids=true, to_apply=%region_22.23 | all-reduce | flops 7024 | bytes 56192 | tf_op jit(solution)/shard_map/psum | solution.py:244
  2210.2 26.4 %reduce-scatter.10.cloned.1.call-done = bf16[512,1064]{0,1:T(8,128)(2,1)} async-done(((bf16[512,8512]{0,1:T(8,128)(2,1)}), bf16[512,1064]{0,1:T(8,128)(2,1)}) %reduce-scatter.10.cloned.1.call-update) | async-done | bytes 1089552 | tf_op jit(solution)/shard_map/reduce_scatter | solution.py:232
  2236.6 6.6 multiply_subtract_fusion
  (404 shorter events, 124.8 us)
Async XLA Ops:
  7.2 91.4 %copy-start.72 = (u32[32]{0:T(128)S(1)}, u32[32]{0:T(128)}, u32[]{:S(2)}) copy-start(u32[32]{0:T(128)} %constant.286) | copy-start | bytes 388
  7.2 93.3 %copy-start.85 = (f32[16]{0:T(128)S(1)}, f32[16]{0:T(128)}, u32[]{:S(2)}) copy-start(f32[16]{0:T(128)} %param.45) | copy-start | bytes 196
  7.2 93.3 %copy-start.86 = (f32[16]{0:T(128)S(1)}, f32[16]{0:T(128)}, u32[]{:S(2)}) copy-start(f32[16]{0:T(128)} %param.46) | copy-start | bytes 196
  7.2 93.3 %copy-start.87 = (f32[16]{0:T(128)S(1)}, f32[16]{0:T(128)}, u32[]{:S(2)}) copy-start(f32[16]{0:T(128)} %param.47) | copy-start | bytes 196
  7.2 93.3 %copy-start.75 = (f32[512]{0:T(512)S(1)}, f32[512]{0:T(512)}, u32[]{:S(2)}) copy-start(f32[512]{0:T(512)} %param.41) | copy-start | bytes 6148
  7.3 93.4 %copy-start.65 = (f32[1024]{0:T(1024)S(1)}, f32[1024]{0:T(1024)}, u32[]{:S(2)}) copy-start(f32[1024]{0:T(1024)} %param.42) | copy-start | bytes 12292
  7.3 93.4 %copy-start.52 = (f32[1088]{0:T(1024)S(1)}, f32[1088]{0:T(1024)}, u32[]{:S(2)}) copy-start(f32[1088]{0:T(1024)} %param.44) | copy-start | bytes 13060
  7.3 127.4 %copy-start.37 = (f32[4,1088]{1,0:T(4,128)S(1)}, f32[4,1088]{1,0:T(4,128)}, u32[]{:S(2)}) copy-start(f32[4,1088]{1,0:T(4,128)} %param.43) | copy-start | bytes 52228
  7.3 135.7 %copy-start.78 = (s32[1,4]{1,0:T(1,128)S(1)}, s32[1,4]{1,0:T(1,128)}, u32[]{:S(2)}) copy-start(s32[1,4]{1,0:T(1,128)} %param.37) | copy-start | bytes 52
  7.3 90.6 %all-gather.7.cloned.1.call-start = ((), (), s32[]{:S(2)}) async-start(), calls=%async_computation.5 | async-start | bytes 9805824 | tf_op jit(solution)/shard_map/all_gather | solution.py:151
  10.1 397.8 %all-gather.9.cloned.1.call-start = ((), (), s32[]{:S(2)}) async-start(), calls=%async_computation.6 | async-start | bytes 43581440 | tf_op jit(solution)/shard_map/all_gather | solution.py:172
  97.9 848.1 %reduce-scatter.12.cloned.1.call-start = ((), (), s32[]{:S(2)}) async-start(), calls=%async_computation.11 | async-start | bytes 20971520 | tf_op jit(solution)/shard_map/reduce_scatter | solution.py:214
  108.7 324.9 %copy-start.50 = (f32[4,1,512]{2,1,0:T(1,128)}, f32[4,1,512]{2,1,0:T(1,128)S(1)}, u32[]{:S(2)}) copy-start(f32[4,1,512]{2,1,0:T(1,128)S(1)} %convert_element_type.226) | copy-start | bytes 24580
  133.9 299.8 %copy-start.88 = (bf16[64]{0:T(256)(128)(2,1)}, bf16[64]{0:T(256)(128)(2,1)S(1)}, u32[]{:S(2)}) copy-start(bf16[64]{0:T(256)(128)(2,1)S(1)} %get-tuple-element.791) | copy-start | bytes 388
  133.9 322.4 %copy-start.68 = (f32[64]{0:T(128)}, f32[64]{0:T(128)S(1)}, u32[]{:S(2)}) copy-start(f32[64]{0:T(128)S(1)} %convert_element_type.201) | copy-start | bytes 772
  143.3 295.0 %copy-start.29 = (f32[4352]{0:T(1024)}, f32[4352]{0:T(1024)S(1)}, u32[]{:S(2)}) copy-start(f32[4352]{0:T(1024)S(1)} %get-tuple-element.718) | copy-start | bytes 52228
  143.3 295.0 %copy-start.31 = (f32[4352]{0:T(1024)}, f32[4352]{0:T(1024)S(1)}, u32[]{:S(2)}) copy-start(f32[4352]{0:T(1024)S(1)} %get-tuple-element.717) | copy-start | bytes 52228
  143.3 295.0 %copy-start.33 = (f32[4352]{0:T(1024)}, f32[4352]{0:T(1024)S(1)}, u32[]{:S(2)}) copy-start(f32[4352]{0:T(1024)S(1)} %get-tuple-element.719) | copy-start | bytes 52228
  143.3 295.0 %copy-start.35 = (f32[4352]{0:T(1024)}, f32[4352]{0:T(1024)S(1)}, u32[]{:S(2)}) copy-start(f32[4352]{0:T(1024)S(1)} %get-tuple-element.720) | copy-start | bytes 52228
  143.3 312.9 %copy-start.70 = (f32[64]{0:T(128)}, f32[64]{0:T(128)S(1)}, u32[]{:S(2)}) copy-start(f32[64]{0:T(128)S(1)} %fusion.184) | copy-start | bytes 772
  145.4 288.2 %copy-start.59 = (f32[512]{0:T(512)}, f32[512]{0:T(512)S(1)}, u32[]{:S(2)}) copy-start(f32[512]{0:T(512)S(1)} %fusion.182) | copy-start | bytes 6148
  146.1 292.2 %copy-start.44 = (f32[1,512]{1,0:T(1,128)}, f32[1,512]{1,0:T(1,128)S(1)}, u32[]{:S(2)}) copy-start(f32[1,512]{1,0:T(1,128)S(1)} %get-tuple-element.862) | copy-start | bytes 6148
  146.1 292.2 %copy-start.46 = (f32[1,512]{1,0:T(1,128)}, f32[1,512]{1,0:T(1,128)S(1)}, u32[]{:S(2)}) copy-start(f32[1,512]{1,0:T(1,128)S(1)} %get-tuple-element.863) | copy-start | bytes 6148
  146.1 292.2 %copy-start.48 = (f32[1,512]{1,0:T(1,128)}, f32[1,512]{1,0:T(1,128)S(1)}, u32[]{:S(2)}) copy-start(f32[1,512]{1,0:T(1,128)S(1)} %get-tuple-element.864) | copy-start | bytes 6148
  775.7 446.7 %copy-start.61 = (f32[512]{0:T(512)}, f32[512]{0:T(512)S(1)}, u32[]{:S(2)}) copy-start(f32[512]{0:T(512)S(1)} %fusion.183) | copy-start | bytes 6148
  792.0 206.2 %reduce-scatter.14.cloned.1.call-start = ((), (), s32[]{:S(2)}) async-start(), calls=%async_computation.12 | async-start | bytes 4718592 | tf_op jit(solution)/shard_map/reduce_scatter | solution.py:233
  946.0 103.0 %all-gather.11.cloned.1.call-start = ((), (), s32[]{:S(2)}) async-start(), calls=%async_computation.7 | async-start | bytes 4718592 | tf_op jit(solution)/shard_map/all_gather | solution.py:152
  1002.9 203.5 %all-gather.13.cloned.1.call-start = ((), (), s32[]{:S(2)}) async-start(), calls=%async_computation.8 | async-start | bytes 20971520 | tf_op jit(solution)/shard_map/all_gather | solution.py:189
  1049.0 1051.6 %reduce-scatter.8.cloned.1.call-start = ((), (), s32[]{:S(2)}) async-start(), calls=%async_computation.9 | async-start | bytes 43581440 | tf_op jit(solution)/shard_map/reduce_scatter | solution.py:223
  1297.6 30.4 %copy-start.18 = (pred[256,256]{1,0:T(8,128)(4,1)}, pred[256,256]{1,0:T(8,128)(4,1)S(1)}, u32[]{:S(2)}) copy-start(pred[256,256]{1,0:T(8,128)(4,1)S(1)} %get-tuple-element.1103) | copy-start | bytes 196612 | tf_op jit(solution)/shard_map/transpose(jvp(vmap()))/while
  1298.3 30.1 %copy-start.2 = (f32[1,256,64,64]{1,3,2,0:T(8,128)S(1)}, f32[1,256,64,64]{1,3,2,0:T(8,128)}, u32[]{:S(2)}) copy-start(f32[1,256,64,64]{1,3,2,0:T(8,128)} %get-tuple-element.1104) | copy-start | bytes 12582916 | tf_op jit(solution)/shard_map/transpose(jvp(vmap()))/while
  1384.2 86.3 %copy-start.26 = (f32[2,1,256,64]{2,0,3,1:T(2,128)}, f32[2,1,256,64]{2,0,3,1:T(2,128)S(1)}, u32[]{:S(2)}) copy-start(f32[2,1,256,64]{2,0,3,1:T(2,128)S(1)} %dynamic_update_slice.89) | copy-start | bytes 393220 | tf_op jit(solution)/shard_map/transpose(jvp(vmap()))/while
  1386.0 84.5 %copy-start.22 = (f32[2,1,256,128]{2,0,3,1:T(2,128)}, f32[2,1,256,128]{2,0,3,1:T(2,128)S(1)}, u32[]{:S(2)}) copy-start(f32[2,1,256,128]{2,0,3,1:T(2,128)S(1)} %dynamic_update_slice.88) | copy-start | bytes 786436 | tf_op jit(solution)/shard_map/transpose(jvp(vmap()))/while
  1508.5 30.1 %copy-start.18 = (pred[256,256]{1,0:T(8,128)(4,1)}, pred[256,256]{1,0:T(8,128)(4,1)S(1)}, u32[]{:S(2)}) copy-start(pred[256,256]{1,0:T(8,128)(4,1)S(1)} %get-tuple-element.1103) | copy-start | bytes 196612 | tf_op jit(solution)/shard_map/transpose(jvp(vmap()))/while
  1509.2 29.8 %copy-start.2 = (f32[1,256,64,64]{1,3,2,0:T(8,128)S(1)}, f32[1,256,64,64]{1,3,2,0:T(8,128)}, u32[]{:S(2)}) copy-start(f32[1,256,64,64]{1,3,2,0:T(8,128)} %get-tuple-element.1104) | copy-start | bytes 12582916 | tf_op jit(solution)/shard_map/transpose(jvp(vmap()))/while
  1595.1 86.3 %copy-start.26 = (f32[2,1,256,64]{2,0,3,1:T(2,128)}, f32[2,1,256,64]{2,0,3,1:T(2,128)S(1)}, u32[]{:S(2)}) copy-start(f32[2,1,256,64]{2,0,3,1:T(2,128)S(1)} %dynamic_update_slice.89) | copy-start | bytes 393220 | tf_op jit(solution)/shard_map/transpose(jvp(vmap()))/while
  1596.9 84.5 %copy-start.22 = (f32[2,1,256,128]{2,0,3,1:T(2,128)}, f32[2,1,256,128]{2,0,3,1:T(2,128)S(1)}, u32[]{:S(2)}) copy-start(f32[2,1,256,128]{2,0,3,1:T(2,128)S(1)} %dynamic_update_slice.88) | copy-start | bytes 786436 | tf_op jit(solution)/shard_map/transpose(jvp(vmap()))/while
  1714.8 28.5 %copy-start.32 = (f32[4352]{0:T(1024)S(1)}, f32[4352]{0:T(1024)}, u32[]{:S(2)}) copy-start(f32[4352]{0:T(1024)} %copy-done.31) | copy-start | bytes 52228
  1714.8 28.5 %copy-start.34 = (f32[4352]{0:T(1024)S(1)}, f32[4352]{0:T(1024)}, u32[]{:S(2)}) copy-start(f32[4352]{0:T(1024)} %copy-done.33) | copy-start | bytes 52228
  1714.8 28.5 %copy-start.36 = (f32[4352]{0:T(1024)S(1)}, f32[4352]{0:T(1024)}, u32[]{:S(2)}) copy-start(f32[4352]{0:T(1024)} %copy-done.35) | copy-start | bytes 52228
  1801.3 302.0 %copy-start.39 = (f32[4096]{0:T(1024)S(1)}, f32[4096]{0:T(1024)}, u32[]{:S(2)}) copy-start(f32[4096]{0:T(1024)} %get-tuple-element.817) | copy-start | bytes 49156
  1801.3 302.2 %copy-start.89 = (bf16[64]{0:T(256)(128)(2,1)S(1)}, bf16[64]{0:T(256)(128)(2,1)}, u32[]{:S(2)}) copy-start(bf16[64]{0:T(256)(128)(2,1)} %copy-done.88) | copy-start | bytes 388
  1801.3 375.1 %reduce-scatter.16.cloned.1.call-start = ((), (), s32[]{:S(2)}) async-start(), calls=%async_computation.13 | async-start | bytes 2785280
  1803.6 433.1 %reduce-scatter.10.cloned.1.call-start = ((), (), s32[]{:S(2)}) async-start(), calls=%async_computation.10 | async-start | bytes 9805824 | tf_op jit(solution)/shard_map/reduce_scatter | solution.py:232
  2103.5 33.6 %copy-start.58 = (f32[4096]{0:T(1024)S(1)}, f32[4096]{0:T(1024)}, u32[]{:S(2)}) copy-start(f32[4096]{0:T(1024)} %get-tuple-element.711) | copy-start | bytes 49156
  2103.5 50.1 %copy-start.55 = (f32[512]{0:T(512)S(1)}, f32[512]{0:T(512)}, u32[]{:S(2)}) copy-start(f32[512]{0:T(512)} %copy-done.54) | copy-start | bytes 6148
  2137.0 22.8 %copy-start.74 = (f32[512]{0:T(512)S(1)}, f32[512]{0:T(512)}, u32[]{:S(2)}) copy-start(f32[512]{0:T(512)} %fusion.181) | copy-start | bytes 6148
  2159.9 46.7 %copy-start.83 = (f32[16]{0:T(128)S(1)}, f32[16]{0:T(128)}, u32[]{:S(2)}) copy-start(f32[16]{0:T(128)} %param.60) | copy-start | bytes 196
  2159.9 46.7 %copy-start.84 = (f32[16]{0:T(128)S(1)}, f32[16]{0:T(128)}, u32[]{:S(2)}) copy-start(f32[16]{0:T(128)} %param.61) | copy-start | bytes 196
  2159.9 47.2 %copy-start.79 = (f32[16]{0:T(128)S(1)}, f32[16]{0:T(128)}, u32[]{:S(2)}) copy-start(f32[16]{0:T(128)} %param.64) | copy-start | bytes 196
  2159.9 47.2 %copy-start.80 = (f32[16]{0:T(128)S(1)}, f32[16]{0:T(128)}, u32[]{:S(2)}) copy-start(f32[16]{0:T(128)} %param.65) | copy-start | bytes 196
  2159.9 47.2 %copy-start.81 = (f32[16]{0:T(128)S(1)}, f32[16]{0:T(128)}, u32[]{:S(2)}) copy-start(f32[16]{0:T(128)} %param.63) | copy-start | bytes 196
  2159.9 47.2 %copy-start.82 = (f32[16]{0:T(128)S(1)}, f32[16]{0:T(128)}, u32[]{:S(2)}) copy-start(f32[16]{0:T(128)} %param.62) | copy-start | bytes 196
  2159.9 47.8 %copy-start.76 = (f32[512]{0:T(512)S(1)}, f32[512]{0:T(512)}, u32[]{:S(2)}) copy-start(f32[512]{0:T(512)} %param.52) | copy-start | bytes 6148
  2160.0 47.7 %copy-start.77 = (f32[512]{0:T(512)S(1)}, f32[512]{0:T(512)}, u32[]{:S(2)}) copy-start(f32[512]{0:T(512)} %param.53) | copy-start | bytes 6148
  2160.0 48.3 %copy-start.66 = (f32[1024]{0:T(1024)S(1)}, f32[1024]{0:T(1024)}, u32[]{:S(2)}) copy-start(f32[1024]{0:T(1024)} %param.54) | copy-start | bytes 12292
  2160.0 48.3 %copy-start.67 = (f32[1024]{0:T(1024)S(1)}, f32[1024]{0:T(1024)}, u32[]{:S(2)}) copy-start(f32[1024]{0:T(1024)} %param.55) | copy-start | bytes 12292
  2160.0 48.9 %copy-start.53 = (f32[1088]{0:T(1024)S(1)}, f32[1088]{0:T(1024)}, u32[]{:S(2)}) copy-start(f32[1088]{0:T(1024)} %param.44) | copy-start | bytes 13060
  2160.0 48.9 %copy-start.63 = (f32[1088]{0:T(1024)S(1)}, f32[1088]{0:T(1024)}, u32[]{:S(2)}) copy-start(f32[1088]{0:T(1024)} %param.58) | copy-start | bytes 13060
  2160.0 48.9 %copy-start.64 = (f32[1088]{0:T(1024)S(1)}, f32[1088]{0:T(1024)}, u32[]{:S(2)}) copy-start(f32[1088]{0:T(1024)} %param.59) | copy-start | bytes 13060
  2160.0 49.5 %copy-start.38 = (f32[4,1088]{1,0:T(4,128)S(1)}, f32[4,1088]{1,0:T(4,128)}, u32[]{:S(2)}) copy-start(f32[4,1088]{1,0:T(4,128)} %param.43) | copy-start | bytes 52228
  2160.0 49.5 %copy-start.56 = (f32[4,1088]{1,0:T(4,128)S(1)}, f32[4,1088]{1,0:T(4,128)}, u32[]{:S(2)}) copy-start(f32[4,1088]{1,0:T(4,128)} %param.56) | copy-start | bytes 52228
  2160.1 49.5 %copy-start.57 = (f32[4,1088]{1,0:T(4,128)S(1)}, f32[4,1088]{1,0:T(4,128)}, u32[]{:S(2)}) copy-start(f32[4,1088]{1,0:T(4,128)} %param.57) | copy-start | bytes 52228
  2160.1 76.6 %copy-start.8 = (f32[512,1064]{0,1:T(8,128)S(1)}, f32[512,1064]{0,1:T(8,128)}, u32[]{:S(2)}) copy-start(f32[512,1064]{0,1:T(8,128)} %param.39) | copy-start | bytes 6537220
  (55 other events, 575.9 us)
Sparse Core Ops, SparseCore 0:
  10.4 87.4 all-gather.6
  99.7 308.1 all-gather.8
  792.1 153.8 reduce-scatter.11
  948.1 50.0 reduce-scatter.13
  1003.0 45.9 all-gather.10
  1050.7 155.6 all-gather.12
  1801.4 299.2 reduce-scatter.7
  2103.9 36.2 reduce-scatter.15
  2142.7 93.9 reduce-scatter.9
where the time goes:
time: 2280 us; the launch traced here: 2250 us
  waiting for transfers between devices  1080 us (47%)
  local copies, waits for them, and re-layouts  531 us (23%)
  matrix products  360 us (16%)
  other arithmetic  157 us (7%)
  blocking collectives  84.4 us (4%)
    dynamic_update_slice x22, local copies, waits for them, and re-layouts, mixer(): lax.scan(jax.checkpoint(block_state), start_carry, scan_inputs)  387 us
    reduce_scatter x1, waiting for transfers between devices, shards(): lax.psum_scatter(jnp.einsum('rld,rle->de', columns, d_low, preferred_elem...  297 us
    all_gather x1, waiting for transfers between devices, shards(): lax.all_gather(in_rows, 'fsdp', axis=0, tiled=True)  262 us
    all_gather x1, waiting for transfers between devices, shards(): lax.all_gather(out_rows, 'fsdp', axis=0, tiled=True)  157 us
    reduce_scatter x1, waiting for transfers between devices, shards(): lax.psum_scatter(jnp.einsum('rli,rld->id', columns, d_branch, preferred_e...  154 us
    dot_general x6, matrix products, block_state(): jnp.einsum('tsh,shp->thp', weights, x_block, precision=highest)  138 us
    all_gather x1, waiting for transfers between devices, shards(): lax.all_gather(w_in.astype(jnp.bfloat16), 'dp', axis=1, tiled=True)  87.7 us
    reduce_scatter x1, waiting for transfers between devices, shards(): lax.psum_scatter(out_summed, 'dp', scatter_dimension=1, tiled=True)  52.1 us
  transfers between devices with their start and end apart: 9, of which 8 were waited for; matrix products, arithmetic and copies ran while one was open for 3% of the time, Pallas kernels for 0%

commit v1 on v0

v1 whole, which is shorter than its diff:
```python
import functools
import math

import jax
import jax.numpy as jnp
from jax import lax
from jax.experimental import pallas as pl
from jax.experimental.pallas import tpu as pltpu
from jax.sharding import PartitionSpec as P

NH = 64
HP = 64
NS = 128
CONVW = 4
DI = 4096
CONV = 4352

EPSILON = 1e-05
BETA_ONE = 0.9
BETA_TWO = 0.95
ADAM_EPS = 1e-08
LEARN_RATE = 0.01
DECAY_RATE = 0.1
adam_step = 10
highest = lax.Precision.HIGHEST

Q = 128
BC = 512
HB = BC // HP
PAIRS = BC // 128
F32 = jnp.float32
BF16 = jnp.bfloat16


def dot(a, b):
    return jnp.dot(a, b, preferred_element_type=F32)


def dot_nt(a, b):
    return lax.dot_general(a, b, (((1,), (1,)), ((), ())), preferred_element_type=F32)


def sigmoid(v):
    return 1.0 / (1.0 + jnp.exp(-v))


def segment_of(starts_ref, position):
    count = jnp.zeros_like(position)
    for k in range(starts_ref.shape[1]):
        count = count + (starts_ref[0, k] <= position).astype(jnp.int32)
    return count


def conv_forward(values, weights, bias, same_ref):
    total = values * weights[CONVW - 1 : CONVW] + bias
    for lag in range(1, CONVW):
        moved = pltpu.roll(values, lag, 0) * same_ref[lag - 1]
        total = total + moved * weights[CONVW - 1 - lag : CONVW - lag]
    return total


def conv_backward(d_conv, values, weights, same_ref):
    length = values.shape[0]
    d_in = d_conv * weights[CONVW - 1 : CONVW]
    sums = [jnp.sum(d_conv * values, axis=0, keepdims=True)]
    for lag in range(1, CONVW):
        masked = d_conv * same_ref[lag - 1]
        sums.append(jnp.sum(masked * pltpu.roll(values, lag, 0), axis=0, keepdims=True))
        d_in = d_in + pltpu.roll(masked, length - lag, 0) * weights[CONVW - 1 - lag : CONVW - lag]
    return d_in, jnp.concatenate(sums[::-1], axis=0), jnp.sum(d_conv, axis=0, keepdims=True)


def prepare_masks(starts_ref, length, same_ref, enter_ref, last_ref):
    col = lax.broadcasted_iota(jnp.int32, (length, 128), 0)
    seg = segment_of(starts_ref, col)
    for lag in range(1, CONVW):
        same_ref[lag - 1] = (segment_of(starts_ref, col - lag) == seg).astype(F32)
    begin = col - lax.rem(col, Q)
    enter_ref[...] = ((segment_of(starts_ref, begin - 1) == seg) & (begin > 0)).astype(F32)
    last_ref[...] = (segment_of(starts_ref, begin + (Q - 1)) == seg).astype(F32)


def keep_mask(starts_ref, chunk):
    rows = lax.broadcasted_iota(jnp.int32, (Q, Q), 0) + chunk * Q
    cols = lax.broadcasted_iota(jnp.int32, (Q, Q), 1) + chunk * Q
    return (rows >= cols) & (segment_of(starts_ref, rows) == segment_of(starts_ref, cols))


def step_rows(dt_ref, shift_ref, logd_ref):
    pre = dt_ref[...] + shift_ref[...]
    step = jnp.maximum(pre, 0.0) + jnp.log1p(jnp.exp(-jnp.abs(pre)))
    decay = jnp.exp(logd_ref[...])
    return pre, step, -step * decay, decay


def cumulate(rate, chunks):
    rows = lax.broadcasted_iota(jnp.int32, (Q, Q), 0)
    cols = lax.broadcasted_iota(jnp.int32, (Q, Q), 1)
    upper = (rows <= cols).astype(F32)
    parts = [
        jnp.dot(rate[:, c * Q : (c + 1) * Q], upper, precision=highest, preferred_element_type=F32)
        for c in range(chunks)
    ]
    return jnp.concatenate(parts, axis=1)


def halves(lo, pair):
    zero = jnp.zeros_like(pair)
    return jnp.concatenate([jnp.where(lo, pair, zero), jnp.where(lo, zero, pair)], axis=0)


def forward_kernel(
    starts_ref, gate_ref, xin_ref, bc_ref, dt_ref, cw_ref, cb_ref, cwbc_ref, cbbc_ref,
    shift_ref, logd_ref, skip_ref, gain_ref,
    mixed_ref, y_ref, state_ref, q_ref,
    same_ref, enter_ref, last_ref, cmat_ref, bt_ref, score_ref, gated_ref, square_ref,
    x_ref, carry_ref, step_ref, cum_ref, cumt_ref,
):
    j = pl.program_id(0)
    length = gate_ref.shape[0]
    chunks = length // Q
    lo = lax.broadcasted_iota(jnp.int32, (Q, 128), 1) < HP

    @pl.when(j == 0)
    def _():
        prepare_masks(starts_ref, length, same_ref, enter_ref, last_ref)
        square_ref[...] = jnp.zeros_like(square_ref)
        both = []
        for part in range(2):
            cols = slice(part * NS, (part + 1) * NS)
            conv = conv_forward(bc_ref[:, cols].astype(F32), cwbc_ref[:, cols], cbbc_ref[:, cols], same_ref)
            both.append(conv * sigmoid(conv))
        bmat, cmat = both
        cmat_ref[...] = cmat.astype(BF16)
        bt = bmat.T
        bt_ref[...] = bt.astype(BF16)
        for c in range(chunks):
            rows = slice(c * Q, (c + 1) * Q)
            score = jnp.dot(cmat[rows].astype(BF16), bt[:, rows].astype(BF16), preferred_element_type=F32)
            score_ref[c] = jnp.where(keep_mask(starts_ref, c), score, 0.0)

    _, step, rate, _ = step_rows(dt_ref, shift_ref, logd_ref)
    cum = cumulate(rate, chunks)
    cumt_ref[...] = cum
    cum_ref[...] = cum.T
    step_ref[...] = step.T
    carry_ref[...] = jnp.zeros_like(carry_ref)
    for p in range(PAIRS):
        cols = slice(p * 128, (p + 1) * 128)
        conv = conv_forward(xin_ref[:, cols].astype(F32), cw_ref[:, cols], cb_ref[:, cols], same_ref)
        x_ref[:, cols] = conv * sigmoid(conv)
    for c in range(chunks):
        rows = slice(c * Q, (c + 1) * Q)
        entering_state = carry_ref[...].astype(BF16)
        state_ref[c] = entering_state
        if c > 0:
            outside = dot(cmat_ref[rows, :], entering_state)
        score = score_ref[c]
        for p in range(PAIRS):
            cols = slice(p * 128, (p + 1) * 128)
            cum_a = jnp.broadcast_to(cum_ref[rows, 2 * p : 2 * p + 1], (Q, Q))
            cum_b = jnp.broadcast_to(cum_ref[rows, 2 * p + 1 : 2 * p + 2], (Q, Q))
            low_a = (score * jnp.exp(jnp.minimum(cum_a - cumt_ref[2 * p : 2 * p + 1, rows], 0.0))).astype(BF16)
            low_b = (score * jnp.exp(jnp.minimum(cum_b - cumt_ref[2 * p + 1 : 2 * p + 2, rows], 0.0))).astype(BF16)
            cum_x = jnp.where(lo, cum_a, cum_b)
            step_x = jnp.where(lo, step_ref[rows, 2 * p : 2 * p + 1], step_ref[rows, 2 * p + 1 : 2 * p + 2])
            x = x_ref[rows, cols]
            xs = (x * step_x).astype(BF16)
            y = dot(jnp.concatenate([low_a, low_b], axis=1), halves(lo, xs))
            reach = jnp.exp(cum_x) * enter_ref[rows]
            if c > 0:
                y = y + reach * outside[:, cols]
            if c < chunks - 1:
                tail = jnp.exp(cum_x[Q - 1 : Q] - cum_x) * last_ref[rows]
                carry_ref[:, cols] = reach[Q - 1 : Q] * carry_ref[:, cols] + dot(
                    bt_ref[:, rows], (xs.astype(F32) * tail).astype(BF16)
                )
            y_ref[rows, cols] = y
            gate = gate_ref[rows, cols].astype(F32)
            gated = (y + skip_ref[:, cols] * x) * (gate * sigmoid(gate))
            square_ref[rows, :] += gated * gated
            gated_ref[rows, pl.ds(pl.multiple_of(j * BC + p * 128, 128), 128)] = gated

    @pl.when(j == pl.num_programs(0) - 1)
    def _():
        mean = jnp.sum(square_ref[...], axis=1, keepdims=True) * (1.0 / DI)
        q = lax.rsqrt(mean + EPSILON)
        q_ref[...] = q
        for c in range(DI // 512):
            cols = slice(c * 512, (c + 1) * 512)
            mixed_ref[:, cols] = (gated_ref[:, cols] * q * gain_ref[:, cols]).astype(BF16)


def backward_kernel(
    starts_ref, gate_ref, xin_ref, bc_ref, dt_ref, cw_ref, cb_ref, cwbc_ref, cbbc_ref,
    shift_ref, logd_ref, skip_ref, gain_ref, y_ref, state_ref, q_ref, mean_ref, dm_ref,
    dgate_ref, dxin_ref, dbc_ref, ddt_ref, sgain_ref, scw_ref, scb_ref, scwbc_ref, scbbc_ref,
    sshift_ref, slogd_ref, sskip_ref,
    same_ref, enter_ref, last_ref, bmat_ref, cmat_ref, ct_ref, score_ref, scoret_ref,
    x_ref, slope_ref, dy_ref, dxs_ref, carry_ref, step_ref, cum_ref, cumt_ref,
    dscore_ref, db_ref, dc_ref, v1_ref, v2_ref, v3_ref, v4_ref,
):
    j = pl.program_id(0)
    length = gate_ref.shape[0]
    chunks = length // Q
    lo = lax.broadcasted_iota(jnp.int32, (Q, 128), 1) < HP

    def activate_bc(part):
        cols = slice(part * NS, (part + 1) * NS)
        return conv_forward(bc_ref[:, cols].astype(F32), cwbc_ref[:, cols], cbbc_ref[:, cols], same_ref)

    @pl.when(j == 0)
    def _():
        prepare_masks(starts_ref, length, same_ref, enter_ref, last_ref)
        both = []
        for part in range(2):
            conv = activate_bc(part)
            both.append(conv * sigmoid(conv))
        bmat, cmat = both
        bmat_ref[...] = bmat.astype(BF16)
        cmat_ref[...] = cmat.astype(BF16)
        bt = bmat.T
        ct_ref[...] = cmat.T.astype(BF16)
        for c in range(chunks):
            rows = slice(c * Q, (c + 1) * Q)
            score = jnp.dot(cmat[rows].astype(BF16), bt[:, rows].astype(BF16), preferred_element_type=F32)
            score = jnp.where(keep_mask(starts_ref, c), score, 0.0)
            score_ref[c] = score
            scoret_ref[c] = score.T
        dscore_ref[...] = jnp.zeros_like(dscore_ref)
        db_ref[...] = jnp.zeros_like(db_ref)
        dc_ref[...] = jnp.zeros_like(dc_ref)

    pre, step, rate, decay = step_rows(dt_ref, shift_ref, logd_ref)
    cum = cumulate(rate, chunks)
    cumt_ref[...] = cum
    cum_ref[...] = cum.T
    step_ref[...] = step.T
    carry_ref[...] = jnp.zeros_like(carry_ref)
    q = q_ref[...]
    mean = mean_ref[...]
    for p in range(PAIRS):
        cols = slice(p * 128, (p + 1) * 128)
        conv = conv_forward(xin_ref[:, cols].astype(F32), cw_ref[:, cols], cb_ref[:, cols], same_ref)
        sig = sigmoid(conv)
        x = conv * sig
        x_ref[:, cols] = x
        slope_ref[:, cols] = sig * (1.0 + conv - x)
        gate = gate_ref[:, cols].astype(F32)
        gsig = sigmoid(gate)
        silu = gate * gsig
        scanned = y_ref[:, cols] + skip_ref[:, cols] * x
        gated = scanned * silu
        scaled = dm_ref[:, cols].astype(F32) * q
        sgain_ref[:, cols] = jnp.sum(gated * scaled, axis=0, keepdims=True)
        d_gated = scaled * gain_ref[:, cols] - gated * mean
        dgate_ref[:, cols] = (d_gated * scanned * (gsig * (1.0 + gate - silu))).astype(dgate_ref.dtype)
        d_scanned = d_gated * silu
        dy_ref[:, cols] = d_scanned
        sskip_ref[:, cols] = jnp.sum(d_scanned * x, axis=0, keepdims=True)

    for c in reversed(range(chunks)):
        rows = slice(c * Q, (c + 1) * Q)
        score = score_ref[c]
        scoret = scoret_ref[c]
        d_state = carry_ref[...]
        d_state_low = d_state.astype(BF16)
        if c < chunks - 1:
            from_state = dot(bmat_ref[rows, :], d_state_low)
        d_score = dscore_ref[c]
        for p in range(PAIRS):
            cols = slice(p * 128, (p + 1) * 128)
            cum_a = jnp.broadcast_to(cum_ref[rows, 2 * p : 2 * p + 1], (Q, Q))
            cum_b = jnp.broadcast_to(cum_ref[rows, 2 * p + 1 : 2 * p + 2], (Q, Q))
            row_a = cumt_ref[2 * p : 2 * p + 1, rows]
            row_b = cumt_ref[2 * p + 1 : 2 * p + 2, rows]
            cum_x = jnp.where(lo, cum_a, cum_b)
            step_x = jnp.where(lo, step_ref[rows, 2 * p : 2 * p + 1], step_ref[rows, 2 * p + 1 : 2 * p + 2])
            x = x_ref[rows, cols]
            xs = (x * step_x).astype(BF16)
            xs_wide = xs.astype(F32)
            d_y = dy_ref[rows, cols]
            d_y_low = d_y.astype(BF16)
            pair = dot_nt(d_y_low, halves(lo, xs))
            d_score = d_score + pair[:, :Q] * jnp.exp(jnp.minimum(cum_a - row_a, 0.0))
            d_score = d_score + pair[:, Q:] * jnp.exp(jnp.minimum(cum_b - row_b, 0.0))
            up_a = (scoret * jnp.exp(jnp.minimum(row_a - cum_a, 0.0))).astype(BF16)
            up_b = (scoret * jnp.exp(jnp.minimum(row_b - cum_b, 0.0))).astype(BF16)
            d_xs = dot(jnp.concatenate([up_a, up_b], axis=1), halves(lo, d_y_low))
            v1_ref[rows, cols] = d_y_low.astype(F32) * y_ref[rows, cols] - xs_wide * d_xs
            reach = jnp.exp(cum_x) * enter_ref[rows]
            if c < chunks - 1:
                tail = jnp.exp(cum_x[Q - 1 : Q] - cum_x) * last_ref[rows]
                d_tail = tail * from_state[:, cols]
                v3_ref[rows, cols] = xs_wide * d_tail
                d_xs = d_xs + d_tail
                db_ref[rows, :] += dot_nt((xs_wide * tail).astype(BF16), d_state_low[:, cols])
                entered = state_ref[c, :, cols]
                v4_ref[c : c + 1, cols] = reach[Q - 1 : Q] * jnp.sum(
                    d_state[:, cols] * entered.astype(F32), axis=0, keepdims=True
                )
            else:
                v3_ref[rows, cols] = jnp.zeros((Q, 128), F32)
                v4_ref[c : c + 1, cols] = jnp.zeros((1, 128), F32)
            if c > 0:
                reached = (reach * d_y).astype(BF16)
                dc_ref[rows, :] += dot_nt(reached, state_ref[c, :, cols])
                carry_ref[:, cols] = reach[Q - 1 : Q] * d_state[:, cols] + dot(ct_ref[:, rows], reached)
            v2_ref[rows, cols] = x * d_xs
            dxs_ref[rows, cols] = step_x * d_xs + skip_ref[:, cols] * d_y
        dscore_ref[c] = d_score

    head = lax.broadcasted_iota(jnp.int32, (HB, BC), 0)
    lane = lax.broadcasted_iota(jnp.int32, (HB, BC), 1)
    pick = ((lane >= head * HP) & (lane < (head + 1) * HP)).astype(BF16)

    def by_head(values):
        high = values.astype(BF16)
        rest = (values - high.astype(F32)).astype(BF16)
        return dot_nt(pick, high) + dot_nt(pick, rest)

    h1 = by_head(v1_ref[...])
    h2 = by_head(v2_ref[...])
    h3 = by_head(v3_ref[...])
    h4 = by_head(v4_ref[...])
    rows_i = lax.broadcasted_iota(jnp.int32, (Q, Q), 0)
    cols_i = lax.broadcasted_iota(jnp.int32, (Q, Q), 1)
    suffix = (rows_i >= cols_i).astype(F32)
    prefix = (rows_i < cols_i).astype(F32)
    parts = []
    for c in range(chunks):
        rows = slice(c * Q, (c + 1) * Q)
        parts.append(
            jnp.dot(h1[:, rows], suffix, precision=highest, preferred_element_type=F32)
            + jnp.dot(h3[:, rows], prefix, precision=highest, preferred_element_type=F32)
            + h4[:, c : c + 1]
        )
    d_rate = jnp.concatenate(parts, axis=1)
    d_step = h2 - d_rate * decay
    d_raw = d_step * sigmoid(pre)
    ddt_ref[...] = d_raw
    sshift_ref[...] = jnp.sum(d_raw, axis=1, keepdims=True)
    slogd_ref[...] = jnp.sum(d_rate * rate, axis=1, keepdims=True)

    for p in range(PAIRS):
        cols = slice(p * 128, (p + 1) * 128)
        d_conv = dxs_ref[:, cols] * slope_ref[:, cols]
        d_in, s_w, s_b = conv_backward(d_conv, xin_ref[:, cols].astype(F32), cw_ref[:, cols], same_ref)
        dxin_ref[:, cols] = d_in.astype(dxin_ref.dtype)
        scw_ref[:, cols] = s_w
        scb_ref[:, cols] = s_b

    @pl.when(j == pl.num_programs(0) - 1)
    def _():
        for c in range(chunks):
            rows = slice(c * Q, (c + 1) * Q)
            masked = jnp.where(keep_mask(starts_ref, c), dscore_ref[c], 0.0)
            dc_ref[rows, :] += dot(masked.astype(BF16), bmat_ref[rows, :])
            db_ref[rows, :] += dot(masked.T.astype(BF16), cmat_ref[rows, :])
        for part, grad_ref in ((0, db_ref), (1, dc_ref)):
            cols = slice(part * NS, (part + 1) * NS)
            conv = activate_bc(part)
            sig = sigmoid(conv)
            d_conv = grad_ref[...] * (sig * (1.0 + conv - conv * sig))
            d_in, s_w, s_b = conv_backward(d_conv, bc_ref[:, cols].astype(F32), cwbc_ref[:, cols], same_ref)
            dbc_ref[:, cols] = d_in.astype(dbc_ref.dtype)
            scwbc_ref[:, cols] = s_w
            scbbc_ref[:, cols] = s_b


def column_block(rows, offset=0):
    return pl.BlockSpec((rows, BC), lambda j: (0, j + offset))


def whole(*shape):
    return pl.BlockSpec(shape, lambda j: (0,) * len(shape))


def common_specs(length):
    heads = pl.BlockSpec((HB, 1), lambda j: (j, 0))
    return [
        pl.BlockSpec(memory_space=pltpu.SMEM),
        column_block(length),
        column_block(length, DI // BC),
        pl.BlockSpec((length, 2 * NS), lambda j: (0, 2 * DI // (2 * NS))),
        pl.BlockSpec((HB, length), lambda j: (j, 0)),
        column_block(CONVW),
        column_block(1),
        pl.BlockSpec((CONVW, 2 * NS), lambda j: (0, DI // (2 * NS))),
        pl.BlockSpec((1, 2 * NS), lambda j: (0, DI // (2 * NS))),
        heads,
        heads,
        column_block(1),
    ]


def mix_forward(starts, projected, dt_rows, conv_w, conv_b, shift, logd, skip_cols, gain):
    length = projected.shape[0]
    chunks = length // Q
    vmem = pltpu.VMEM
    return pl.pallas_call(
        forward_kernel,
        grid=(DI // BC,),
        in_specs=common_specs(length) + [whole(1, DI)],
        out_specs=[
            whole(length, DI),
            column_block(length),
            pl.BlockSpec((chunks, NS, BC), lambda j: (0, 0, j)),
            whole(length, 1),
        ],
        out_shape=[
            jax.ShapeDtypeStruct((length, DI), BF16),
            jax.ShapeDtypeStruct((length, DI), F32),
            jax.ShapeDtypeStruct((chunks, NS, DI), BF16),
            jax.ShapeDtypeStruct((length, 1), F32),
        ],
        scratch_shapes=[
            vmem((CONVW - 1, length, 128), F32),
            vmem((length, 128), F32),
            vmem((length, 128), F32),
            vmem((length, NS), BF16),
            vmem((NS, length), BF16),
            vmem((chunks, Q, Q), F32),
            vmem((length, DI), F32),
            vmem((length, 128), F32),
            vmem((length, BC), F32),
            vmem((NS, BC), F32),
            vmem((length, HB), F32),
            vmem((length, HB), F32),
            vmem((HB, length), F32),
        ],
        compiler_params=pltpu.CompilerParams(vmem_limit_bytes=56 * 1024 * 1024),
        name="mix_forward",
    )(starts, projected, projected, projected, dt_rows, conv_w, conv_b, conv_w, conv_b, shift, logd, skip_cols, gain)


def mix_backward(starts, projected, dt_rows, conv_w, conv_b, shift, logd, skip_cols, gain, y, states, q, mean, d_mixed):
    length = projected.shape[0]
    chunks = length // Q
    vmem = pltpu.VMEM
    heads = pl.BlockSpec((HB, 1), lambda j: (j, 0))
    col = whole(length, 1)
    shape = jax.ShapeDtypeStruct
    return pl.pallas_call(
        backward_kernel,
        grid=(DI // BC,),
        in_specs=common_specs(length)
        + [
            column_block(1),
            column_block(length),
            pl.BlockSpec((chunks, NS, BC), lambda j: (0, 0, j)),
            col,
            col,
            column_block(length),
        ],
        out_specs=[
            column_block(length),
            column_block(length),
            whole(length, 2 * NS),
            pl.BlockSpec((HB, length), lambda j: (j, 0)),
            column_block(1),
            column_block(CONVW),
            column_block(1),
            whole(CONVW, 2 * NS),
            whole(1, 2 * NS),
            heads,
            heads,
            column_block(1),
        ],
        out_shape=[
            shape((length, DI), BF16),
            shape((length, DI), BF16),
            shape((length, 2 * NS), BF16),
            shape((NH, length), F32),
            shape((1, DI), F32),
            shape((CONVW, DI), F32),
            shape((1, DI), F32),
            shape((CONVW, 2 * NS), F32),
            shape((1, 2 * NS), F32),
            shape((NH, 1), F32),
            shape((NH, 1), F32),
            shape((1, DI), F32),
        ],
        scratch_shapes=[
            vmem((CONVW - 1, length, 128), F32),
            vmem((length, 128), F32),
            vmem((length, 128), F32),
            vmem((length, NS), BF16),
            vmem((length, NS), BF16),
            vmem((NS, length), BF16),
            vmem((chunks, Q, Q), F32),
            vmem((chunks, Q, Q), F32),
            vmem((length, BC), F32),
            vmem((length, BC), F32),
            vmem((length, BC), F32),
            vmem((length, BC), F32),
            vmem((NS, BC), F32),
            vmem((length, HB), F32),
            vmem((length, HB), F32),
            vmem((HB, length), F32),
            vmem((chunks, Q, Q), F32),
            vmem((length, NS), F32),
            vmem((length, NS), F32),
            vmem((length, BC), F32),
            vmem((length, BC), F32),
            vmem((length, BC), F32),
            vmem((8, BC), F32),
        ],
        compiler_params=pltpu.CompilerParams(vmem_limit_bytes=56 * 1024 * 1024),
        name="mix_backward",
    )(
        starts, projected, projected, projected, dt_rows, conv_w, conv_b, conv_w, conv_b, shift, logd, skip_cols,
        gain, y, states, q, mean, d_mixed,
    )


def rms_scale(values, gain):
    return values * lax.rsqrt(jnp.mean(values * values, axis=-1, keepdims=True) + EPSILON) * gain


def adam_direction(weight, gradient, first, second, decayed):
    first_new = BETA_ONE * first + (1.0 - BETA_ONE) * gradient
    second_new = BETA_TWO * second + (1.0 - BETA_TWO) * gradient * gradient
    first_hat = first_new / (1.0 - BETA_ONE**adam_step)
    second_hat = second_new / (1.0 - BETA_TWO**adam_step)
    direction = first_hat / (jnp.sqrt(second_hat) + ADAM_EPS)
    if decayed:
        direction = direction + DECAY_RATE * weight
    return (direction, first_new, second_new)


def gather_small(values):
    flat = jnp.concatenate([v.astype(BF16).reshape(-1) for v in values])
    every = lax.all_gather(flat, "fsdp", axis=0, tiled=False)
    result, at = [], 0
    for v in values:
        size = v.size
        piece = every[:, at : at + size].astype(F32)
        at += size
        if v.ndim == 1:
            result.append(piece.reshape(1, -1))
        else:
            result.append(jnp.moveaxis(piece.reshape((-1,) + v.shape), 0, 1).reshape(v.shape[0], -1))
    return result


def shards(
    tokens, cotangent, doc_starts, valid_len,
    w_in, w_out, norm_gain, gate_gain, conv_w, conv_b, dt_bias, a_log, d_skip,
    first_w_in, second_w_in, first_w_out, second_w_out,
    first_norm_gain, second_norm_gain, first_gate_gain, second_gate_gain,
    first_conv_w, second_conv_w, first_conv_b, second_conv_b,
    first_dt_bias, second_dt_bias, first_a_log, second_a_log, first_d_skip, second_d_skip,
):
    length = tokens.shape[1]
    hidden = tokens[0].astype(F32)
    upstream = cotangent[0].astype(F32)
    small = (norm_gain, gate_gain, conv_w, conv_b, dt_bias, a_log, d_skip)
    norm_full, gate_full, convw_full, convb_full, shift_full, logd_full, skip_full = gather_small(small)
    in_full = lax.all_gather(
        lax.all_gather(w_in.astype(BF16), "dp", axis=1, tiled=True), "fsdp", axis=0, tiled=True
    )
    out_full = lax.all_gather(
        lax.all_gather(w_out.astype(BF16), "dp", axis=1, tiled=True), "fsdp", axis=0, tiled=True
    )
    scale = lax.rsqrt(jnp.mean(hidden * hidden, axis=-1, keepdims=True) + EPSILON)
    normed = (hidden * scale * norm_full).astype(BF16)
    projected = dot(normed, in_full)
    dt_rows = projected[:, DI + CONV :].T
    common = (
        doc_starts, projected, dt_rows, convw_full, convb_full, shift_full.T, logd_full.T,
        jnp.repeat(skip_full, HP, axis=1), gate_full,
    )
    mixed, y, states, q = mix_forward(*common)
    position = jnp.arange(length, dtype=jnp.int32)
    live = (position < valid_len[0]).astype(F32)[:, None]
    d_branch = (upstream * live).astype(BF16)
    branch = dot(mixed, out_full)
    out_tokens = (hidden + branch * live).astype(BF16)
    d_mixed = dot_nt(d_branch, out_full)
    mean = q * q * jnp.sum(mixed.astype(F32) * d_mixed, axis=1, keepdims=True) * (1.0 / DI)
    (
        d_gate_in, d_x_in, d_bc_in, d_dt, s_gain, s_cw, s_cb, s_cwbc, s_cbbc, s_shift, s_logd, s_skip,
    ) = mix_backward(*common, y, states, q, mean, d_mixed)
    d_low = jnp.concatenate([d_gate_in, d_x_in, d_bc_in, d_dt.T.astype(BF16)], axis=1)
    d_normed = dot_nt(d_low, in_full)
    weighted = norm_full * d_normed
    inner = jnp.mean(hidden * weighted, axis=-1, keepdims=True)
    grad_tokens = upstream + scale * weighted - hidden * (scale * scale * scale * inner)
    s_norm = jnp.sum(hidden * scale * d_normed, axis=0)
    contract = (((0,), (0,)), ((), ()))
    out_sum = lax.dot_general(mixed, d_branch, contract, preferred_element_type=F32).astype(BF16)
    in_sum = lax.dot_general(normed, d_low, contract, preferred_element_type=F32).astype(BF16)
    out_summed = lax.psum_scatter(out_sum, "fsdp", scatter_dimension=0, tiled=True)
    in_summed = lax.psum_scatter(in_sum, "fsdp", scatter_dimension=0, tiled=True)
    grad_in = lax.psum_scatter(in_summed, "dp", scatter_dimension=1, tiled=True).astype(F32)
    grad_out = lax.psum_scatter(out_summed, "dp", scatter_dimension=1, tiled=True).astype(F32)

    sums = (
        s_norm[None],
        s_gain,
        jnp.concatenate([s_cw, s_cwbc], axis=1),
        jnp.concatenate([s_cb, s_cbbc], axis=1),
        s_shift.T,
        s_logd.T,
        s_skip.reshape(1, NH, HP).sum(axis=2),
    )
    parts = lax.axis_size("fsdp")
    flat = jnp.concatenate(
        [jnp.moveaxis(s.reshape(s.shape[0], parts, -1), 1, 0).reshape(parts, -1) for s in sums], axis=1
    )
    total = lax.psum(flat, ("dp", "fsdp"))
    mine = lax.dynamic_index_in_dim(total, lax.axis_index("fsdp"), 0, keepdims=False)
    small_grads, at = [], 0
    for v in small:
        small_grads.append(mine[at : at + v.size].reshape(v.shape))
        at += v.size

    factor = 1.0 / math.sqrt(length * lax.axis_size("dp") * lax.axis_size("fsdp"))
    weights = (w_in, w_out) + small
    grads = (grad_in, grad_out) + tuple(small_grads)
    firsts = (
        first_w_in, first_w_out, first_norm_gain, first_gate_gain, first_conv_w, first_conv_b,
        first_dt_bias, first_a_log, first_d_skip,
    )
    seconds = (
        second_w_in, second_w_out, second_norm_gain, second_gate_gain, second_conv_w, second_conv_b,
        second_dt_bias, second_a_log, second_d_skip,
    )
    decay_flags = (True, True, False, False, True, True, False, False, False)
    results = []
    for i, (weight, gradient, first, second) in enumerate(zip(weights, grads, firsts, seconds)):
        direction, first_new, second_new = adam_direction(weight, gradient * factor, first, second, decay_flags[i])
        if i < 2:
            direction = weight - LEARN_RATE * direction
        results.extend((direction, first_new, second_new))
    return (out_tokens[None], grad_tokens[None]) + tuple(results)


def solution(mesh):
    rows3 = P(("dp", "fsdp"), None, None)
    both, split, last = P("fsdp", "dp"), P("fsdp"), P(None, "fsdp")
    small = (split, split, last, split, split, split, split)
    placed = (rows3, rows3, P(("dp", "fsdp"), None), P(("dp", "fsdp")), both, both) + small
    placed = placed + (both,) * 4 + tuple(s for s in small for _ in range(2))
    out = (rows3, rows3) + (both,) * 6 + tuple(s for s in small for _ in range(3))
    return jax.shard_map(shards, mesh=mesh, in_specs=placed, out_specs=out, check_vma=False)
```

time: 2280 us -> 1570 us (0.69)
  local copies, waits for them, and re-layouts: 531 us -> 29.8 us
  matrix products: 360 us -> 128 us
  waiting for transfers between devices: 1080 us -> 1240 us
  other arithmetic: 157 us -> 30.8 us
  Pallas kernels: 0 us -> 98.9 us
  blocking collectives: 84.4 us -> 16.9 us
    dynamic_update_slice x22 -> x0, local copies, waits for them, and re-layouts: 387 us -> none  [mixer(): lax.scan(jax.checkpoint(block_state), start_carry, scan_inputs)]
    dot_general x40 -> x6, matrix products: 360 us -> 128 us  [the longest x2 45.6 us: dot_nt(): lax.dot_general(a, b, (((1,), (1,)), ((), ())), preferred_element_type=F32)]
    psum x0 -> x1, waiting for transfers between devices: none -> 107 us  [shards(): total = lax.psum(flat, ('dp', 'fsdp'))]
    pallas_call x0 -> x2, Pallas kernels: none -> 98.9 us  [the longest x1 67.1 us: mix_backward(): pl.pallas_call(backward_kernel, grid=(DI // BC,), in_specs=common_specs(l...]
    reduce_sum x11 -> x2, other arithmetic: 66.2 us -> 0.59 us  [the longest x1 0.48 us: shards(): jnp.mean(hidden * hidden, axis=-1, keepdims=True) + EPSILON]
    reduce_scatter x1, waiting for transfers between devices: 26.4 us -> 88.4 us  [shards(): lax.psum_scatter(in_summed, 'dp', scatter_dimension=1, tiled=True)]
    reduce_scatter x2, waiting for transfers between devices: 451 us -> 418 us  [the longest x1 264 us: shards(): lax.psum_scatter(in_sum, 'fsdp', scatter_dimension=0, tiled=True)]
    psum x1 -> x0, blocking collectives: 28.9 us -> none  [shards(): lax.psum((part_norm, part_gate, part_convw, part_convb, part_shift, part_...]
  transfers between devices with their start and end apart: 9 -> 9, of which waited for: 8 -> 9; matrix products, arithmetic and copies ran while one was open for 3% -> 4% of each run, Pallas kernels for 0% -> 0%
where the time goes in v1:
time: 1570 us; the launch traced here: 1560 us
  waiting for transfers between devices  1240 us (79%)
  matrix products  128 us (8%)
  Pallas kernels  98.9 us (6%)
  other arithmetic  30.8 us (2%)
  local copies, waits for them, and re-layouts  29.8 us (2%)
  blocking collectives  16.9 us (1%)
  between operations  16.3 us (1%)
    all_gather x1, waiting for transfers between devices, shards(): lax.all_gather(lax.all_gather(w_in.astype(BF16), 'dp', axis=1, tiled=True...  284 us
    reduce_scatter x1, waiting for transfers between devices, shards(): lax.psum_scatter(in_sum, 'fsdp', scatter_dimension=0, tiled=True)  264 us
    all_gather x1, waiting for transfers between devices, shards(): lax.all_gather(lax.all_gather(w_out.astype(BF16), 'dp', axis=1, tiled=Tru...  157 us
    reduce_scatter x1, waiting for transfers between devices, shards(): lax.psum_scatter(out_sum, 'fsdp', scatter_dimension=0, tiled=True)  154 us
    psum x1, waiting for transfers between devices, shards(): total = lax.psum(flat, ('dp', 'fsdp'))  107 us
    reduce_scatter x1, waiting for transfers between devices, shards(): lax.psum_scatter(in_summed, 'dp', scatter_dimension=1, tiled=True)  88.4 us
    all_gather x1, waiting for transfers between devices, shards(): lax.all_gather(w_in.astype(BF16), 'dp', axis=1, tiled=True)  87.7 us
    pallas_call x1, Pallas kernels, mix_backward(): pl.pallas_call(backward_kernel, grid=(DI // BC,), in_specs=common_specs(l...  67.1 us
  transfers between devices with their start and end apart: 9, of which 9 were waited for; matrix products, arithmetic and copies ran while one was open for 4% of the time, Pallas kernels for 0%

profile of v1, /device:TPU:0, one launch (start us, length us, event | category | flops | bytes accessed | tf_op | source)
XLA Modules:
  0.0 1562.3 jit_solution(2587490413083612041)
XLA Ops:
  7.2 2.7 convert_element_type.93
  10.1 87.7 %all-gather.6.cloned.1.call-done = bf16[512,8512]{0,1:T(8,128)(2,1)} async-done(((bf16[512,1064]{0,1:T(8,128)(2,1)}), bf16[512,8512]{0,1:T(8,128)(2,1)}) %all-gather.6.cloned.1.call-update) | async-done | bytes 8716304 | tf_op jit(solution)/shard_map/all_gather | solution.py:561
  97.9 0.5 copy-done.28
  98.5 0.1 reshape.192
  98.7 0.6 dynamic-slice
  99.9 0.1 concatenate.15
  100.0 0.4 dynamic-update-slice
  100.4 16.9 %all-reduce = bf16[28096]{0:T(1024)(128)(2,1)S(1)} all-reduce(bf16[28096]{0:T(1024)(128)(2,1)S(1)} %dynamic-update-slice), channel_id=2, replica_groups=mesh['dp'=8,'fsdp'=4] {'fsdp'}, use_global_device_ids=true, to_apply=%add | all-reduce | flops 28096 | bytes 112384
  117.3 0.1 reshape.221
  117.5 0.1 reshape.220
  117.7 0.8 reshape.208.cw_ref.cwbc_ref
  118.4 0.7 reshape.210.cb_ref.cbbc_ref
  119.2 0.7 reshape.227.shift_ref
  119.9 0.7 reshape.228.logd_ref
  120.8 0.7 broadcast_in_dim.18.skip_ref
  121.5 0.6 copy.88
  122.8 0.5 fusion.7
  123.3 284.0 %all-gather.8.cloned.1.call-done = bf16[2048,8512]{0,1:T(8,128)(2,1)} async-done(((bf16[512,8512]{0,1:T(8,128)(2,1)}), bf16[2048,8512]{0,1:T(8,128)(2,1)}) %all-gather.8.cloned.1.call-update) | async-done | bytes 34865168 | tf_op jit(solution)/shard_map/all_gather | solution.py:560
  407.3 25.1 %fusion.22 = f32[512,8512]{0,1:T(8,128)} fusion(bf16[2048,8512]{0,1:T(8,128)(2,1)} %all-gather.8.cloned.1.call-done, bf16[1,512,2048]{2,1,0:T(8,128)(2,1)S(1)} %copy-done.1, f32[2048]{0:T(1024)S(1)} %bitcast.73, f32[512]{0:T(512)S(1)} %add_rsqrt_fusion), kind=kOutput, calls=%fused_computation.38 | convolution fusion | flops 17855152128 | bytes 54405120 | tf_op jit(solution)/shard_map/dot_general | solution.py:36
  432.4 17.8 %copy.74.gate_ref.xin_ref.bc_ref = f32[512,8512]{1,0:T(8,128)} copy(f32[512,8512]{0,1:T(8,128)} %fusion.22) | data formatting | bytes 34865152 | tf_op jit(solution)/shard_map/dot_general | solution.py:36
  450.2 1.6 slice_bitcast_fusion.dt_ref
  451.8 31.7 %mix_forward.1 = (bf16[512,4096]{1,0:T(8,128)(2,1)}, f32[512,4096]{1,0:T(8,128)}, bf16[4,128,4096]{2,1,0:T(8,128)(2,1)}, f32[512,1]{1,0:T(8,128)}) custom-call(s32[1,4]{1,0:T(1,128)} %starts_ref.3, f32[512,8512]{1,0:T(8,128)} %copy.74.gate_ref.xin_ref.bc_ref, f32[512,8512]{1,0:T(8,128)} %copy.74.gate_ref.xin_ref.bc_ref, ...), custom_call_target="tpu_custom_call" | custom-call | tf_op jit(solution)/shard_map/mix_forward/pallas_call | solution.py:401
  483.5 15.4 convolution_convert_fusion.1
  499.0 153.9 %reduce-scatter.9.cloned.1.call-done = bf16[1024,2048]{1,0:T(8,128)(2,1)} async-done(((bf16[4096,2048]{1,0:T(8,128)(2,1)}), bf16[1024,2048]{1,0:T(8,128)(2,1)}) %reduce-scatter.9.cloned.1.call-update) | async-done | bytes 4194320 | tf_op jit(solution)/shard_map/reduce_scatter | solution.py:594
  653.0 52.1 %reduce-scatter.11.cloned.1.call-done = bf16[1024,256]{1,0:T(8,128)(2,1)} async-done(((bf16[1024,2048]{1,0:T(8,128)(2,1)}), bf16[1024,256]{1,0:T(8,128)(2,1)}) %reduce-scatter.11.cloned.1.call-update) | async-done | bytes 524304 | tf_op jit(solution)/shard_map/reduce_scatter | solution.py:597
  705.1 4.1 multiply_subtract_fusion.1
  709.3 46.0 %all-gather.10.cloned.1.call-done = bf16[1024,2048]{1,0:T(8,128)(2,1)} async-done(((bf16[1024,256]{1,0:T(8,128)(2,1)}), bf16[1024,2048]{1,0:T(8,128)(2,1)}) %all-gather.10.cloned.1.call-update) | async-done | bytes 4194320 | tf_op jit(solution)/shard_map/all_gather | solution.py:564
  755.4 157.3 %all-gather.12.cloned.1.call-done = bf16[4096,2048]{1,0:T(8,128)(2,1)} async-done(((bf16[1024,2048]{1,0:T(8,128)(2,1)}), bf16[4096,2048]{1,0:T(8,128)(2,1)}) %all-gather.12.cloned.1.call-update) | async-done | bytes 16777232 | tf_op jit(solution)/shard_map/all_gather | solution.py:563
  912.7 15.8 %multiply_reduce_fusion = (f32[512]{0:T(512)S(1)}, f32[512,4096]{1,0:T(8,128)}) fusion(bf16[512,4096]{1,0:T(8,128)(2,1)} %get-tuple-element.45, bf16[4096,2048]{1,0:T(8,128)(2,1)} %all-gather.12.cloned.1.call-done, bf16[1,512,2048]{2,1,0:T(8,128)(2,1)} %param.32, f32[512]{0:T(512)S(1)} %fusion.25), kind=kOutput, calls=%fused_computation.8 | convolution fusion | flops 8599371776 | bytes 31461376 | tf_op jit(solution)/shard_map/dot_general | solution.py:40
  928.5 0.1 copy.79
  928.7 0.7 multiply_multiply_fusion.mean_ref
  929.4 67.1 %mix_backward.1 = (bf16[512,4096]{1,0:T(8,128)(2,1)}, bf16[512,4096]{1,0:T(8,128)(2,1)}, bf16[512,256]{1,0:T(8,128)(2,1)}, f32[64,512]{1,0:T(8,128)}, f32[1,4096...) custom-call(s32[1,4]{1,0:T(1,128)} %starts_ref.3, ...), custom_call_target="tpu_custom_call" | custom-call | tf_op jit(solution)/shard_map/mix_backward/pallas_call | solution.py:444
  996.5 0.9 convert_bitcast_fusion
  997.5 0.1 copy.85
  997.6 28.1 %convolution_convert_fusion = bf16[2048,8512]{0,1:T(8,128)(2,1)} fusion(bf16[512,64]{1,0:T(8,128)(2,1)S(1)} %copy.85, bf16[512,256]{1,0:T(8,128)(2,1)} %get-tuple-element.51, bf16[512,4096]{1,0:T(8,128)(2,1)} %get-tuple-element.50, bf16[512,4096]{1,0:T(8,128)(2,1)} %get-tuple-element.49, bf16[1,512,2048]{2,1,0:T(8,128)(2,1)S(1)} %copy-done.1, ...), kind=kOutput, calls=%fused_computation | convolution fusion | flops 17907449856 | bytes 45688832 | tf_op jit(solution)/shard_map/dot_general | solution.py:593
  1025.9 0.8 copy-done.37
  1026.7 29.8 %fusion.3 = (f32[2048]{0:T(1024)S(1)}, f32[512]{0:T(512)S(1)}, f32[512,2048]{1,0:T(8,128)}) fusion(bf16[1,512,2048]{2,1,0:T(8,128)(2,1)S(1)} %copy-done.1, f32[512]{0:T(512)S(1)} %add_rsqrt_fusion, f32[2048]{0:T(1024)S(1)} %bitcast.75, bf16[2048,8512]{0,1:T(8,128)(2,1)} %all-gather.8.cloned.1.call-done, bf16[512,64]{1,0:T(8,128)(2,1)S(1)} %copy.85, ...), kind=kOutput, calls=%fused_computation.14 | convolution fusion | flops 17893160960 | bytes 49893376 | tf_op jit(solution)/shard_map/dot_general | solution.py:40
  1056.5 0.5 broadcast.188
  1057.0 0.7 reduce.19
  1057.8 0.1 reshape.202
  1057.9 0.1 reshape.203
  1058.1 0.1 reshape_transpose_reshape.10
  1058.2 0.1 reduce.3
  1058.4 0.1 reduce.4
  1058.6 0.7 reduce.20
  1059.4 0.1 reduce_sum.49
  1059.6 0.8 concatenate.19
  1060.4 0.3 reduce-scatter.7.cloned.1.call-start
  1060.7 264.4 %reduce-scatter.5.cloned.1.call-done = bf16[512,8512]{0,1:T(8,128)(2,1)} async-done(((bf16[2048,8512]{0,1:T(8,128)(2,1)}), bf16[512,8512]{0,1:T(8,128)(2,1)}) %reduce-scatter.5.cloned.1.call-update) | async-done | bytes 8716304 | tf_op jit(solution)/shard_map/reduce_scatter | solution.py:595
  1325.1 0.7 copy-done.14
  1325.8 6.0 fusion.6
  1332.1 13.5 fusion.10
  1345.6 107.2 %all-reduce.3.cloned.1.call-done = f32[4,7024]{1,0:T(4,128)} async-done(((f32[4,7024]{1,0:T(4,128)}), f32[4,7024]{1,0:T(4,128)}) %all-reduce.3.cloned.1.call-update) | async-done | bytes 112400 | tf_op jit(solution)/shard_map/psum | solution.py:612
  1452.8 1.0 multiply_reduce_fusion.2
  1454.0 0.8 multiply_reduce_fusion.4
  1454.9 0.7 multiply_multiply_fusion.3
  1455.6 0.8 multiply_multiply_fusion.1
  1456.4 1.4 add_divide_fusion.2
  1457.9 0.6 add_divide_fusion.1
  1458.5 0.6 add_divide_fusion
  1459.1 0.6 multiply_add_fusion.3
  1459.7 0.6 multiply_add_fusion
  1460.4 88.4 %reduce-scatter.7.cloned.1.call-done = bf16[512,1064]{0,1:T(8,128)(2,1)} async-done(((bf16[512,8512]{0,1:T(8,128)(2,1)}), bf16[512,1064]{0,1:T(8,128)(2,1)}) %reduce-scatter.7.cloned.1.call-update) | async-done | bytes 1089552 | tf_op jit(solution)/shard_map/reduce_scatter | solution.py:596
  1548.8 6.6 multiply_subtract_fusion
  (129 shorter events, 1.7 us)
Async XLA Ops:
  7.2 90.6 %all-gather.6.cloned.1.call-start = ((), (), s32[]{:S(2)}) async-start(), calls=%async_computation.4 | async-start | bytes 9805824 | tf_op jit(solution)/shard_map/all_gather | solution.py:561
  10.0 397.3 %all-gather.8.cloned.1.call-start = ((), (), s32[]{:S(2)}) async-start(), calls=%async_computation.5 | async-start | bytes 43581440 | tf_op jit(solution)/shard_map/all_gather | solution.py:560
  97.8 0.7 copy-start.28
  97.8 0.7 copy-start.25
  97.8 0.7 copy-start.6
  97.8 0.8 copy-start.11
  97.8 0.9 copy-start.38
  97.8 0.9 copy-start.39
  97.8 0.9 copy-start.40
  97.8 0.9 copy-start.41
  97.8 25.0 %copy-start.1 = (bf16[1,512,2048]{2,1,0:T(8,128)(2,1)S(1)}, bf16[1,512,2048]{2,1,0:T(8,128)(2,1)}, u32[]{:S(2)}) copy-start(bf16[1,512,2048]{2,1,0:T(8,128)(2,1)} %param.31) | copy-start | bytes 6291460
  97.8 555.1 %reduce-scatter.9.cloned.1.call-start = ((), (), s32[]{:S(2)}) async-start(), calls=%async_computation.10 | async-start | bytes 20971520 | tf_op jit(solution)/shard_map/reduce_scatter | solution.py:594
  123.3 309.1 %copy-start.13 = (f32[512]{0:T(512)}, f32[512]{0:T(512)S(1)}, u32[]{:S(2)}) copy-start(f32[512]{0:T(512)S(1)} %fusion.7) | copy-start | bytes 6148
  451.8 31.8 %copy-start.3 = (bf16[1,512,2048]{2,1,0:T(8,128)(2,1)S(1)}, bf16[1,512,2048]{2,1,0:T(8,128)(2,1)}, u32[]{:S(2)}) copy-start(bf16[1,512,2048]{2,1,0:T(8,128)(2,1)} %param.32) | copy-start | bytes 6291460
  498.9 206.2 %copy-start.5 = (f32[1024,256]{1,0:T(8,128)S(1)}, f32[1024,256]{1,0:T(8,128)}, u32[]{:S(2)}) copy-start(f32[1024,256]{1,0:T(8,128)} %param.36) | copy-start | bytes 3145732
  498.9 206.2 %reduce-scatter.11.cloned.1.call-start = ((), (), s32[]{:S(2)}) async-start(), calls=%async_computation.11 | async-start | bytes 4718592 | tf_op jit(solution)/shard_map/reduce_scatter | solution.py:597
  653.0 102.4 %all-gather.10.cloned.1.call-start = ((), (), s32[]{:S(2)}) async-start(), calls=%async_computation.6 | async-start | bytes 4718592 | tf_op jit(solution)/shard_map/all_gather | solution.py:564
  709.2 203.5 %all-gather.12.cloned.1.call-start = ((), (), s32[]{:S(2)}) async-start(), calls=%async_computation.7 | async-start | bytes 20971520 | tf_op jit(solution)/shard_map/all_gather | solution.py:563
  755.4 173.3 %copy-start.4 = (f32[512,1]{1,0:T(8,128)S(1)}, f32[512,1]{1,0:T(8,128)}, u32[]{:S(2)}) copy-start(f32[512,1]{1,0:T(8,128)} %get-tuple-element.48.q_ref) | copy-start | bytes 6148
  755.4 569.7 %reduce-scatter.5.cloned.1.call-start = ((), (), s32[]{:S(2)}) async-start(), calls=%async_computation.8 | async-start | bytes 43581440 | tf_op jit(solution)/shard_map/reduce_scatter | solution.py:595
  1025.7 0.9 copy-start.37
  1025.7 31.3 %copy-start.19 = (f32[1,4096]{1,0:T(1,128)S(1)}, f32[1,4096]{1,0:T(1,128)}, u32[]{:S(2)}) copy-start(f32[1,4096]{1,0:T(1,128)} %get-tuple-element.53) | copy-start | bytes 49156
  1025.8 32.0 %copy-start.8 = (f32[4,4096]{1,0:T(4,128)S(1)}, f32[4,4096]{1,0:T(4,128)}, u32[]{:S(2)}) copy-start(f32[4,4096]{1,0:T(4,128)} %get-tuple-element.54) | copy-start | bytes 196612
  1025.8 32.0 %copy-start.24 = (f32[4,256]{1,0:T(4,128)S(1)}, f32[4,256]{1,0:T(4,128)}, u32[]{:S(2)}) copy-start(f32[4,256]{1,0:T(4,128)} %get-tuple-element.55) | copy-start | bytes 12292
  1025.8 32.3 %copy-start.17 = (f32[1,4096]{1,0:T(1,128)S(1)}, f32[1,4096]{1,0:T(1,128)}, u32[]{:S(2)}) copy-start(f32[1,4096]{1,0:T(1,128)} %get-tuple-element.56) | copy-start | bytes 49156
  1025.8 32.3 %copy-start.29 = (f32[1,256]{1,0:T(1,128)S(1)}, f32[1,256]{1,0:T(1,128)}, u32[]{:S(2)}) copy-start(f32[1,256]{1,0:T(1,128)} %get-tuple-element.57) | copy-start | bytes 3076
  1025.8 32.4 %copy-start.10 = (f32[64,1]{1,0:T(8,128)S(1)}, f32[64,1]{1,0:T(8,128)}, u32[]{:S(2)}) copy-start(f32[64,1]{1,0:T(8,128)} %get-tuple-element.58) | copy-start | bytes 772
  1025.8 32.6 %copy-start.9 = (f32[64,1]{1,0:T(8,128)S(1)}, f32[64,1]{1,0:T(8,128)}, u32[]{:S(2)}) copy-start(f32[64,1]{1,0:T(8,128)} %get-tuple-element.59) | copy-start | bytes 772
  1025.8 32.8 %copy-start.18 = (f32[1,4096]{1,0:T(1,128)S(1)}, f32[1,4096]{1,0:T(1,128)}, u32[]{:S(2)}) copy-start(f32[1,4096]{1,0:T(1,128)} %get-tuple-element.60) | copy-start | bytes 49156
  1025.8 427.0 %all-reduce.3.cloned.1.call-start = ((), (), s32[]{:S(2)}) async-start(), calls=%async_computation.12 | async-start | bytes 225280 | tf_op jit(solution)/shard_map/psum | solution.py:612
  1060.4 488.5 %reduce-scatter.7.cloned.1.call-start = ((), (), s32[]{:S(2)}) async-start(), calls=%async_computation.9 | async-start | bytes 9805824 | tf_op jit(solution)/shard_map/reduce_scatter | solution.py:596
  1325.1 0.7 copy-start.14
  1325.8 6.1 copy-start.2
  1325.8 6.1 copy-start.36
  1331.9 124.5 %copy-start.30 = (f32[16]{0:T(128)S(1)}, f32[16]{0:T(128)}, u32[]{:S(2)}) copy-start(f32[16]{0:T(128)} %param.60) | copy-start | bytes 196
  1331.9 124.5 %copy-start.31 = (f32[16]{0:T(128)S(1)}, f32[16]{0:T(128)}, u32[]{:S(2)}) copy-start(f32[16]{0:T(128)} %param.61) | copy-start | bytes 196
  1331.9 124.5 %copy-start.32 = (f32[16]{0:T(128)S(1)}, f32[16]{0:T(128)}, u32[]{:S(2)}) copy-start(f32[16]{0:T(128)} %param.59) | copy-start | bytes 196
  1331.9 124.5 %copy-start.33 = (f32[16]{0:T(128)S(1)}, f32[16]{0:T(128)}, u32[]{:S(2)}) copy-start(f32[16]{0:T(128)} %param.58) | copy-start | bytes 196
  1331.9 124.5 %copy-start.34 = (f32[16]{0:T(128)S(1)}, f32[16]{0:T(128)}, u32[]{:S(2)}) copy-start(f32[16]{0:T(128)} %param.57) | copy-start | bytes 196
  1331.9 124.5 %copy-start.35 = (f32[16]{0:T(128)S(1)}, f32[16]{0:T(128)}, u32[]{:S(2)}) copy-start(f32[16]{0:T(128)} %param.56) | copy-start | bytes 196
  1331.9 125.9 %copy-start.26 = (f32[512]{0:T(512)S(1)}, f32[512]{0:T(512)}, u32[]{:S(2)}) copy-start(f32[512]{0:T(512)} %param.48) | copy-start | bytes 6148
  1331.9 125.9 %copy-start.27 = (f32[512]{0:T(512)S(1)}, f32[512]{0:T(512)}, u32[]{:S(2)}) copy-start(f32[512]{0:T(512)} %param.49) | copy-start | bytes 6148
  1332.0 126.5 %copy-start.22 = (f32[1024]{0:T(1024)S(1)}, f32[1024]{0:T(1024)}, u32[]{:S(2)}) copy-start(f32[1024]{0:T(1024)} %param.50) | copy-start | bytes 12292
  1332.0 126.5 %copy-start.23 = (f32[1024]{0:T(1024)S(1)}, f32[1024]{0:T(1024)}, u32[]{:S(2)}) copy-start(f32[1024]{0:T(1024)} %param.51) | copy-start | bytes 12292
  1332.0 127.1 %copy-start.12 = (f32[1088]{0:T(1024)S(1)}, f32[1088]{0:T(1024)}, u32[]{:S(2)}) copy-start(f32[1088]{0:T(1024)} %param.40) | copy-start | bytes 13060
  1332.0 127.1 %copy-start.20 = (f32[1088]{0:T(1024)S(1)}, f32[1088]{0:T(1024)}, u32[]{:S(2)}) copy-start(f32[1088]{0:T(1024)} %param.54) | copy-start | bytes 13060
  1332.0 127.1 %copy-start.21 = (f32[1088]{0:T(1024)S(1)}, f32[1088]{0:T(1024)}, u32[]{:S(2)}) copy-start(f32[1088]{0:T(1024)} %param.55) | copy-start | bytes 13060
  1332.0 127.7 %copy-start.7 = (f32[4,1088]{1,0:T(4,128)S(1)}, f32[4,1088]{1,0:T(4,128)}, u32[]{:S(2)}) copy-start(f32[4,1088]{1,0:T(4,128)} %param.39) | copy-start | bytes 52228
  1332.0 127.7 %copy-start.15 = (f32[4,1088]{1,0:T(4,128)S(1)}, f32[4,1088]{1,0:T(4,128)}, u32[]{:S(2)}) copy-start(f32[4,1088]{1,0:T(4,128)} %param.52) | copy-start | bytes 52228
  1332.0 127.7 %copy-start.16 = (f32[4,1088]{1,0:T(4,128)S(1)}, f32[4,1088]{1,0:T(4,128)}, u32[]{:S(2)}) copy-start(f32[4,1088]{1,0:T(4,128)} %param.53) | copy-start | bytes 52228
  1332.1 216.8 %copy-start = (f32[512,1064]{0,1:T(8,128)S(1)}, f32[512,1064]{0,1:T(8,128)}, u32[]{:S(2)}) copy-start(f32[512,1064]{0,1:T(8,128)} %param.35) | copy-start | bytes 6537220
Sparse Core Ops, SparseCore 0:
  10.3 87.4 all-gather.5
  99.6 307.6 all-gather.7
  499.1 153.8 reduce-scatter.8
  655.1 50.0 reduce-scatter.10
  709.4 45.9 all-gather.9
  757.0 155.6 all-gather.11
  1025.9 299.2 reduce-scatter.4
  1332.2 120.5 all-reduce.2
  1455.2 93.5 reduce-scatter.6

commit v2 on v1

--- a/solution.py
+++ b/solution.py
@@ -5,6 +5,7 @@
 import jax.numpy as jnp
 from jax import lax
 from jax.experimental import pallas as pl
+from jax.experimental.layout import Layout, with_layout_constraint
 from jax.experimental.pallas import tpu as pltpu
 from jax.sharding import PartitionSpec as P
 
@@ -45,9 +46,10 @@
 
 
 def segment_of(starts_ref, position):
+    row = pl.program_id(0)
     count = jnp.zeros_like(position)
     for k in range(starts_ref.shape[1]):
-        count = count + (starts_ref[0, k] <= position).astype(jnp.int32)
+        count = count + (starts_ref[row, k] <= position).astype(jnp.int32)
     return count
 
 
@@ -111,12 +113,12 @@
 
 def forward_kernel(
     starts_ref, gate_ref, xin_ref, bc_ref, dt_ref, cw_ref, cb_ref, cwbc_ref, cbbc_ref,
-    shift_ref, logd_ref, skip_ref, gain_ref,
-    mixed_ref, y_ref, state_ref, q_ref,
-    same_ref, enter_ref, last_ref, cmat_ref, bt_ref, score_ref, gated_ref, square_ref,
+    shift_ref, logd_ref, skip_ref,
+    gated_ref, y_ref, state_ref, total_ref,
+    same_ref, enter_ref, last_ref, cmat_ref, bt_ref, score_ref, square_ref,
     x_ref, carry_ref, step_ref, cum_ref, cumt_ref,
 ):
-    j = pl.program_id(0)
+    j = pl.program_id(1)
     length = gate_ref.shape[0]
     chunks = length // Q
     lo = lax.broadcasted_iota(jnp.int32, (Q, 128), 1) < HP
@@ -152,7 +154,7 @@
     for c in range(chunks):
         rows = slice(c * Q, (c + 1) * Q)
         entering_state = carry_ref[...].astype(BF16)
-        state_ref[c] = entering_state
+        state_ref[0, c] = entering_state
         if c > 0:
             outside = dot(cmat_ref[rows, :], entering_state)
         score = score_ref[c]
@@ -179,28 +181,23 @@
             gate = gate_ref[rows, cols].astype(F32)
             gated = (y + skip_ref[:, cols] * x) * (gate * sigmoid(gate))
             square_ref[rows, :] += gated * gated
-            gated_ref[rows, pl.ds(pl.multiple_of(j * BC + p * 128, 128), 128)] = gated
-
-    @pl.when(j == pl.num_programs(0) - 1)
+            gated_ref[rows, cols] = gated
+
+    @pl.when(j == pl.num_programs(1) - 1)
     def _():
-        mean = jnp.sum(square_ref[...], axis=1, keepdims=True) * (1.0 / DI)
-        q = lax.rsqrt(mean + EPSILON)
-        q_ref[...] = q
-        for c in range(DI // 512):
-            cols = slice(c * 512, (c + 1) * 512)
-            mixed_ref[:, cols] = (gated_ref[:, cols] * q * gain_ref[:, cols]).astype(BF16)
-
-
-def backward_kernel(
+        total_ref[...] = jnp.sum(square_ref[...], axis=1, keepdims=True)
+
+
+def backward_body(
     starts_ref, gate_ref, xin_ref, bc_ref, dt_ref, cw_ref, cb_ref, cwbc_ref, cbbc_ref,
     shift_ref, logd_ref, skip_ref, gain_ref, y_ref, state_ref, q_ref, mean_ref, dm_ref,
-    dgate_ref, dxin_ref, dbc_ref, ddt_ref, sgain_ref, scw_ref, scb_ref, scwbc_ref, scbbc_ref,
+    before_ref, dgate_ref, dbc_ref, ddt_ref, sgain_ref, scw_ref, scb_ref, scwbc_ref, scbbc_ref,
     sshift_ref, slogd_ref, sskip_ref,
     same_ref, enter_ref, last_ref, bmat_ref, cmat_ref, ct_ref, score_ref, scoret_ref,
     x_ref, slope_ref, dy_ref, dxs_ref, carry_ref, step_ref, cum_ref, cumt_ref,
-    dscore_ref, db_ref, dc_ref, v1_ref, v2_ref, v3_ref, v4_ref,
+    dscore_ref, db_ref, dc_ref, v1_ref, v2_ref, v3_ref, v4_ref, dxin_ref,
 ):
-    j = pl.program_id(0)
+    j = pl.program_id(1)
     length = gate_ref.shape[0]
     chunks = length // Q
     lo = lax.broadcasted_iota(jnp.int32, (Q, 128), 1) < HP
@@ -252,12 +249,12 @@
         scanned = y_ref[:, cols] + skip_ref[:, cols] * x
         gated = scanned * silu
         scaled = dm_ref[:, cols].astype(F32) * q
-        sgain_ref[:, cols] = jnp.sum(gated * scaled, axis=0, keepdims=True)
+        sgain_ref[0, :, cols] = jnp.sum(gated * scaled, axis=0, keepdims=True)
         d_gated = scaled * gain_ref[:, cols] - gated * mean
         dgate_ref[:, cols] = (d_gated * scanned * (gsig * (1.0 + gate - silu))).astype(dgate_ref.dtype)
         d_scanned = d_gated * silu
         dy_ref[:, cols] = d_scanned
-        sskip_ref[:, cols] = jnp.sum(d_scanned * x, axis=0, keepdims=True)
+        sskip_ref[0, :, cols] = jnp.sum(d_scanned * x, axis=0, keepdims=True)
 
     for c in reversed(range(chunks)):
         rows = slice(c * Q, (c + 1) * Q)
@@ -295,7 +292,7 @@
                 v3_ref[rows, cols] = xs_wide * d_tail
                 d_xs = d_xs + d_tail
                 db_ref[rows, :] += dot_nt((xs_wide * tail).astype(BF16), d_state_low[:, cols])
-                entered = state_ref[c, :, cols]
+                entered = state_ref[0, c, :, cols]
                 v4_ref[c : c + 1, cols] = reach[Q - 1 : Q] * jnp.sum(
                     d_state[:, cols] * entered.astype(F32), axis=0, keepdims=True
                 )
@@ -304,7 +301,7 @@
                 v4_ref[c : c + 1, cols] = jnp.zeros((1, 128), F32)
             if c > 0:
                 reached = (reach * d_y).astype(BF16)
-                dc_ref[rows, :] += dot_nt(reached, state_ref[c, :, cols])
+                dc_ref[rows, :] += dot_nt(reached, state_ref[0, c, :, cols])
                 carry_ref[:, cols] = reach[Q - 1 : Q] * d_state[:, cols] + dot(ct_ref[:, rows], reached)
             v2_ref[rows, cols] = x * d_xs
             dxs_ref[rows, cols] = step_x * d_xs + skip_ref[:, cols] * d_y
@@ -339,18 +336,18 @@
     d_step = h2 - d_rate * decay
     d_raw = d_step * sigmoid(pre)
     ddt_ref[...] = d_raw
-    sshift_ref[...] = jnp.sum(d_raw, axis=1, keepdims=True)
-    slogd_ref[...] = jnp.sum(d_rate * rate, axis=1, keepdims=True)
+    sshift_ref[0] = jnp.sum(d_raw, axis=1, keepdims=True)
+    slogd_ref[0] = jnp.sum(d_rate * rate, axis=1, keepdims=True)
 
     for p in range(PAIRS):
         cols = slice(p * 128, (p + 1) * 128)
         d_conv = dxs_ref[:, cols] * slope_ref[:, cols]
         d_in, s_w, s_b = conv_backward(d_conv, xin_ref[:, cols].astype(F32), cw_ref[:, cols], same_ref)
         dxin_ref[:, cols] = d_in.astype(dxin_ref.dtype)
-        scw_ref[:, cols] = s_w
-        scb_ref[:, cols] = s_b
-
-    @pl.when(j == pl.num_programs(0) - 1)
+        scw_ref[0, :, cols] = s_w
+        scb_ref[0, :, cols] = s_b
+
+    @pl.when(j == pl.num_programs(1) - 1)
     def _():
         for c in range(chunks):
             rows = slice(c * Q, (c + 1) * Q)
@@ -364,55 +361,80 @@
             d_conv = grad_ref[...] * (sig * (1.0 + conv - conv * sig))
             d_in, s_w, s_b = conv_backward(d_conv, bc_ref[:, cols].astype(F32), cwbc_ref[:, cols], same_ref)
             dbc_ref[:, cols] = d_in.astype(dbc_ref.dtype)
-            scwbc_ref[:, cols] = s_w
-            scbbc_ref[:, cols] = s_b
-
-
-def column_block(rows, offset=0):
-    return pl.BlockSpec((rows, BC), lambda j: (0, j + offset))
+            scwbc_ref[0, :, cols] = s_w
+            scbbc_ref[0, :, cols] = s_b
+
+
+def backward_kernel(*refs):
+    outputs_at = 18
+
+    @pl.when(pl.program_id(2) == 0)
+    def _():
+        backward_body(*refs)
+
+    @pl.when(pl.program_id(2) == 1)
+    def _():
+        refs[outputs_at + 1][...] = refs[-1][...]
+
+
+def backward_first(*refs):
+    backward_kernel(*refs[:18], None, *refs[18:])
+
+
+def row_block(first, rows, offset=0):
+    return pl.BlockSpec((rows, BC), lambda r, j, *s: (first + r, j + offset))
+
+
+def columns(rows):
+    return pl.BlockSpec((rows, BC), lambda r, j, *s: (0, j))
 
 
 def whole(*shape):
-    return pl.BlockSpec(shape, lambda j: (0,) * len(shape))
-
-
-def common_specs(length):
-    heads = pl.BlockSpec((HB, 1), lambda j: (j, 0))
+    return pl.BlockSpec(shape, lambda r, j, *s: (0,) * len(shape))
+
+
+def row_sums(rows):
+    return pl.BlockSpec((1, rows, BC), lambda r, j, *s: (r, 0, j))
+
+
+def common_specs(first, length, channels):
+    heads = pl.BlockSpec((HB, 1), lambda r, j, *s: (j, 0))
     return [
         pl.BlockSpec(memory_space=pltpu.SMEM),
-        column_block(length),
-        column_block(length, DI // BC),
-        pl.BlockSpec((length, 2 * NS), lambda j: (0, 2 * DI // (2 * NS))),
-        pl.BlockSpec((HB, length), lambda j: (j, 0)),
-        column_block(CONVW),
-        column_block(1),
-        pl.BlockSpec((CONVW, 2 * NS), lambda j: (0, DI // (2 * NS))),
-        pl.BlockSpec((1, 2 * NS), lambda j: (0, DI // (2 * NS))),
+        row_block(first, length),
+        row_block(first, length, channels // BC),
+        pl.BlockSpec((length, 2 * NS), lambda r, j, *s: (first + r, 0)),
+        pl.BlockSpec((HB, length), lambda r, j, *s: (j, first + r)),
+        columns(CONVW),
+        columns(1),
+        whole(CONVW, 2 * NS),
+        whole(1, 2 * NS),
         heads,
         heads,
-        column_block(1),
+        columns(1),
     ]
 
 
-def mix_forward(starts, projected, dt_rows, conv_w, conv_b, shift, logd, skip_cols, gain):
-    length = projected.shape[0]
+def mix_forward(first, length, starts, main, extra, dt_rows, conv_w, conv_b, cw_bc, cb_bc, shift, logd, skip_cols):
+    rows = starts.shape[0]
+    channels = main.shape[1] // 2
     chunks = length // Q
     vmem = pltpu.VMEM
     return pl.pallas_call(
         forward_kernel,
-        grid=(DI // BC,),
-        in_specs=common_specs(length) + [whole(1, DI)],
+        grid=(rows, channels // BC),
+        in_specs=common_specs(first, length, channels),
         out_specs=[
-            whole(length, DI),
-            column_block(length),
-            pl.BlockSpec((chunks, NS, BC), lambda j: (0, 0, j)),
-            whole(length, 1),
+            row_block(0, length),
+            row_block(0, length),
+            pl.BlockSpec((1, chunks, NS, BC), lambda r, j: (r, 0, 0, j)),
+            pl.BlockSpec((length, 1), lambda r, j: (r, 0)),
         ],
         out_shape=[
-            jax.ShapeDtypeStruct((length, DI), BF16),
-            jax.ShapeDtypeStruct((length, DI), F32),
-            jax.ShapeDtypeStruct((chunks, NS, DI), BF16),
-            jax.ShapeDtypeStruct((length, 1), F32),
+            jax.ShapeDtypeStruct((rows * length, channels), F32),
+            jax.ShapeDtypeStruct((rows * length, channels), F32),
+            jax.ShapeDtypeStruct((rows, chunks, NS, channels), BF16),
+            jax.ShapeDtypeStruct((rows * length, 1), F32),
         ],
         scratch_shapes=[
             vmem((CONVW - 1, length, 128), F32),
@@ -421,7 +443,6 @@
             vmem((length, NS), BF16),
             vmem((NS, length), BF16),
             vmem((chunks, Q, Q), F32),
-            vmem((length, DI), F32),
             vmem((length, 128), F32),
             vmem((length, BC), F32),
             vmem((NS, BC), F32),
@@ -429,57 +450,70 @@
             vmem((length, HB), F32),
             vmem((HB, length), F32),
         ],
-        compiler_params=pltpu.CompilerParams(vmem_limit_bytes=56 * 1024 * 1024),
+        compiler_params=pltpu.CompilerParams(vmem_limit_bytes=48 * 1024 * 1024),
         name="mix_forward",
-    )(starts, projected, projected, projected, dt_rows, conv_w, conv_b, conv_w, conv_b, shift, logd, skip_cols, gain)
-
-
-def mix_backward(starts, projected, dt_rows, conv_w, conv_b, shift, logd, skip_cols, gain, y, states, q, mean, d_mixed):
-    length = projected.shape[0]
+    )(starts, main, main, extra, dt_rows, conv_w, conv_b, cw_bc, cb_bc, shift, logd, skip_cols)
+
+
+def mix_backward(
+    first, total, length, before, starts, main, extra, dt_rows, conv_w, conv_b, cw_bc, cb_bc, shift, logd, skip_cols,
+    gain, y, states, q, mean, d_mixed,
+):
+    rows = starts.shape[0]
+    channels = main.shape[1] // 2
+    heads = channels // HP
+    blocks = channels // BC
     chunks = length // Q
     vmem = pltpu.VMEM
-    heads = pl.BlockSpec((HB, 1), lambda j: (j, 0))
-    col = whole(length, 1)
+    per_head = pl.BlockSpec((1, HB, 1), lambda r, j, s: (r, j, 0))
+    col = pl.BlockSpec((length, 1), lambda r, j, s: (first + r, 0))
     shape = jax.ShapeDtypeStruct
+    operands = (
+        starts, main, main, extra, dt_rows, conv_w, conv_b, cw_bc, cb_bc, shift, logd, skip_cols,
+        gain, y, states, q, mean, d_mixed,
+    )
+    in_specs = common_specs(first, length, channels) + [
+        columns(1),
+        row_block(0, length),
+        pl.BlockSpec((1, chunks, NS, BC), lambda r, j, s: (r, 0, 0, j)),
+        col,
+        col,
+        row_block(first, length),
+    ]
+    aliases = {}
+    if before is not None:
+        aliases = {len(operands): 0}
+        operands = operands + (before,)
+        in_specs = in_specs + [pl.BlockSpec(memory_space=pl.ANY)]
     return pl.pallas_call(
-        backward_kernel,
-        grid=(DI // BC,),
-        in_specs=common_specs(length)
-        + [
-            column_block(1),
-            column_block(length),
-            pl.BlockSpec((chunks, NS, BC), lambda j: (0, 0, j)),
-            col,
-            col,
-            column_block(length),
-        ],
+        backward_first if before is None else backward_kernel,
+        grid=(rows, blocks, 2),
+        in_specs=in_specs,
         out_specs=[
-            column_block(length),
-            column_block(length),
-            whole(length, 2 * NS),
-            pl.BlockSpec((HB, length), lambda j: (j, 0)),
-            column_block(1),
-            column_block(CONVW),
-            column_block(1),
-            whole(CONVW, 2 * NS),
-            whole(1, 2 * NS),
-            heads,
-            heads,
-            column_block(1),
+            pl.BlockSpec((length, BC), lambda r, j, s: (first + r, j + blocks * s)),
+            pl.BlockSpec((length, 2 * NS), lambda r, j, s: (r, 0)),
+            pl.BlockSpec((HB, length), lambda r, j, s: (j, r)),
+            row_sums(1),
+            row_sums(CONVW),
+            row_sums(1),
+            pl.BlockSpec((1, CONVW, 2 * NS), lambda r, j, s: (r, 0, 0)),
+            pl.BlockSpec((1, 1, 2 * NS), lambda r, j, s: (r, 0, 0)),
+            per_head,
+            per_head,
+            row_sums(1),
         ],
         out_shape=[
-            shape((length, DI), BF16),
-            shape((length, DI), BF16),
-            shape((length, 2 * NS), BF16),
-            shape((NH, length), F32),
-            shape((1, DI), F32),
-            shape((CONVW, DI), F32),
-            shape((1, DI), F32),
-            shape((CONVW, 2 * NS), F32),
-            shape((1, 2 * NS), F32),
-            shape((NH, 1), F32),
-            shape((NH, 1), F32),
-            shape((1, DI), F32),
+            shape((total * length, 2 * channels), BF16),
+            shape((rows * length, 2 * NS), BF16),
+            shape((heads, rows * length), F32),
+            shape((rows, 1, channels), F32),
+            shape((rows, CONVW, channels), F32),
+            shape((rows, 1, channels), F32),
+            shape((rows, CONVW, 2 * NS), F32),
+            shape((rows, 1, 2 * NS), F32),
+            shape((rows, heads, 1), F32),
+            shape((rows, heads, 1), F32),
+            shape((rows, 1, channels), F32),
         ],
         scratch_shapes=[
             vmem((CONVW - 1, length, 128), F32),
@@ -505,17 +539,16 @@
             vmem((length, BC), F32),
             vmem((length, BC), F32),
             vmem((8, BC), F32),
+            vmem((length, BC), BF16),
         ],
-        compiler_params=pltpu.CompilerParams(vmem_limit_bytes=56 * 1024 * 1024),
+        input_output_aliases=aliases,
+        compiler_params=pltpu.CompilerParams(vmem_limit_bytes=48 * 1024 * 1024),
         name="mix_backward",
-    )(
-        starts, projected, projected, projected, dt_rows, conv_w, conv_b, conv_w, conv_b, shift, logd, skip_cols,
-        gain, y, states, q, mean, d_mixed,
-    )
-
-
-def rms_scale(values, gain):
-    return values * lax.rsqrt(jnp.mean(values * values, axis=-1, keepdims=True) + EPSILON) * gain
+    )(*operands)
+
+
+MAIN = 2 * DI
+EXTRA = 2 * NS + NH
 
 
 def adam_direction(weight, gradient, first, second, decayed):
@@ -529,34 +562,508 @@
     return (direction, first_new, second_new)
 
 
-def gather_small(values):
-    flat = jnp.concatenate([v.astype(BF16).reshape(-1) for v in values])
-    every = lax.all_gather(flat, "fsdp", axis=0, tiled=False)
+def swap(value, axis, mask):
+    size = lax.axis_size(axis)
+    return lax.ppermute(value, axis, [(i, i ^ mask) for i in range(size)])
+
+
+def bits_of(size):
+    return [1 << b for b in reversed(range(size.bit_length() - 1))]
+
+
+def place(buffer, shape, block, at, items):
+    arrays, copies, table = [], [], [at[0], at[1]]
+    for array, lead, row, col, valid, cuts in items:
+        if not any(array is a for a in arrays):
+            arrays.append(array)
+        source = [array is a for a in arrays].index(True)
+        for start, end in zip(cuts[:-1], cuts[1:]):
+            copies.append((source, lead, start, end - start))
+            table.extend([row, col, valid])
+    table = jnp.stack([jnp.asarray(v, jnp.int32) for v in table])
+    operands = [table] + arrays + ([] if buffer is None else [buffer])
+
+    def kernel(table_ref, *refs):
+        out_ref = refs[-1]
+        for i, (source, lead, start, size) in enumerate(copies):
+            piece = refs[source]
+            row = pl.multiple_of(table_ref[3 * i + 2] + start, 16)
+            col = pl.multiple_of(table_ref[3 * i + 3], 128)
+
+            @pl.when(table_ref[3 * i + 4] > start)
+            def _():
+                rows = pl.ds(start, size)
+                value = piece[rows, :] if lead is None else piece[lead, rows, :]
+                out_ref[pl.ds(row, size), pl.ds(col, value.shape[1])] = value
+
+    def all_of(a):
+        return pl.BlockSpec(a.shape, lambda i, t: (0,) * a.ndim)
+
+    return pl.pallas_call(
+        kernel,
+        grid_spec=pltpu.PrefetchScalarGridSpec(
+            num_scalar_prefetch=1,
+            grid=(1,),
+            in_specs=[all_of(a) for a in arrays] + ([] if buffer is None else [pl.BlockSpec(memory_space=pl.ANY)]),
+            out_specs=pl.BlockSpec(block, lambda i, t: (t[0], t[1])),
+        ),
+        out_shape=jax.ShapeDtypeStruct(shape, BF16),
+        input_output_aliases={} if buffer is None else {len(operands) - 1: 0},
+        compiler_params=pltpu.CompilerParams(vmem_limit_bytes=32 * 1024 * 1024),
+        name="place",
+    )(*operands)
+
+
+def rows_into(buffer, row, rows, pieces, gain=None):
+    size, width = sum(p.shape[0] for p in pieces), pieces[0].shape[1]
+    operands = list(pieces) + ([] if gain is None else [gain]) + ([] if buffer is None else [buffer])
+
+    def kernel(*refs):
+        at = 0
+        for i, piece in enumerate(pieces):
+            for start in range(0, piece.shape[0], 128):
+                value = refs[i][start : start + 128, :]
+                if gain is not None:
+                    value = value.astype(F32)
+                    mean = jnp.mean(value * value, axis=1, keepdims=True)
+                    value = (value * lax.rsqrt(mean + EPSILON) * refs[len(pieces)][...]).astype(BF16)
+                refs[-1][at + start : at + start + 128, :] = value
+            at += piece.shape[0]
+
+    specs = [pl.BlockSpec(p.shape, lambda i: (0, 0)) for p in operands]
+    if buffer is not None:
+        specs[-1] = pl.BlockSpec(memory_space=pl.ANY)
+    return pl.pallas_call(
+        kernel,
+        grid=(1,),
+        in_specs=specs,
+        out_specs=pl.BlockSpec((size, width), lambda i: (row, 0)),
+        out_shape=jax.ShapeDtypeStruct((rows * size, width), BF16),
+        input_output_aliases={} if buffer is None else {len(operands) - 1: 0},
+        compiler_params=pltpu.CompilerParams(vmem_limit_bytes=32 * 1024 * 1024),
+        name="rows_into",
+    )(*operands)
+
+
+def prefix_count(g, n, unit, period):
+    return (n // period) * unit + jnp.clip(n % period - g * unit, 0, unit)
+
+
+def static_count(g, n, unit, period):
+    return (n // period) * unit + min(max(n % period - g * unit, 0), unit)
+
+
+def then(value, *earlier):
+    return lax.optimization_barrier((value,) + earlier)[0]
+
+
+def spread_z(bundle, masks, late=()):
+    have, order = bundle[None], [0]
+    for i, mask in enumerate(masks):
+        if i > 0:
+            have = then(have, *late)
+        have = jnp.concatenate([have, swap(have, "dp", 2 * mask)])
+        order = order + [rel ^ mask for rel in order]
+    return have, order
+
+
+def grouped(tokens, cotangent, doc_starts, valid_len, weights, firsts, seconds):
+    w_in, w_out, norm_gain, gate_gain, conv_w, conv_b, dt_bias, a_log, d_skip = weights
+    small = weights[2:]
+    dp, groups = lax.axis_size("dp"), lax.axis_size("fsdp")
+    zs = dp // 2
+    d, f = lax.axis_index("dp"), lax.axis_index("fsdp")
+    z, c = d // 2, d % 2
+    z_masks = bits_of(zs)
+    length, width = tokens.shape[1], tokens.shape[2]
+    local = DI // groups
+    unit = local // groups
+    k_rows, per_dev = w_in.shape
+    k_half = k_rows // 2
+    per_chip = 2 * per_dev
+    out_cols = w_out.shape[1]
+    sizes = {
+        (zz, g): static_count(g, min(per_chip * (zz + 1), MAIN), unit, local)
+        - static_count(g, min(per_chip * zz, MAIN), unit, local)
+        for zz in range(zs)
+        for g in range(groups)
+    }
+    cuts = [0] + sorted(set(sizes.values()) - {0})
+    most = cuts[-1]
+
+    def first_row(zz):
+        return prefix_count(f, jnp.minimum(per_chip * zz, MAIN), unit, local)
+
+    def rows_valid(zz):
+        return first_row(zz + 1) - first_row(zz)
+
+    def slice_row(row):
+        return jnp.minimum(row, 2 * local - most)
+
+    low = w_in.astype(BF16)
+    mine = lax.dynamic_slice_in_dim(low, k_half * c, k_half, 0)
+    other = swap(lax.dynamic_slice_in_dim(low, k_half * (1 - c), k_half, 0), "dp", 1)
+    chip = jnp.concatenate([jnp.where(c == 0, mine, other), jnp.where(c == 0, other, mine)], axis=1)
+    half = length // 2
+
+    def neighbours(row, which):
+        parts = (row[:half], row[half:])
+        return [swap(parts[which], "fsdp", 1), swap(parts[1 - which], "fsdp", 2)]
+
+    def corners(first):
+        return [swap(first[0], "fsdp", 2), swap(first[1], "fsdp", 1)]
+
+    def pieces_of(first, second, third):
+        return [[first[0], second[0]], [second[1], first[1]], third]
+
+    near = neighbours(tokens[0], 0)
+    chip = then(chip, *near)
+    column = per_chip * z + jnp.arange(per_chip, dtype=jnp.int32)
+    owner = (column // unit) % groups
+    begin = prefix_count(owner, per_chip * z, unit, local)
+    rank = prefix_count(owner, column, unit, local) - begin
+    moved = begin - slice_row(begin)
+    extra_key = groups * most + column - MAIN
+    places = jnp.arange(groups * most + EXTRA, dtype=jnp.int32)[:, None]
+
+    def picks(ranks):
+        key = jnp.where(column < MAIN, (owner ^ f) * most + ranks, extra_key)
+        return (places == key[None, :]).astype(BF16)
+
+    parts = dot_nt(picks(rank), chip).astype(BF16)
+
+    def own_channels(v):
+        v = v.reshape(v.shape[0], groups, groups, -1)
+        return lax.dynamic_index_in_dim(v, f, 2, keepdims=False).reshape(v.shape[0], -1)
+
+    blocks = [parts[m * most : (m + 1) * most] for m in range(groups)]
+    blocks = blocks[:1] + [swap(blocks[m], "fsdp", m) for m in range(1, groups)]
+    first = jnp.concatenate([blocks[0], parts[groups * most :]])[None]
+    second = jnp.concatenate(blocks[1:])[None]
+    got = swap(first, "dp", 2 * z_masks[0])
+    first_2 = jnp.concatenate([first, got])
+    sent_a = then(first_2, second)
+    sent_b = then(second, first_2)
+    got_a = swap(sent_a, "dp", 2 * z_masks[1])
+    got_b = swap(sent_b, "dp", 2 * z_masks[0])
+    far = corners([then(v, sent_a) for v in near])
+    near_2 = neighbours(then(tokens[0], sent_a), 1)
+    marks = jnp.concatenate([doc_starts[0], valid_len])
+    marks = jnp.concatenate([(marks // 32).astype(BF16), (marks % 32).astype(BF16)])
+    flat = then(jnp.concatenate([marks] + [v.astype(BF16).reshape(-1) for v in small])[None], first_2)
+    rel_small = jnp.concatenate([flat] + [swap(flat, "fsdp", m) for m in range(1, groups)])
+    count = marks.shape[0] // 2
+    marks = rel_small[:, : 2 * count].astype(jnp.int32)
+    marks = marks[:, :count] * 32 + marks[:, count:]
+    rel_small = rel_small[:, 2 * count :]
+    order = jnp.arange(groups, dtype=jnp.int32) ^ f
+    every = jnp.sum(
+        jnp.where((order[None, :] == jnp.arange(groups)[:, None])[:, :, None], rel_small[None], 0), axis=1
+    ).astype(F32)
+    full, at = [], 0
+    for v in small:
+        piece = every[:, at : at + v.size]
+        at += v.size
+        if v.ndim == 1:
+            full.append(piece.reshape(1, -1))
+        else:
+            full.append(jnp.moveaxis(piece.reshape((-1,) + v.shape), 0, 1).reshape(v.shape[0], -1))
+    norm_full, gate_full, convw_full, convb_full, shift_full, logd_full, skip_full = full
+
+    hidden = tokens[0].astype(F32)
+    upstream = cotangent[0].astype(F32)
+    live = (jnp.arange(length, dtype=jnp.int32) < valid_len[0]).astype(F32)[:, None]
+    starts = marks[:, :-1]
+    live_all = jnp.concatenate([(jnp.arange(length) < marks[r, -1]).astype(F32)[:, None] for r in range(groups)])
+
+    second_2 = then(jnp.concatenate([second, got_b]), got_a, *near_2)
+    got_b2 = swap(second_2, "dp", 2 * z_masks[1])
+    spread_a = jnp.concatenate([first_2, got_a])
+    order_z = [0, z_masks[0]] + [z_masks[1], z_masks[0] ^ z_masks[1]]
+    sibling_a = swap(then(spread_a, second_2), "dp", 1)
+    sibling_b = swap(second_2, "dp", 1)
+    near_pieces = pieces_of(near, near_2, far)
+    normed_all = None
+    for m in range(groups - 1):
+        row = [then(tokens[0], second_2)] if m == 0 else near_pieces[m - 1]
+        normed_all = rows_into(normed_all, m, groups, row, norm_full)
+    extra_at = jnp.stack([jnp.int32(r) for r in order_z]) == (z ^ (zs - 1))
+    extra_at = jnp.sum(jnp.where(extra_at, jnp.arange(zs, dtype=jnp.int32), 0))
+    extra_own = lax.dynamic_index_in_dim(then(spread_a, second_2), extra_at, 0, keepdims=False)[most:]
+    extra_got = jnp.stack([extra_own] + [swap(extra_own, "fsdp", m) for m in range(1, groups)])
+    extra_got = then(extra_got, normed_all)
+    extra_pair = [extra_got, swap(extra_got, "dp", 1)]
+    up_near = neighbours(then(cotangent[0], second_2), 0)
+    got_b2 = then(got_b2, normed_all, *far)
+    sibling_b2 = swap(got_b2, "dp", 1)
+    normed_all = rows_into(then(normed_all, got_b2), groups - 1, groups, near_pieces[-1], norm_full)
+    bundles_in = [
+        [(spread_a, range(zs))],
+        [(second_2, range(2)), (got_b2, range(2, zs))],
+        [(sibling_a, range(zs))],
+        [(sibling_b, range(2)), (sibling_b2, range(2, zs))],
+    ]
+    w_main = None
+    for rc in range(2):
+        for m in range(groups):
+            items, skip = [], 0 if m == 0 else most * (m - 1)
+            for array, ranks in bundles_in[2 * rc + (m > 0)]:
+                for at, i in enumerate(ranks):
+                    zz = z ^ order_z[i]
+                    valid = rows_valid(zz) + skip
+                    items.append((array, at, first_row(zz) - skip, 0, valid, [e + skip for e in cuts]))
+            w_main = place(w_main, (2 * local, width), (2 * local, k_half), (0, 2 * (f ^ m) + (c ^ rc)), items)
+    extra_items = []
+    for m in range(groups):
+        for rc in range(2):
+            extra_items.append((extra_pair[rc], m, 0, k_rows * (f ^ m) + k_half * (c ^ rc), EXTRA, (0, EXTRA)))
+    w_extra = place(None, (EXTRA, width), (EXTRA, width), (0, 0), extra_items)
+
+    out_low = w_out.astype(BF16).reshape(groups, unit, out_cols)
+    blocks = [lax.dynamic_index_in_dim(out_low, f ^ m, 0, keepdims=False) for m in range(groups)]
+    blocks = jnp.concatenate([blocks[0]] + [swap(blocks[m], "fsdp", m) for m in range(1, groups)])
+    out_1 = then(blocks[None], w_main)
+    out_2 = jnp.concatenate([out_1, swap(out_1, "dp", 2 * z_masks[0])])
+    out_got = swap(out_2, "dp", 2 * z_masks[1])
+    out_spread = jnp.concatenate([out_2, out_got])
+    out_items = []
+    for rc, array in enumerate((out_spread, swap(out_spread, "dp", 1))):
+        for i, rel in enumerate(order_z):
+            col = out_cols * (2 * (z ^ rel) + (c ^ rc))
+            for m in range(groups):
+                out_items.append((array, i, unit * (f ^ m) - unit * m, col, local, (unit * m, unit * (m + 1))))
+    w_out_own = place(None, (local, width), (local, width), (0, 0), out_items)
+    up_near_2 = neighbours(then(cotangent[0], w_main), 1)
+    up_far = corners([then(v, w_main) for v in up_near])
+
+    extra = dot_nt(normed_all, w_extra)
+    main = dot_nt(then(normed_all, extra), w_main)
+    raw_dt = extra[:, 2 * NS :].reshape(-1, groups, groups, NH // groups // groups)
+    dt_rows = lax.dynamic_index_in_dim(raw_dt, f, 2, keepdims=False).reshape(groups * length, -1).T
+    common = (
+        main, extra, dt_rows,
+        own_channels(convw_full[:, :DI]), own_channels(convb_full[:, :DI]), convw_full[:, DI:], convb_full[:, DI:],
+        own_channels(shift_full).T, own_channels(logd_full).T, own_channels(jnp.repeat(skip_full, HP, axis=1)),
+    )
+    due = [[out_2, *up_near_2], [out_spread, *up_far]]
+    up_pieces = pieces_of(up_near, up_near_2, up_far)
+    half_rows = groups // 2
+    results = []
+    for i in range(2):
+        begin = then(starts[i * half_rows : (i + 1) * half_rows], *due[i], *[v[3] for v in results])
+        results.append(mix_forward(i * half_rows, length, begin, *common))
+    gated, y, states, squares = zip(*results)
+    gain = own_channels(gate_full)
+
+    def group_sum(v):
+        for mask in bits_of(groups):
+            got = swap(v, "fsdp", mask)
+            v = v + jnp.stack([got[r ^ mask] for r in range(groups)])
+        return v
+
+    squares = group_sum(jnp.concatenate(squares).reshape(groups, length))
+    q = lax.rsqrt(squares.reshape(-1, 1) * (1.0 / DI) + EPSILON)
+    mixed = jnp.concatenate(
+        [(g * q[i * half_rows * length : (i + 1) * half_rows * length] * gain).astype(BF16) for i, g in enumerate(gated)]
+    )
+    upstream_all = None
+    for m in range(groups):
+        upstream_all = rows_into(upstream_all, m, groups, [cotangent[0]] if m == 0 else up_pieces[m - 1])
+    mixed_live = mixed * live_all.astype(BF16)
+    d_mixed = (dot_nt(upstream_all, w_out_own) * live_all).astype(BF16)
+    inner = jnp.sum(mixed.astype(F32) * d_mixed.astype(F32), axis=1).reshape(groups, length)
+    mean = q * q * group_sum(inner).reshape(-1, 1) * (1.0 / DI)
+
+    def sum_low(a, b):
+        return (a.astype(F32) + b.astype(F32)).astype(BF16)
+
+    def rows_home(partial):
+        pieces, sent = [], []
+        for at, (one, two) in ((0, (1, 2)), (half, (2, 1))):
+            rows = [partial[m * length + at : m * length + at + half] for m in range(groups)]
+            got = swap(jnp.concatenate([rows[one], rows[3]]), "fsdp", one)
+            passed = sum_low(rows[two], got[half:])
+            sent.append(passed)
+            pieces.append((rows[0], got[:half], swap(passed, "fsdp", two)))
+        return pieces, sent
+
+    def added(pieces):
+        return jnp.concatenate([a.astype(F32) + b.astype(F32) + c.astype(F32) for a, b, c in pieces])
+
+    contract = (((0,), (0,)), ((), ()))
+
+    def sum_rows(a, b):
+        return with_layout_constraint(
+            lax.dot_general(a, b, contract, preferred_element_type=F32).astype(BF16), Layout((0, 1))
+        )
+
+
+    def out_columns(core):
+        cols = [lax.dynamic_slice_in_dim(upstream_all, out_cols * (2 * i + core), out_cols, 1) for i in range(zs)]
+        return jnp.concatenate(cols, axis=1)
+
+    out_theirs = swap(sum_rows(mixed_live, out_columns(1 - c)), "dp", 1)
+    out_ours = sum_rows(mixed_live, out_columns(c))
+    branch_home, branch_sent = rows_home(dot(then(mixed, mean), w_out_own).astype(BF16))
+    out_sum = sum_low(out_ours, out_theirs)
+    flying = [lax.dynamic_slice_in_dim(out_sum, out_cols * (z ^ r), out_cols, 1) for r in range(zs)]
+    d_main, backs = None, []
+    operand = d_mixed
+    for i in range(2):
+        if i < len(z_masks):
+            mask = z_masks[-1 - i]
+            sent = jnp.stack(flying[1::2])
+            operand = then(d_mixed, sent, *([] if i == 0 else branch_sent))
+            got = swap(sent, "dp", 2 * mask)
+            keep = flying[0::2]
+        begin = starts[i * half_rows : (i + 1) * half_rows]
+        result = mix_backward(
+            i * half_rows, groups, length, d_main, begin, *common, gain, y[i], states[i], q, mean, operand
+        )
+        d_main = result[0]
+        if i < len(z_masks):
+            got = then(got, d_main)
+            flying = [sum_low(k, got[j]) for j, k in enumerate(keep)]
+        backs.append(result[1:])
+    for mask in z_masks[::-1][2:]:
+        got = swap(jnp.stack(flying[1::2]), "dp", 2 * mask)
+        flying = [sum_low(k, got[j]) for j, k in enumerate(flying[0::2])]
+    out_rows = [lax.dynamic_slice_in_dim(flying[0], unit * (f ^ m), unit, 0) for m in range(groups)]
+    out_parts = jnp.stack([out_rows[0]] + [swap(out_rows[m], "fsdp", m) for m in range(1, groups)])
+    d_bc_in = jnp.concatenate([b[0] for b in backs])
+    d_dt = jnp.concatenate([b[1] for b in backs], axis=1)
+    s_gain, s_cw, s_cb, s_cwbc, s_cbbc, s_shift, s_logd, s_skip = [
+        sum(p.sum(axis=0) for p in v) for v in list(zip(*backs))[2:]
+    ]
+    here = (jnp.arange(groups, dtype=jnp.int32) == f).astype(F32)
+
+    def all_channels(v):
+        v = v.reshape(v.shape[0], groups, 1, -1)
+        return (v * here[None, None, :, None]).reshape(v.shape[0], -1)
+
+    d_extra = jnp.concatenate([d_bc_in, all_channels(d_dt.T).astype(BF16)], axis=1)
+
+    bundles = [(groups - 2, groups - 1), (0, 1)]
+
+    def bundle_sum(source, bundle, rc):
+        block = [lax.dynamic_slice_in_dim(normed_all, k_rows * (f ^ m) + k_half * (c ^ rc), k_half, 1) for m in bundle]
+        return sum_rows(source, jnp.concatenate(block, axis=1))
+
+    def chip_blocks(ours, got):
+        blocks = []
+        for r in range(zs):
+            row = slice_row(first_row(z ^ r))
+            blocks.append(sum_low(*[lax.dynamic_slice_in_dim(v, row, most, 0) for v in (ours, got)]))
+        return blocks
+
+    def send_z(blocks, mask):
+        sent = jnp.stack(blocks[1::2])
+        return blocks[0::2], swap(sent, "dp", 2 * mask), sent
+
+    def add_z(flying):
+        keep, got, _ = flying
+        return [sum_low(k, got[i]) for i, k in enumerate(keep)]
+
+    extra_sum = sum_rows(d_extra, normed_all)
+    halves_e = extra_sum.reshape(EXTRA, groups, 2, k_half)
+    extra_theirs = swap(lax.dynamic_index_in_dim(halves_e, 1 - c, 2, keepdims=False), "dp", 1)
+    extra_ours = lax.dynamic_index_in_dim(halves_e, c, 2, keepdims=False)
+    theirs_a = bundle_sum(then(d_main, extra_sum), bundles[0], 1)
+    got_a = swap(theirs_a, "dp", 1)
+    ours_a = bundle_sum(then(d_main, theirs_a), bundles[0], 0)
+    both = then(extra_ours.astype(F32) + extra_theirs.astype(F32), ours_a)
+    flying_a = send_z(chip_blocks(ours_a, got_a), z_masks[-1])
+    theirs_b = bundle_sum(then(d_main, flying_a[2]), bundles[1], 1)
+    got_b = swap(theirs_b, "dp", 1)
+    ours_b = bundle_sum(then(d_main, theirs_b), bundles[1], 0)
+    total = lax.dynamic_index_in_dim(both, f, 1, keepdims=False)
+    for m in range(1, groups):
+        total = total + swap(
+            lax.dynamic_index_in_dim(both, f ^ m, 1, keepdims=False).astype(BF16), "fsdp", m
+        ).astype(F32)
+    total = then(total.astype(BF16), ours_b)
+    flying_b = send_z([then(v, total) for v in chip_blocks(ours_b, got_b)], z_masks[-1])
+    partial = (dot(then(d_main, flying_b[2]), w_main) + dot(d_extra, w_extra)).astype(BF16)
+    d_normed_home, d_normed_sent = rows_home(partial)
+    held = [partial, *[v for piece in branch_home for v in piece]]
+    flying_a = send_z([then(v, *held) for v in add_z(flying_a)], z_masks[0])
+    total = sum_low(total, swap(then(total, flying_a[2]), "dp", 2 * z_masks[-1]))
+    flying_b = send_z([then(v, flying_a[2]) for v in add_z(flying_b)], z_masks[0])
+    total = sum_low(total, swap(then(total, flying_b[2]), "dp", 2 * z_masks[0]))
+    flying_a = (flying_a[0], then(flying_a[1], flying_b[2]), None)
+    flying_b = (flying_b[0], then(flying_b[1], *d_normed_sent), None)
+    recv = [None] * groups
+    for flying, bundle in ((flying_a, bundles[0]), (flying_b, bundles[1])):
+        block = add_z(flying)[0]
+        for i, m in enumerate(bundle):
+            piece = block[:, i * k_half : (i + 1) * k_half]
+            recv[m] = piece if m == 0 else swap(piece, "fsdp", m)
+
+
+    out_parts = then(out_parts, flying_a[1])
+    grad_out = jnp.concatenate(
+        [lax.dynamic_index_in_dim(out_parts, f ^ g, 0, keepdims=False) for g in range(groups)]
+    ).astype(F32)
+    blocks = jnp.concatenate(recv + [total])
+    grad_chip = lax.dot_general(blocks, picks(rank + moved), contract, preferred_element_type=F32).astype(BF16)
+    left, right = grad_chip[:, :per_dev], grad_chip[:, per_dev:]
+    own = jnp.where(c == 0, left, right)
+    got = swap(jnp.where(c == 0, right, left), "dp", 1)
+    grad_in = jnp.concatenate([jnp.where(c == 0, own, got), jnp.where(c == 0, got, own)]).astype(F32)
+
+    out_tokens = (hidden + added(branch_home) * live).astype(BF16)
+    d_normed = added(d_normed_home)
+    scale = lax.rsqrt(jnp.mean(hidden * hidden, axis=-1, keepdims=True) + EPSILON)
+    weighted = norm_full * d_normed
+    average = jnp.mean(hidden * weighted, axis=-1, keepdims=True)
+    grad_tokens = upstream + scale * weighted - hidden * (scale * scale * scale * average)
+    s_norm = jnp.sum(hidden * scale * d_normed, axis=0)
+
+    small_sums = (
+        s_norm[None],
+        all_channels(s_gain),
+        jnp.concatenate([all_channels(s_cw), s_cwbc], axis=1),
+        jnp.concatenate([all_channels(s_cb), s_cbbc], axis=1),
+        all_channels(s_shift.T),
+        all_channels(s_logd.T),
+        all_channels(s_skip.reshape(1, -1, HP).sum(axis=2)),
+    )
+    flat = jnp.concatenate(
+        [jnp.moveaxis(s.reshape(s.shape[0], groups, -1), 1, 0).reshape(groups, -1) for s in small_sums], axis=1
+    )
+    mine = lax.dynamic_index_in_dim(flat, f, 0, keepdims=True)
+    for m in range(1, groups):
+        mine = mine + swap(lax.dynamic_index_in_dim(flat, f ^ m, 0, keepdims=True), "fsdp", m)
+    for mask in bits_of(dp):
+        mine = mine + swap(mine, "dp", mask)
+    return out_tokens, grad_tokens, (grad_in, grad_out) + split_small(mine[0], small)
+
+
+def split_small(flat, small):
     result, at = [], 0
-    for v in values:
-        size = v.size
-        piece = every[:, at : at + size].astype(F32)
-        at += size
-        if v.ndim == 1:
-            result.append(piece.reshape(1, -1))
-        else:
-            result.append(jnp.moveaxis(piece.reshape((-1,) + v.shape), 0, 1).reshape(v.shape[0], -1))
-    return result
-
-
-def shards(
-    tokens, cotangent, doc_starts, valid_len,
-    w_in, w_out, norm_gain, gate_gain, conv_w, conv_b, dt_bias, a_log, d_skip,
-    first_w_in, second_w_in, first_w_out, second_w_out,
-    first_norm_gain, second_norm_gain, first_gate_gain, second_gate_gain,
-    first_conv_w, second_conv_w, first_conv_b, second_conv_b,
-    first_dt_bias, second_dt_bias, first_a_log, second_a_log, first_d_skip, second_d_skip,
-):
+    for v in small:
+        result.append(flat[at : at + v.size].reshape(v.shape))
+        at += v.size
+    return tuple(result)
+
+
+def alone(tokens, cotangent, doc_starts, valid_len, weights, firsts, seconds):
+    w_in, w_out = weights[:2]
+    small = weights[2:]
     length = tokens.shape[1]
     hidden = tokens[0].astype(F32)
     upstream = cotangent[0].astype(F32)
-    small = (norm_gain, gate_gain, conv_w, conv_b, dt_bias, a_log, d_skip)
-    norm_full, gate_full, convw_full, convb_full, shift_full, logd_full, skip_full = gather_small(small)
+    flat = jnp.concatenate([v.astype(BF16).reshape(-1) for v in small])
+    every = lax.all_gather(flat, "fsdp", axis=0, tiled=False)
+    full, at = [], 0
+    for v in small:
+        piece = every[:, at : at + v.size].astype(F32)
+        at += v.size
+        if v.ndim == 1:
+            full.append(piece.reshape(1, -1))
+        else:
+            full.append(jnp.moveaxis(piece.reshape((-1,) + v.shape), 0, 1).reshape(v.shape[0], -1))
+    norm_full, gate_full, convw_full, convb_full, shift_full, logd_full, skip_full = full
     in_full = lax.all_gather(
         lax.all_gather(w_in.astype(BF16), "dp", axis=1, tiled=True), "fsdp", axis=0, tiled=True
     )
@@ -566,36 +1073,36 @@
     scale = lax.rsqrt(jnp.mean(hidden * hidden, axis=-1, keepdims=True) + EPSILON)
     normed = (hidden * scale * norm_full).astype(BF16)
     projected = dot(normed, in_full)
-    dt_rows = projected[:, DI + CONV :].T
+    extra = projected[:, MAIN:]
     common = (
-        doc_starts, projected, dt_rows, convw_full, convb_full, shift_full.T, logd_full.T,
-        jnp.repeat(skip_full, HP, axis=1), gate_full,
+        projected[:, :MAIN], extra, extra[:, 2 * NS :].T, convw_full[:, :DI], convb_full[:, :DI],
+        convw_full[:, DI:], convb_full[:, DI:], shift_full.T, logd_full.T, jnp.repeat(skip_full, HP, axis=1),
     )
-    mixed, y, states, q = mix_forward(*common)
-    position = jnp.arange(length, dtype=jnp.int32)
-    live = (position < valid_len[0]).astype(F32)[:, None]
+    gated, y, states, squares = mix_forward(0, length, doc_starts, *common)
+    q = lax.rsqrt(squares * (1.0 / DI) + EPSILON)
+    mixed = (gated * q * gate_full).astype(BF16)
+    live = (jnp.arange(length, dtype=jnp.int32) < valid_len[0]).astype(F32)[:, None]
     d_branch = (upstream * live).astype(BF16)
-    branch = dot(mixed, out_full)
-    out_tokens = (hidden + branch * live).astype(BF16)
+    out_tokens = (hidden + dot(mixed, out_full) * live).astype(BF16)
     d_mixed = dot_nt(d_branch, out_full)
     mean = q * q * jnp.sum(mixed.astype(F32) * d_mixed, axis=1, keepdims=True) * (1.0 / DI)
-    (
-        d_gate_in, d_x_in, d_bc_in, d_dt, s_gain, s_cw, s_cb, s_cwbc, s_cbbc, s_shift, s_logd, s_skip,
-    ) = mix_backward(*common, y, states, q, mean, d_mixed)
-    d_low = jnp.concatenate([d_gate_in, d_x_in, d_bc_in, d_dt.T.astype(BF16)], axis=1)
+    d_main, d_bc_in, d_dt, *sums = mix_backward(
+        0, 1, length, None, doc_starts, *common, gate_full, y, states, q, mean, d_mixed
+    )
+    s_gain, s_cw, s_cb, s_cwbc, s_cbbc, s_shift, s_logd, s_skip = [v[0] for v in sums]
+    d_low = jnp.concatenate([d_main, d_bc_in, d_dt.T.astype(BF16)], axis=1)
     d_normed = dot_nt(d_low, in_full)
     weighted = norm_full * d_normed
-    inner = jnp.mean(hidden * weighted, axis=-1, keepdims=True)
-    grad_tokens = upstream + scale * weighted - hidden * (scale * scale * scale * inner)
+    average = jnp.mean(hidden * weighted, axis=-1, keepdims=True)
+    grad_tokens = upstream + scale * weighted - hidden * (scale * scale * scale * average)
     s_norm = jnp.sum(hidden * scale * d_normed, axis=0)
     contract = (((0,), (0,)), ((), ()))
     out_sum = lax.dot_general(mixed, d_branch, contract, preferred_element_type=F32).astype(BF16)
     in_sum = lax.dot_general(normed, d_low, contract, preferred_element_type=F32).astype(BF16)
-    out_summed = lax.psum_scatter(out_sum, "fsdp", scatter_dimension=0, tiled=True)
-    in_summed = lax.psum_scatter(in_sum, "fsdp", scatter_dimension=0, tiled=True)
-    grad_in = lax.psum_scatter(in_summed, "dp", scatter_dimension=1, tiled=True).astype(F32)
-    grad_out = lax.psum_scatter(out_summed, "dp", scatter_dimension=1, tiled=True).astype(F32)
-
+    grads = []
+    for total in (in_sum, out_sum):
+        total = lax.psum_scatter(total, "fsdp", scatter_dimension=0, tiled=True)
+        grads.append(lax.psum_scatter(total, "dp", scatter_dimension=1, tiled=True).astype(F32))
     sums = (
         s_norm[None],
         s_gain,
@@ -611,22 +1118,28 @@
     )
     total = lax.psum(flat, ("dp", "fsdp"))
     mine = lax.dynamic_index_in_dim(total, lax.axis_index("fsdp"), 0, keepdims=False)
-    small_grads, at = [], 0
-    for v in small:
-        small_grads.append(mine[at : at + v.size].reshape(v.shape))
-        at += v.size
-
-    factor = 1.0 / math.sqrt(length * lax.axis_size("dp") * lax.axis_size("fsdp"))
-    weights = (w_in, w_out) + small
-    grads = (grad_in, grad_out) + tuple(small_grads)
-    firsts = (
-        first_w_in, first_w_out, first_norm_gain, first_gate_gain, first_conv_w, first_conv_b,
-        first_dt_bias, first_a_log, first_d_skip,
-    )
-    seconds = (
-        second_w_in, second_w_out, second_norm_gain, second_gate_gain, second_conv_w, second_conv_b,
-        second_dt_bias, second_a_log, second_d_skip,
-    )
+    return out_tokens, grad_tokens, tuple(grads) + split_small(mine, small)
+
+
+def regular(w_in, dp, groups):
+    zs = dp // 2
+    if dp % 2 or zs & (zs - 1) or zs < 4 or groups & (groups - 1) or DI % (groups * groups * 128):
+        return False
+    local = DI // groups
+    per_chip = 2 * w_in.shape[1]
+    edges = [
+        static_count(g, min(per_chip * zz, MAIN), local // groups, local) for zz in range(zs + 1) for g in range(groups)
+    ]
+    return local % BC == 0 and groups == 4 and zs == 4 and all(e % 16 == 0 for e in edges) and w_in.shape[0] % 256 == 0
+
+
+def shards(tokens, cotangent, doc_starts, valid_len, *rest):
+    weights, moments = rest[:9], rest[9:]
+    firsts, seconds = moments[0::2], moments[1::2]
+    dp, groups = lax.axis_size("dp"), lax.axis_size("fsdp")
+    plan = grouped if regular(weights[0], dp, groups) else alone
+    out_tokens, grad_tokens, grads = plan(tokens, cotangent, doc_starts, valid_len, weights, firsts, seconds)
+    factor = 1.0 / math.sqrt(tokens.shape[0] * tokens.shape[1] * dp * groups)
     decay_flags = (True, True, False, False, True, True, False, False, False)
     results = []
     for i, (weight, gradient, first, second) in enumerate(zip(weights, grads, firsts, seconds)):

time: 1570 us -> 860 us (0.55)
  waiting for transfers between devices: 1240 us -> 208 us
  local copies, waits for them, and re-layouts: 29.8 us -> 123 us
  starting transfers between devices: 0.61 us -> 81.8 us
  other arithmetic: 30.8 us -> 104 us
  Pallas kernels: 98.9 us -> 168 us
  matrix products: 128 us -> 151 us
  blocking collectives: 16.9 us -> 0 us
    all_gather x4 -> x0, waiting for transfers between devices: 575 us -> none  [the longest x1 284 us: shards(): lax.all_gather(lax.all_gather(w_in.astype(BF16), 'dp', axis=1, tiled=True...]
    reduce_scatter x4 -> x0, waiting for transfers between devices: 559 us -> none  [the longest x1 264 us: shards(): lax.psum_scatter(in_sum, 'fsdp', scatter_dimension=0, tiled=True)]
    ppermute x0 -> x76, waiting for transfers between devices: none -> 208 us  [swap(): return lax.ppermute(value, axis, [(i, i ^ mask) for i in range(size)])]
    psum x1 -> x0, waiting for transfers between devices: 107 us -> none  [shards(): total = lax.psum(flat, ('dp', 'fsdp'))]
    ppermute x0 -> x76, starting transfers between devices: none -> 81.8 us  [swap(): return lax.ppermute(value, axis, [(i, i ^ mask) for i in range(size)])]
    pallas_call x2 -> x22, Pallas kernels: 98.9 us -> 168 us  [the longest x2 92.8 us: mix_backward(): pl.pallas_call(backward_first if before is None else backward_kernel, gri...]
    unnamed x89 -> x282, local copies, waits for them, and re-layouts: 3.86 us -> 56.5 us
    convert_element_type x10 -> x29, other arithmetic: 3.68 us -> 28.1 us  [the longest x10 16.9 us: sum_low(): return (a.astype(F32) + b.astype(F32)).astype(BF16)]
  transfers between devices with their start and end apart: 9 -> 76, of which waited for: 9 -> 18; matrix products, arithmetic and copies ran while one was open for 4% -> 36% of each run, Pallas kernels for 0% -> 17%
where the time goes in v2:
time: 860 us; the launch traced here: 843 us
  waiting for transfers between devices  208 us (24%)
  Pallas kernels  168 us (20%)
  matrix products  151 us (18%)
  local copies, waits for them, and re-layouts  123 us (14%)
  other arithmetic  104 us (12%)
  starting transfers between devices  81.8 us (10%)
    ppermute x76, waiting for transfers between devices, swap(): return lax.ppermute(value, axis, [(i, i ^ mask) for i in range(size)])  208 us
    pallas_call x2, Pallas kernels, mix_backward(): pl.pallas_call(backward_first if before is None else backward_kernel, gri...  92.8 us
    ppermute x76, starting transfers between devices, swap(): return lax.ppermute(value, axis, [(i, i ^ mask) for i in range(size)])  81.8 us
    dot_general x7, matrix products, sum_rows(): lax.dot_general(a, b, contract, preferred_element_type=F32).astype(BF16)  56.7 us
    unnamed x282, local copies, waits for them, and re-layouts  56.5 us
    dot_general x4, matrix products, dot_nt(): lax.dot_general(a, b, (((1,), (1,)), ((), ())), preferred_element_type=F32)  45.6 us
    dot_general x3, matrix products, dot(): return jnp.dot(a, b, preferred_element_type=F32)  42.2 us
    pallas_call x2, Pallas kernels, mix_forward(): pl.pallas_call(forward_kernel, grid=(rows, channels // BC), in_specs=comm...  36.2 us
  transfers between devices with their start and end apart: 76, of which 18 were waited for; matrix products, arithmetic and copies ran while one was open for 36% of the time, Pallas kernels for 17%

profile of v2, /device:TPU:0, one launch (start us, length us, event | category | flops | bytes accessed | tf_op | source)
XLA Modules:
  0.0 843.0 jit_solution(3104902894337768415)
XLA Ops:
  18.5 13.8 %collective-permute-done.1.refs_0_ = bf16[256,2048]{1,0:T(8,128)(2,1)} collective-permute-done((bf16[256,2048]{1,0:T(8,128)(2,1)}, bf16[256,2048]{1,0:T(8,128)(2,1)}, u32[]{:S(2)}, u32[]{:S(2)}) %collective-permute-start.1) | collective-permute-done | bytes 1048608 | tf_op jit(solution)/shard_map/ppermute | solution.py:567
  32.3 4.7 collective-permute-done.2.refs_1_
  37.0 4.4 fusion.29
  46.9 2.6 collective-permute-start.3
  55.1 3.3 copy-done.3
  64.9 3.7 collective-permute-done.3
  75.0 3.4 collective-permute-start.13
  85.7 28.4 %collective-permute-done.13 = bf16[1,1776,256]{2,1,0:T(8,128)(2,1)} collective-permute-done((bf16[1,1776,256]{2,1,0:T(8,128)(2,1)}, bf16[1,1776,256]{2,1,0:T(8,128)(2,1)}, u32[]{:S(2)}, u32[]{:S(2)}) %collective-permute-start.13) | collective-permute-done | bytes 909344 | tf_op jit(solution)/shard_map/ppermute | solution.py:567
  115.5 2.8 pad_maximum_fusion.7.refs_0_
  118.3 4.1 collective-permute-start.18
  127.6 2.9 pad_maximum_fusion.6.refs_0_
  141.5 3.3 copy-done.6
  146.7 14.2 %collective-permute-done.18.refs_1_ = bf16[2,1776,256]{2,1,0:T(8,128)(2,1)} collective-permute-done((bf16[2,1776,256]{2,1,0:T(8,128)(2,1)}, bf16[2,1776,256]{2,1,0:T(8,128)(2,1)}, u32[]{:S(2)}, u32[]{:S(2)}) %collective-permute-start.18) | collective-permute-done | bytes 1818656 | tf_op jit(solution)/shard_map/ppermute | solution.py:567
  173.8 2.9 place.10.refs_2_
  176.7 3.4 copy-done
  187.1 3.3 copy-done.7
  190.4 4.4 fusion.143
  202.4 3.4 copy-done.1
  205.8 2.9 place.11.refs_2_
  208.7 2.9 place.12.refs_2_
  211.6 2.9 place.13.refs_1_
  216.8 2.9 place.15.refs_2_
  219.7 3.1 place.16.refs_2_
  222.9 3.1 place.17
  226.0 3.4 copy-done.2
  235.5 19.8 %collective-permute-done.23 = bf16[1,1024,256]{2,1,0:T(8,128)(2,1)S(1)} collective-permute-done((bf16[1,1024,256]{2,1,0:T(8,128)(2,1)S(1)}, bf16[1,1024,256]{2,1,0:T(8,128)(2,1)S(1)}, u32[]{:S(2)}, u32[]{:S(2)}) %collective-permute-start.23) | collective-permute-done | bytes 524320 | tf_op jit(solution)/shard_map/ppermute | solution.py:567
  256.4 22.8 %fusion.144.gate_ref.xin_ref.refs_1_.refs_2_ = f32[2048,2048]{1,0:T(8,128)} fusion(bf16[2048,2048]{1,0:T(8,128)(2,1)S(1)} %bitcast.315, bf16[2048,2048]{1,0:T(8,128)(2,1)} %copy-done.2), kind=kOutput, calls=%fused_computation.388 | convolution fusion | flops 17179869184 | bytes 33554432 | tf_op jit(solution)/shard_map/dot_general | solution.py:41
  281.1 18.0 %mix_forward.2 = (f32[1024,1024]{1,0:T(8,128)}, f32[1024,1024]{1,0:T(8,128)}, bf16[2,4,128,1024]{3,2,1,0:T(8,128)(2,1)S(1)}, f32[1024,1]{1,0:T(8,128)S(1)}) custom-call(s32[2,4]{1,0:T(2,128)S(1)} %get-tuple-element.118.starts_ref.refs_0_, f32[2048,2048]{1,0:T(8,128)} %fusion.144.gate_ref.xin_ref.refs_1_.refs_2_, ...), custom_call_target="tpu_custom_call" | custom-call | tf_op jit(solution)/shard_map/mix_forward/pallas_call | solution.py:423
  302.4 3.4 copy-done.4
  311.7 3.3 copy-done.5
  317.2 18.2 %mix_forward.3 = (f32[1024,1024]{1,0:T(8,128)}, f32[1024,1024]{1,0:T(8,128)}, bf16[2,4,128,1024]{3,2,1,0:T(8,128)(2,1)S(1)}, f32[1024,1]{1,0:T(8,128)S(1)}) custom-call(s32[2,4]{1,0:T(2,128)S(1)} %get-tuple-element.127.starts_ref.refs_0_, f32[2048,2048]{1,0:T(8,128)} %fusion.144.gate_ref.xin_ref.refs_1_.refs_2_, ...), custom_call_target="tpu_custom_call" | custom-call | tf_op jit(solution)/shard_map/mix_forward/pallas_call | solution.py:423
  339.5 7.0 constant_dynamic-slice_fusion.23
  354.5 3.9 multiply_convert_fusion.2
  358.4 2.9 place.19
  361.4 14.0 %multiply_reduce_fusion = (f32[2048]{0:T(1024)S(1)}, bf16[2048,1024]{1,0:T(8,128)(2,1)}) fusion(bf16[1024,1024]{1,0:T(8,128)(2,1)} %get-tuple-element.342, bf16[1024,1024]{1,0:T(8,128)(2,1)S(1)} %get-tuple-element.341, f32[2048]{0:T(1024)S(1)} %bitcast.377, bf16[2048,2048]{1,0:T(8,128)(2,1)S(1)} %bitcast.311, bf16[1024,2048]{1,0:T(8,128)(2,1)S(1)} %place.19), kind=kOutput, calls=%fused_computation.7 | convolution fusion | flops 8608806912 | bytes 20987904 | tf_op jit(solution)/shard_map/dot_general | solution.py:41
  376.9 9.6 %fusion.49 = bf16[1024,1024]{1,0:T(8,128)(2,1)} fusion(bf16[2048,256]{1,0:T(8,128)(2,1)} %get-tuple-element.239, bf16[2048,256]{1,0:T(8,128)(2,1)} %get-tuple-element.240, bf16[2048,256]{1,0:T(8,128)(2,1)} %get-tuple-element.241, bf16[2048,256]{1,0:T(8,128)(2,1)} %get-tuple-element.242, bf16[2048]{0:T(1024)(128)(2,1)S(1)} %copy-done.101, ...), kind=kOutput, calls=%fused_computation.88 | convolution fusion | flops 4325376000 | bytes 10489856 | tf_op jit(solution)/shard_map/dot_general | solution.py:897
  394.8 3.2 fusion.64.refs_16_
  398.0 10.9 %convolution_convert_fusion = bf16[2048,2048]{1,0:T(8,128)(2,1)S(1)} fusion(bf16[2048,1024]{1,0:T(8,128)(2,1)} %pad_maximum_fusion, bf16[1024,2048]{1,0:T(8,128)(2,1)S(1)} %copy-done.20), kind=kOutput, calls=%fused_computation.9 | convolution fusion | flops 8594128896 | bytes 16777216 | tf_op jit(solution)/shard_map/dot_general | solution.py:37
  409.3 2.8 copy-done.42
  417.0 4.9 fusion.10
  431.4 7.0 constant_dynamic-slice_fusion.9
  438.5 46.3 %mix_backward.2 = (bf16[2048,2048]{1,0:T(8,128)(2,1)}, bf16[1024,256]{1,0:T(8,128)(2,1)S(1)}, f32[16,1024]{1,0:T(8,128)S(1)}, f32[2,1,1024]{2,1,0:T(1,128)S(1)},...) custom-call(s32[2,4]{1,0:T(2,128)S(1)} %get-tuple-element.118.starts, ...), custom_call_target="tpu_custom_call" | custom-call | tf_op jit(solution)/shard_map/mix_backward/pallas_call | solution.py:488
  487.9 4.5 add_convert_fusion.5
  492.3 46.6 %mix_backward.3 = (bf16[2048,2048]{1,0:T(8,128)(2,1)}, bf16[1024,256]{1,0:T(8,128)(2,1)S(1)}, f32[16,1024]{1,0:T(8,128)S(1)}, f32[2,1,1024]{2,1,0:T(1,128)S(1)},...) custom-call(s32[2,4]{1,0:T(2,128)S(1)} %get-tuple-element.127.starts, ...), custom_call_target="tpu_custom_call", output_to_operand_aliasing={{0}: (18, {})} | custom-call | tf_op jit(solution)/shard_map/mix_backward/pallas_call | solution.py:488
  540.9 7.6 convolution_convert_fusion.5
  548.5 6.5 convolution_convert_fusion.4
  555.0 3.6 reshape.855
  560.1 3.8 constant_dynamic-slice_fusion.6
  565.1 9.9 %convolution_convert_fusion.3 = bf16[2048,512]{1,0:T(8,128)(2,1)} fusion(bf16[2048,2048]{1,0:T(8,128)(2,1)} %get-tuple-element.152, bf16[2048,256]{1,0:T(8,128)(2,1)S(1)} %copy-done.67, bf16[2048,256]{1,0:T(8,128)(2,1)S(1)} %copy-done.68), kind=kOutput, calls=%fused_computation.55 | convolution fusion | flops 4300210176 | bytes 12582912 | tf_op jit(solution)/shard_map/dot_general | solution.py:897
  575.3 9.3 %fusion.71 = f32[2048,2048]{1,0:T(8,128)} fusion(bf16[320,2048]{1,0:T(8,128)(2,1)S(1)} %copy-done.18, bf16[2048,64]{1,0:T(8,128)(2,1)S(1)} %multiply_convert_fusion.3, bf16[1024,256]{1,0:T(8,128)(2,1)S(1)} %copy-done.32, bf16[1024,256]{1,0:T(8,128)(2,1)S(1)} %get-tuple-element.140), kind=kOutput, calls=%fused_computation.147 | convolution fusion | flops 2688286720 | bytes 19398656 | tf_op jit(solution)/shard_map/dot_general | solution.py:37
  594.3 10.0 %convolution_convert_fusion.2 = bf16[2048,512]{1,0:T(8,128)(2,1)} fusion(bf16[2048,2048]{1,0:T(8,128)(2,1)} %get-tuple-element.152, bf16[2048,256]{1,0:T(8,128)(2,1)S(1)} %copy-done.61, bf16[2048,256]{1,0:T(8,128)(2,1)S(1)} %copy-done.62), kind=kOutput, calls=%fused_computation.54 | convolution fusion | flops 4300210176 | bytes 12582912 | tf_op jit(solution)/shard_map/dot_general | solution.py:897
  611.5 8.3 convolution_convert_fusion.1
  619.8 3.9 add_convert_fusion.7
  624.9 22.0 %add_convert_fusion = bf16[2048,2048]{1,0:T(8,128)(2,1)S(1)} fusion(f32[2048,2048]{1,0:T(8,128)} %fusion.71, bf16[2048,2048]{1,0:T(8,128)(2,1)} %get-tuple-element.152, bf16[2048,2048]{1,0:T(8,128)(2,1)S(1)} %bitcast.309), kind=kOutput, calls=%fused_computation.4 | convolution fusion | flops 17188257792 | bytes 41943040 | tf_op jit(solution)/shard_map/dot_general | solution.py:37
  656.7 45.9 %collective-permute-done.67 = bf16[256,256]{1,0:T(8,128)(2,1)S(1)} collective-permute-done((bf16[256,256]{1,0:T(8,128)(2,1)S(1)}, bf16[256,256]{1,0:T(8,128)(2,1)S(1)}, u32[]{:S(2)}, u32[]{:S(2)}) %collective-permute-start.67) | collective-permute-done | bytes 131104 | tf_op jit(solution)/shard_map/ppermute | solution.py:567
  706.0 6.7 add_bitcast_fusion.1
  719.6 28.2 %collective-permute-done.63 = bf16[320,256]{1,0:T(8,128)(2,1)S(1)} collective-permute-done((bf16[320,256]{1,0:T(8,128)(2,1)S(1)}, bf16[320,256]{1,0:T(8,128)(2,1)S(1)}, u32[]{:S(2)}, u32[]{:S(2)}) %collective-permute-start.63) | collective-permute-done | bytes 163872 | tf_op jit(solution)/shard_map/ppermute | solution.py:567
  753.2 6.3 collective-permute-done.54
  760.5 21.5 %collective-permute-done.53 = bf16[256,2048]{1,0:T(8,128)(2,1)S(1)} collective-permute-done((bf16[256,2048]{1,0:T(8,128)(2,1)S(1)}, bf16[256,2048]{1,0:T(8,128)(2,1)S(1)}, u32[]{:S(2)}, u32[]{:S(2)}) %collective-permute-start.53) | collective-permute-done | bytes 1048608 | tf_op jit(solution)/shard_map/ppermute | solution.py:567
  790.5 4.2 collective-permute-done.59
  794.9 6.5 fusion.28
  802.3 9.9 %collective-permute-done.55 = bf16[256,2048]{1,0:T(8,128)(2,1)S(1)} collective-permute-done((bf16[256,2048]{1,0:T(8,128)(2,1)S(1)}, bf16[256,2048]{1,0:T(8,128)(2,1)S(1)}, u32[]{:S(2)}, u32[]{:S(2)}) %collective-permute-start.55) | collective-permute-done | bytes 1048608 | tf_op jit(solution)/shard_map/ppermute | solution.py:567
  823.1 6.5 multiply_subtract_fusion
  833.9 5.3 fusion.5
  (656 shorter events, 231.6 us)
Async XLA Ops:
  3.6 13.4 %collective-permute-start = (bf16[256,1064]{0,1:T(8,128)(2,1)}, bf16[256,1064]{0,1:T(8,128)(2,1)}, u32[]{:S(2)}, u32[]{:S(2)}) collective-permute-start(bf16[256,1064]{0,1:T(8,128)(2,1)} %constant_dynamic-slice_fusion.31), channel_id=1, source_target_pairs={{0,4},{4,0},{8,12},{12,8},{16,20},{20,16},{24,28},{28,24},{1,5},{5... | collective-permute-start | bytes 1634312 | tf_op jit(solution)/shard_map/ppermute | solution.py:567
  5.5 26.8 %collective-permute-start.1 = (bf16[256,2048]{1,0:T(8,128)(2,1)}, bf16[256,2048]{1,0:T(8,128)(2,1)}, u32[]{:S(2)}, u32[]{:S(2)}) collective-permute-start(bf16[256,2048]{1,0:T(8,128)(2,1)} %get-tuple-element.269), channel_id=1, source_target_pairs={{0,1},{1,0},{2,3},{3,2},{4,5},{5,4},{6,7},{7,6},{8,9},{9,8},{10,11... | collective-permute-start | bytes 3145736 | tf_op jit(solution)/shard_map/ppermute | solution.py:567
  8.0 29.0 %collective-permute-start.2 = (bf16[256,2048]{1,0:T(8,128)(2,1)}, bf16[256,2048]{1,0:T(8,128)(2,1)S(1)}, u32[]{:S(2)}, u32[]{:S(2)}) collective-permute-start(bf16[256,2048]{1,0:T(8,128)(2,1)} %get-tuple-element.268), channel_id=1, source_target_pairs={{0,2},{1,3},{2,0},{3,1},{4,6},{5,7},{6,4},{7,5},{8,10},{9,11},{10,... | collective-permute-start | bytes 3145736 | tf_op jit(solution)/shard_map/ppermute | solution.py:567
  13.4 33.4 %collective-permute-start.9 = (bf16[256,256]{1,0:T(8,128)(2,1)}, bf16[256,256]{1,0:T(8,128)(2,1)}, u32[]{:S(2)}, u32[]{:S(2)}) collective-permute-start(bf16[256,256]{1,0:T(8,128)(2,1)} %get-tuple-element.302), channel_id=1, source_target_pairs={{0,3},{1,2},{2,1},{3,0},{4,7},{5,6},{6,5},{7,4},{8,11},{9,10},{10,... | collective-permute-start | bytes 393224 | tf_op jit(solution)/shard_map/ppermute | solution.py:567
  13.4 33.5 %collective-permute-start.8 = (bf16[256,256]{1,0:T(8,128)(2,1)}, bf16[256,256]{1,0:T(8,128)(2,1)}, u32[]{:S(2)}, u32[]{:S(2)}) collective-permute-start(bf16[256,256]{1,0:T(8,128)(2,1)} %get-tuple-element.303), channel_id=1, source_target_pairs={{0,2},{1,3},{2,0},{3,1},{4,6},{5,7},{6,4},{7,5},{8,10},{9,11},{10,... | collective-permute-start | bytes 393224 | tf_op jit(solution)/shard_map/ppermute | solution.py:567
  42.4 20.3 %collective-permute-start.12 = (bf16[592,256]{1,0:T(8,128)(2,1)}, bf16[592,256]{1,0:T(8,128)(2,1)}, u32[]{:S(2)}, u32[]{:S(2)}) collective-permute-start(bf16[592,256]{1,0:T(8,128)(2,1)} %get-tuple-element.275), channel_id=1, source_target_pairs={{0,3},{1,2},{2,1},{3,0},{4,7},{5,6},{6,5},{7,4},{8,11},{9,10},{10,... | collective-permute-start | bytes 909320 | tf_op jit(solution)/shard_map/ppermute | solution.py:567
  44.0 18.8 %collective-permute-start.11 = (bf16[592,256]{1,0:T(8,128)(2,1)}, bf16[592,256]{1,0:T(8,128)(2,1)}, u32[]{:S(2)}, u32[]{:S(2)}) collective-permute-start(bf16[592,256]{1,0:T(8,128)(2,1)} %get-tuple-element.276), channel_id=1, source_target_pairs={{0,2},{1,3},{2,0},{3,1},{4,6},{5,7},{6,4},{7,5},{8,10},{9,11},{10,... | collective-permute-start | bytes 909320 | tf_op jit(solution)/shard_map/ppermute | solution.py:567
  44.1 18.7 %collective-permute-start.10 = (bf16[592,256]{1,0:T(8,128)(2,1)}, bf16[592,256]{1,0:T(8,128)(2,1)}, u32[]{:S(2)}, u32[]{:S(2)}) collective-permute-start(bf16[592,256]{1,0:T(8,128)(2,1)} %get-tuple-element.274), channel_id=1, source_target_pairs={{0,1},{1,0},{2,3},{3,2},{4,5},{5,4},{6,7},{7,6},{8,9},{9,8},{10,11... | collective-permute-start | bytes 909320 | tf_op jit(solution)/shard_map/ppermute | solution.py:567
  46.8 14.1 %collective-permute-start.7 = (bf16[256,256]{1,0:T(8,128)(2,1)S(1)}, bf16[256,256]{1,0:T(8,128)(2,1)}, u32[]{:S(2)}, u32[]{:S(2)}) collective-permute-start(bf16[256,256]{1,0:T(8,128)(2,1)S(1)} %get-tuple-element.304), channel_id=1, source_target_pairs={{0,1},{1,0},{2,3},{3,2},{4,5},{5,4},{6,7},{7,6},{8,9},{9,8},{10,11... | collective-permute-start | bytes 393224 | tf_op jit(solution)/shard_map/ppermute | solution.py:567
  46.9 21.7 %collective-permute-start.3 = (bf16[1,912,256]{2,1,0:T(8,128)(2,1)}, bf16[1,912,256]{2,1,0:T(8,128)(2,1)}, u32[]{:S(2)}, u32[]{:S(2)}) collective-permute-start(bf16[1,912,256]{2,1,0:T(8,128)(2,1)} %maximum_bitcast_fusion.2), channel_id=1, source_target_pairs={{0,16},{4,20},{8,24},{12,28},{16,0},{20,4},{24,8},{28,12},{1,17},{... | collective-permute-start | bytes 1400840 | tf_op jit(solution)/shard_map/ppermute | solution.py:567
  74.3 44.0 %collective-permute-start.14 = (bf16[2,912,256]{2,1,0:T(8,128)(2,1)}, bf16[2,912,256]{2,1,0:T(8,128)(2,1)}, u32[]{:S(2)}, u32[]{:S(2)}) collective-permute-start(bf16[2,912,256]{2,1,0:T(8,128)(2,1)} %pad_maximum_fusion.14), channel_id=1, source_target_pairs={{0,8},{4,12},{8,0},{12,4},{16,24},{20,28},{24,16},{28,20},{1,9},{5... | collective-permute-start | bytes 2801672 | tf_op jit(solution)/shard_map/ppermute | solution.py:567
  75.0 39.2 %collective-permute-start.13 = (bf16[1,1776,256]{2,1,0:T(8,128)(2,1)}, bf16[1,1776,256]{2,1,0:T(8,128)(2,1)}, u32[]{:S(2)}, u32[]{:S(2)}) collective-permute-start(bf16[1,1776,256]{2,1,0:T(8,128)(2,1)} %maximum_bitcast_fusion), channel_id=1, source_target_pairs={{0,16},{4,20},{8,24},{12,28},{16,0},{20,4},{24,8},{28,12},{1,17},{... | collective-permute-start | bytes 2727944 | tf_op jit(solution)/shard_map/ppermute | solution.py:567
  79.8 38.5 %collective-permute-start.15 = (bf16[256,2048]{1,0:T(8,128)(2,1)}, bf16[256,2048]{1,0:T(8,128)(2,1)}, u32[]{:S(2)}, u32[]{:S(2)}) collective-permute-start(bf16[256,2048]{1,0:T(8,128)(2,1)} %get-tuple-element.267), channel_id=1, source_target_pairs={{0,1},{1,0},{2,3},{3,2},{4,5},{5,4},{6,7},{7,6},{8,9},{9,8},{10,11... | collective-permute-start | bytes 3145736 | tf_op jit(solution)/shard_map/ppermute | solution.py:567
  81.2 37.2 %collective-permute-start.16 = (bf16[256,2048]{1,0:T(8,128)(2,1)}, bf16[256,2048]{1,0:T(8,128)(2,1)}, u32[]{:S(2)}, u32[]{:S(2)}) collective-permute-start(bf16[256,2048]{1,0:T(8,128)(2,1)} %get-tuple-element.266), channel_id=1, source_target_pairs={{0,2},{1,3},{2,0},{3,1},{4,6},{5,7},{6,4},{7,5},{8,10},{9,11},{10,... | collective-permute-start | bytes 3145736 | tf_op jit(solution)/shard_map/ppermute | solution.py:567
  82.9 50.6 %collective-permute-start.19 = (bf16[256,2048]{1,0:T(8,128)(2,1)}, bf16[256,2048]{1,0:T(8,128)(2,1)}, u32[]{:S(2)}, u32[]{:S(2)}) collective-permute-start(bf16[256,2048]{1,0:T(8,128)(2,1)} %collective-permute-done.1.refs_0_), channel_id=1, source_target_pairs={{0,2},{1,3},{2,0},{3,1},{4,6},{5,7},{6,4},{7,5},{8,10},{9,11},{10,... | collective-permute-start | bytes 3145736 | tf_op jit(solution)/shard_map/ppermute | solution.py:567
  114.1 31.6 %collective-permute-start.20 = (bf16[256,2048]{1,0:T(8,128)(2,1)S(1)}, bf16[256,2048]{1,0:T(8,128)(2,1)S(1)}, u32[]{:S(2)}, u32[]{:S(2)}) collective-permute-start(bf16[256,2048]{1,0:T(8,128)(2,1)S(1)} %collective-permute-done.2.refs_1_), channel_id=1, source_target_pairs={{0,1},{1,0},{2,3},{3,2},{4,5},{5,4},{6,7},{7,6},{8,9},{9,8},{10,11... | collective-permute-start | bytes 3145736 | tf_op jit(solution)/shard_map/ppermute | solution.py:567
  118.3 42.5 %collective-permute-start.18 = (bf16[2,1776,256]{2,1,0:T(8,128)(2,1)}, bf16[2,1776,256]{2,1,0:T(8,128)(2,1)}, u32[]{:S(2)}, u32[]{:S(2)}) collective-permute-start(bf16[2,1776,256]{2,1,0:T(8,128)(2,1)} %pad_maximum_fusion.7.refs_0_), channel_id=1, source_target_pairs={{0,8},{4,12},{8,0},{12,4},{16,24},{20,28},{24,16},{28,20},{1,9},{5... | collective-permute-start | bytes 5455880 | tf_op jit(solution)/shard_map/ppermute | solution.py:567
  131.4 29.5 %collective-permute-start.28 = (bf16[320,256]{1,0:T(8,128)(2,1)S(1)}, bf16[320,256]{1,0:T(8,128)(2,1)S(1)}, u32[]{:S(2)}, u32[]{:S(2)}) collective-permute-start(bf16[320,256]{1,0:T(8,128)(2,1)S(1)} %fusion.163), channel_id=1, source_target_pairs={{0,3},{1,2},{2,1},{3,0},{4,7},{5,6},{6,5},{7,4},{8,11},{9,10},{10,... | collective-permute-start | bytes 491528 | tf_op jit(solution)/shard_map/ppermute | solution.py:567
  133.0 28.4 %collective-permute-start.27 = (bf16[320,256]{1,0:T(8,128)(2,1)S(1)}, bf16[320,256]{1,0:T(8,128)(2,1)S(1)}, u32[]{:S(2)}, u32[]{:S(2)}) collective-permute-start(bf16[320,256]{1,0:T(8,128)(2,1)S(1)} %fusion.163), channel_id=1, source_target_pairs={{0,2},{1,3},{2,0},{3,1},{4,6},{5,7},{6,4},{7,5},{8,10},{9,11},{10,... | collective-permute-start | bytes 491528 | tf_op jit(solution)/shard_map/ppermute | solution.py:567
  133.5 27.8 %collective-permute-start.26 = (bf16[320,256]{1,0:T(8,128)(2,1)S(1)}, bf16[320,256]{1,0:T(8,128)(2,1)S(1)}, u32[]{:S(2)}, u32[]{:S(2)}) collective-permute-start(bf16[320,256]{1,0:T(8,128)(2,1)S(1)} %fusion.163), channel_id=1, source_target_pairs={{0,1},{1,0},{2,3},{3,2},{4,5},{5,4},{6,7},{7,6},{8,9},{9,8},{10,11... | collective-permute-start | bytes 491528 | tf_op jit(solution)/shard_map/ppermute | solution.py:567
  146.7 70.1 %collective-permute-start.17 = (bf16[2,1776,256]{2,1,0:T(8,128)(2,1)}, bf16[2,1776,256]{2,1,0:T(8,128)(2,1)}, u32[]{:S(2)}, u32[]{:S(2)}) collective-permute-start(bf16[2,1776,256]{2,1,0:T(8,128)(2,1)} %pad_maximum_fusion.7.refs_0_), channel_id=1, source_target_pairs={{0,4},{4,0},{8,12},{12,8},{16,20},{20,16},{24,28},{28,24},{1,5},{5... | collective-permute-start | bytes 5455880 | tf_op jit(solution)/shard_map/ppermute | solution.py:567
  160.9 53.6 %collective-permute-start.22 = (bf16[4,912,256]{2,1,0:T(8,128)(2,1)}, bf16[4,912,256]{2,1,0:T(8,128)(2,1)}, u32[]{:S(2)}, u32[]{:S(2)}) collective-permute-start(bf16[4,912,256]{2,1,0:T(8,128)(2,1)} %pad_maximum_fusion.6.refs_0_), channel_id=1, source_target_pairs={{0,4},{4,0},{8,12},{12,8},{16,20},{20,16},{24,28},{28,24},{1,5},{5... | collective-permute-start | bytes 5603336 | tf_op jit(solution)/shard_map/ppermute | solution.py:567
  160.9 55.9 %collective-permute-start.21 = (bf16[2,1776,256]{2,1,0:T(8,128)(2,1)}, bf16[2,1776,256]{2,1,0:T(8,128)(2,1)}, u32[]{:S(2)}, u32[]{:S(2)}) collective-permute-start(bf16[2,1776,256]{2,1,0:T(8,128)(2,1)} %collective-permute-done.18.refs_1_), channel_id=1, source_target_pairs={{0,4},{4,0},{8,12},{12,8},{16,20},{20,16},{24,28},{28,24},{1,5},{5... | collective-permute-start | bytes 5455880 | tf_op jit(solution)/shard_map/ppermute | solution.py:567
  161.5 20.7 %collective-permute-start.29 = (bf16[4,320,256]{2,1,0:T(8,128)(2,1)S(1)}, bf16[4,320,256]{2,1,0:T(8,128)(2,1)S(1)}, u32[]{:S(2)}, u32[]{:S(2)}) collective-permute-start(bf16[4,320,256]{2,1,0:T(8,128)(2,1)S(1)} %pad_maximum_fusion.15.refs_0_), channel_id=1, source_target_pairs={{0,4},{4,0},{8,12},{12,8},{16,20},{20,16},{24,28},{28,24},{1,5},{5... | collective-permute-start | bytes 1966088 | tf_op jit(solution)/shard_map/ppermute | solution.py:567
  181.5 48.6 %collective-permute-start.31 = (bf16[256,2048]{1,0:T(8,128)(2,1)}, bf16[256,2048]{1,0:T(8,128)(2,1)}, u32[]{:S(2)}, u32[]{:S(2)}) collective-permute-start(bf16[256,2048]{1,0:T(8,128)(2,1)} %get-tuple-element.265), channel_id=1, source_target_pairs={{0,1},{1,0},{2,3},{3,2},{4,5},{5,4},{6,7},{7,6},{8,9},{9,8},{10,11... | collective-permute-start | bytes 3145736 | tf_op jit(solution)/shard_map/ppermute | solution.py:567
  182.2 48.6 %collective-permute-start.33 = (bf16[256,2048]{1,0:T(8,128)(2,1)}, bf16[256,2048]{1,0:T(8,128)(2,1)}, u32[]{:S(2)}, u32[]{:S(2)}) collective-permute-start(bf16[256,2048]{1,0:T(8,128)(2,1)} %get-tuple-element.264), channel_id=1, source_target_pairs={{0,2},{1,3},{2,0},{3,1},{4,6},{5,7},{6,4},{7,5},{8,10},{9,11},{10,... | collective-permute-start | bytes 3145736 | tf_op jit(solution)/shard_map/ppermute | solution.py:567
  229.4 25.9 %collective-permute-start.23 = (bf16[1,1024,256]{2,1,0:T(8,128)(2,1)S(1)}, bf16[1,1024,256]{2,1,0:T(8,128)(2,1)S(1)}, u32[]{:S(2)}, u32[]{:S(2)}) collective-permute-start(bf16[1,1024,256]{2,1,0:T(8,128)(2,1)S(1)} %copy-done.59), channel_id=1, source_target_pairs={{0,16},{4,20},{8,24},{12,28},{16,0},{20,4},{24,8},{28,12},{1,17},{... | collective-permute-start | bytes 1572872 | tf_op jit(solution)/shard_map/ppermute | solution.py:567
  230.2 79.8 %collective-permute-start.32 = (bf16[256,2048]{1,0:T(8,128)(2,1)}, bf16[256,2048]{1,0:T(8,128)(2,1)}, u32[]{:S(2)}, u32[]{:S(2)}) collective-permute-start(bf16[256,2048]{1,0:T(8,128)(2,1)} %collective-permute-done.31.refs_0_), channel_id=1, source_target_pairs={{0,2},{1,3},{2,0},{3,1},{4,6},{5,7},{6,4},{7,5},{8,10},{9,11},{10,... | collective-permute-start | bytes 3145736 | tf_op jit(solution)/shard_map/ppermute | solution.py:567
  230.8 79.2 %collective-permute-start.34 = (bf16[256,2048]{1,0:T(8,128)(2,1)}, bf16[256,2048]{1,0:T(8,128)(2,1)}, u32[]{:S(2)}, u32[]{:S(2)}) collective-permute-start(bf16[256,2048]{1,0:T(8,128)(2,1)} %collective-permute-done.33.refs_1_), channel_id=1, source_target_pairs={{0,1},{1,0},{2,3},{3,2},{4,5},{5,4},{6,7},{7,6},{8,9},{9,8},{10,11... | collective-permute-start | bytes 3145736 | tf_op jit(solution)/shard_map/ppermute | solution.py:567
  232.3 46.9 %collective-permute-start.24 = (bf16[256,2048]{1,0:T(8,128)(2,1)S(1)}, bf16[256,2048]{1,0:T(8,128)(2,1)S(1)}, u32[]{:S(2)}, u32[]{:S(2)}) collective-permute-start(bf16[256,2048]{1,0:T(8,128)(2,1)S(1)} %get-tuple-element.263), channel_id=1, source_target_pairs={{0,1},{1,0},{2,3},{3,2},{4,5},{5,4},{6,7},{7,6},{8,9},{9,8},{10,11... | collective-permute-start | bytes 3145736 | tf_op jit(solution)/shard_map/ppermute | solution.py:567
  233.0 47.1 %collective-permute-start.25 = (bf16[256,2048]{1,0:T(8,128)(2,1)S(1)}, bf16[256,2048]{1,0:T(8,128)(2,1)S(1)}, u32[]{:S(2)}, u32[]{:S(2)}) collective-permute-start(bf16[256,2048]{1,0:T(8,128)(2,1)S(1)} %get-tuple-element.262), channel_id=1, source_target_pairs={{0,2},{1,3},{2,0},{3,1},{4,6},{5,7},{6,4},{7,5},{8,10},{9,11},{10,... | collective-permute-start | bytes 3145736 | tf_op jit(solution)/shard_map/ppermute | solution.py:567
  256.3 58.6 %collective-permute-start.30 = (bf16[2,1024,256]{2,1,0:T(8,128)(2,1)}, bf16[2,1024,256]{2,1,0:T(8,128)(2,1)}, u32[]{:S(2)}, u32[]{:S(2)}) collective-permute-start(bf16[2,1024,256]{2,1,0:T(8,128)(2,1)} %get-tuple-element.297), channel_id=1, source_target_pairs={{0,8},{4,12},{8,0},{12,4},{16,24},{20,28},{24,16},{28,20},{1,9},{5... | collective-permute-start | bytes 3145736 | tf_op jit(solution)/shard_map/ppermute | solution.py:567
  346.5 11.9 %collective-permute-start.37 = (bf16[4,1024,256]{2,1,0:T(8,128)(2,1)}, bf16[4,1024,256]{2,1,0:T(8,128)(2,1)S(1)}, u32[]{:S(2)}, u32[]{:S(2)}) collective-permute-start(bf16[4,1024,256]{2,1,0:T(8,128)(2,1)} %constant_dynamic-update-slice_fusion.2.refs_0_), channel_id=1, source_target_pairs={{0,4},{4,0},{8,12},{12,8},{16,20},{20,16},{24,28},{28,24},{1,5},{5... | collective-permute-start | bytes 6291464 | tf_op jit(solution)/shard_map/ppermute | solution.py:567
  375.4 11.1 %collective-permute-start.38 = (f32[4,512]{1,0:T(4,128)S(1)}, f32[4,512]{1,0:T(4,128)S(1)}, u32[]{:S(2)}, u32[]{:S(2)}) collective-permute-start(f32[4,512]{1,0:T(4,128)S(1)} %reshape.853), channel_id=1, source_target_pairs={{0,2},{1,3},{2,0},{3,1},{4,6},{5,7},{6,4},{7,5},{8,10},{9,11},{10,... | collective-permute-start | bytes 24584 | tf_op jit(solution)/shard_map/ppermute | solution.py:567
  390.7 31.2 %collective-permute-start.44 = (bf16[1024,1024]{1,0:T(8,128)(2,1)}, bf16[1024,1024]{1,0:T(8,128)(2,1)}, u32[]{:S(2)}, u32[]{:S(2)}) collective-permute-start(bf16[1024,1024]{1,0:T(8,128)(2,1)} %fusion.49), channel_id=1, source_target_pairs={{0,4},{4,0},{8,12},{12,8},{16,20},{20,16},{24,28},{28,24},{1,5},{5... | collective-permute-start | bytes 6291464 | tf_op jit(solution)/shard_map/ppermute | solution.py:567
  413.7 74.2 %collective-permute-start.40 = (bf16[512,2048]{1,0:T(8,128)(2,1)}, bf16[512,2048]{1,0:T(8,128)(2,1)}, u32[]{:S(2)}, u32[]{:S(2)}) collective-permute-start(bf16[512,2048]{1,0:T(8,128)(2,1)} %pad_maximum_fusion.2), channel_id=1, source_target_pairs={{0,1},{1,0},{2,3},{3,2},{4,5},{5,4},{6,7},{7,6},{8,9},{9,8},{10,11... | collective-permute-start | bytes 6291464 | tf_op jit(solution)/shard_map/ppermute | solution.py:567
  415.6 72.3 %collective-permute-start.42 = (bf16[512,2048]{1,0:T(8,128)(2,1)}, bf16[512,2048]{1,0:T(8,128)(2,1)}, u32[]{:S(2)}, u32[]{:S(2)}) collective-permute-start(bf16[512,2048]{1,0:T(8,128)(2,1)} %pad_maximum_fusion.3), channel_id=1, source_target_pairs={{0,2},{1,3},{2,0},{3,1},{4,6},{5,7},{6,4},{7,5},{8,10},{9,11},{10,... | collective-permute-start | bytes 6291464 | tf_op jit(solution)/shard_map/ppermute | solution.py:567
  426.1 59.0 %collective-permute-start.45 = (bf16[2,1024,256]{2,1,0:T(8,128)(2,1)}, bf16[2,1024,256]{2,1,0:T(8,128)(2,1)}, u32[]{:S(2)}, u32[]{:S(2)}) collective-permute-start(bf16[2,1024,256]{2,1,0:T(8,128)(2,1)} %pad_maximum_fusion.13), channel_id=1, source_target_pairs={{0,8},{4,12},{8,0},{12,4},{16,24},{20,28},{24,16},{28,20},{1,9},{5... | collective-permute-start | bytes 3145736 | tf_op jit(solution)/shard_map/ppermute | solution.py:567
  487.3 87.9 %collective-permute-start.66 = (bf16[1,1024,256]{2,1,0:T(8,128)(2,1)}, bf16[1,1024,256]{2,1,0:T(8,128)(2,1)}, u32[]{:S(2)}, u32[]{:S(2)}) collective-permute-start(bf16[1,1024,256]{2,1,0:T(8,128)(2,1)} %fusion.74), channel_id=1, source_target_pairs={{0,16},{4,20},{8,24},{12,28},{16,0},{20,4},{24,8},{28,12},{1,17},{... | collective-permute-start | bytes 1572872 | tf_op jit(solution)/shard_map/ppermute | solution.py:567
  555.0 35.4 %collective-permute-start.46 = (bf16[2048,512]{1,0:T(8,128)(2,1)}, bf16[2048,512]{1,0:T(8,128)(2,1)}, u32[]{:S(2)}, u32[]{:S(2)}) collective-permute-start(bf16[2048,512]{1,0:T(8,128)(2,1)} %convolution_convert_fusion.4), channel_id=1, source_target_pairs={{0,4},{4,0},{8,12},{12,8},{16,20},{20,16},{24,28},{28,24},{1,5},{5... | collective-permute-start | bytes 6291464 | tf_op jit(solution)/shard_map/ppermute | solution.py:567
  558.6 145.9 %collective-permute-start.41 = (bf16[256,2048]{1,0:T(8,128)(2,1)}, bf16[256,2048]{1,0:T(8,128)(2,1)}, u32[]{:S(2)}, u32[]{:S(2)}) collective-permute-start(bf16[256,2048]{1,0:T(8,128)(2,1)} %get-tuple-element.248), channel_id=1, source_target_pairs={{0,2},{1,3},{2,0},{3,1},{4,6},{5,7},{6,4},{7,5},{8,10},{9,11},{10,... | collective-permute-start | bytes 3145736 | tf_op jit(solution)/shard_map/ppermute | solution.py:567
  564.9 19.8 %collective-permute-start.48 = (bf16[320,4,256]{2,0,1:T(8,128)(2,1)}, bf16[320,4,256]{2,0,1:T(8,128)(2,1)}, u32[]{:S(2)}, u32[]{:S(2)}) collective-permute-start(bf16[320,4,256]{2,0,1:T(8,128)(2,1)} %bitcast.305), channel_id=1, source_target_pairs={{0,4},{4,0},{8,12},{12,8},{16,20},{20,16},{24,28},{28,24},{1,5},{5... | collective-permute-start | bytes 1966088 | tf_op jit(solution)/shard_map/ppermute | solution.py:567
  586.9 19.9 %collective-permute-start.51 = (bf16[320,256]{1,0:T(8,128)(2,1)}, bf16[320,256]{1,0:T(8,128)(2,1)S(1)}, u32[]{:S(2)}, u32[]{:S(2)}) collective-permute-start(bf16[320,256]{1,0:T(8,128)(2,1)} %get-tuple-element.279), channel_id=1, source_target_pairs={{0,3},{1,2},{2,1},{3,0},{4,7},{5,6},{6,5},{7,4},{8,11},{9,10},{10,... | collective-permute-start | bytes 491528 | tf_op jit(solution)/shard_map/ppermute | solution.py:567
  588.6 19.8 %collective-permute-start.50 = (bf16[320,256]{1,0:T(8,128)(2,1)}, bf16[320,256]{1,0:T(8,128)(2,1)}, u32[]{:S(2)}, u32[]{:S(2)}) collective-permute-start(bf16[320,256]{1,0:T(8,128)(2,1)} %get-tuple-element.280), channel_id=1, source_target_pairs={{0,2},{1,3},{2,0},{3,1},{4,6},{5,7},{6,4},{7,5},{8,10},{9,11},{10,... | collective-permute-start | bytes 491528 | tf_op jit(solution)/shard_map/ppermute | solution.py:567
  590.0 18.9 %collective-permute-start.49 = (bf16[320,256]{1,0:T(8,128)(2,1)}, bf16[320,256]{1,0:T(8,128)(2,1)}, u32[]{:S(2)}, u32[]{:S(2)}) collective-permute-start(bf16[320,256]{1,0:T(8,128)(2,1)} %get-tuple-element.278), channel_id=1, source_target_pairs={{0,1},{1,0},{2,3},{3,2},{4,5},{5,4},{6,7},{7,6},{8,9},{9,8},{10,11... | collective-permute-start | bytes 491528 | tf_op jit(solution)/shard_map/ppermute | solution.py:567
  604.3 15.6 %collective-permute-start.47 = (bf16[2048,512]{1,0:T(8,128)(2,1)}, bf16[2048,512]{1,0:T(8,128)(2,1)}, u32[]{:S(2)}, u32[]{:S(2)}) collective-permute-start(bf16[2048,512]{1,0:T(8,128)(2,1)} %convolution_convert_fusion.2), channel_id=1, source_target_pairs={{0,4},{4,0},{8,12},{12,8},{16,20},{20,16},{24,28},{28,24},{1,5},{5... | collective-permute-start | bytes 6291464 | tf_op jit(solution)/shard_map/ppermute | solution.py:567
  606.8 99.1 %collective-permute-start.43 = (bf16[256,2048]{1,0:T(8,128)(2,1)}, bf16[256,2048]{1,0:T(8,128)(2,1)}, u32[]{:S(2)}, u32[]{:S(2)}) collective-permute-start(bf16[256,2048]{1,0:T(8,128)(2,1)} %get-tuple-element.249), channel_id=1, source_target_pairs={{0,1},{1,0},{2,3},{3,2},{4,5},{5,4},{6,7},{7,6},{8,9},{9,8},{10,11... | collective-permute-start | bytes 3145736 | tf_op jit(solution)/shard_map/ppermute | solution.py:567
  608.4 47.2 %collective-permute-start.69 = (bf16[256,256]{1,0:T(8,128)(2,1)}, bf16[256,256]{1,0:T(8,128)(2,1)}, u32[]{:S(2)}, u32[]{:S(2)}) collective-permute-start(bf16[256,256]{1,0:T(8,128)(2,1)} %get-tuple-element.294), channel_id=1, source_target_pairs={{0,3},{1,2},{2,1},{3,0},{4,7},{5,6},{6,5},{7,4},{8,11},{9,10},{10,... | collective-permute-start | bytes 393224 | tf_op jit(solution)/shard_map/ppermute | solution.py:567
  608.9 47.3 %collective-permute-start.68 = (bf16[256,256]{1,0:T(8,128)(2,1)}, bf16[256,256]{1,0:T(8,128)(2,1)}, u32[]{:S(2)}, u32[]{:S(2)}) collective-permute-start(bf16[256,256]{1,0:T(8,128)(2,1)} %get-tuple-element.295), channel_id=1, source_target_pairs={{0,2},{1,3},{2,0},{3,1},{4,6},{5,7},{6,4},{7,5},{8,10},{9,11},{10,... | collective-permute-start | bytes 393224 | tf_op jit(solution)/shard_map/ppermute | solution.py:567
  652.5 65.3 %collective-permute-start.52 = (bf16[512,2048]{1,0:T(8,128)(2,1)}, bf16[512,2048]{1,0:T(8,128)(2,1)}, u32[]{:S(2)}, u32[]{:S(2)}) collective-permute-start(bf16[512,2048]{1,0:T(8,128)(2,1)} %pad_maximum_fusion.4), channel_id=1, source_target_pairs={{0,1},{1,0},{2,3},{3,2},{4,5},{5,4},{6,7},{7,6},{8,9},{9,8},{10,11... | collective-permute-start | bytes 6291464 | tf_op jit(solution)/shard_map/ppermute | solution.py:567
  655.7 46.9 %collective-permute-start.67 = (bf16[256,256]{1,0:T(8,128)(2,1)S(1)}, bf16[256,256]{1,0:T(8,128)(2,1)S(1)}, u32[]{:S(2)}, u32[]{:S(2)}) collective-permute-start(bf16[256,256]{1,0:T(8,128)(2,1)S(1)} %copy-done.74), channel_id=1, source_target_pairs={{0,1},{1,0},{2,3},{3,2},{4,5},{5,4},{6,7},{7,6},{8,9},{9,8},{10,11... | collective-permute-start | bytes 393224 | tf_op jit(solution)/shard_map/ppermute | solution.py:567
  656.2 56.5 %collective-permute-start.57 = (bf16[2,592,512]{2,1,0:T(8,128)(2,1)}, bf16[2,592,512]{2,1,0:T(8,128)(2,1)S(1)}, u32[]{:S(2)}, u32[]{:S(2)}) collective-permute-start(bf16[2,592,512]{2,1,0:T(8,128)(2,1)} %pad_maximum_fusion.9), channel_id=1, source_target_pairs={{0,8},{4,12},{8,0},{12,4},{16,24},{20,28},{24,16},{28,20},{1,9},{5... | collective-permute-start | bytes 3637256 | tf_op jit(solution)/shard_map/ppermute | solution.py:567
  703.6 44.2 %collective-permute-start.56 = (bf16[2,592,512]{2,1,0:T(8,128)(2,1)}, bf16[2,592,512]{2,1,0:T(8,128)(2,1)S(1)}, u32[]{:S(2)}, u32[]{:S(2)}) collective-permute-start(bf16[2,592,512]{2,1,0:T(8,128)(2,1)} %pad_maximum_fusion.10), channel_id=1, source_target_pairs={{0,8},{4,12},{8,0},{12,4},{16,24},{20,28},{24,16},{28,20},{1,9},{5... | collective-permute-start | bytes 3637256 | tf_op jit(solution)/shard_map/ppermute | solution.py:567
  704.5 55.1 %collective-permute-start.54 = (bf16[512,2048]{1,0:T(8,128)(2,1)S(1)}, bf16[512,2048]{1,0:T(8,128)(2,1)S(1)}, u32[]{:S(2)}, u32[]{:S(2)}) collective-permute-start(bf16[512,2048]{1,0:T(8,128)(2,1)S(1)} %pad_maximum_fusion.5), channel_id=1, source_target_pairs={{0,2},{1,3},{2,0},{3,1},{4,6},{5,7},{6,4},{7,5},{8,10},{9,11},{10,... | collective-permute-start | bytes 6291464 | tf_op jit(solution)/shard_map/ppermute | solution.py:567
  714.8 35.0 %collective-permute-start.60 = (bf16[1,592,512]{2,1,0:T(8,128)(2,1)S(1)}, bf16[1,592,512]{2,1,0:T(8,128)(2,1)S(1)}, u32[]{:S(2)}, u32[]{:S(2)}) collective-permute-start(bf16[1,592,512]{2,1,0:T(8,128)(2,1)S(1)} %bitcast.353), channel_id=1, source_target_pairs={{0,16},{4,20},{8,24},{12,28},{16,0},{20,4},{24,8},{28,12},{1,17},{... | collective-permute-start | bytes 1818632 | tf_op jit(solution)/shard_map/ppermute | solution.py:567
  715.8 32.0 %collective-permute-start.63 = (bf16[320,256]{1,0:T(8,128)(2,1)S(1)}, bf16[320,256]{1,0:T(8,128)(2,1)S(1)}, u32[]{:S(2)}, u32[]{:S(2)}) collective-permute-start(bf16[320,256]{1,0:T(8,128)(2,1)S(1)} %fusion.77), channel_id=1, source_target_pairs={{0,8},{4,12},{8,0},{12,4},{16,24},{20,28},{24,16},{28,20},{1,9},{5... | collective-permute-start | bytes 491528 | tf_op jit(solution)/shard_map/ppermute | solution.py:567
  719.4 62.7 %collective-permute-start.53 = (bf16[256,2048]{1,0:T(8,128)(2,1)S(1)}, bf16[256,2048]{1,0:T(8,128)(2,1)S(1)}, u32[]{:S(2)}, u32[]{:S(2)}) collective-permute-start(bf16[256,2048]{1,0:T(8,128)(2,1)S(1)} %add_convert_fusion.3), channel_id=1, source_target_pairs={{0,2},{1,3},{2,0},{3,1},{4,6},{5,7},{6,4},{7,5},{8,10},{9,11},{10,... | collective-permute-start | bytes 3145736 | tf_op jit(solution)/shard_map/ppermute | solution.py:567
  748.2 36.1 %collective-permute-start.58 = (bf16[1,592,512]{2,1,0:T(8,128)(2,1)S(1)}, bf16[1,592,512]{2,1,0:T(8,128)(2,1)S(1)}, u32[]{:S(2)}, u32[]{:S(2)}) collective-permute-start(bf16[1,592,512]{2,1,0:T(8,128)(2,1)S(1)} %bitcast.352), channel_id=1, source_target_pairs={{0,16},{4,20},{8,24},{12,28},{16,0},{20,4},{24,8},{28,12},{1,17},{... | collective-permute-start | bytes 1818632 | tf_op jit(solution)/shard_map/ppermute | solution.py:567
  750.0 44.7 %collective-permute-start.61 = (bf16[592,256]{1,0:T(8,128)(2,1)S(1)}, bf16[592,256]{1,0:T(8,128)(2,1)S(1)}, u32[]{:S(2)}, u32[]{:S(2)}) collective-permute-start(bf16[592,256]{1,0:T(8,128)(2,1)S(1)} %get-tuple-element.286), channel_id=1, source_target_pairs={{0,2},{1,3},{2,0},{3,1},{4,6},{5,7},{6,4},{7,5},{8,10},{9,11},{10,... | collective-permute-start | bytes 909320 | tf_op jit(solution)/shard_map/ppermute | solution.py:567
  751.5 43.3 %collective-permute-start.62 = (bf16[592,256]{1,0:T(8,128)(2,1)S(1)}, bf16[592,256]{1,0:T(8,128)(2,1)S(1)}, u32[]{:S(2)}, u32[]{:S(2)}) collective-permute-start(bf16[592,256]{1,0:T(8,128)(2,1)S(1)} %get-tuple-element.285), channel_id=1, source_target_pairs={{0,3},{1,2},{2,1},{3,0},{4,7},{5,6},{6,5},{7,4},{8,11},{9,10},{10,... | collective-permute-start | bytes 909320 | tf_op jit(solution)/shard_map/ppermute | solution.py:567
  759.6 35.3 %collective-permute-start.64 = (bf16[320,256]{1,0:T(8,128)(2,1)S(1)}, bf16[320,256]{1,0:T(8,128)(2,1)S(1)}, u32[]{:S(2)}, u32[]{:S(2)}) collective-permute-start(bf16[320,256]{1,0:T(8,128)(2,1)S(1)} %add_convert_fusion.15), channel_id=1, source_target_pairs={{0,16},{4,20},{8,24},{12,28},{16,0},{20,4},{24,8},{28,12},{1,17},{... | collective-permute-start | bytes 491528 | tf_op jit(solution)/shard_map/ppermute | solution.py:567
  784.5 10.2 %collective-permute-start.59 = (bf16[592,256]{1,0:T(8,128)(2,1)S(1)}, bf16[592,256]{1,0:T(8,128)(2,1)S(1)}, u32[]{:S(2)}, u32[]{:S(2)}) collective-permute-start(bf16[592,256]{1,0:T(8,128)(2,1)S(1)} %get-tuple-element.287), channel_id=1, source_target_pairs={{0,1},{1,0},{2,3},{3,2},{4,5},{5,4},{6,7},{7,6},{8,9},{9,8},{10,11... | collective-permute-start | bytes 909320 | tf_op jit(solution)/shard_map/ppermute | solution.py:567
  788.8 23.4 %collective-permute-start.55 = (bf16[256,2048]{1,0:T(8,128)(2,1)S(1)}, bf16[256,2048]{1,0:T(8,128)(2,1)S(1)}, u32[]{:S(2)}, u32[]{:S(2)}) collective-permute-start(bf16[256,2048]{1,0:T(8,128)(2,1)S(1)} %get-tuple-element.225), channel_id=1, source_target_pairs={{0,1},{1,0},{2,3},{3,2},{4,5},{5,4},{6,7},{7,6},{8,9},{9,8},{10,11... | collective-permute-start | bytes 3145736 | tf_op jit(solution)/shard_map/ppermute | solution.py:567
  802.3 15.6 %collective-permute-start.65 = (bf16[256,1064]{0,1:T(8,128)(2,1)}, bf16[256,1064]{0,1:T(8,128)(2,1)}, u32[]{:S(2)}, u32[]{:S(2)}) collective-permute-start(bf16[256,1064]{0,1:T(8,128)(2,1)} %broadcast_select_fusion.2), channel_id=1, source_target_pairs={{0,4},{4,0},{8,12},{12,8},{16,20},{20,16},{24,28},{28,24},{1,5},{5... | collective-permute-start | bytes 1634312 | tf_op jit(solution)/shard_map/ppermute | solution.py:567
  (140 other events, 1217.0 us)

commit v3 on v2

--- a/solution.py
+++ b/solution.py
@@ -116,7 +116,7 @@
     shift_ref, logd_ref, skip_ref,
     gated_ref, y_ref, state_ref, total_ref,
     same_ref, enter_ref, last_ref, cmat_ref, bt_ref, score_ref, square_ref,
-    x_ref, carry_ref, step_ref, cum_ref, cumt_ref,
+    x_ref, carry_ref, step_ref, cum_ref, cumt_ref, tailed_ref, decay_ref,
 ):
     j = pl.program_id(1)
     length = gate_ref.shape[0]
@@ -174,14 +174,15 @@
                 y = y + reach * outside[:, cols]
             if c < chunks - 1:
                 tail = jnp.exp(cum_x[Q - 1 : Q] - cum_x) * last_ref[rows]
-                carry_ref[:, cols] = reach[Q - 1 : Q] * carry_ref[:, cols] + dot(
-                    bt_ref[:, rows], (xs.astype(F32) * tail).astype(BF16)
-                )
+                tailed_ref[:, cols] = (xs.astype(F32) * tail).astype(BF16)
+                decay_ref[0:1, cols] = reach[Q - 1 : Q]
             y_ref[rows, cols] = y
             gate = gate_ref[rows, cols].astype(F32)
             gated = (y + skip_ref[:, cols] * x) * (gate * sigmoid(gate))
             square_ref[rows, :] += gated * gated
             gated_ref[rows, cols] = gated
+        if c < chunks - 1:
+            carry_ref[...] = decay_ref[0:1, :] * carry_ref[...] + dot(bt_ref[:, rows], tailed_ref[...])
 
     @pl.when(j == pl.num_programs(1) - 1)
     def _():
@@ -195,9 +196,9 @@
     sshift_ref, slogd_ref, sskip_ref,
     same_ref, enter_ref, last_ref, bmat_ref, cmat_ref, ct_ref, score_ref, scoret_ref,
     x_ref, slope_ref, dy_ref, dxs_ref, carry_ref, step_ref, cum_ref, cumt_ref,
-    dscore_ref, db_ref, dc_ref, v1_ref, v2_ref, v3_ref, v4_ref, dxin_ref,
+    dscore_ref, db_ref, dc_ref, v1_ref, v2_ref, v3_ref, v4_ref, tailed_ref, reached_ref, decay_ref, held_ref,
 ):
-    j = pl.program_id(1)
+    j = pl.program_id(2)
     length = gate_ref.shape[0]
     chunks = length // Q
     lo = lax.broadcasted_iota(jnp.int32, (Q, 128), 1) < HP
@@ -291,7 +292,7 @@
                 d_tail = tail * from_state[:, cols]
                 v3_ref[rows, cols] = xs_wide * d_tail
                 d_xs = d_xs + d_tail
-                db_ref[rows, :] += dot_nt((xs_wide * tail).astype(BF16), d_state_low[:, cols])
+                tailed_ref[:, cols] = (xs_wide * tail).astype(BF16)
                 entered = state_ref[0, c, :, cols]
                 v4_ref[c : c + 1, cols] = reach[Q - 1 : Q] * jnp.sum(
                     d_state[:, cols] * entered.astype(F32), axis=0, keepdims=True
@@ -300,12 +301,17 @@
                 v3_ref[rows, cols] = jnp.zeros((Q, 128), F32)
                 v4_ref[c : c + 1, cols] = jnp.zeros((1, 128), F32)
             if c > 0:
-                reached = (reach * d_y).astype(BF16)
-                dc_ref[rows, :] += dot_nt(reached, state_ref[0, c, :, cols])
-                carry_ref[:, cols] = reach[Q - 1 : Q] * d_state[:, cols] + dot(ct_ref[:, rows], reached)
+                reached_ref[:, cols] = (reach * d_y).astype(BF16)
+                decay_ref[0:1, cols] = reach[Q - 1 : Q]
             v2_ref[rows, cols] = x * d_xs
             dxs_ref[rows, cols] = step_x * d_xs + skip_ref[:, cols] * d_y
         dscore_ref[c] = d_score
+        if c < chunks - 1:
+            db_ref[rows, :] += dot_nt(tailed_ref[...], d_state_low)
+        if c > 0:
+            reached = reached_ref[...]
+            dc_ref[rows, :] += dot_nt(reached, state_ref[0, c])
+            carry_ref[...] = decay_ref[0:1, :] * d_state + dot(ct_ref[:, rows], reached)
 
     head = lax.broadcasted_iota(jnp.int32, (HB, BC), 0)
     lane = lax.broadcasted_iota(jnp.int32, (HB, BC), 1)
@@ -343,11 +349,11 @@
         cols = slice(p * 128, (p + 1) * 128)
         d_conv = dxs_ref[:, cols] * slope_ref[:, cols]
         d_in, s_w, s_b = conv_backward(d_conv, xin_ref[:, cols].astype(F32), cw_ref[:, cols], same_ref)
-        dxin_ref[:, cols] = d_in.astype(dxin_ref.dtype)
+        held_ref[j, :, cols] = d_in.astype(BF16)
         scw_ref[0, :, cols] = s_w
         scb_ref[0, :, cols] = s_b
 
-    @pl.when(j == pl.num_programs(1) - 1)
+    @pl.when(j == pl.num_programs(2) - 1)
     def _():
         for c in range(chunks):
             rows = slice(c * Q, (c + 1) * Q)
@@ -368,51 +374,55 @@
 def backward_kernel(*refs):
     outputs_at = 18
 
-    @pl.when(pl.program_id(2) == 0)
+    @pl.when(pl.program_id(1) == 0)
     def _():
         backward_body(*refs)
 
-    @pl.when(pl.program_id(2) == 1)
+    @pl.when(pl.program_id(1) == 1)
     def _():
-        refs[outputs_at + 1][...] = refs[-1][...]
+        refs[outputs_at + 1][...] = refs[-1][pl.program_id(2)]
 
 
 def backward_first(*refs):
     backward_kernel(*refs[:18], None, *refs[18:])
 
 
-def row_block(first, rows, offset=0):
-    return pl.BlockSpec((rows, BC), lambda r, j, *s: (first + r, j + offset))
-
-
-def columns(rows):
-    return pl.BlockSpec((rows, BC), lambda r, j, *s: (0, j))
-
-
-def whole(*shape):
-    return pl.BlockSpec(shape, lambda r, j, *s: (0,) * len(shape))
-
-
-def row_sums(rows):
-    return pl.BlockSpec((1, rows, BC), lambda r, j, *s: (r, 0, j))
-
-
-def common_specs(first, length, channels):
-    heads = pl.BlockSpec((HB, 1), lambda r, j, *s: (j, 0))
-    return [
+def forward_index(first, rows):
+    return lambda r, j: (first + r, r, j)
+
+
+def backward_index(first, rows):
+    def index(r, s, j):
+        r = jnp.minimum(r + s, rows - 1)
+        return first + r, r, j * (1 - s)
+
+    return index
+
+
+def common_specs(index, length, channels):
+    def at(shape, where):
+        return pl.BlockSpec(shape, lambda *g: where(*index(*g)))
+
+    blocks = channels // BC
+    heads = at((HB, 1), lambda a, r, j: (j, 0))
+    return at, [
         pl.BlockSpec(memory_space=pltpu.SMEM),
-        row_block(first, length),
-        row_block(first, length, channels // BC),
-        pl.BlockSpec((length, 2 * NS), lambda r, j, *s: (first + r, 0)),
-        pl.BlockSpec((HB, length), lambda r, j, *s: (j, first + r)),
-        columns(CONVW),
-        columns(1),
-        whole(CONVW, 2 * NS),
-        whole(1, 2 * NS),
+        at((length, BC), lambda a, r, j: (a, j)),
+        at((length, BC), lambda a, r, j: (a, j + blocks)),
+        at((length, 2 * NS), lambda a, r, j: (a, 0)),
+        at((HB, length), lambda a, r, j: (j, a)),
+        at((CONVW, BC), lambda a, r, j: (0, j)),
+        at((1, BC), lambda a, r, j: (0, j)),
+        at((CONVW, 2 * NS), lambda a, r, j: (0, 0)),
+        at((1, 2 * NS), lambda a, r, j: (0, 0)),
         heads,
         heads,
-        columns(1),
+        at((1, BC), lambda a, r, j: (0, j)),
     ]
+
+
+def row_cost(size, weight):
+    return pl.CostEstimate(flops=1000 * weight * size, bytes_accessed=12 * size, transcendentals=0)
 
 
 def mix_forward(first, length, starts, main, extra, dt_rows, conv_w, conv_b, cw_bc, cb_bc, shift, logd, skip_cols):
@@ -420,13 +430,14 @@
     channels = main.shape[1] // 2
     chunks = length // Q
     vmem = pltpu.VMEM
+    _, in_specs = common_specs(forward_index(first, rows), length, channels)
     return pl.pallas_call(
         forward_kernel,
         grid=(rows, channels // BC),
-        in_specs=common_specs(first, length, channels),
+        in_specs=in_specs,
         out_specs=[
-            row_block(0, length),
-            row_block(0, length),
+            pl.BlockSpec((length, BC), lambda r, j: (r, j)),
+            pl.BlockSpec((length, BC), lambda r, j: (r, j)),
             pl.BlockSpec((1, chunks, NS, BC), lambda r, j: (r, 0, 0, j)),
             pl.BlockSpec((length, 1), lambda r, j: (r, 0)),
         ],
@@ -449,8 +460,11 @@
             vmem((length, HB), F32),
             vmem((length, HB), F32),
             vmem((HB, length), F32),
+            vmem((Q, BC), BF16),
+            vmem((8, BC), F32),
         ],
         compiler_params=pltpu.CompilerParams(vmem_limit_bytes=48 * 1024 * 1024),
+        cost_estimate=row_cost(rows * length * channels, 18),
         name="mix_forward",
     )(starts, main, main, extra, dt_rows, conv_w, conv_b, cw_bc, cb_bc, shift, logd, skip_cols)
 
@@ -465,20 +479,28 @@
     blocks = channels // BC
     chunks = length // Q
     vmem = pltpu.VMEM
-    per_head = pl.BlockSpec((1, HB, 1), lambda r, j, s: (r, j, 0))
-    col = pl.BlockSpec((length, 1), lambda r, j, s: (first + r, 0))
+    at, in_specs = common_specs(backward_index(first, rows), length, channels)
+    col = at((length, 1), lambda a, r, j: (a, 0))
+
+    def result(shape, where):
+        return pl.BlockSpec(shape, lambda r, s, j: where(r, jnp.maximum(j, s * (blocks - 1))))
+
+    def row_sums(count):
+        return result((1, count, BC), lambda r, j: (r, 0, j))
+
+    per_head = result((1, HB, 1), lambda r, j: (r, j, 0))
     shape = jax.ShapeDtypeStruct
     operands = (
         starts, main, main, extra, dt_rows, conv_w, conv_b, cw_bc, cb_bc, shift, logd, skip_cols,
         gain, y, states, q, mean, d_mixed,
     )
-    in_specs = common_specs(first, length, channels) + [
-        columns(1),
-        row_block(0, length),
-        pl.BlockSpec((1, chunks, NS, BC), lambda r, j, s: (r, 0, 0, j)),
+    in_specs = in_specs + [
+        at((1, BC), lambda a, r, j: (0, j)),
+        at((length, BC), lambda a, r, j: (r, j)),
+        at((1, chunks, NS, BC), lambda a, r, j: (r, 0, 0, j)),
         col,
         col,
-        row_block(first, length),
+        at((length, BC), lambda a, r, j: (a, j)),
     ]
     aliases = {}
     if before is not None:
@@ -487,17 +509,17 @@
         in_specs = in_specs + [pl.BlockSpec(memory_space=pl.ANY)]
     return pl.pallas_call(
         backward_first if before is None else backward_kernel,
-        grid=(rows, blocks, 2),
+        grid=(rows, 2, blocks),
         in_specs=in_specs,
         out_specs=[
-            pl.BlockSpec((length, BC), lambda r, j, s: (first + r, j + blocks * s)),
-            pl.BlockSpec((length, 2 * NS), lambda r, j, s: (r, 0)),
-            pl.BlockSpec((HB, length), lambda r, j, s: (j, r)),
+            pl.BlockSpec((length, BC), lambda r, s, j: (first + r, j + blocks * s)),
+            result((length, 2 * NS), lambda r, j: (r, 0)),
+            result((HB, length), lambda r, j: (j, r)),
             row_sums(1),
             row_sums(CONVW),
             row_sums(1),
-            pl.BlockSpec((1, CONVW, 2 * NS), lambda r, j, s: (r, 0, 0)),
-            pl.BlockSpec((1, 1, 2 * NS), lambda r, j, s: (r, 0, 0)),
+            result((1, CONVW, 2 * NS), lambda r, j: (r, 0, 0)),
+            result((1, 1, 2 * NS), lambda r, j: (r, 0, 0)),
             per_head,
             per_head,
             row_sums(1),
@@ -539,10 +561,14 @@
             vmem((length, BC), F32),
             vmem((length, BC), F32),
             vmem((8, BC), F32),
-            vmem((length, BC), BF16),
+            vmem((Q, BC), BF16),
+            vmem((Q, BC), BF16),
+            vmem((8, BC), F32),
+            vmem((blocks, length, BC), BF16),
         ],
         input_output_aliases=aliases,
         compiler_params=pltpu.CompilerParams(vmem_limit_bytes=48 * 1024 * 1024),
+        cost_estimate=row_cost(rows * length * channels, 42),
         name="mix_backward",
     )(*operands)
 
@@ -609,38 +635,148 @@
         ),
         out_shape=jax.ShapeDtypeStruct(shape, BF16),
         input_output_aliases={} if buffer is None else {len(operands) - 1: 0},
-        compiler_params=pltpu.CompilerParams(vmem_limit_bytes=32 * 1024 * 1024),
+        compiler_params=pltpu.CompilerParams(vmem_limit_bytes=60 * 1024 * 1024),
         name="place",
     )(*operands)
 
 
-def rows_into(buffer, row, rows, pieces, gain=None):
-    size, width = sum(p.shape[0] for p in pieces), pieces[0].shape[1]
+def place_blocks(buffer, shape, arrays, size, order, columns, first_rows, counts, cuts):
+    width, steps = arrays[0].shape[2], len(columns)
+    pieces = [(a, n) for a, array in enumerate(arrays) for n in range(array.shape[0])]
+    table = [jnp.asarray(v, jnp.int32) for v in columns]
+    for rel in order:
+        table.extend([first_rows(rel), counts(rel)])
+    operands = [jnp.stack(table)] + list(arrays) + ([] if buffer is None else [buffer])
+
+    def kernel(table_ref, *refs):
+        for i, (a, n) in enumerate(pieces):
+            begin = pl.multiple_of(table_ref[steps + 2 * i], 16)
+            for start, end in zip(cuts[:-1], cuts[1:]):
+
+                @pl.when(table_ref[steps + 2 * i + 1] > start)
+                def _():
+                    refs[-1][pl.ds(pl.multiple_of(begin + start, 16), end - start), :] = refs[a][n, start:end, :]
+
+    return pl.pallas_call(
+        kernel,
+        grid_spec=pltpu.PrefetchScalarGridSpec(
+            num_scalar_prefetch=1,
+            grid=(steps,),
+            in_specs=[pl.BlockSpec((a.shape[0], size, width), lambda i, t: (0, i, 0)) for a in arrays]
+            + ([] if buffer is None else [pl.BlockSpec(memory_space=pl.ANY)]),
+            out_specs=pl.BlockSpec((shape[0], width), lambda i, t: (0, t[i])),
+        ),
+        out_shape=jax.ShapeDtypeStruct(shape, BF16),
+        input_output_aliases={} if buffer is None else {len(operands) - 1: 0},
+        compiler_params=pltpu.CompilerParams(vmem_limit_bytes=60 * 1024 * 1024),
+        name="place_blocks",
+    )(*operands)
+
+
+def matmul(a, b, kind, out_dtype=BF16, scale=None):
+    m = a.shape[1] if kind == "tn" else a.shape[0]
+    k = a.shape[0] if kind == "tn" else a.shape[1]
+    n = b.shape[0] if kind == "nt" else b.shape[1]
+    tm, tn = min(m, 1024), min(n, 512)
+    dims = {"nn": ((1,), (0,)), "nt": ((1,), (1,)), "tn": ((0,), (0,))}[kind]
+
+    def kernel(*refs):
+        first = refs[0][...]
+        if scale is not None:
+            first = first * refs[2][...]
+        total = lax.dot_general(first, refs[1][...], (dims, ((), ())), preferred_element_type=F32)
+        refs[-1][...] = total.astype(out_dtype)
+
+    in_specs = [
+        pl.BlockSpec((k, tm), lambda i, j: (0, i)) if kind == "tn" else pl.BlockSpec((tm, k), lambda i, j: (i, 0)),
+        pl.BlockSpec((tn, k), lambda i, j: (j, 0)) if kind == "nt" else pl.BlockSpec((k, tn), lambda i, j: (0, j)),
+    ]
+    operands = [a, b]
+    if scale is not None:
+        in_specs.append(pl.BlockSpec((k, 1), lambda i, j: (0, 0)))
+        operands.append(scale)
+    return pl.pallas_call(
+        kernel,
+        grid=(m // tm, n // tn),
+        in_specs=in_specs,
+        out_specs=pl.BlockSpec((tm, tn), lambda i, j: (i, j)),
+        out_shape=jax.ShapeDtypeStruct((m, n), out_dtype),
+        compiler_params=pltpu.CompilerParams(vmem_limit_bytes=56 * 1024 * 1024),
+        cost_estimate=pl.CostEstimate(flops=2 * m * n * k, bytes_accessed=2 * (m * k + n * k + m * n), transcendentals=0),
+        name="matmul_" + kind,
+    )(*operands)
+
+
+def mixed_gradient(upstream, weights, live, mixed):
+    rows, width = upstream.shape
+    local = weights.shape[0]
+    tm, tn = min(rows, 1024), min(local, 512)
+
+    def kernel(up_ref, w_ref, live_ref, mixed_ref, out_ref, inner_ref):
+        total = (dot_nt(up_ref[...], w_ref[...]) * live_ref[...]).astype(BF16)
+        out_ref[...] = total
+        part = jnp.sum(total.astype(F32) * mixed_ref[...].astype(F32), axis=1, keepdims=True)
+
+        @pl.when(pl.program_id(1) == 0)
+        def _():
+            inner_ref[...] = part
+
+        @pl.when(pl.program_id(1) > 0)
+        def _():
+            inner_ref[...] += part
+
+    return pl.pallas_call(
+        kernel,
+        grid=(rows // tm, local // tn),
+        in_specs=[
+            pl.BlockSpec((tm, width), lambda i, j: (i, 0)),
+            pl.BlockSpec((tn, width), lambda i, j: (j, 0)),
+            pl.BlockSpec((tm, 1), lambda i, j: (i, 0)),
+            pl.BlockSpec((tm, tn), lambda i, j: (i, j)),
+        ],
+        out_specs=[pl.BlockSpec((tm, tn), lambda i, j: (i, j)), pl.BlockSpec((tm, 1), lambda i, j: (i, 0))],
+        out_shape=[jax.ShapeDtypeStruct((rows, local), BF16), jax.ShapeDtypeStruct((rows, 1), F32)],
+        compiler_params=pltpu.CompilerParams(vmem_limit_bytes=56 * 1024 * 1024),
+        name="mixed_gradient",
+    )(upstream, weights, live, mixed)
+
+
+def rows_into(buffer, row, rows, length, pieces, gain=None):
+    tile = 128
+    counts = [p.shape[0] // tile for p in pieces]
+    starts = [sum(counts[:i]) for i in range(len(counts) + 1)]
+    width = pieces[0].shape[1]
     operands = list(pieces) + ([] if gain is None else [gain]) + ([] if buffer is None else [buffer])
 
     def kernel(*refs):
-        at = 0
-        for i, piece in enumerate(pieces):
-            for start in range(0, piece.shape[0], 128):
-                value = refs[i][start : start + 128, :]
+        step = pl.program_id(0)
+        for i in range(len(pieces)):
+
+            @pl.when((step >= starts[i]) & (step < starts[i + 1]))
+            def _():
+                value = refs[i][...]
                 if gain is not None:
                     value = value.astype(F32)
                     mean = jnp.mean(value * value, axis=1, keepdims=True)
                     value = (value * lax.rsqrt(mean + EPSILON) * refs[len(pieces)][...]).astype(BF16)
-                refs[-1][at + start : at + start + 128, :] = value
-            at += piece.shape[0]
-
-    specs = [pl.BlockSpec(p.shape, lambda i: (0, 0)) for p in operands]
+                refs[-1][...] = value
+
+    def piece_spec(i):
+        return pl.BlockSpec((tile, width), lambda s: (jnp.clip(s - starts[i], 0, counts[i] - 1), 0))
+
+    specs = [piece_spec(i) for i in range(len(pieces))]
+    if gain is not None:
+        specs.append(pl.BlockSpec(gain.shape, lambda s: (0, 0)))
     if buffer is not None:
-        specs[-1] = pl.BlockSpec(memory_space=pl.ANY)
+        specs.append(pl.BlockSpec(memory_space=pl.ANY))
     return pl.pallas_call(
         kernel,
-        grid=(1,),
+        grid=(starts[-1],),
         in_specs=specs,
-        out_specs=pl.BlockSpec((size, width), lambda i: (row, 0)),
-        out_shape=jax.ShapeDtypeStruct((rows * size, width), BF16),
+        out_specs=pl.BlockSpec((tile, width), lambda s: (row * length // tile + s, 0)),
+        out_shape=jax.ShapeDtypeStruct((rows * length, width), BF16),
         input_output_aliases={} if buffer is None else {len(operands) - 1: 0},
-        compiler_params=pltpu.CompilerParams(vmem_limit_bytes=32 * 1024 * 1024),
+        compiler_params=pltpu.CompilerParams(vmem_limit_bytes=60 * 1024 * 1024),
         name="rows_into",
     )(*operands)
 
@@ -704,20 +840,6 @@
     mine = lax.dynamic_slice_in_dim(low, k_half * c, k_half, 0)
     other = swap(lax.dynamic_slice_in_dim(low, k_half * (1 - c), k_half, 0), "dp", 1)
     chip = jnp.concatenate([jnp.where(c == 0, mine, other), jnp.where(c == 0, other, mine)], axis=1)
-    half = length // 2
-
-    def neighbours(row, which):
-        parts = (row[:half], row[half:])
-        return [swap(parts[which], "fsdp", 1), swap(parts[1 - which], "fsdp", 2)]
-
-    def corners(first):
-        return [swap(first[0], "fsdp", 2), swap(first[1], "fsdp", 1)]
-
-    def pieces_of(first, second, third):
-        return [[first[0], second[0]], [second[1], first[1]], third]
-
-    near = neighbours(tokens[0], 0)
-    chip = then(chip, *near)
     column = per_chip * z + jnp.arange(per_chip, dtype=jnp.int32)
     owner = (column // unit) % groups
     begin = prefix_count(owner, per_chip * z, unit, local)
@@ -736,30 +858,35 @@
         v = v.reshape(v.shape[0], groups, groups, -1)
         return lax.dynamic_index_in_dim(v, f, 2, keepdims=False).reshape(v.shape[0], -1)
 
+    out_low = w_out.astype(BF16).reshape(groups, unit, out_cols)
+    out_blocks = [lax.dynamic_index_in_dim(out_low, f ^ m, 0, keepdims=False) for m in range(groups)]
     blocks = [parts[m * most : (m + 1) * most] for m in range(groups)]
-    blocks = blocks[:1] + [swap(blocks[m], "fsdp", m) for m in range(1, groups)]
+    pairs = [swap(jnp.concatenate([blocks[m], out_blocks[m]]), "fsdp", m) for m in range(1, groups)]
+    blocks = blocks[:1] + [p[:most] for p in pairs]
+    out_cat = jnp.stack(out_blocks[:1] + [p[most:] for p in pairs])
+    out_cat = jnp.concatenate([lax.dynamic_index_in_dim(out_cat, f ^ m, 0, keepdims=False) for m in range(groups)])
     first = jnp.concatenate([blocks[0], parts[groups * most :]])[None]
-    second = jnp.concatenate(blocks[1:])[None]
+    marks = jnp.concatenate([doc_starts[0], valid_len])
+    marks = jnp.concatenate([(marks // 32).astype(BF16), (marks % 32).astype(BF16)])
+    flat = then(jnp.concatenate([marks] + [v.astype(BF16).reshape(-1) for v in small])[None], mine)
+    rel_small = jnp.concatenate([flat] + [swap(flat, "fsdp", m) for m in range(1, groups)])
+    order = jnp.arange(groups, dtype=jnp.int32) ^ f
+    every = jnp.sum(
+        jnp.where((order[None, :] == jnp.arange(groups)[:, None])[:, :, None], rel_small[None], 0), axis=1
+    ).astype(F32)
+    count = marks.shape[0] // 2
+    marks = every[:, : 2 * count].astype(jnp.int32)
+    marks = marks[:, :count] * 32 + marks[:, count:]
+    every = every[:, 2 * count :]
+    second = then(jnp.concatenate(blocks[1:])[None], rel_small)
+    token_rows = lax.all_gather(tokens[0], "fsdp", axis=0, tiled=True)
+    upstream_all = lax.all_gather(cotangent[0], "fsdp", axis=0, tiled=True)
     got = swap(first, "dp", 2 * z_masks[0])
     first_2 = jnp.concatenate([first, got])
     sent_a = then(first_2, second)
     sent_b = then(second, first_2)
     got_a = swap(sent_a, "dp", 2 * z_masks[1])
     got_b = swap(sent_b, "dp", 2 * z_masks[0])
-    far = corners([then(v, sent_a) for v in near])
-    near_2 = neighbours(then(tokens[0], sent_a), 1)
-    marks = jnp.concatenate([doc_starts[0], valid_len])
-    marks = jnp.concatenate([(marks // 32).astype(BF16), (marks % 32).astype(BF16)])
-    flat = then(jnp.concatenate([marks] + [v.astype(BF16).reshape(-1) for v in small])[None], first_2)
-    rel_small = jnp.concatenate([flat] + [swap(flat, "fsdp", m) for m in range(1, groups)])
-    count = marks.shape[0] // 2
-    marks = rel_small[:, : 2 * count].astype(jnp.int32)
-    marks = marks[:, :count] * 32 + marks[:, count:]
-    rel_small = rel_small[:, 2 * count :]
-    order = jnp.arange(groups, dtype=jnp.int32) ^ f
-    every = jnp.sum(
-        jnp.where((order[None, :] == jnp.arange(groups)[:, None])[:, :, None], rel_small[None], 0), axis=1
-    ).astype(F32)
     full, at = [], 0
     for v in small:
         piece = every[:, at : at + v.size]
@@ -776,160 +903,113 @@
     starts = marks[:, :-1]
     live_all = jnp.concatenate([(jnp.arange(length) < marks[r, -1]).astype(F32)[:, None] for r in range(groups)])
 
-    second_2 = then(jnp.concatenate([second, got_b]), got_a, *near_2)
+    second_2 = then(jnp.concatenate([second, got_b]), got_a)
     got_b2 = swap(second_2, "dp", 2 * z_masks[1])
     spread_a = jnp.concatenate([first_2, got_a])
     order_z = [0, z_masks[0]] + [z_masks[1], z_masks[0] ^ z_masks[1]]
     sibling_a = swap(then(spread_a, second_2), "dp", 1)
     sibling_b = swap(second_2, "dp", 1)
-    near_pieces = pieces_of(near, near_2, far)
-    normed_all = None
-    for m in range(groups - 1):
-        row = [then(tokens[0], second_2)] if m == 0 else near_pieces[m - 1]
-        normed_all = rows_into(normed_all, m, groups, row, norm_full)
+    normed_all = rows_into(None, 0, groups, length, [token_rows], norm_full)
     extra_at = jnp.stack([jnp.int32(r) for r in order_z]) == (z ^ (zs - 1))
     extra_at = jnp.sum(jnp.where(extra_at, jnp.arange(zs, dtype=jnp.int32), 0))
     extra_own = lax.dynamic_index_in_dim(then(spread_a, second_2), extra_at, 0, keepdims=False)[most:]
     extra_got = jnp.stack([extra_own] + [swap(extra_own, "fsdp", m) for m in range(1, groups)])
-    extra_got = then(extra_got, normed_all)
     extra_pair = [extra_got, swap(extra_got, "dp", 1)]
-    up_near = neighbours(then(cotangent[0], second_2), 0)
-    got_b2 = then(got_b2, normed_all, *far)
+    w_shape = (2 * local, width)
+
+    def place_main(buffer, arrays, ms, rc):
+        where = [2 * (f ^ m) + (c ^ rc) for m in ms]
+        return place_blocks(
+            buffer, w_shape, arrays, most, order_z, where, lambda r: first_row(z ^ r), lambda r: rows_valid(z ^ r), cuts
+        )
+
+    w_main = place_main(None, [spread_a], [0], 0)
+    w_main = place_main(w_main, [sibling_a], [0], 1)
+    got_b2 = then(got_b2, normed_all, w_main)
     sibling_b2 = swap(got_b2, "dp", 1)
-    normed_all = rows_into(then(normed_all, got_b2), groups - 1, groups, near_pieces[-1], norm_full)
-    bundles_in = [
-        [(spread_a, range(zs))],
-        [(second_2, range(2)), (got_b2, range(2, zs))],
-        [(sibling_a, range(zs))],
-        [(sibling_b, range(2)), (sibling_b2, range(2, zs))],
-    ]
-    w_main = None
-    for rc in range(2):
-        for m in range(groups):
-            items, skip = [], 0 if m == 0 else most * (m - 1)
-            for array, ranks in bundles_in[2 * rc + (m > 0)]:
-                for at, i in enumerate(ranks):
-                    zz = z ^ order_z[i]
-                    valid = rows_valid(zz) + skip
-                    items.append((array, at, first_row(zz) - skip, 0, valid, [e + skip for e in cuts]))
-            w_main = place(w_main, (2 * local, width), (2 * local, k_half), (0, 2 * (f ^ m) + (c ^ rc)), items)
+    others = range(1, groups)
+    w_main = place_main(w_main, [second_2, got_b2], others, 0)
+    w_main = place_main(w_main, [sibling_b, sibling_b2], others, 1)
     extra_items = []
     for m in range(groups):
         for rc in range(2):
             extra_items.append((extra_pair[rc], m, 0, k_rows * (f ^ m) + k_half * (c ^ rc), EXTRA, (0, EXTRA)))
     w_extra = place(None, (EXTRA, width), (EXTRA, width), (0, 0), extra_items)
 
-    out_low = w_out.astype(BF16).reshape(groups, unit, out_cols)
-    blocks = [lax.dynamic_index_in_dim(out_low, f ^ m, 0, keepdims=False) for m in range(groups)]
-    blocks = jnp.concatenate([blocks[0]] + [swap(blocks[m], "fsdp", m) for m in range(1, groups)])
-    out_1 = then(blocks[None], w_main)
-    out_2 = jnp.concatenate([out_1, swap(out_1, "dp", 2 * z_masks[0])])
-    out_got = swap(out_2, "dp", 2 * z_masks[1])
-    out_spread = jnp.concatenate([out_2, out_got])
-    out_items = []
-    for rc, array in enumerate((out_spread, swap(out_spread, "dp", 1))):
-        for i, rel in enumerate(order_z):
-            col = out_cols * (2 * (z ^ rel) + (c ^ rc))
-            for m in range(groups):
-                out_items.append((array, i, unit * (f ^ m) - unit * m, col, local, (unit * m, unit * (m + 1))))
-    w_out_own = place(None, (local, width), (local, width), (0, 0), out_items)
-    up_near_2 = neighbours(then(cotangent[0], w_main), 1)
-    up_far = corners([then(v, w_main) for v in up_near])
-
-    extra = dot_nt(normed_all, w_extra)
-    main = dot_nt(then(normed_all, extra), w_main)
-    raw_dt = extra[:, 2 * NS :].reshape(-1, groups, groups, NH // groups // groups)
-    dt_rows = lax.dynamic_index_in_dim(raw_dt, f, 2, keepdims=False).reshape(groups * length, -1).T
+    out_1 = then(out_cat[None], got_b2)
+    out_got = swap(out_1, "dp", 2 * z_masks[0])
+
+    w_dt = w_extra[2 * NS :].reshape(groups, groups, -1, width)
+    w_dt = lax.dynamic_index_in_dim(w_dt, f, 1, keepdims=False).reshape(-1, width)
+    w_own = jnp.concatenate([w_extra[: 2 * NS], w_dt, jnp.zeros((128 - w_dt.shape[0], width), BF16)])
+    extra = matmul(normed_all, w_own, "nt", F32)
+    dt_rows = extra[:, 2 * NS : 2 * NS + w_dt.shape[0]].T
+    main = matmul(then(normed_all, extra), w_main, "nt", F32)
     common = (
         main, extra, dt_rows,
         own_channels(convw_full[:, :DI]), own_channels(convb_full[:, :DI]), convw_full[:, DI:], convb_full[:, DI:],
         own_channels(shift_full).T, own_channels(logd_full).T, own_channels(jnp.repeat(skip_full, HP, axis=1)),
     )
-    due = [[out_2, *up_near_2], [out_spread, *up_far]]
-    up_pieces = pieces_of(up_near, up_near_2, up_far)
     half_rows = groups // 2
-    results = []
-    for i in range(2):
-        begin = then(starts[i * half_rows : (i + 1) * half_rows], *due[i], *[v[3] for v in results])
-        results.append(mix_forward(i * half_rows, length, begin, *common))
+    out_2 = jnp.concatenate([out_1, then(out_got, main)])
+    out_got = swap(out_2, "dp", 2 * z_masks[1])
+    results = [mix_forward(0, length, then(starts[:half_rows], out_2), *common)]
+    out_4 = jnp.concatenate([out_2, then(out_got, results[0][3])])
+    out_sibling = swap(out_4, "dp", 1)
+    results.append(mix_forward(half_rows, length, then(starts[half_rows:], out_4), *common))
+    out_sibling = then(out_sibling, results[1][3])
     gated, y, states, squares = zip(*results)
+    out_items = []
+    for rc, array in enumerate((out_4, out_sibling)):
+        for i, rel in enumerate(order_z):
+            out_items.append((array, i, 0, out_cols * (2 * (z ^ rel) + (c ^ rc)), local, (0, local)))
+    w_out_own = place(None, (local, width), (local, width), (0, 0), out_items)
     gain = own_channels(gate_full)
 
     def group_sum(v):
-        for mask in bits_of(groups):
-            got = swap(v, "fsdp", mask)
-            v = v + jnp.stack([got[r ^ mask] for r in range(groups)])
+        return v, [swap(v, "fsdp", m) for m in range(1, groups)]
+
+    def summed(parts, *late):
+        v, got = parts
+        for other in got:
+            v = v + then(other, *late)
         return v
 
     squares = group_sum(jnp.concatenate(squares).reshape(groups, length))
+    squares = summed(squares, w_out_own)
     q = lax.rsqrt(squares.reshape(-1, 1) * (1.0 / DI) + EPSILON)
     mixed = jnp.concatenate(
         [(g * q[i * half_rows * length : (i + 1) * half_rows * length] * gain).astype(BF16) for i, g in enumerate(gated)]
     )
-    upstream_all = None
-    for m in range(groups):
-        upstream_all = rows_into(upstream_all, m, groups, [cotangent[0]] if m == 0 else up_pieces[m - 1])
-    mixed_live = mixed * live_all.astype(BF16)
-    d_mixed = (dot_nt(upstream_all, w_out_own) * live_all).astype(BF16)
-    inner = jnp.sum(mixed.astype(F32) * d_mixed.astype(F32), axis=1).reshape(groups, length)
-    mean = q * q * group_sum(inner).reshape(-1, 1) * (1.0 / DI)
+    d_mixed, inner = mixed_gradient(upstream_all, w_out_own, live_all, mixed)
+    inner = group_sum(inner.reshape(groups, length))
+    out_full = matmul(then(mixed, inner[0]), upstream_all, "tn", scale=live_all.astype(BF16))
+    branch = matmul(then(mixed, out_full), w_out_own, "nn")
+    mean = q * q * summed(inner, out_full).reshape(-1, 1) * (1.0 / DI)
 
     def sum_low(a, b):
         return (a.astype(F32) + b.astype(F32)).astype(BF16)
 
-    def rows_home(partial):
-        pieces, sent = [], []
-        for at, (one, two) in ((0, (1, 2)), (half, (2, 1))):
-            rows = [partial[m * length + at : m * length + at + half] for m in range(groups)]
-            got = swap(jnp.concatenate([rows[one], rows[3]]), "fsdp", one)
-            passed = sum_low(rows[two], got[half:])
-            sent.append(passed)
-            pieces.append((rows[0], got[:half], swap(passed, "fsdp", two)))
-        return pieces, sent
-
-    def added(pieces):
-        return jnp.concatenate([a.astype(F32) + b.astype(F32) + c.astype(F32) for a, b, c in pieces])
-
     contract = (((0,), (0,)), ((), ()))
 
-    def sum_rows(a, b):
-        return with_layout_constraint(
-            lax.dot_general(a, b, contract, preferred_element_type=F32).astype(BF16), Layout((0, 1))
-        )
-
-
-    def out_columns(core):
-        cols = [lax.dynamic_slice_in_dim(upstream_all, out_cols * (2 * i + core), out_cols, 1) for i in range(zs)]
-        return jnp.concatenate(cols, axis=1)
-
-    out_theirs = swap(sum_rows(mixed_live, out_columns(1 - c)), "dp", 1)
-    out_ours = sum_rows(mixed_live, out_columns(c))
-    branch_home, branch_sent = rows_home(dot(then(mixed, mean), w_out_own).astype(BF16))
-    out_sum = sum_low(out_ours, out_theirs)
-    flying = [lax.dynamic_slice_in_dim(out_sum, out_cols * (z ^ r), out_cols, 1) for r in range(zs)]
+
+    out_own = lax.psum_scatter(out_full, "dp", scatter_dimension=1, tiled=True)
+    d_mixed = then(d_mixed, branch)
+    branch = lax.psum_scatter(branch, "fsdp", scatter_dimension=0, tiled=True)
     d_main, backs = None, []
-    operand = d_mixed
     for i in range(2):
-        if i < len(z_masks):
-            mask = z_masks[-1 - i]
-            sent = jnp.stack(flying[1::2])
-            operand = then(d_mixed, sent, *([] if i == 0 else branch_sent))
-            got = swap(sent, "dp", 2 * mask)
-            keep = flying[0::2]
         begin = starts[i * half_rows : (i + 1) * half_rows]
+        operand = d_mixed
+        if i == 1:
+            own = then(out_own, d_main)
+            out_rows = [lax.dynamic_slice_in_dim(own, unit * (f ^ m), unit, 0) for m in range(groups)]
+            operand = then(d_mixed, *out_rows)
+            out_parts = [swap(out_rows[m], "fsdp", m) for m in range(1, groups)]
         result = mix_backward(
             i * half_rows, groups, length, d_main, begin, *common, gain, y[i], states[i], q, mean, operand
         )
         d_main = result[0]
-        if i < len(z_masks):
-            got = then(got, d_main)
-            flying = [sum_low(k, got[j]) for j, k in enumerate(keep)]
         backs.append(result[1:])
-    for mask in z_masks[::-1][2:]:
-        got = swap(jnp.stack(flying[1::2]), "dp", 2 * mask)
-        flying = [sum_low(k, got[j]) for j, k in enumerate(flying[0::2])]
-    out_rows = [lax.dynamic_slice_in_dim(flying[0], unit * (f ^ m), unit, 0) for m in range(groups)]
-    out_parts = jnp.stack([out_rows[0]] + [swap(out_rows[m], "fsdp", m) for m in range(1, groups)])
     d_bc_in = jnp.concatenate([b[0] for b in backs])
     d_dt = jnp.concatenate([b[1] for b in backs], axis=1)
     s_gain, s_cw, s_cb, s_cwbc, s_cbbc, s_shift, s_logd, s_skip = [
@@ -945,62 +1025,77 @@
 
     bundles = [(groups - 2, groups - 1), (0, 1)]
 
-    def bundle_sum(source, bundle, rc):
-        block = [lax.dynamic_slice_in_dim(normed_all, k_rows * (f ^ m) + k_half * (c ^ rc), k_half, 1) for m in bundle]
-        return sum_rows(source, jnp.concatenate(block, axis=1))
-
-    def chip_blocks(ours, got):
+    def bundle_columns(value, bundle, core):
+        return [lax.dynamic_slice_in_dim(value, k_rows * (f ^ m) + k_half * core, k_half, 1) for m in bundle]
+
+    def chip_blocks(bundle, got):
         blocks = []
         for r in range(zs):
             row = slice_row(first_row(z ^ r))
-            blocks.append(sum_low(*[lax.dynamic_slice_in_dim(v, row, most, 0) for v in (ours, got)]))
+            ours = [lax.dynamic_slice(main_sum, (row, k_rows * (f ^ m) + k_half * c), (most, k_half)) for m in bundle]
+            theirs = lax.dynamic_slice_in_dim(got, row, most, 0)
+            blocks.append(sum_low(jnp.concatenate(ours, axis=1), theirs))
         return blocks
 
-    def send_z(blocks, mask):
-        sent = jnp.stack(blocks[1::2])
-        return blocks[0::2], swap(sent, "dp", 2 * mask), sent
-
-    def add_z(flying):
-        keep, got, _ = flying
-        return [sum_low(k, got[i]) for i, k in enumerate(keep)]
-
-    extra_sum = sum_rows(d_extra, normed_all)
-    halves_e = extra_sum.reshape(EXTRA, groups, 2, k_half)
-    extra_theirs = swap(lax.dynamic_index_in_dim(halves_e, 1 - c, 2, keepdims=False), "dp", 1)
-    extra_ours = lax.dynamic_index_in_dim(halves_e, c, 2, keepdims=False)
-    theirs_a = bundle_sum(then(d_main, extra_sum), bundles[0], 1)
-    got_a = swap(theirs_a, "dp", 1)
-    ours_a = bundle_sum(then(d_main, theirs_a), bundles[0], 0)
-    both = then(extra_ours.astype(F32) + extra_theirs.astype(F32), ours_a)
-    flying_a = send_z(chip_blocks(ours_a, got_a), z_masks[-1])
-    theirs_b = bundle_sum(then(d_main, flying_a[2]), bundles[1], 1)
-    got_b = swap(theirs_b, "dp", 1)
-    ours_b = bundle_sum(then(d_main, theirs_b), bundles[1], 0)
-    total = lax.dynamic_index_in_dim(both, f, 1, keepdims=False)
-    for m in range(1, groups):
-        total = total + swap(
-            lax.dynamic_index_in_dim(both, f ^ m, 1, keepdims=False).astype(BF16), "fsdp", m
-        ).astype(F32)
-    total = then(total.astype(BF16), ours_b)
-    flying_b = send_z([then(v, total) for v in chip_blocks(ours_b, got_b)], z_masks[-1])
-    partial = (dot(then(d_main, flying_b[2]), w_main) + dot(d_extra, w_extra)).astype(BF16)
-    d_normed_home, d_normed_sent = rows_home(partial)
-    held = [partial, *[v for piece in branch_home for v in piece]]
-    flying_a = send_z([then(v, *held) for v in add_z(flying_a)], z_masks[0])
-    total = sum_low(total, swap(then(total, flying_a[2]), "dp", 2 * z_masks[-1]))
-    flying_b = send_z([then(v, flying_a[2]) for v in add_z(flying_b)], z_masks[0])
-    total = sum_low(total, swap(then(total, flying_b[2]), "dp", 2 * z_masks[0]))
-    flying_a = (flying_a[0], then(flying_a[1], flying_b[2]), None)
-    flying_b = (flying_b[0], then(flying_b[1], *d_normed_sent), None)
+    main_sum = matmul(then(d_main, *out_parts), normed_all, "tn")
+    out_parts = jnp.stack(out_rows[:1] + out_parts)
+    got_a = swap(jnp.concatenate(bundle_columns(main_sum, bundles[0], 1 - c), axis=1), "dp", 1)
+    got_b = swap(jnp.concatenate(bundle_columns(main_sum, bundles[1], 1 - c), axis=1), "dp", 1)
+    extra_sum = lax.dot_general(then(d_extra, main_sum), normed_all, contract, preferred_element_type=F32).astype(BF16)
+    extra_sum = with_layout_constraint(extra_sum, Layout((0, 1)))
+    halves_e = [jnp.stack(bundle_columns(extra_sum, range(groups), core)) for core in (c, 1 - c)]
+    extra_theirs = swap(halves_e[1], "dp", 1)
+    blocks_a = chip_blocks(bundles[0], then(got_a, extra_sum))
+    blocks_b = chip_blocks(bundles[1], then(got_b, extra_sum))
+    both = halves_e[0].astype(F32) + extra_theirs.astype(F32)
+    total, both_low = both[0], both.astype(BF16)
+    arriving = [swap(both_low[m], "fsdp", m) for m in range(1, groups)]
+    sent_a, sent_b = jnp.stack(blocks_a[1::2]), jnp.stack(blocks_b[1::2])
+    flying_a = swap(sent_a, "dp", 2 * z_masks[-1])
+    flying_b = swap(sent_b, "dp", 2 * z_masks[-1])
+    source = then(d_main, sent_a, sent_b, both_low, branch, *blocks_a[0::2], *blocks_b[0::2])
+    middle = width // 2
+
+    def to_normed(source, cols):
+        return (dot(source, w_main[:, cols]) + dot(d_extra, w_extra[:, cols])).astype(BF16)
+
+    partial = to_normed(source, slice(0, middle))
+    d_normed = [lax.psum_scatter(partial, "fsdp", scatter_dimension=0, tiled=True)]
+    flying_a = then(flying_a, partial)
+    keep_a, sent_a = [sum_low(k, flying_a[i]) for i, k in enumerate(blocks_a[0::2])]
+    flying_a = swap(sent_a, "dp", 2 * z_masks[0])
+    partial = to_normed(then(d_main, keep_a, sent_a), slice(middle, width))
+    d_normed.append(lax.psum_scatter(partial, "fsdp", scatter_dimension=0, tiled=True))
+    flying_b, flying_a, _ = lax.optimization_barrier((flying_b, flying_a, partial))
+    keep_b, sent_b = [sum_low(k, flying_b[i]) for i, k in enumerate(blocks_b[0::2])]
+    done_a = sum_low(keep_a, flying_a)
+    flying_b = swap(sent_b, "dp", 2 * z_masks[0])
+    d_normed = jnp.concatenate(d_normed, axis=1).astype(F32)
+
+    hidden = tokens[0].astype(F32)
+    live = (jnp.arange(length, dtype=jnp.int32) < valid_len[0]).astype(F32)[:, None]
+    scale = lax.rsqrt(jnp.mean(hidden * hidden, axis=-1, keepdims=True) + EPSILON)
+    weighted = norm_full * d_normed
+    average = jnp.mean(hidden * weighted, axis=-1, keepdims=True)
+    grad_tokens = cotangent[0].astype(F32) + scale * weighted - hidden * (scale * scale * scale * average)
+    s_norm = jnp.sum(hidden * scale * d_normed, axis=0)
+    for got in arriving:
+        total = total + then(got, sent_b).astype(F32)
+    total = total.astype(BF16)
+    total = sum_low(total, swap(total, "dp", 2 * z_masks[-1]))
+    total = sum_low(total, swap(total, "dp", 2 * z_masks[0]))
+    out_parts = then(out_parts, sent_b)
+    s_gain, s_cw, s_cb, s_cwbc, s_cbbc, s_shift, s_logd, s_skip = [
+        then(v, sent_b) for v in (s_gain, s_cw, s_cb, s_cwbc, s_cbbc, s_shift, s_logd, s_skip)
+    ]
+    done_b = sum_low(keep_b, then(flying_b, s_norm))
     recv = [None] * groups
-    for flying, bundle in ((flying_a, bundles[0]), (flying_b, bundles[1])):
-        block = add_z(flying)[0]
+    for block, bundle in ((done_a, bundles[0]), (done_b, bundles[1])):
         for i, m in enumerate(bundle):
             piece = block[:, i * k_half : (i + 1) * k_half]
             recv[m] = piece if m == 0 else swap(piece, "fsdp", m)
 
 
-    out_parts = then(out_parts, flying_a[1])
     grad_out = jnp.concatenate(
         [lax.dynamic_index_in_dim(out_parts, f ^ g, 0, keepdims=False) for g in range(groups)]
     ).astype(F32)
@@ -1011,13 +1106,7 @@
     got = swap(jnp.where(c == 0, right, left), "dp", 1)
     grad_in = jnp.concatenate([jnp.where(c == 0, own, got), jnp.where(c == 0, got, own)]).astype(F32)
 
-    out_tokens = (hidden + added(branch_home) * live).astype(BF16)
-    d_normed = added(d_normed_home)
-    scale = lax.rsqrt(jnp.mean(hidden * hidden, axis=-1, keepdims=True) + EPSILON)
-    weighted = norm_full * d_normed
-    average = jnp.mean(hidden * weighted, axis=-1, keepdims=True)
-    grad_tokens = upstream + scale * weighted - hidden * (scale * scale * scale * average)
-    s_norm = jnp.sum(hidden * scale * d_normed, axis=0)
+    out_tokens = (hidden + branch.astype(F32) * live).astype(BF16)
 
     small_sums = (
         s_norm[None],

time: 860 us -> 692 us (0.80); the launches traced: 843 us -> 684 us
  matrix products: 151 us -> 51.3 us
  Pallas kernels: 168 us -> 263 us
  local copies, waits for them, and re-layouts: 123 us -> 62.3 us
  waiting for transfers between devices: 208 us -> 157 us
  other arithmetic: 104 us -> 70.5 us
  starting transfers between devices: 81.8 us -> 60.1 us
  between operations: 6.4 us -> 19.6 us
    pallas_call x10 -> x13, Pallas kernels: 48.5 us -> 170 us  [the longest x5 87 us: matmul(): pl.pallas_call(kernel, grid=(m // tm, n // tn), in_specs=in_specs, out_sp...]
    ppermute x76 -> x52, waiting for transfers between devices: 208 us -> 144 us  [swap(): return lax.ppermute(value, axis, [(i, i ^ mask) for i in range(size)])]
    dot_general x7 -> x1, matrix products: 56.7 us -> 2.91 us  [grouped(): lax.dot_general(then(d_extra, main_sum), normed_all, contract, preferred_...]
    dot_general x4 -> x1, matrix products: 45.6 us -> 4.4 us  [dot_nt(): lax.dot_general(a, b, (((1,), (1,)), ((), ())), preferred_element_type=F32)]
    unnamed x282 -> x214, local copies, waits for them, and re-layouts: 56.5 us -> 24.4 us
    ppermute x76 -> x52, starting transfers between devices: 81.8 us -> 59.5 us  [swap(): return lax.ppermute(value, axis, [(i, i ^ mask) for i in range(size)])]
    pallas_call x10 -> x2, Pallas kernels: 26.7 us -> 9.16 us  [place(): pl.pallas_call(kernel, grid_spec=pltpu.PrefetchScalarGridSpec(num_scalar_...]
    reduce_scatter x0 -> x4, waiting for transfers between devices: none -> 12.3 us  [the longest x2 12.3 us: grouped(): lax.psum_scatter(partial, 'fsdp', scatter_dimension=0, tiled=True)]
  transfers between devices with their start and end apart: 76 -> 58, of which waited for: 18 -> 14; matrix products, arithmetic and copies ran while one was open for 36% -> 20% of each run, Pallas kernels for 17% -> 34%
where the time goes in v3:
time: 692 us; the launch traced here: 684 us
  Pallas kernels  263 us (38%)
  waiting for transfers between devices  157 us (23%)
  other arithmetic  70.5 us (10%)
  local copies, waits for them, and re-layouts  62.3 us (9%)
  starting transfers between devices  60.1 us (9%)
  matrix products  51.3 us (7%)
  between operations  19.6 us (3%)
    ppermute x52, waiting for transfers between devices, swap(): return lax.ppermute(value, axis, [(i, i ^ mask) for i in range(size)])  144 us
    pallas_call x5, Pallas kernels, matmul(): pl.pallas_call(kernel, grid=(m // tm, n // tn), in_specs=in_specs, out_sp...  87 us
    pallas_call x2, Pallas kernels, mix_backward(): pl.pallas_call(backward_first if before is None else backward_kernel, gri...  83.7 us
    ppermute x52, starting transfers between devices, swap(): return lax.ppermute(value, axis, [(i, i ^ mask) for i in range(size)])  59.5 us
    dot_general x4, matrix products, dot(): return jnp.dot(a, b, preferred_element_type=F32)  37.8 us
    pallas_call x2, Pallas kernels, mix_forward(): pl.pallas_call(forward_kernel, grid=(rows, channels // BC), in_specs=in_s...  36.2 us
    unnamed x214, local copies, waits for them, and re-layouts  24.4 us
    pallas_call x4, Pallas kernels, place_blocks(): pl.pallas_call(kernel, grid_spec=pltpu.PrefetchScalarGridSpec(num_scalar_...  17.2 us
  transfers between devices with their start and end apart: 58, of which 14 were waited for; matrix products, arithmetic and copies ran while one was open for 20% of the time, Pallas kernels for 34%

profile of v3, /device:TPU:0, one launch (start us, length us, event | category | flops | bytes accessed | tf_op | source)
XLA Modules:
  0.0 683.9 jit_solution(9617908107400023939)
XLA Ops:
  8.0 1.8 convert_element_type.365
  20.4 3.5 collective-permute-start.2
  24.6 4.4 fusion.18
  29.2 2.0 collective-permute-start.4
  33.0 3.0 collective-permute-start.7
  36.4 15.0 %collective-permute-done.4 = bf16[848,256]{1,0:T(8,128)(2,1)S(1)} collective-permute-done((bf16[848,256]{1,0:T(8,128)(2,1)S(1)}, bf16[848,256]{1,0:T(8,128)(2,1)S(1)}, u32[]{:S(2)}, u32[]{:S(2)}) %collective-permute-start.4) | collective-permute-done | bytes 434208 | tf_op jit(solution)/shard_map/ppermute | solution.py:593
  51.4 2.4 collective-permute-done.5
  53.8 13.7 %collective-permute-done.6 = bf16[848,256]{1,0:T(8,128)(2,1)S(1)} collective-permute-done((bf16[848,256]{1,0:T(8,128)(2,1)S(1)}, bf16[848,256]{1,0:T(8,128)(2,1)S(1)}, u32[]{:S(2)}, u32[]{:S(2)}) %collective-permute-start.6) | collective-permute-done | bytes 434208 | tf_op jit(solution)/shard_map/ppermute | solution.py:593
  68.5 2.5 collective-permute-start.8
  74.5 36.5 %collective-permute-done.8 = bf16[1,1776,256]{2,1,0:T(8,128)(2,1)} collective-permute-done((bf16[1,1776,256]{2,1,0:T(8,128)(2,1)S(1)}, bf16[1,1776,256]{2,1,0:T(8,128)(2,1)}, u32[]{:S(2)}, u32[]{:S(2)}) %collective-permute-start.8) | collective-permute-done | bytes 909344 | tf_op jit(solution)/shard_map/ppermute | solution.py:593
  110.9 2.6 pad_maximum_fusion.5.refs_0_
  125.7 3.1 place_blocks.4.refs_1_
  131.6 3.4 place_blocks.5.refs_2_
  135.0 13.5 %rows_into.1.refs_0_.refs_1_ = bf16[2048,2048]{1,0:T(8,128)(2,1)} custom-call(bf16[2048,2048]{1,0:T(8,128)(2,1)} %bitcast.290, f32[1,2048]{1,0:T(1,128)} %bitcast.309), custom_call_target="tpu_custom_call" | custom-call | tf_op jit(solution)/shard_map/rows_into/pallas_call | solution.py:772
  148.5 9.4 %collective-permute-done.10.refs_1_ = bf16[2,1776,256]{2,1,0:T(8,128)(2,1)} collective-permute-done((bf16[2,1776,256]{2,1,0:T(8,128)(2,1)}, bf16[2,1776,256]{2,1,0:T(8,128)(2,1)}, u32[]{:S(2)}, u32[]{:S(2)}) %collective-permute-start.10) | collective-permute-done | bytes 1818656 | tf_op jit(solution)/shard_map/ppermute | solution.py:593
  160.7 3.7 place.2
  167.1 8.6 %matmul_nt.2.bc_ref.refs_3_ = f32[2048,384]{1,0:T(8,128)} custom-call(bf16[2048,2048]{1,0:T(8,128)(2,1)} %rows_into.1.refs_0_.refs_1_, bf16[384,2048]{1,0:T(8,128)(2,1)} %maximum_maximum_fusion.refs_1_), custom_call_target="tpu_custom_call" | custom-call | flops 3221225472 | bytes 11534336 | tf_op jit(solution)/shard_map/matmul_nt/pallas_call | solution.py:698
  177.2 5.3 place_blocks.6.refs_2_
  182.5 2.2 collective-permute-start.12
  184.7 2.1 constant_dynamic-update-slice_fusion.1
  186.8 5.3 place_blocks.7.refs_1_
  192.2 25.2 %matmul_nt.3.gate_ref.xin_ref.refs_1_.refs_2_ = f32[2048,2048]{1,0:T(8,128)} custom-call(bf16[2048,2048]{1,0:T(8,128)(2,1)} %rows_into.1.refs_0_.refs_1_, bf16[2048,2048]{1,0:T(8,128)(2,1)} %place_blocks.7.refs_1_), custom_call_target="tpu_custom_call" | custom-call | flops 17179869184 | bytes 25165824 | tf_op jit(solution)/shard_map/matmul_nt/pallas_call | solution.py:698
  219.9 18.0 %mix_forward.2 = (f32[1024,1024]{1,0:T(8,128)}, f32[1024,1024]{1,0:T(8,128)}, bf16[2,4,128,1024]{3,2,1,0:T(8,128)(2,1)S(1)}, f32[1024,1]{1,0:T(8,128)S(1)}) custom-call(s32[2,4]{1,0:T(2,128)S(1)} %get-tuple-element.118.starts_ref.refs_0_, f32[2048,2048]{1,0:T(8,128)} %matmul_nt.3.gate_ref.xin_ref.refs_1_.refs_2_, ...), custom_call_target="tpu_custom_call" | custom-call | flops 18874368000 | bytes 12582912 | tf_op jit(solution)/shard_map/mix_forward/pallas_call | solution.py:434
  240.0 3.4 collective-permute-done.19
  245.7 18.2 %mix_forward.3 = (f32[1024,1024]{1,0:T(8,128)}, f32[1024,1024]{1,0:T(8,128)}, bf16[2,4,128,1024]{3,2,1,0:T(8,128)(2,1)S(1)}, f32[1024,1]{1,0:T(8,128)S(1)}) custom-call(s32[2,4]{1,0:T(2,128)S(1)} %get-tuple-element.122.starts_ref.refs_0_, f32[2048,2048]{1,0:T(8,128)} %matmul_nt.3.gate_ref.xin_ref.refs_1_.refs_2_, ...), custom_call_target="tpu_custom_call" | custom-call | flops 18874368000 | bytes 12582912 | tf_op jit(solution)/shard_map/mix_forward/pallas_call | solution.py:434
  273.3 5.5 place.3.w_ref.refs_1_
  278.8 4.0 multiply_convert_fusion.1
  282.8 2.5 pad_maximum_fusion.mixed_ref.refs_0_
  285.3 15.8 %mixed_gradient.1 = (bf16[2048,1024]{1,0:T(8,128)(2,1)}, f32[2048,1]{1,0:T(8,128)}) custom-call(bf16[2048,2048]{1,0:T(8,128)(2,1)} %bitcast.288, bf16[1024,2048]{1,0:T(8,128)(2,1)} %place.3.w_ref.refs_1_, f32[2048,1]{1,0:T(8,128)} %copy.184.live_ref, bf16[2048,1024]{1,0:T(8,128)(2,1)} %pad_maximum_fusion.mixed_ref.refs_0_), custom_call_target="tpu_custom_call" | custom-call | tf_op jit(solution)/shard_map/mixed_gradient/pallas_call | solution.py:728
  302.7 13.9 %matmul_tn.2 = bf16[1024,2048]{1,0:T(8,128)(2,1)} custom-call(bf16[2048,1024]{1,0:T(8,128)(2,1)} %pad_maximum_fusion.mixed_ref.refs_0_, bf16[2048,2048]{1,0:T(8,128)(2,1)} %bitcast.289, bf16[2048,1]{1,0:T(8,128)(2,1)} %copy.185.refs_2_), custom_call_target="tpu_custom_call" | custom-call | flops 8589934592 | bytes 16777216 | tf_op jit(solution)/shard_map/matmul_tn/pallas_call | solution.py:698
  316.6 14.8 %matmul_nn.1 = bf16[2048,2048]{1,0:T(8,128)(2,1)} custom-call(bf16[2048,1024]{1,0:T(8,128)(2,1)} %pad_maximum_fusion.mixed_ref.refs_0_, bf16[1024,2048]{1,0:T(8,128)(2,1)} %place.3.w_ref.refs_1_), custom_call_target="tpu_custom_call" | custom-call | flops 8589934592 | bytes 16777216 | tf_op jit(solution)/shard_map/matmul_nn/pallas_call | solution.py:698
  341.1 41.8 %mix_backward.2 = (bf16[2048,2048]{1,0:T(8,128)(2,1)}, bf16[1024,256]{1,0:T(8,128)(2,1)S(1)}, f32[16,1024]{1,0:T(8,128)S(1)}, f32[2,1,1024]{2,1,0:T(1,128)S(1)},...) custom-call(s32[2,4]{1,0:T(2,128)S(1)} %get-tuple-element.118.starts, ...), custom_call_target="tpu_custom_call" | custom-call | flops 44040192000 | bytes 12582912 | tf_op jit(solution)/shard_map/mix_backward/pallas_call | solution.py:510
  382.9 1.9 constant_dynamic-slice_fusion.7
  394.0 42.0 %mix_backward.3 = (bf16[2048,2048]{1,0:T(8,128)(2,1)}, bf16[1024,256]{1,0:T(8,128)(2,1)S(1)}, f32[16,1024]{1,0:T(8,128)S(1)}, f32[2,1,1024]{2,1,0:T(1,128)S(1)},...) custom-call(s32[2,4]{1,0:T(2,128)S(1)} %copy-done.22, ...), custom_call_target="tpu_custom_call", output_to_operand_aliasing={{0}: (18, {})} | custom-call | flops 44040192000 | bytes 12582912 | tf_op jit(solution)/shard_map/mix_backward/pallas_call | solution.py:510
  438.6 24.5 %matmul_tn.3 = bf16[2048,2048]{1,0:T(8,128)(2,1)} custom-call(bf16[2048,2048]{1,0:T(8,128)(2,1)} %get-tuple-element.155.refs_0_, bf16[2048,2048]{1,0:T(8,128)(2,1)} %rows_into.1.refs_0_.refs_1_), custom_call_target="tpu_custom_call" | custom-call | flops 17179869184 | bytes 25165824 | tf_op jit(solution)/shard_map/matmul_tn/pallas_call | solution.py:698
  463.0 2.7 constant_dynamic-slice_fusion.4
  468.1 2.9 convolution_convert_fusion
  472.3 5.6 fusion.40
  477.9 3.5 fusion.85
  482.9 2.0 add_convert_fusion.6
  486.0 2.0 add_convert_fusion.4
  489.1 15.9 %add_convert_fusion.1 = bf16[2048,1024]{1,0:T(8,128)(2,1)} fusion(f32[2048,1024]{1,0:T(8,128)} %fusion.40, bf16[2048,2048]{1,0:T(8,128)(2,1)} %get-tuple-element.155.refs_0_, bf16[2048,2048]{1,0:T(8,128)(2,1)} %place_blocks.7.refs_1_), kind=kOutput, calls=%fused_computation.7 | convolution fusion | flops 8594128896 | bytes 25165824 | tf_op jit(solution)/shard_map/dot_general | solution.py:37
  505.1 2.5 collective-permute-start.33
  507.5 2.4 fusion.38
  509.9 24.3 %collective-permute-done.33 = bf16[2,592,512]{2,1,0:T(8,128)(2,1)S(1)} collective-permute-done((bf16[2,592,512]{2,1,0:T(8,128)(2,1)}, bf16[2,592,512]{2,1,0:T(8,128)(2,1)S(1)}, u32[]{:S(2)}, u32[]{:S(2)}) %collective-permute-start.33) | collective-permute-done | bytes 1212448 | tf_op jit(solution)/shard_map/ppermute | solution.py:593
  535.3 14.0 %add_convert_fusion = bf16[2048,1024]{1,0:T(8,128)(2,1)} fusion(f32[2048,1024]{1,0:T(8,128)S(1)} %fusion.38, bf16[2048,2048]{1,0:T(8,128)(2,1)} %get-tuple-element.155.refs_0_, bf16[2048,2048]{1,0:T(8,128)(2,1)} %place_blocks.7.refs_1_), kind=kOutput, calls=%fused_computation.6 | convolution fusion | flops 8594128896 | bytes 25165824 | tf_op jit(solution)/shard_map/dot_general | solution.py:37
  551.8 1.8 collective-permute-start.34
  557.1 2.0 pad_maximum_fusion.14
  559.1 1.9 slice_bitcast_fusion.3
  562.0 1.6 collective-permute-start.42
  564.4 28.4 %collective-permute-done.34 = bf16[2,592,512]{2,1,0:T(8,128)(2,1)} collective-permute-done((bf16[2,592,512]{2,1,0:T(8,128)(2,1)}, bf16[2,592,512]{2,1,0:T(8,128)(2,1)}, u32[]{:S(2)}, u32[]{:S(2)}) %collective-permute-start.34) | collective-permute-done | bytes 1212448 | tf_op jit(solution)/shard_map/ppermute | solution.py:593
  592.9 2.0 fusion.27
  594.9 2.3 collective-permute-start.36
  609.5 2.3 multiply_subtract_fusion.1
  612.4 12.3 %reduce-scatter.11.cloned.1.call-done = bf16[512,1024]{1,0:T(8,128)(2,1)} async-done(((bf16[2048,1024]{1,0:T(8,128)(2,1)}), bf16[512,1024]{1,0:T(8,128)(2,1)}) %reduce-scatter.11.cloned.1.call-update) | async-done | bytes 1048592 | tf_op jit(solution)/shard_map/reduce_scatter | solution.py:1068
  624.7 5.4 fusion.8
  631.2 2.7 collective-permute-start.46
  635.4 1.7 add_convert_fusion.3
  637.1 3.3 collective-permute-start.44
  642.0 6.5 collective-permute-done.49
  649.3 1.7 collective-permute-start.37
  652.7 3.0 fusion.12
  660.5 6.3 fusion.17
  671.2 5.6 multiply_subtract_fusion
  (544 shorter events, 120.9 us)
Async XLA Ops:
  7.2 127.8 %all-gather.5.cloned.1.call-start = ((), (), s32[]{:S(2)}) async-start(), calls=%async_computation.8 | async-start | bytes 10485760 | tf_op jit(solution)/shard_map/all_gather | solution.py:882
  7.9 277.3 %all-gather.7.cloned.1.call-start = ((), (), s32[]{:S(2)}) async-start(), calls=%async_computation.9 | async-start | bytes 10485760 | tf_op jit(solution)/shard_map/all_gather | solution.py:883
  10.7 9.5 %collective-permute-start.3 = (bf16[256,1064]{0,1:T(8,128)(2,1)}, bf16[256,1064]{0,1:T(8,128)(2,1)S(1)}, u32[]{:S(2)}, u32[]{:S(2)}) collective-permute-start(bf16[256,1064]{0,1:T(8,128)(2,1)} %constant_dynamic-slice_fusion.17), channel_id=1, source_target_pairs={{0,4},{4,0},{8,12},{12,8},{16,20},{20,16},{24,28},{28,24},{1,5},{5... | collective-permute-start | bytes 1634312 | tf_op jit(solution)/shard_map/ppermute | solution.py:593
  11.2 371.7 %reduce-scatter.7.cloned.1.call-start = ((), (), s32[]{:S(2)}) async-start(), calls=%async_computation.5 | async-start | bytes 4718592 | tf_op jit(solution)/shard_map/reduce_scatter | solution.py:996
  20.4 12.4 %collective-permute-start.2 = (bf16[1,7034]{1,0:T(2,128)(2,1)S(1)}, bf16[1,7034]{1,0:T(2,128)(2,1)S(1)}, u32[]{:S(2)}, u32[]{:S(2)}) collective-permute-start(bf16[1,7034]{1,0:T(2,128)(2,1)S(1)} %broadcast_in_dim.43), channel_id=1, source_target_pairs={{0,3},{1,2},{2,1},{3,0},{4,7},{5,6},{6,5},{7,4},{8,11},{9,10},{10,... | collective-permute-start | bytes 42212 | tf_op jit(solution)/shard_map/ppermute | solution.py:593
  23.9 9.1 %collective-permute-start.1 = (bf16[1,7034]{1,0:T(2,128)(2,1)S(1)}, bf16[1,7034]{1,0:T(2,128)(2,1)S(1)}, u32[]{:S(2)}, u32[]{:S(2)}) collective-permute-start(bf16[1,7034]{1,0:T(2,128)(2,1)S(1)} %broadcast_in_dim.43), channel_id=1, source_target_pairs={{0,2},{1,3},{2,0},{3,1},{4,6},{5,7},{6,4},{7,5},{8,10},{9,11},{10,... | collective-permute-start | bytes 42212 | tf_op jit(solution)/shard_map/ppermute | solution.py:593
  24.4 11.6 %collective-permute-start = (bf16[1,7034]{1,0:T(2,128)(2,1)S(1)}, bf16[1,7034]{1,0:T(2,128)(2,1)S(1)}, u32[]{:S(2)}, u32[]{:S(2)}) collective-permute-start(bf16[1,7034]{1,0:T(2,128)(2,1)S(1)} %broadcast_in_dim.43), channel_id=1, source_target_pairs={{0,1},{1,0},{2,3},{3,2},{4,5},{5,4},{6,7},{7,6},{8,9},{9,8},{10,11... | collective-permute-start | bytes 42212 | tf_op jit(solution)/shard_map/ppermute | solution.py:593
  29.2 22.2 %collective-permute-start.4 = (bf16[848,256]{1,0:T(8,128)(2,1)S(1)}, bf16[848,256]{1,0:T(8,128)(2,1)S(1)}, u32[]{:S(2)}, u32[]{:S(2)}) collective-permute-start(bf16[848,256]{1,0:T(8,128)(2,1)S(1)} %pad_maximum_fusion.16), channel_id=1, source_target_pairs={{0,1},{1,0},{2,3},{3,2},{4,5},{5,4},{6,7},{7,6},{8,9},{9,8},{10,11... | collective-permute-start | bytes 1302536 | tf_op jit(solution)/shard_map/ppermute | solution.py:593
  31.2 22.6 %collective-permute-start.5 = (bf16[848,256]{1,0:T(8,128)(2,1)S(1)}, bf16[848,256]{1,0:T(8,128)(2,1)S(1)}, u32[]{:S(2)}, u32[]{:S(2)}) collective-permute-start(bf16[848,256]{1,0:T(8,128)(2,1)S(1)} %pad_maximum_fusion.17), channel_id=1, source_target_pairs={{0,2},{1,3},{2,0},{3,1},{4,6},{5,7},{6,4},{7,5},{8,10},{9,11},{10,... | collective-permute-start | bytes 1302536 | tf_op jit(solution)/shard_map/ppermute | solution.py:593
  32.8 34.7 %collective-permute-start.6 = (bf16[848,256]{1,0:T(8,128)(2,1)S(1)}, bf16[848,256]{1,0:T(8,128)(2,1)S(1)}, u32[]{:S(2)}, u32[]{:S(2)}) collective-permute-start(bf16[848,256]{1,0:T(8,128)(2,1)S(1)} %pad_maximum_fusion.18), channel_id=1, source_target_pairs={{0,3},{1,2},{2,1},{3,0},{4,7},{5,6},{6,5},{7,4},{8,11},{9,10},{10,... | collective-permute-start | bytes 1302536 | tf_op jit(solution)/shard_map/ppermute | solution.py:593
  33.0 35.4 %collective-permute-start.7 = (bf16[1,912,256]{2,1,0:T(8,128)(2,1)S(1)}, bf16[1,912,256]{2,1,0:T(8,128)(2,1)S(1)}, u32[]{:S(2)}, u32[]{:S(2)}) collective-permute-start(bf16[1,912,256]{2,1,0:T(8,128)(2,1)S(1)} %maximum_bitcast_fusion.2), channel_id=1, source_target_pairs={{0,16},{4,20},{8,24},{12,28},{16,0},{20,4},{24,8},{28,12},{1,17},{... | collective-permute-start | bytes 1400840 | tf_op jit(solution)/shard_map/ppermute | solution.py:593
  68.5 42.4 %collective-permute-start.8 = (bf16[1,1776,256]{2,1,0:T(8,128)(2,1)S(1)}, bf16[1,1776,256]{2,1,0:T(8,128)(2,1)}, u32[]{:S(2)}, u32[]{:S(2)}) collective-permute-start(bf16[1,1776,256]{2,1,0:T(8,128)(2,1)S(1)} %maximum_bitcast_fusion), channel_id=1, source_target_pairs={{0,16},{4,20},{8,24},{12,28},{16,0},{20,4},{24,8},{28,12},{1,17},{... | collective-permute-start | bytes 2727944 | tf_op jit(solution)/shard_map/ppermute | solution.py:593
  71.5 42.0 %collective-permute-start.9 = (bf16[2,912,256]{2,1,0:T(8,128)(2,1)S(1)}, bf16[2,912,256]{2,1,0:T(8,128)(2,1)S(1)}, u32[]{:S(2)}, u32[]{:S(2)}) collective-permute-start(bf16[2,912,256]{2,1,0:T(8,128)(2,1)S(1)} %pad_maximum_fusion.10), channel_id=1, source_target_pairs={{0,8},{4,12},{8,0},{12,4},{16,24},{20,28},{24,16},{28,20},{1,9},{5... | collective-permute-start | bytes 2801672 | tf_op jit(solution)/shard_map/ppermute | solution.py:593
  113.7 17.9 %collective-permute-start.11 = (bf16[4,912,256]{2,1,0:T(8,128)(2,1)S(1)}, bf16[4,912,256]{2,1,0:T(8,128)(2,1)}, u32[]{:S(2)}, u32[]{:S(2)}) collective-permute-start(bf16[4,912,256]{2,1,0:T(8,128)(2,1)S(1)} %pad_maximum_fusion.4.refs_0_), channel_id=1, source_target_pairs={{0,4},{4,0},{8,12},{12,8},{16,20},{20,16},{24,28},{28,24},{1,5},{5... | collective-permute-start | bytes 5603336 | tf_op jit(solution)/shard_map/ppermute | solution.py:593
  114.5 226.1 %copy-start.19 = (f32[1,256]{1,0:T(1,128)}, f32[1,256]{1,0:T(1,128)S(1)}, u32[]{:S(2)}) copy-start(f32[1,256]{1,0:T(1,128)S(1)} %slice.295.cbbc_ref.refs_8_) | copy-start | bytes 3076
  114.9 225.8 %copy-start.7 = (f32[4,256]{1,0:T(4,128)}, f32[4,256]{1,0:T(4,128)S(1)}, u32[]{:S(2)}) copy-start(f32[4,256]{1,0:T(4,128)S(1)} %slice.294.cwbc_ref.refs_7_) | copy-start | bytes 12292
  115.3 225.4 %copy-start.9 = (f32[1,1,4,256]{3,1,2,0:T(1,128)}, f32[1,1,4,256]{3,1,2,0:T(1,128)S(1)}, u32[]{:S(2)}) copy-start(f32[1,1,4,256]{3,1,2,0:T(1,128)S(1)} %copy.201) | copy-start | bytes 12292
  115.5 42.4 %collective-permute-start.10 = (bf16[2,1776,256]{2,1,0:T(8,128)(2,1)}, bf16[2,1776,256]{2,1,0:T(8,128)(2,1)}, u32[]{:S(2)}, u32[]{:S(2)}) collective-permute-start(bf16[2,1776,256]{2,1,0:T(8,128)(2,1)} %pad_maximum_fusion.5.refs_0_), channel_id=1, source_target_pairs={{0,8},{4,12},{8,0},{12,4},{16,24},{20,28},{24,16},{28,20},{1,9},{5... | collective-permute-start | bytes 5455880 | tf_op jit(solution)/shard_map/ppermute | solution.py:593
  121.1 219.6 %copy-start.11 = (f32[1,4,1,256]{3,2,1,0:T(1,128)}, f32[1,4,1,256]{3,2,1,0:T(1,128)S(1)}, u32[]{:S(2)}) copy-start(f32[1,4,1,256]{3,2,1,0:T(1,128)S(1)} %constant_dynamic-slice_fusion.15) | copy-start | bytes 12292
  121.2 124.5 %copy-start.21 = (s32[2,4]{1,0:T(2,128)}, s32[2,4]{1,0:T(2,128)S(1)}, u32[]{:S(2)}) copy-start(s32[2,4]{1,0:T(2,128)S(1)} %get-tuple-element.122.starts_ref.refs_0_) | copy-start | bytes 100
  121.2 8.6 %collective-permute-start.15 = (bf16[320,256]{1,0:T(8,128)(2,1)S(1)}, bf16[320,256]{1,0:T(8,128)(2,1)S(1)}, u32[]{:S(2)}, u32[]{:S(2)}) collective-permute-start(bf16[320,256]{1,0:T(8,128)(2,1)S(1)} %fusion.97), channel_id=1, source_target_pairs={{0,3},{1,2},{2,1},{3,0},{4,7},{5,6},{6,5},{7,4},{8,11},{9,10},{10,... | collective-permute-start | bytes 491528 | tf_op jit(solution)/shard_map/ppermute | solution.py:593
  121.9 9.5 %collective-permute-start.14 = (bf16[320,256]{1,0:T(8,128)(2,1)S(1)}, bf16[320,256]{1,0:T(8,128)(2,1)S(1)}, u32[]{:S(2)}, u32[]{:S(2)}) collective-permute-start(bf16[320,256]{1,0:T(8,128)(2,1)S(1)} %fusion.97), channel_id=1, source_target_pairs={{0,2},{1,3},{2,0},{3,1},{4,6},{5,7},{6,4},{7,5},{8,10},{9,11},{10,... | collective-permute-start | bytes 491528 | tf_op jit(solution)/shard_map/ppermute | solution.py:593
  123.3 8.1 %collective-permute-start.13 = (bf16[320,256]{1,0:T(8,128)(2,1)S(1)}, bf16[320,256]{1,0:T(8,128)(2,1)S(1)}, u32[]{:S(2)}, u32[]{:S(2)}) collective-permute-start(bf16[320,256]{1,0:T(8,128)(2,1)S(1)} %fusion.97), channel_id=1, source_target_pairs={{0,1},{1,0},{2,3},{3,2},{4,5},{5,4},{6,7},{7,6},{8,9},{9,8},{10,11... | collective-permute-start | bytes 491528 | tf_op jit(solution)/shard_map/ppermute | solution.py:593
  129.8 57.0 %collective-permute-start.17 = (bf16[2,1776,256]{2,1,0:T(8,128)(2,1)}, bf16[2,1776,256]{2,1,0:T(8,128)(2,1)}, u32[]{:S(2)}, u32[]{:S(2)}) collective-permute-start(bf16[2,1776,256]{2,1,0:T(8,128)(2,1)} %pad_maximum_fusion.5.refs_0_), channel_id=1, source_target_pairs={{0,4},{4,0},{8,12},{12,8},{16,20},{20,16},{24,28},{28,24},{1,5},{5... | collective-permute-start | bytes 5455880 | tf_op jit(solution)/shard_map/ppermute | solution.py:593
  131.5 29.2 %collective-permute-start.16 = (bf16[4,320,256]{2,1,0:T(8,128)(2,1)S(1)}, bf16[4,320,256]{2,1,0:T(8,128)(2,1)}, u32[]{:S(2)}, u32[]{:S(2)}) collective-permute-start(bf16[4,320,256]{2,1,0:T(8,128)(2,1)S(1)} %pad_maximum_fusion.11.refs_0_), channel_id=1, source_target_pairs={{0,4},{4,0},{8,12},{12,8},{16,20},{20,16},{24,28},{28,24},{1,5},{5... | collective-permute-start | bytes 1966088 | tf_op jit(solution)/shard_map/ppermute | solution.py:593
  157.9 28.9 %collective-permute-start.18 = (bf16[2,1776,256]{2,1,0:T(8,128)(2,1)}, bf16[2,1776,256]{2,1,0:T(8,128)(2,1)}, u32[]{:S(2)}, u32[]{:S(2)}) collective-permute-start(bf16[2,1776,256]{2,1,0:T(8,128)(2,1)} %collective-permute-done.10.refs_1_), channel_id=1, source_target_pairs={{0,4},{4,0},{8,12},{12,8},{16,20},{20,16},{24,28},{28,24},{1,5},{5... | collective-permute-start | bytes 5455880 | tf_op jit(solution)/shard_map/ppermute | solution.py:593
  182.5 34.9 %collective-permute-start.12 = (bf16[1,1024,256]{2,1,0:T(8,128)(2,1)}, bf16[1,1024,256]{2,1,0:T(8,128)(2,1)S(1)}, u32[]{:S(2)}, u32[]{:S(2)}) collective-permute-start(bf16[1,1024,256]{2,1,0:T(8,128)(2,1)} %maximum_bitcast_fusion.1), channel_id=1, source_target_pairs={{0,16},{4,20},{8,24},{12,28},{16,0},{20,4},{24,8},{28,12},{1,17},{... | collective-permute-start | bytes 1572872 | tf_op jit(solution)/shard_map/ppermute | solution.py:593
  218.3 25.2 %collective-permute-start.19 = (bf16[2,1024,256]{2,1,0:T(8,128)(2,1)S(1)}, bf16[2,1024,256]{2,1,0:T(8,128)(2,1)S(1)}, u32[]{:S(2)}, u32[]{:S(2)}) collective-permute-start(bf16[2,1024,256]{2,1,0:T(8,128)(2,1)S(1)} %get-tuple-element.286), channel_id=1, source_target_pairs={{0,8},{4,12},{8,0},{12,4},{16,24},{20,28},{24,16},{28,20},{1,9},{5... | collective-permute-start | bytes 3145736 | tf_op jit(solution)/shard_map/ppermute | solution.py:593
  244.5 28.8 %collective-permute-start.21 = (bf16[4,1024,256]{2,1,0:T(8,128)(2,1)}, bf16[4,1024,256]{2,1,0:T(8,128)(2,1)}, u32[]{:S(2)}, u32[]{:S(2)}) collective-permute-start(bf16[4,1024,256]{2,1,0:T(8,128)(2,1)} %constant_dynamic-update-slice_fusion.2.refs_0_), channel_id=1, source_target_pairs={{0,4},{4,0},{8,12},{12,8},{16,20},{20,16},{24,28},{28,24},{1,5},{5... | collective-permute-start | bytes 6291464 | tf_op jit(solution)/shard_map/ppermute | solution.py:593
  267.3 11.4 %collective-permute-start.23 = (f32[4,512]{1,0:T(4,128)S(1)}, f32[4,512]{1,0:T(4,128)S(1)}, u32[]{:S(2)}, u32[]{:S(2)}) collective-permute-start(f32[4,512]{1,0:T(4,128)S(1)} %reshape.729), channel_id=1, source_target_pairs={{0,3},{1,2},{2,1},{3,0},{4,7},{5,6},{6,5},{7,4},{8,11},{9,10},{10,... | collective-permute-start | bytes 24584 | tf_op jit(solution)/shard_map/ppermute | solution.py:593
  268.2 10.6 %collective-permute-start.22 = (f32[4,512]{1,0:T(4,128)S(1)}, f32[4,512]{1,0:T(4,128)S(1)}, u32[]{:S(2)}, u32[]{:S(2)}) collective-permute-start(f32[4,512]{1,0:T(4,128)S(1)} %reshape.729), channel_id=1, source_target_pairs={{0,2},{1,3},{2,0},{3,1},{4,6},{5,7},{6,4},{7,5},{8,10},{9,11},{10,... | collective-permute-start | bytes 24584 | tf_op jit(solution)/shard_map/ppermute | solution.py:593
  269.6 9.2 %collective-permute-start.20 = (f32[4,512]{1,0:T(4,128)S(1)}, f32[4,512]{1,0:T(4,128)S(1)}, u32[]{:S(2)}, u32[]{:S(2)}) collective-permute-start(f32[4,512]{1,0:T(4,128)S(1)} %reshape.729), channel_id=1, source_target_pairs={{0,1},{1,0},{2,3},{3,2},{4,5},{5,4},{6,7},{7,6},{8,9},{9,8},{10,11... | collective-permute-start | bytes 24584 | tf_op jit(solution)/shard_map/ppermute | solution.py:593
  316.6 172.6 %reduce-scatter.5.cloned.1.call-start = ((), (), s32[]{:S(2)}) async-start(), calls=%async_computation.4 | async-start | bytes 10485760 | tf_op jit(solution)/shard_map/reduce_scatter | solution.py:998
  331.5 280.9 %reduce-scatter.9.cloned.1.call-start = ((), (), s32[]{:S(2)}) async-start(), calls=%async_computation.6 | async-start | bytes 5242880 | tf_op jit(solution)/shard_map/reduce_scatter | solution.py:1063
  331.9 5.0 collective-permute-start.26
  332.8 4.2 collective-permute-start.25
  334.2 3.7 collective-permute-start.24
  384.8 53.7 %collective-permute-start.29 = (bf16[256,256]{1,0:T(8,128)(2,1)}, bf16[256,256]{1,0:T(8,128)(2,1)}, u32[]{:S(2)}, u32[]{:S(2)}) collective-permute-start(bf16[256,256]{1,0:T(8,128)(2,1)} %get-tuple-element.282), channel_id=1, source_target_pairs={{0,3},{1,2},{2,1},{3,0},{4,7},{5,6},{6,5},{7,4},{8,11},{9,10},{10,... | collective-permute-start | bytes 393224 | tf_op jit(solution)/shard_map/ppermute | solution.py:593
  386.3 52.3 %collective-permute-start.28 = (bf16[256,256]{1,0:T(8,128)(2,1)}, bf16[256,256]{1,0:T(8,128)(2,1)}, u32[]{:S(2)}, u32[]{:S(2)}) collective-permute-start(bf16[256,256]{1,0:T(8,128)(2,1)} %get-tuple-element.283), channel_id=1, source_target_pairs={{0,2},{1,3},{2,0},{3,1},{4,6},{5,7},{6,4},{7,5},{8,10},{9,11},{10,... | collective-permute-start | bytes 393224 | tf_op jit(solution)/shard_map/ppermute | solution.py:593
  387.6 51.0 %collective-permute-start.27 = (bf16[256,256]{1,0:T(8,128)(2,1)}, bf16[256,256]{1,0:T(8,128)(2,1)}, u32[]{:S(2)}, u32[]{:S(2)}) collective-permute-start(bf16[256,256]{1,0:T(8,128)(2,1)} %get-tuple-element.284), channel_id=1, source_target_pairs={{0,1},{1,0},{2,3},{3,2},{4,5},{5,4},{6,7},{7,6},{8,9},{9,8},{10,11... | collective-permute-start | bytes 393224 | tf_op jit(solution)/shard_map/ppermute | solution.py:593
  465.9 17.0 %collective-permute-start.30 = (bf16[2048,512]{1,0:T(8,128)(2,1)S(1)}, bf16[2048,512]{1,0:T(8,128)(2,1)S(1)}, u32[]{:S(2)}, u32[]{:S(2)}) collective-permute-start(bf16[2048,512]{1,0:T(8,128)(2,1)S(1)} %pad_maximum_fusion.1), channel_id=1, source_target_pairs={{0,4},{4,0},{8,12},{12,8},{16,20},{20,16},{24,28},{28,24},{1,5},{5... | collective-permute-start | bytes 6291464 | tf_op jit(solution)/shard_map/ppermute | solution.py:593
  466.1 16.8 %collective-permute-start.31 = (bf16[2048,512]{1,0:T(8,128)(2,1)S(1)}, bf16[2048,512]{1,0:T(8,128)(2,1)S(1)}, u32[]{:S(2)}, u32[]{:S(2)}) collective-permute-start(bf16[2048,512]{1,0:T(8,128)(2,1)S(1)} %pad_maximum_fusion.2), channel_id=1, source_target_pairs={{0,4},{4,0},{8,12},{12,8},{16,20},{20,16},{24,28},{28,24},{1,5},{5... | collective-permute-start | bytes 6291464 | tf_op jit(solution)/shard_map/ppermute | solution.py:593
  471.3 10.1 %collective-permute-start.32 = (bf16[4,320,256]{2,1,0:T(8,128)(2,1)S(1)}, bf16[4,320,256]{2,1,0:T(8,128)(2,1)S(1)}, u32[]{:S(2)}, u32[]{:S(2)}) collective-permute-start(bf16[4,320,256]{2,1,0:T(8,128)(2,1)S(1)} %pad_maximum_fusion.12), channel_id=1, source_target_pairs={{0,4},{4,0},{8,12},{12,8},{16,20},{20,16},{24,28},{28,24},{1,5},{5... | collective-permute-start | bytes 1966088 | tf_op jit(solution)/shard_map/ppermute | solution.py:593
  505.0 119.8 %reduce-scatter.11.cloned.1.call-start = ((), (), s32[]{:S(2)}) async-start(), calls=%async_computation.7 | async-start | bytes 5242880 | tf_op jit(solution)/shard_map/reduce_scatter | solution.py:1068
  505.1 29.1 %collective-permute-start.33 = (bf16[2,592,512]{2,1,0:T(8,128)(2,1)}, bf16[2,592,512]{2,1,0:T(8,128)(2,1)S(1)}, u32[]{:S(2)}, u32[]{:S(2)}) collective-permute-start(bf16[2,592,512]{2,1,0:T(8,128)(2,1)} %pad_maximum_fusion.7), channel_id=1, source_target_pairs={{0,8},{4,12},{8,0},{12,4},{16,24},{20,28},{24,16},{28,20},{1,9},{5... | collective-permute-start | bytes 3637256 | tf_op jit(solution)/shard_map/ppermute | solution.py:593
  551.8 41.0 %collective-permute-start.34 = (bf16[2,592,512]{2,1,0:T(8,128)(2,1)}, bf16[2,592,512]{2,1,0:T(8,128)(2,1)}, u32[]{:S(2)}, u32[]{:S(2)}) collective-permute-start(bf16[2,592,512]{2,1,0:T(8,128)(2,1)} %pad_maximum_fusion.8), channel_id=1, source_target_pairs={{0,8},{4,12},{8,0},{12,4},{16,24},{20,28},{24,16},{28,20},{1,9},{5... | collective-permute-start | bytes 3637256 | tf_op jit(solution)/shard_map/ppermute | solution.py:593
  556.5 36.3 %collective-permute-start.35 = (bf16[592,512]{1,0:T(8,128)(2,1)}, bf16[592,512]{1,0:T(8,128)(2,1)}, u32[]{:S(2)}, u32[]{:S(2)}) collective-permute-start(bf16[592,512]{1,0:T(8,128)(2,1)} %get-tuple-element.269), channel_id=1, source_target_pairs={{0,16},{4,20},{8,24},{12,28},{16,0},{20,4},{24,8},{28,12},{1,17},{... | collective-permute-start | bytes 1818632 | tf_op jit(solution)/shard_map/ppermute | solution.py:593
  557.0 45.4 %copy-start.67 = (f32[4]{0:T(128)S(1)}, f32[4]{0:T(128)}, u32[]{:S(2)}) copy-start(f32[4]{0:T(128)} %copy-done.65) | copy-start | bytes 52
  561.0 40.2 %collective-permute-start.40 = (bf16[320,256]{1,0:T(8,128)(2,1)}, bf16[320,256]{1,0:T(8,128)(2,1)S(1)}, u32[]{:S(2)}, u32[]{:S(2)}) collective-permute-start(bf16[320,256]{1,0:T(8,128)(2,1)} %get-tuple-element.271), channel_id=1, source_target_pairs={{0,1},{1,0},{2,3},{3,2},{4,5},{5,4},{6,7},{7,6},{8,9},{9,8},{10,11... | collective-permute-start | bytes 491528 | tf_op jit(solution)/shard_map/ppermute | solution.py:593
  562.0 39.1 %collective-permute-start.42 = (bf16[320,256]{1,0:T(8,128)(2,1)}, bf16[320,256]{1,0:T(8,128)(2,1)}, u32[]{:S(2)}, u32[]{:S(2)}) collective-permute-start(bf16[320,256]{1,0:T(8,128)(2,1)} %get-tuple-element.272), channel_id=1, source_target_pairs={{0,3},{1,2},{2,1},{3,0},{4,7},{5,6},{6,5},{7,4},{8,11},{9,10},{10,... | collective-permute-start | bytes 491528 | tf_op jit(solution)/shard_map/ppermute | solution.py:593
  563.6 37.5 %collective-permute-start.41 = (bf16[320,256]{1,0:T(8,128)(2,1)}, bf16[320,256]{1,0:T(8,128)(2,1)}, u32[]{:S(2)}, u32[]{:S(2)}) collective-permute-start(bf16[320,256]{1,0:T(8,128)(2,1)} %get-tuple-element.273), channel_id=1, source_target_pairs={{0,2},{1,3},{2,0},{3,1},{4,6},{5,7},{6,4},{7,5},{8,10},{9,11},{10,... | collective-permute-start | bytes 491528 | tf_op jit(solution)/shard_map/ppermute | solution.py:593
  594.9 38.9 %collective-permute-start.36 = (bf16[592,512]{1,0:T(8,128)(2,1)}, bf16[592,512]{1,0:T(8,128)(2,1)}, u32[]{:S(2)}, u32[]{:S(2)}) collective-permute-start(bf16[592,512]{1,0:T(8,128)(2,1)} %fusion.27), channel_id=1, source_target_pairs={{0,16},{4,20},{8,24},{12,28},{16,0},{20,4},{24,8},{28,12},{1,17},{... | collective-permute-start | bytes 1818632 | tf_op jit(solution)/shard_map/ppermute | solution.py:593
  604.5 7.8 %collective-permute-start.43 = (bf16[320,256]{1,0:T(8,128)(2,1)S(1)}, bf16[320,256]{1,0:T(8,128)(2,1)S(1)}, u32[]{:S(2)}, u32[]{:S(2)}) collective-permute-start(bf16[320,256]{1,0:T(8,128)(2,1)S(1)} %fusion.49), channel_id=1, source_target_pairs={{0,8},{4,12},{8,0},{12,4},{16,24},{20,28},{24,16},{28,20},{1,9},{5... | collective-permute-start | bytes 491528 | tf_op jit(solution)/shard_map/ppermute | solution.py:593
  606.8 52.6 %collective-permute-start.39 = (bf16[592,256]{1,0:T(8,128)(2,1)}, bf16[592,256]{1,0:T(8,128)(2,1)}, u32[]{:S(2)}, u32[]{:S(2)}) collective-permute-start(bf16[592,256]{1,0:T(8,128)(2,1)} %get-tuple-element.274), channel_id=1, source_target_pairs={{0,3},{1,2},{2,1},{3,0},{4,7},{5,6},{6,5},{7,4},{8,11},{9,10},{10,... | collective-permute-start | bytes 909320 | tf_op jit(solution)/shard_map/ppermute | solution.py:593
  608.3 50.1 %collective-permute-start.38 = (bf16[592,256]{1,0:T(8,128)(2,1)}, bf16[592,256]{1,0:T(8,128)(2,1)}, u32[]{:S(2)}, u32[]{:S(2)}) collective-permute-start(bf16[592,256]{1,0:T(8,128)(2,1)} %get-tuple-element.275), channel_id=1, source_target_pairs={{0,2},{1,3},{2,0},{3,1},{4,6},{5,7},{6,4},{7,5},{8,10},{9,11},{10,... | collective-permute-start | bytes 909320 | tf_op jit(solution)/shard_map/ppermute | solution.py:593
  631.2 5.9 collective-permute-start.46
  633.8 6.5 collective-permute-start.48
  633.9 6.5 collective-permute-start.47
  637.1 23.3 %collective-permute-start.44 = (bf16[320,256]{1,0:T(8,128)(2,1)S(1)}, bf16[320,256]{1,0:T(8,128)(2,1)S(1)}, u32[]{:S(2)}, u32[]{:S(2)}) collective-permute-start(bf16[320,256]{1,0:T(8,128)(2,1)S(1)} %add_convert_fusion.13), channel_id=1, source_target_pairs={{0,16},{4,20},{8,24},{12,28},{16,0},{20,4},{24,8},{28,12},{1,17},{... | collective-permute-start | bytes 491528 | tf_op jit(solution)/shard_map/ppermute | solution.py:593
  640.4 8.0 %collective-permute-start.49 = (f32[1,7024]{1,0:T(1,128)S(1)}, f32[1,7024]{1,0:T(1,128)S(1)}, u32[]{:S(2)}, u32[]{:S(2)}) collective-permute-start(f32[1,7024]{1,0:T(1,128)S(1)} %add_add_fusion), channel_id=1, source_target_pairs={{0,16},{4,20},{8,24},{12,28},{16,0},{20,4},{24,8},{28,12},{1,17},{... | collective-permute-start | bytes 84296 | tf_op jit(solution)/shard_map/ppermute | solution.py:593
  648.5 3.9 collective-permute-start.50
  649.3 9.1 %collective-permute-start.37 = (bf16[592,256]{1,0:T(8,128)(2,1)S(1)}, bf16[592,256]{1,0:T(8,128)(2,1)S(1)}, u32[]{:S(2)}, u32[]{:S(2)}) collective-permute-start(bf16[592,256]{1,0:T(8,128)(2,1)S(1)} %get-tuple-element.276), channel_id=1, source_target_pairs={{0,1},{1,0},{2,3},{3,2},{4,5},{5,4},{6,7},{7,6},{8,9},{9,8},{10,11... | collective-permute-start | bytes 909320 | tf_op jit(solution)/shard_map/ppermute | solution.py:593
  652.4 3.3 collective-permute-start.51
  667.6 2.4 collective-permute-start.45
  (91 other events, 646.7 us)
Sparse Core Ops, SparseCore 0:
  9.9 110.1 all-gather.4
  121.9 87.6 all-gather.6
  316.7 47.7 reduce-scatter.6
  367.3 90.1 reduce-scatter.4
  505.1 51.7 reduce-scatter.8
  560.3 64.4 reduce-scatter.10

commit v4 on v3

--- a/solution.py
+++ b/solution.py
@@ -673,7 +673,7 @@
     )(*operands)
 
 
-def matmul(a, b, kind, out_dtype=BF16, scale=None):
+def matmul(a, b, kind, out_dtype=BF16, scale=None, more=None):
     m = a.shape[1] if kind == "tn" else a.shape[0]
     k = a.shape[0] if kind == "tn" else a.shape[1]
     n = b.shape[0] if kind == "nt" else b.shape[1]
@@ -685,6 +685,8 @@
         if scale is not None:
             first = first * refs[2][...]
         total = lax.dot_general(first, refs[1][...], (dims, ((), ())), preferred_element_type=F32)
+        if more is not None:
+            total = total + dot(refs[2][...], refs[3][...])
         refs[-1][...] = total.astype(out_dtype)
 
     in_specs = [
@@ -692,6 +694,10 @@
         pl.BlockSpec((tn, k), lambda i, j: (j, 0)) if kind == "nt" else pl.BlockSpec((k, tn), lambda i, j: (0, j)),
     ]
     operands = [a, b]
+    if more is not None:
+        inner = more[0].shape[1]
+        in_specs += [pl.BlockSpec((tm, inner), lambda i, j: (i, 0)), pl.BlockSpec((inner, tn), lambda i, j: (0, j))]
+        operands += list(more)
     if scale is not None:
         in_specs.append(pl.BlockSpec((k, 1), lambda i, j: (0, 0)))
         operands.append(scale)
@@ -705,6 +711,41 @@
         cost_estimate=pl.CostEstimate(flops=2 * m * n * k, bytes_accessed=2 * (m * k + n * k + m * n), transcendentals=0),
         name="matmul_" + kind,
     )(*operands)
+
+
+def matmul_blocks(a, b, size, chosen):
+    k, m = a.shape
+    tm, count = min(m, 2048), len(chosen) // 2
+
+    def kernel(chosen_ref, a_ref, b_ref, first_ref, second_ref):
+        total = lax.dot_general(a_ref[...], b_ref[...], (((0,), (0,)), ((), ())), preferred_element_type=F32)
+
+        @pl.when(pl.program_id(1) < count)
+        def _():
+            first_ref[...] = total.astype(BF16)
+
+        @pl.when(pl.program_id(1) >= count)
+        def _():
+            second_ref[...] = total.astype(BF16)
+
+    return pl.pallas_call(
+        kernel,
+        grid_spec=pltpu.PrefetchScalarGridSpec(
+            num_scalar_prefetch=1,
+            grid=(m // tm, 2 * count),
+            in_specs=[
+                pl.BlockSpec((k, tm), lambda i, j, t: (0, i)),
+                pl.BlockSpec((k, size), lambda i, j, t: (0, t[j])),
+            ],
+            out_specs=[
+                pl.BlockSpec((tm, size), lambda i, j, t: (i, jnp.minimum(j, count - 1))),
+                pl.BlockSpec((tm, size), lambda i, j, t: (i, jnp.maximum(j - count, 0))),
+            ],
+        ),
+        out_shape=[jax.ShapeDtypeStruct((m, size * count), BF16)] * 2,
+        compiler_params=pltpu.CompilerParams(vmem_limit_bytes=56 * 1024 * 1024),
+        name="matmul_blocks",
+    )(jnp.stack([jnp.asarray(v, jnp.int32) for v in chosen]), a, b)
 
 
 def mixed_gradient(upstream, weights, live, mixed):
@@ -787,6 +828,10 @@
 
 def static_count(g, n, unit, period):
     return (n // period) * unit + min(max(n % period - g * unit, 0), unit)
+
+
+def together(*values):
+    return lax.optimization_barrier(values)
 
 
 def then(value, *earlier):
@@ -861,10 +906,7 @@
     out_low = w_out.astype(BF16).reshape(groups, unit, out_cols)
     out_blocks = [lax.dynamic_index_in_dim(out_low, f ^ m, 0, keepdims=False) for m in range(groups)]
     blocks = [parts[m * most : (m + 1) * most] for m in range(groups)]
-    pairs = [swap(jnp.concatenate([blocks[m], out_blocks[m]]), "fsdp", m) for m in range(1, groups)]
-    blocks = blocks[:1] + [p[:most] for p in pairs]
-    out_cat = jnp.stack(out_blocks[:1] + [p[most:] for p in pairs])
-    out_cat = jnp.concatenate([lax.dynamic_index_in_dim(out_cat, f ^ m, 0, keepdims=False) for m in range(groups)])
+    blocks = blocks[:1] + [swap(blocks[m], "fsdp", m) for m in range(1, groups)]
     first = jnp.concatenate([blocks[0], parts[groups * most :]])[None]
     marks = jnp.concatenate([doc_starts[0], valid_len])
     marks = jnp.concatenate([(marks // 32).astype(BF16), (marks % 32).astype(BF16)])
@@ -903,18 +945,19 @@
     starts = marks[:, :-1]
     live_all = jnp.concatenate([(jnp.arange(length) < marks[r, -1]).astype(F32)[:, None] for r in range(groups)])
 
-    second_2 = then(jnp.concatenate([second, got_b]), got_a)
+    out_blocks = [then(v, sent_b) for v in out_blocks]
+    out_cat = jnp.stack(out_blocks[:1] + [swap(out_blocks[m], "fsdp", m) for m in range(1, groups)])
+    out_cat = jnp.concatenate([lax.dynamic_index_in_dim(out_cat, f ^ m, 0, keepdims=False) for m in range(groups)])
+    second_2, got_a, out_cat = together(jnp.concatenate([second, got_b]), got_a, out_cat)
     got_b2 = swap(second_2, "dp", 2 * z_masks[1])
     spread_a = jnp.concatenate([first_2, got_a])
     order_z = [0, z_masks[0]] + [z_masks[1], z_masks[0] ^ z_masks[1]]
     sibling_a = swap(then(spread_a, second_2), "dp", 1)
     sibling_b = swap(second_2, "dp", 1)
-    normed_all = rows_into(None, 0, groups, length, [token_rows], norm_full)
     extra_at = jnp.stack([jnp.int32(r) for r in order_z]) == (z ^ (zs - 1))
     extra_at = jnp.sum(jnp.where(extra_at, jnp.arange(zs, dtype=jnp.int32), 0))
     extra_own = lax.dynamic_index_in_dim(then(spread_a, second_2), extra_at, 0, keepdims=False)[most:]
     extra_got = jnp.stack([extra_own] + [swap(extra_own, "fsdp", m) for m in range(1, groups)])
-    extra_pair = [extra_got, swap(extra_got, "dp", 1)]
     w_shape = (2 * local, width)
 
     def place_main(buffer, arrays, ms, rc):
@@ -925,25 +968,28 @@
 
     w_main = place_main(None, [spread_a], [0], 0)
     w_main = place_main(w_main, [sibling_a], [0], 1)
-    got_b2 = then(got_b2, normed_all, w_main)
-    sibling_b2 = swap(got_b2, "dp", 1)
-    others = range(1, groups)
-    w_main = place_main(w_main, [second_2, got_b2], others, 0)
-    w_main = place_main(w_main, [sibling_b, sibling_b2], others, 1)
+    normed_all = rows_into(None, 0, groups, length, [then(token_rows, w_main)], norm_full)
+    extra_got = then(extra_got, w_main)
+    extra_pair = [extra_got, swap(extra_got, "dp", 1)]
+    extra_pair[1] = then(extra_pair[1], normed_all)
     extra_items = []
     for m in range(groups):
         for rc in range(2):
             extra_items.append((extra_pair[rc], m, 0, k_rows * (f ^ m) + k_half * (c ^ rc), EXTRA, (0, EXTRA)))
     w_extra = place(None, (EXTRA, width), (EXTRA, width), (0, 0), extra_items)
-
-    out_1 = then(out_cat[None], got_b2)
-    out_got = swap(out_1, "dp", 2 * z_masks[0])
-
     w_dt = w_extra[2 * NS :].reshape(groups, groups, -1, width)
     w_dt = lax.dynamic_index_in_dim(w_dt, f, 1, keepdims=False).reshape(-1, width)
     w_own = jnp.concatenate([w_extra[: 2 * NS], w_dt, jnp.zeros((128 - w_dt.shape[0], width), BF16)])
     extra = matmul(normed_all, w_own, "nt", F32)
     dt_rows = extra[:, 2 * NS : 2 * NS + w_dt.shape[0]].T
+    got_b2 = then(got_b2, normed_all, w_main, extra)
+    sibling_b2 = swap(got_b2, "dp", 1)
+    others = range(1, groups)
+    w_main = place_main(w_main, [second_2, got_b2], others, 0)
+    w_main = place_main(w_main, [sibling_b, sibling_b2], others, 1)
+    out_1 = then(out_cat[None], got_b2)
+    out_got = swap(out_1, "dp", 2 * z_masks[0])
+
     main = matmul(then(normed_all, extra), w_main, "nt", F32)
     common = (
         main, extra, dt_rows,
@@ -999,22 +1045,13 @@
     d_main, backs = None, []
     for i in range(2):
         begin = starts[i * half_rows : (i + 1) * half_rows]
-        operand = d_mixed
-        if i == 1:
-            own = then(out_own, d_main)
-            out_rows = [lax.dynamic_slice_in_dim(own, unit * (f ^ m), unit, 0) for m in range(groups)]
-            operand = then(d_mixed, *out_rows)
-            out_parts = [swap(out_rows[m], "fsdp", m) for m in range(1, groups)]
-        result = mix_backward(
-            i * half_rows, groups, length, d_main, begin, *common, gain, y[i], states[i], q, mean, operand
+        d_main, *result = mix_backward(
+            i * half_rows, groups, length, d_main, begin, *common, gain, y[i], states[i], q, mean, d_mixed
         )
-        d_main = result[0]
-        backs.append(result[1:])
+        backs.append(result)
     d_bc_in = jnp.concatenate([b[0] for b in backs])
     d_dt = jnp.concatenate([b[1] for b in backs], axis=1)
-    s_gain, s_cw, s_cb, s_cwbc, s_cbbc, s_shift, s_logd, s_skip = [
-        sum(p.sum(axis=0) for p in v) for v in list(zip(*backs))[2:]
-    ]
+    sums = [jnp.concatenate(v) for v in list(zip(*backs))[2:]]
     here = (jnp.arange(groups, dtype=jnp.int32) == f).astype(F32)
 
     def all_channels(v):
@@ -1029,77 +1066,73 @@
         return [lax.dynamic_slice_in_dim(value, k_rows * (f ^ m) + k_half * core, k_half, 1) for m in bundle]
 
     def chip_blocks(bundle, got):
+        size = 2 * k_half
         blocks = []
         for r in range(zs):
             row = slice_row(first_row(z ^ r))
-            ours = [lax.dynamic_slice(main_sum, (row, k_rows * (f ^ m) + k_half * c), (most, k_half)) for m in bundle]
-            theirs = lax.dynamic_slice_in_dim(got, row, most, 0)
-            blocks.append(sum_low(jnp.concatenate(ours, axis=1), theirs))
+            blocks.append(sum_low(*[lax.dynamic_slice(v, (row, bundle * size), (most, size)) for v in (main_sum, got)]))
         return blocks
 
-    main_sum = matmul(then(d_main, *out_parts), normed_all, "tn")
-    out_parts = jnp.stack(out_rows[:1] + out_parts)
-    got_a = swap(jnp.concatenate(bundle_columns(main_sum, bundles[0], 1 - c), axis=1), "dp", 1)
-    got_b = swap(jnp.concatenate(bundle_columns(main_sum, bundles[1], 1 - c), axis=1), "dp", 1)
-    extra_sum = lax.dot_general(then(d_extra, main_sum), normed_all, contract, preferred_element_type=F32).astype(BF16)
+    middle = width // 2
+    order_m = bundles[0] + bundles[1]
+    extra_sum = lax.dot_general(d_extra, normed_all, contract, preferred_element_type=F32).astype(BF16)
     extra_sum = with_layout_constraint(extra_sum, Layout((0, 1)))
     halves_e = [jnp.stack(bundle_columns(extra_sum, range(groups), core)) for core in (c, 1 - c)]
     extra_theirs = swap(halves_e[1], "dp", 1)
-    blocks_a = chip_blocks(bundles[0], then(got_a, extra_sum))
-    blocks_b = chip_blocks(bundles[1], then(got_b, extra_sum))
+    partial = matmul(then(d_main, halves_e[1]), w_main, "nn", more=(d_extra, w_extra))
+    partial, extra_theirs = together(partial, extra_theirs)
+    d_normed = lax.psum_scatter(partial, "fsdp", scatter_dimension=0, tiled=True).astype(F32)
     both = halves_e[0].astype(F32) + extra_theirs.astype(F32)
     total, both_low = both[0], both.astype(BF16)
     arriving = [swap(both_low[m], "fsdp", m) for m in range(1, groups)]
-    sent_a, sent_b = jnp.stack(blocks_a[1::2]), jnp.stack(blocks_b[1::2])
-    flying_a = swap(sent_a, "dp", 2 * z_masks[-1])
-    flying_b = swap(sent_b, "dp", 2 * z_masks[-1])
-    source = then(d_main, sent_a, sent_b, both_low, branch, *blocks_a[0::2], *blocks_b[0::2])
-    middle = width // 2
-
-    def to_normed(source, cols):
-        return (dot(source, w_main[:, cols]) + dot(d_extra, w_extra[:, cols])).astype(BF16)
-
-    partial = to_normed(source, slice(0, middle))
-    d_normed = [lax.psum_scatter(partial, "fsdp", scatter_dimension=0, tiled=True)]
-    flying_a = then(flying_a, partial)
-    keep_a, sent_a = [sum_low(k, flying_a[i]) for i, k in enumerate(blocks_a[0::2])]
-    flying_a = swap(sent_a, "dp", 2 * z_masks[0])
-    partial = to_normed(then(d_main, keep_a, sent_a), slice(middle, width))
-    d_normed.append(lax.psum_scatter(partial, "fsdp", scatter_dimension=0, tiled=True))
-    flying_b, flying_a, _ = lax.optimization_barrier((flying_b, flying_a, partial))
-    keep_b, sent_b = [sum_low(k, flying_b[i]) for i, k in enumerate(blocks_b[0::2])]
-    done_a = sum_low(keep_a, flying_a)
-    flying_b = swap(sent_b, "dp", 2 * z_masks[0])
-    d_normed = jnp.concatenate(d_normed, axis=1).astype(F32)
-
-    hidden = tokens[0].astype(F32)
+    chosen = [2 * (f ^ m) + core for core in (1 - c, c) for m in order_m]
+    sum_theirs, main_sum = matmul_blocks(then(d_main, both_low, branch), normed_all, k_half, chosen)
+    sum_theirs, *arriving = together(sum_theirs, *arriving)
+    got = swap(sum_theirs, "dp", 1)
+    for other in arriving:
+        total = total + other.astype(F32)
+    total = total.astype(BF16)
+    got, total = together(got, total)
+    blocks_a, blocks_b = chip_blocks(0, got), chip_blocks(1, got)
+    near, far = z_masks[-1], z_masks[0]
+    sent_a = jnp.stack([blocks_a[near], blocks_a[near | far]])
+    sent_b = jnp.stack([blocks_b[far], blocks_b[near | far]])
+    got_a, got_b, got_e = together(
+        swap(sent_a, "dp", 2 * near), swap(sent_b, "dp", 2 * far), swap(total, "dp", 2 * near)
+    )
+    total = sum_low(total, got_e)
+    keep_a, sent_a = sum_low(blocks_a[0], got_a[0]), sum_low(blocks_a[far], got_a[1])
+    keep_b, sent_b = sum_low(blocks_b[0], got_b[0]), sum_low(blocks_b[near], got_b[1])
+    got_a, got_b, got_e = together(
+        swap(sent_a, "dp", 2 * far), swap(sent_b, "dp", 2 * near), swap(total, "dp", 2 * far)
+    )
+    total = sum_low(total, got_e)
+    done_a, done_b = sum_low(keep_a, got_a), sum_low(keep_b, got_b)
+    recv = [None] * groups
+    for block, bundle in ((done_a, bundles[0]), (done_b, bundles[1])):
+        for i, m in enumerate(bundle):
+            piece = block[:, i * k_half : (i + 1) * k_half]
+            recv[m] = piece if m == 0 else swap(piece, "fsdp", m)
+    recv = together(*recv)
+    sent_b = recv[-1]
+
+    hidden = then(tokens[0], sent_b).astype(F32)
     live = (jnp.arange(length, dtype=jnp.int32) < valid_len[0]).astype(F32)[:, None]
     scale = lax.rsqrt(jnp.mean(hidden * hidden, axis=-1, keepdims=True) + EPSILON)
     weighted = norm_full * d_normed
     average = jnp.mean(hidden * weighted, axis=-1, keepdims=True)
     grad_tokens = cotangent[0].astype(F32) + scale * weighted - hidden * (scale * scale * scale * average)
     s_norm = jnp.sum(hidden * scale * d_normed, axis=0)
-    for got in arriving:
-        total = total + then(got, sent_b).astype(F32)
-    total = total.astype(BF16)
-    total = sum_low(total, swap(total, "dp", 2 * z_masks[-1]))
-    total = sum_low(total, swap(total, "dp", 2 * z_masks[0]))
-    out_parts = then(out_parts, sent_b)
+    own = then(out_own, sent_b)
+    out_rows = [lax.dynamic_slice_in_dim(own, unit * (f ^ m), unit, 0) for m in range(groups)]
+    out_parts = jnp.stack(out_rows[:1] + [swap(out_rows[m], "fsdp", m) for m in range(1, groups)])
     s_gain, s_cw, s_cb, s_cwbc, s_cbbc, s_shift, s_logd, s_skip = [
-        then(v, sent_b) for v in (s_gain, s_cw, s_cb, s_cwbc, s_cbbc, s_shift, s_logd, s_skip)
+        then(v, sent_b).sum(axis=0) for v in sums
     ]
-    done_b = sum_low(keep_b, then(flying_b, s_norm))
-    recv = [None] * groups
-    for block, bundle in ((done_a, bundles[0]), (done_b, bundles[1])):
-        for i, m in enumerate(bundle):
-            piece = block[:, i * k_half : (i + 1) * k_half]
-            recv[m] = piece if m == 0 else swap(piece, "fsdp", m)
-
-
     grad_out = jnp.concatenate(
         [lax.dynamic_index_in_dim(out_parts, f ^ g, 0, keepdims=False) for g in range(groups)]
     ).astype(F32)
-    blocks = jnp.concatenate(recv + [total])
+    blocks = jnp.concatenate([*recv, total])
     grad_chip = lax.dot_general(blocks, picks(rank + moved), contract, preferred_element_type=F32).astype(BF16)
     left, right = grad_chip[:, :per_dev], grad_chip[:, per_dev:]
     own = jnp.where(c == 0, left, right)

time: 692 us -> 682 us (0.986)
  matrix products: 51.3 us -> 17.2 us
  Pallas kernels: 263 us -> 295 us
  local copies, waits for them, and re-layouts: 62.3 us -> 37.9 us
  waiting for transfers between devices: 157 us -> 180 us
    ppermute x52 -> x54, waiting for transfers between devices: 144 us -> 179 us  [swap(): return lax.ppermute(value, axis, [(i, i ^ mask) for i in range(size)])]
    dot_general x5 -> x1, matrix products: 40.7 us -> 6.3 us  [grouped(): lax.dot_general(d_extra, normed_all, contract, preferred_element_type=F32)]
    pallas_call x0 -> x1, Pallas kernels: none -> 27.6 us  [matmul_blocks(): pl.pallas_call(kernel, grid_spec=pltpu.PrefetchScalarGridSpec(num_scalar_...]
    reduce_scatter x2 -> x1, waiting for transfers between devices: 12.3 us -> 0.02 us  [grouped(): lax.psum_scatter(partial, 'fsdp', scatter_dimension=0, tiled=True)]
    dynamic_slice x4 -> x0, local copies, waits for them, and re-layouts: 8.75 us -> none  [the longest x1 3.5 us: chip_blocks(): lax.dynamic_slice(main_sum, (row, k_rows * (f ^ m) + k_half * c), (most,...]
    unnamed x214 -> x133, local copies, waits for them, and re-layouts: 24.4 us -> 16 us
    ppermute x52 -> x54, starting transfers between devices: 59.5 us -> 57.5 us  [swap(): return lax.ppermute(value, axis, [(i, i ^ mask) for i in range(size)])]
  transfers between devices with their start and end apart: 58 -> 59, of which waited for: 14 -> 22; matrix products, arithmetic and copies ran while one was open for 20% -> 15% of each run, Pallas kernels for 34% -> 37%
where the time goes in v4:
time: 682 us; the launch traced here: 673 us
  Pallas kernels  295 us (43%)
  waiting for transfers between devices  180 us (26%)
  other arithmetic  66.4 us (10%)
  starting transfers between devices  57.9 us (8%)
  local copies, waits for them, and re-layouts  37.9 us (6%)
  between operations  19.1 us (3%)
  matrix products  17.2 us (3%)
    ppermute x54, waiting for transfers between devices, swap(): return lax.ppermute(value, axis, [(i, i ^ mask) for i in range(size)])  179 us
    pallas_call x5, Pallas kernels, matmul(): pl.pallas_call(kernel, grid=(m // tm, n // tn), in_specs=in_specs, out_sp...  90.4 us
    pallas_call x2, Pallas kernels, mix_backward(): pl.pallas_call(backward_first if before is None else backward_kernel, gri...  84.2 us
    ppermute x54, starting transfers between devices, swap(): return lax.ppermute(value, axis, [(i, i ^ mask) for i in range(size)])  57.5 us
    pallas_call x2, Pallas kernels, mix_forward(): pl.pallas_call(forward_kernel, grid=(rows, channels // BC), in_specs=in_s...  36.2 us
    pallas_call x1, Pallas kernels, matmul_blocks(): pl.pallas_call(kernel, grid_spec=pltpu.PrefetchScalarGridSpec(num_scalar_...  27.6 us
    pallas_call x4, Pallas kernels, place_blocks(): pl.pallas_call(kernel, grid_spec=pltpu.PrefetchScalarGridSpec(num_scalar_...  17.6 us
    unnamed x133, local copies, waits for them, and re-layouts  16 us
  transfers between devices with their start and end apart: 59, of which 22 were waited for; matrix products, arithmetic and copies ran while one was open for 15% of the time, Pallas kernels for 37%

profile of v4, /device:TPU:0, one launch (start us, length us, event | category | flops | bytes accessed | tf_op | source)
XLA Modules:
  0.0 673.2 jit_solution(3831677226166326787)
XLA Ops:
  8.1 1.8 convert_element_type.345
  12.2 3.9 collective-permute-start.2
  16.8 4.4 fusion.13
  21.3 2.9 collective-permute-start.7
  25.0 3.0 collective-permute-start.4
  28.2 10.2 %collective-permute-done.7 = bf16[592,256]{1,0:T(8,128)(2,1)S(1)} collective-permute-done((bf16[592,256]{1,0:T(8,128)(2,1)S(1)}, bf16[592,256]{1,0:T(8,128)(2,1)S(1)}, u32[]{:S(2)}, u32[]{:S(2)}) %collective-permute-start.7) | collective-permute-done | bytes 303136 | tf_op jit(solution)/shard_map/ppermute | solution.py:593
  38.3 6.5 collective-permute-done.6
  44.8 6.8 %collective-permute-done.5 = bf16[592,256]{1,0:T(8,128)(2,1)S(1)} collective-permute-done((bf16[592,256]{1,0:T(8,128)(2,1)S(1)}, bf16[592,256]{1,0:T(8,128)(2,1)S(1)}, u32[]{:S(2)}, u32[]{:S(2)}) %collective-permute-start.5) | collective-permute-done | bytes 303136 | tf_op jit(solution)/shard_map/ppermute | solution.py:593
  52.8 2.6 collective-permute-start.8
  60.6 3.1 collective-permute-done.10
  63.7 2.5 collective-permute-done.11
  67.2 26.7 %collective-permute-done.8 = bf16[1,1776,256]{2,1,0:T(8,128)(2,1)} collective-permute-done((bf16[1,1776,256]{2,1,0:T(8,128)(2,1)S(1)}, bf16[1,1776,256]{2,1,0:T(8,128)(2,1)}, u32[]{:S(2)}, u32[]{:S(2)}) %collective-permute-start.8) | collective-permute-done | bytes 909344 | tf_op jit(solution)/shard_map/ppermute | solution.py:593
  93.9 2.6 pad_maximum_fusion.2.refs_0_
  109.5 3.1 place_blocks.4.refs_1_
  113.5 3.1 collective-permute-done.16
  116.6 3.3 collective-permute-done.15
  120.0 2.2 collective-permute-done.14
  123.1 3.3 place_blocks.5.refs_2_
  129.6 13.8 %rows_into.1.refs_0_.b_ref = bf16[2048,2048]{1,0:T(8,128)(2,1)} custom-call(bf16[2048,2048]{1,0:T(8,128)(2,1)} %bitcast.265, f32[1,2048]{1,0:T(1,128)} %bitcast.285), custom_call_target="tpu_custom_call" | custom-call | tf_op jit(solution)/shard_map/rows_into/pallas_call | solution.py:813
  144.2 3.7 place.2.refs_3_
  152.0 8.6 %matmul_nt.2.bc_ref.refs_3_ = f32[2048,384]{1,0:T(8,128)} custom-call(bf16[2048,2048]{1,0:T(8,128)(2,1)} %rows_into.1.refs_0_.b_ref, bf16[384,2048]{1,0:T(8,128)(2,1)} %maximum_maximum_fusion.refs_1_), custom_call_target="tpu_custom_call" | custom-call | flops 3221225472 | bytes 11534336 | tf_op jit(solution)/shard_map/matmul_nt/pallas_call | solution.py:704
  166.8 5.9 place_blocks.6.refs_2_
  173.0 2.1 constant_dynamic-update-slice_fusion.1
  175.1 5.3 place_blocks.7.refs_1_
  180.4 25.3 %matmul_nt.3.gate_ref.xin_ref.refs_1_.refs_2_ = f32[2048,2048]{1,0:T(8,128)} custom-call(bf16[2048,2048]{1,0:T(8,128)(2,1)} %rows_into.1.refs_0_.b_ref, bf16[2048,2048]{1,0:T(8,128)(2,1)} %place_blocks.7.refs_1_), custom_call_target="tpu_custom_call" | custom-call | flops 17179869184 | bytes 25165824 | tf_op jit(solution)/shard_map/matmul_nt/pallas_call | solution.py:704
  205.7 1.9 constant_dynamic-update-slice_fusion
  207.6 3.7 collective-permute-start.22
  211.3 18.0 %mix_forward.2 = (f32[1024,1024]{1,0:T(8,128)}, f32[1024,1024]{1,0:T(8,128)}, bf16[2,4,128,1024]{3,2,1,0:T(8,128)(2,1)S(1)}, f32[1024,1]{1,0:T(8,128)S(1)}) custom-call(s32[2,4]{1,0:T(2,128)S(1)} %get-tuple-element.144.starts_ref.refs_0_, f32[2048,2048]{1,0:T(8,128)} %matmul_nt.3.gate_ref.xin_ref.refs_1_.refs_2_, ...), custom_call_target="tpu_custom_call" | custom-call | flops 18874368000 | bytes 12582912 | tf_op jit(solution)/shard_map/mix_forward/pallas_call | solution.py:434
  231.4 3.5 collective-permute-done.22
  237.2 18.2 %mix_forward.3 = (f32[1024,1024]{1,0:T(8,128)}, f32[1024,1024]{1,0:T(8,128)}, bf16[2,4,128,1024]{3,2,1,0:T(8,128)(2,1)S(1)}, f32[1024,1]{1,0:T(8,128)S(1)}) custom-call(s32[2,4]{1,0:T(2,128)S(1)} %get-tuple-element.147.starts_ref.refs_0_, f32[2048,2048]{1,0:T(8,128)} %matmul_nt.3.gate_ref.xin_ref.refs_1_.refs_2_, ...), custom_call_target="tpu_custom_call" | custom-call | flops 18874368000 | bytes 12582912 | tf_op jit(solution)/shard_map/mix_forward/pallas_call | solution.py:434
  258.8 2.7 collective-permute-start.26
  264.8 5.5 place.3.w_ref.refs_1_
  270.3 4.0 multiply_convert_fusion.1
  274.3 2.5 pad_maximum_fusion.mixed_ref.refs_0_
  276.7 15.8 %mixed_gradient.1 = (bf16[2048,1024]{1,0:T(8,128)(2,1)}, f32[2048,1]{1,0:T(8,128)}) custom-call(bf16[2048,2048]{1,0:T(8,128)(2,1)} %bitcast.263, bf16[1024,2048]{1,0:T(8,128)(2,1)} %place.3.w_ref.refs_1_, f32[2048,1]{1,0:T(8,128)} %copy.192.live_ref, bf16[2048,1024]{1,0:T(8,128)(2,1)} %pad_maximum_fusion.mixed_ref.refs_0_), custom_call_target="tpu_custom_call" | custom-call | tf_op jit(solution)/shard_map/mixed_gradient/pallas_call | solution.py:769
  294.1 13.8 %matmul_tn.1 = bf16[1024,2048]{1,0:T(8,128)(2,1)} custom-call(bf16[2048,1024]{1,0:T(8,128)(2,1)} %pad_maximum_fusion.mixed_ref.refs_0_, bf16[2048,2048]{1,0:T(8,128)(2,1)} %bitcast.264, bf16[2048,1]{1,0:T(8,128)(2,1)} %copy.193.refs_2_), custom_call_target="tpu_custom_call" | custom-call | flops 8589934592 | bytes 16777216 | tf_op jit(solution)/shard_map/matmul_tn/pallas_call | solution.py:704
  307.9 14.8 %matmul_nn.2 = bf16[2048,2048]{1,0:T(8,128)(2,1)} custom-call(bf16[2048,1024]{1,0:T(8,128)(2,1)} %pad_maximum_fusion.mixed_ref.refs_0_, bf16[1024,2048]{1,0:T(8,128)(2,1)} %place.3.w_ref.refs_1_), custom_call_target="tpu_custom_call" | custom-call | flops 8589934592 | bytes 16777216 | tf_op jit(solution)/shard_map/matmul_nn/pallas_call | solution.py:704
  323.0 2.7 collective-permute-start.29
  333.1 41.8 %mix_backward.2 = (bf16[2048,2048]{1,0:T(8,128)(2,1)}, bf16[1024,256]{1,0:T(8,128)(2,1)S(1)}, f32[16,1024]{1,0:T(8,128)S(1)}, f32[2,1,1024]{2,1,0:T(1,128)S(1)},...) custom-call(s32[2,4]{1,0:T(2,128)S(1)} %get-tuple-element.144.starts, ...), custom_call_target="tpu_custom_call" | custom-call | flops 44040192000 | bytes 12582912 | tf_op jit(solution)/shard_map/mix_backward/pallas_call | solution.py:510
  374.9 42.3 %mix_backward.3 = (bf16[2048,2048]{1,0:T(8,128)(2,1)}, bf16[1024,256]{1,0:T(8,128)(2,1)S(1)}, f32[16,1024]{1,0:T(8,128)S(1)}, f32[2,1,1024]{2,1,0:T(1,128)S(1)},...) custom-call(s32[2,4]{1,0:T(2,128)S(1)} %get-tuple-element.147.starts, ...), custom_call_target="tpu_custom_call", output_to_operand_aliasing={{0}: (18, {})} | custom-call | flops 44040192000 | bytes 12582912 | tf_op jit(solution)/shard_map/mix_backward/pallas_call | solution.py:510
  418.0 6.3 convolution_convert_fusion
  426.0 28.0 %matmul_nn.3 = bf16[2048,2048]{1,0:T(8,128)(2,1)} custom-call(bf16[2048,2048]{1,0:T(8,128)(2,1)} %get-tuple-element.175.refs_0_.a_ref, bf16[2048,2048]{1,0:T(8,128)(2,1)} %place_blocks.7.refs_1_, bf16[2048,320]{1,0:T(8,128)(2,1)} %pad_maximum_fusion.3.refs_2_, bf16[320,2048]{1,0:T(8,128)(2,1)} %place.2.refs_3_), custom_call_target="tpu_custom_call" | custom-call | flops 17179869184 | bytes 25165824 | tf_op jit(solution)/shard_map/matmul_nn/pallas_call | solution.py:704
  455.4 1.7 collective-permute-start.33
  459.5 27.6 %matmul_blocks.1 = (bf16[2048,1024]{1,0:T(8,128)(2,1)}, bf16[2048,1024]{1,0:T(8,128)(2,1)}) custom-call(s32[8]{0:T(128)} %stack.256.chosen_ref, bf16[2048,2048]{1,0:T(8,128)(2,1)} %get-tuple-element.175.refs_0_.a_ref, bf16[2048,2048]{1,0:T(8,128)(2,1)} %rows_into.1.refs_0_.b_ref), custom_call_target="tpu_custom_call" | custom-call | tf_op jit(solution)/shard_map/matmul_blocks/pallas_call | solution.py:731
  487.4 7.4 %collective-permute-done.34 = bf16[2048,1024]{1,0:T(8,128)(2,1)} collective-permute-done((bf16[2048,1024]{1,0:T(8,128)(2,1)}, bf16[2048,1024]{1,0:T(8,128)(2,1)}, u32[]{:S(2)}, u32[]{:S(2)}) %collective-permute-start.34) | collective-permute-done | bytes 4194336 | tf_op jit(solution)/shard_map/ppermute | solution.py:593
  494.8 3.7 fusion.31
  498.6 1.9 collective-permute-start.35
  504.7 51.6 %collective-permute-done.37 = bf16[320,256]{1,0:T(8,128)(2,1)S(1)} collective-permute-done((bf16[320,256]{1,0:T(8,128)(2,1)S(1)}, bf16[320,256]{1,0:T(8,128)(2,1)S(1)}, u32[]{:S(2)}, u32[]{:S(2)}) %collective-permute-start.37) | collective-permute-done | bytes 163872 | tf_op jit(solution)/shard_map/ppermute | solution.py:593
  557.3 2.7 fusion.19
  562.6 2.1 collective-permute-start.40
  565.0 32.1 %collective-permute-done.40 = bf16[320,256]{1,0:T(8,128)(2,1)S(1)} collective-permute-done((bf16[320,256]{1,0:T(8,128)(2,1)S(1)}, bf16[320,256]{1,0:T(8,128)(2,1)S(1)}, u32[]{:S(2)}, u32[]{:S(2)}) %collective-permute-start.40) | collective-permute-done | bytes 163872 | tf_op jit(solution)/shard_map/ppermute | solution.py:593
  597.1 3.0 add_convert_fusion
  602.1 1.7 collective-permute-start.41
  603.9 7.5 %collective-permute-done.43 = bf16[592,256]{1,0:T(8,128)(2,1)} collective-permute-done((bf16[592,256]{1,0:T(8,128)(2,1)S(1)}, bf16[592,256]{1,0:T(8,128)(2,1)}, u32[]{:S(2)}, u32[]{:S(2)}) %collective-permute-start.43) | collective-permute-done | bytes 303136 | tf_op jit(solution)/shard_map/ppermute | solution.py:593
  611.4 3.6 collective-permute-done.42
  617.5 4.0 fusion.8
  622.6 1.8 collective-permute-start.50
  631.6 6.5 fusion.12
  639.2 1.8 collective-permute-start.45
  641.0 2.1 collective-permute-done.51
  644.1 3.0 collective-permute-done.52
  647.4 3.7 fusion.7
  656.6 3.9 multiply_subtract_fusion.1
  662.3 4.0 multiply_subtract_fusion
  (435 shorter events, 94.6 us)
Async XLA Ops:
  7.2 122.4 %all-gather.5.cloned.1.call-start = ((), (), s32[]{:S(2)}) async-start(), calls=%async_computation.6 | async-start | bytes 10485760 | tf_op jit(solution)/shard_map/all_gather | solution.py:924
  7.9 268.8 %all-gather.7.cloned.1.call-start = ((), (), s32[]{:S(2)}) async-start(), calls=%async_computation.7 | async-start | bytes 10485760 | tf_op jit(solution)/shard_map/all_gather | solution.py:925
  9.9 2.1 collective-permute-start.3
  12.2 12.6 %collective-permute-start.2 = (bf16[1,7034]{1,0:T(2,128)(2,1)S(1)}, bf16[1,7034]{1,0:T(2,128)(2,1)S(1)}, u32[]{:S(2)}, u32[]{:S(2)}) collective-permute-start(bf16[1,7034]{1,0:T(2,128)(2,1)S(1)} %broadcast_in_dim.74), channel_id=1, source_target_pairs={{0,3},{1,2},{2,1},{3,0},{4,7},{5,6},{6,5},{7,4},{8,11},{9,10},{10,... | collective-permute-start | bytes 42212 | tf_op jit(solution)/shard_map/ppermute | solution.py:593
  16.1 8.9 %collective-permute-start.1 = (bf16[1,7034]{1,0:T(2,128)(2,1)S(1)}, bf16[1,7034]{1,0:T(2,128)(2,1)S(1)}, u32[]{:S(2)}, u32[]{:S(2)}) collective-permute-start(bf16[1,7034]{1,0:T(2,128)(2,1)S(1)} %broadcast_in_dim.74), channel_id=1, source_target_pairs={{0,2},{1,3},{2,0},{3,1},{4,6},{5,7},{6,4},{7,5},{8,10},{9,11},{10,... | collective-permute-start | bytes 42212 | tf_op jit(solution)/shard_map/ppermute | solution.py:593
  16.6 11.4 %collective-permute-start = (bf16[1,7034]{1,0:T(2,128)(2,1)S(1)}, bf16[1,7034]{1,0:T(2,128)(2,1)S(1)}, u32[]{:S(2)}, u32[]{:S(2)}) collective-permute-start(bf16[1,7034]{1,0:T(2,128)(2,1)S(1)} %broadcast_in_dim.74), channel_id=1, source_target_pairs={{0,1},{1,0},{2,3},{3,2},{4,5},{5,4},{6,7},{7,6},{8,9},{9,8},{10,11... | collective-permute-start | bytes 42212 | tf_op jit(solution)/shard_map/ppermute | solution.py:593
  21.3 17.0 %collective-permute-start.7 = (bf16[592,256]{1,0:T(8,128)(2,1)S(1)}, bf16[592,256]{1,0:T(8,128)(2,1)S(1)}, u32[]{:S(2)}, u32[]{:S(2)}) collective-permute-start(bf16[592,256]{1,0:T(8,128)(2,1)S(1)} %get-tuple-element.271), channel_id=1, source_target_pairs={{0,3},{1,2},{2,1},{3,0},{4,7},{5,6},{6,5},{7,4},{8,11},{9,10},{10,... | collective-permute-start | bytes 909320 | tf_op jit(solution)/shard_map/ppermute | solution.py:593
  24.3 20.5 %collective-permute-start.6 = (bf16[592,256]{1,0:T(8,128)(2,1)S(1)}, bf16[592,256]{1,0:T(8,128)(2,1)S(1)}, u32[]{:S(2)}, u32[]{:S(2)}) collective-permute-start(bf16[592,256]{1,0:T(8,128)(2,1)S(1)} %get-tuple-element.272), channel_id=1, source_target_pairs={{0,2},{1,3},{2,0},{3,1},{4,6},{5,7},{6,4},{7,5},{8,10},{9,11},{10,... | collective-permute-start | bytes 909320 | tf_op jit(solution)/shard_map/ppermute | solution.py:593
  24.8 32.1 %copy-start.13 = (f32[1024,256]{1,0:T(8,128)S(1)}, f32[1024,256]{1,0:T(8,128)}, u32[]{:S(2)}) copy-start(f32[1024,256]{1,0:T(8,128)} %param.36) | copy-start | bytes 3145732
  24.8 26.8 %collective-permute-start.5 = (bf16[592,256]{1,0:T(8,128)(2,1)S(1)}, bf16[592,256]{1,0:T(8,128)(2,1)S(1)}, u32[]{:S(2)}, u32[]{:S(2)}) collective-permute-start(bf16[592,256]{1,0:T(8,128)(2,1)S(1)} %get-tuple-element.273), channel_id=1, source_target_pairs={{0,1},{1,0},{2,3},{3,2},{4,5},{5,4},{6,7},{7,6},{8,9},{9,8},{10,11... | collective-permute-start | bytes 909320 | tf_op jit(solution)/shard_map/ppermute | solution.py:593
  25.0 26.7 %collective-permute-start.4 = (bf16[1,912,256]{2,1,0:T(8,128)(2,1)S(1)}, bf16[1,912,256]{2,1,0:T(8,128)(2,1)S(1)}, u32[]{:S(2)}, u32[]{:S(2)}) collective-permute-start(bf16[1,912,256]{2,1,0:T(8,128)(2,1)S(1)} %maximum_bitcast_fusion.1), channel_id=1, source_target_pairs={{0,16},{4,20},{8,24},{12,28},{16,0},{20,4},{24,8},{28,12},{1,17},{... | collective-permute-start | bytes 1400840 | tf_op jit(solution)/shard_map/ppermute | solution.py:593
  52.8 41.1 %collective-permute-start.8 = (bf16[1,1776,256]{2,1,0:T(8,128)(2,1)S(1)}, bf16[1,1776,256]{2,1,0:T(8,128)(2,1)}, u32[]{:S(2)}, u32[]{:S(2)}) collective-permute-start(bf16[1,1776,256]{2,1,0:T(8,128)(2,1)S(1)} %maximum_bitcast_fusion), channel_id=1, source_target_pairs={{0,16},{4,20},{8,24},{12,28},{16,0},{20,4},{24,8},{28,12},{1,17},{... | collective-permute-start | bytes 2727944 | tf_op jit(solution)/shard_map/ppermute | solution.py:593
  55.4 41.0 %collective-permute-start.9 = (bf16[2,912,256]{2,1,0:T(8,128)(2,1)}, bf16[2,912,256]{2,1,0:T(8,128)(2,1)}, u32[]{:S(2)}, u32[]{:S(2)}) collective-permute-start(bf16[2,912,256]{2,1,0:T(8,128)(2,1)} %pad_maximum_fusion.7), channel_id=1, source_target_pairs={{0,8},{4,12},{8,0},{12,4},{16,24},{20,28},{24,16},{28,20},{1,9},{5... | collective-permute-start | bytes 2801672 | tf_op jit(solution)/shard_map/ppermute | solution.py:593
  57.1 6.7 collective-permute-start.10
  58.7 7.5 %collective-permute-start.11 = (bf16[256,256]{1,0:T(8,128)(2,1)S(1)}, bf16[256,256]{1,0:T(8,128)(2,1)S(1)}, u32[]{:S(2)}, u32[]{:S(2)}) collective-permute-start(bf16[256,256]{1,0:T(8,128)(2,1)S(1)} %get-tuple-element.131), channel_id=1, source_target_pairs={{0,2},{1,3},{2,0},{3,1},{4,6},{5,7},{6,4},{7,5},{8,10},{9,11},{10,... | collective-permute-start | bytes 393224 | tf_op jit(solution)/shard_map/ppermute | solution.py:593
  59.1 7.0 %collective-permute-start.12 = (bf16[256,256]{1,0:T(8,128)(2,1)S(1)}, bf16[256,256]{1,0:T(8,128)(2,1)S(1)}, u32[]{:S(2)}, u32[]{:S(2)}) collective-permute-start(bf16[256,256]{1,0:T(8,128)(2,1)S(1)} %get-tuple-element.132), channel_id=1, source_target_pairs={{0,3},{1,2},{2,1},{3,0},{4,7},{5,6},{6,5},{7,4},{8,11},{9,10},{10,... | collective-permute-start | bytes 393224 | tf_op jit(solution)/shard_map/ppermute | solution.py:593
  66.3 30.1 %copy-start.19 = (bf16[1,912,256]{2,1,0:T(8,128)(2,1)S(1)}, bf16[1,912,256]{2,1,0:T(8,128)(2,1)}, u32[]{:S(2)}) copy-start(bf16[1,912,256]{2,1,0:T(8,128)(2,1)} %copy-done.18) | copy-start | bytes 1400836
  97.8 25.3 %collective-permute-start.13 = (bf16[4,912,256]{2,1,0:T(8,128)(2,1)S(1)}, bf16[4,912,256]{2,1,0:T(8,128)(2,1)}, u32[]{:S(2)}, u32[]{:S(2)}) collective-permute-start(bf16[4,912,256]{2,1,0:T(8,128)(2,1)S(1)} %pad_maximum_fusion.1.refs_0_), channel_id=1, source_target_pairs={{0,4},{4,0},{8,12},{12,8},{16,20},{20,16},{24,28},{28,24},{1,5},{5... | collective-permute-start | bytes 5603336 | tf_op jit(solution)/shard_map/ppermute | solution.py:593
  97.9 361.6 %reduce-scatter.4.cloned.1.call-start = ((), (), s32[]{:S(2)}) async-start(), calls=%async_computation.3 | async-start | bytes 10485760 | tf_op jit(solution)/shard_map/reduce_scatter | solution.py:1044
  105.1 11.5 %collective-permute-start.16 = (bf16[320,256]{1,0:T(8,128)(2,1)S(1)}, bf16[320,256]{1,0:T(8,128)(2,1)S(1)}, u32[]{:S(2)}, u32[]{:S(2)}) collective-permute-start(bf16[320,256]{1,0:T(8,128)(2,1)S(1)} %fusion.80), channel_id=1, source_target_pairs={{0,3},{1,2},{2,1},{3,0},{4,7},{5,6},{6,5},{7,4},{8,11},{9,10},{10,... | collective-permute-start | bytes 491528 | tf_op jit(solution)/shard_map/ppermute | solution.py:593
  106.6 13.3 %collective-permute-start.15 = (bf16[320,256]{1,0:T(8,128)(2,1)S(1)}, bf16[320,256]{1,0:T(8,128)(2,1)S(1)}, u32[]{:S(2)}, u32[]{:S(2)}) collective-permute-start(bf16[320,256]{1,0:T(8,128)(2,1)S(1)} %fusion.80), channel_id=1, source_target_pairs={{0,2},{1,3},{2,0},{3,1},{4,6},{5,7},{6,4},{7,5},{8,10},{9,11},{10,... | collective-permute-start | bytes 491528 | tf_op jit(solution)/shard_map/ppermute | solution.py:593
  108.2 13.9 %collective-permute-start.14 = (bf16[320,256]{1,0:T(8,128)(2,1)S(1)}, bf16[320,256]{1,0:T(8,128)(2,1)S(1)}, u32[]{:S(2)}, u32[]{:S(2)}) collective-permute-start(bf16[320,256]{1,0:T(8,128)(2,1)S(1)} %fusion.80), channel_id=1, source_target_pairs={{0,1},{1,0},{2,3},{3,2},{4,5},{5,4},{6,7},{7,6},{8,9},{9,8},{10,11... | collective-permute-start | bytes 491528 | tf_op jit(solution)/shard_map/ppermute | solution.py:593
  109.0 51.6 %collective-permute-start.19 = (bf16[2,1776,256]{2,1,0:T(8,128)(2,1)}, bf16[2,1776,256]{2,1,0:T(8,128)(2,1)}, u32[]{:S(2)}, u32[]{:S(2)}) collective-permute-start(bf16[2,1776,256]{2,1,0:T(8,128)(2,1)} %pad_maximum_fusion.2.refs_0_), channel_id=1, source_target_pairs={{0,8},{4,12},{8,0},{12,4},{16,24},{20,28},{24,16},{28,20},{1,9},{5... | collective-permute-start | bytes 5455880 | tf_op jit(solution)/shard_map/ppermute | solution.py:593
  126.4 17.0 %collective-permute-start.17 = (bf16[4,320,256]{2,1,0:T(8,128)(2,1)}, bf16[4,320,256]{2,1,0:T(8,128)(2,1)S(1)}, u32[]{:S(2)}, u32[]{:S(2)}) collective-permute-start(bf16[4,320,256]{2,1,0:T(8,128)(2,1)} %pad_maximum_fusion.8.refs_0_), channel_id=1, source_target_pairs={{0,4},{4,0},{8,12},{12,8},{16,20},{20,16},{24,28},{28,24},{1,5},{5... | collective-permute-start | bytes 1966088 | tf_op jit(solution)/shard_map/ppermute | solution.py:593
  129.1 46.0 %collective-permute-start.18 = (bf16[2,1776,256]{2,1,0:T(8,128)(2,1)S(1)}, bf16[2,1776,256]{2,1,0:T(8,128)(2,1)}, u32[]{:S(2)}, u32[]{:S(2)}) collective-permute-start(bf16[2,1776,256]{2,1,0:T(8,128)(2,1)S(1)} %copy-done.12), channel_id=1, source_target_pairs={{0,4},{4,0},{8,12},{12,8},{16,20},{20,16},{24,28},{28,24},{1,5},{5... | collective-permute-start | bytes 5455880 | tf_op jit(solution)/shard_map/ppermute | solution.py:593
  160.5 14.6 %collective-permute-start.20 = (bf16[2,1776,256]{2,1,0:T(8,128)(2,1)}, bf16[2,1776,256]{2,1,0:T(8,128)(2,1)}, u32[]{:S(2)}, u32[]{:S(2)}) collective-permute-start(bf16[2,1776,256]{2,1,0:T(8,128)(2,1)} %collective-permute-done.19.refs_1_), channel_id=1, source_target_pairs={{0,4},{4,0},{8,12},{12,8},{16,20},{20,16},{24,28},{28,24},{1,5},{5... | collective-permute-start | bytes 5455880 | tf_op jit(solution)/shard_map/ppermute | solution.py:593
  172.7 33.0 %collective-permute-start.21 = (bf16[1,1024,256]{2,1,0:T(8,128)(2,1)}, bf16[1,1024,256]{2,1,0:T(8,128)(2,1)}, u32[]{:S(2)}, u32[]{:S(2)}) collective-permute-start(bf16[1,1024,256]{2,1,0:T(8,128)(2,1)} %bitcast.54), channel_id=1, source_target_pairs={{0,16},{4,20},{8,24},{12,28},{16,0},{20,4},{24,8},{28,12},{1,17},{... | collective-permute-start | bytes 1572872 | tf_op jit(solution)/shard_map/ppermute | solution.py:593
  180.4 25.3 %copy-start.23 = (bf16[2,1024,256]{2,1,0:T(8,128)(2,1)S(1)}, bf16[2,1024,256]{2,1,0:T(8,128)(2,1)}, u32[]{:S(2)}) copy-start(bf16[2,1024,256]{2,1,0:T(8,128)(2,1)} %get-tuple-element.301) | copy-start | bytes 3145732
  180.4 30.9 %copy-start = (f32[2048,384]{1,0:T(8,128)S(1)}, f32[2048,384]{1,0:T(8,128)}, u32[]{:S(2)}) copy-start(f32[2048,384]{1,0:T(8,128)} %matmul_nt.2.bc_ref.refs_3_) | copy-start | bytes 9437188
  207.6 27.3 %collective-permute-start.22 = (bf16[2,1024,256]{2,1,0:T(8,128)(2,1)S(1)}, bf16[2,1024,256]{2,1,0:T(8,128)(2,1)S(1)}, u32[]{:S(2)}, u32[]{:S(2)}) collective-permute-start(bf16[2,1024,256]{2,1,0:T(8,128)(2,1)S(1)} %get-tuple-element.299), channel_id=1, source_target_pairs={{0,8},{4,12},{8,0},{12,4},{16,24},{20,28},{24,16},{28,20},{1,9},{5... | collective-permute-start | bytes 3145736 | tf_op jit(solution)/shard_map/ppermute | solution.py:593
  236.0 28.8 %collective-permute-start.24 = (bf16[4,1024,256]{2,1,0:T(8,128)(2,1)}, bf16[4,1024,256]{2,1,0:T(8,128)(2,1)}, u32[]{:S(2)}, u32[]{:S(2)}) collective-permute-start(bf16[4,1024,256]{2,1,0:T(8,128)(2,1)} %constant_dynamic-update-slice_fusion.2.refs_0_), channel_id=1, source_target_pairs={{0,4},{4,0},{8,12},{12,8},{16,20},{20,16},{24,28},{28,24},{1,5},{5... | collective-permute-start | bytes 6291464 | tf_op jit(solution)/shard_map/ppermute | solution.py:593
  258.8 11.4 %collective-permute-start.26 = (f32[4,512]{1,0:T(4,128)S(1)}, f32[4,512]{1,0:T(4,128)S(1)}, u32[]{:S(2)}, u32[]{:S(2)}) collective-permute-start(f32[4,512]{1,0:T(4,128)S(1)} %reshape.566), channel_id=1, source_target_pairs={{0,3},{1,2},{2,1},{3,0},{4,7},{5,6},{6,5},{7,4},{8,11},{9,10},{10,... | collective-permute-start | bytes 24584 | tf_op jit(solution)/shard_map/ppermute | solution.py:593
  261.5 8.7 %collective-permute-start.25 = (f32[4,512]{1,0:T(4,128)S(1)}, f32[4,512]{1,0:T(4,128)S(1)}, u32[]{:S(2)}, u32[]{:S(2)}) collective-permute-start(f32[4,512]{1,0:T(4,128)S(1)} %reshape.566), channel_id=1, source_target_pairs={{0,2},{1,3},{2,0},{3,1},{4,6},{5,7},{6,4},{7,5},{8,10},{9,11},{10,... | collective-permute-start | bytes 24584 | tf_op jit(solution)/shard_map/ppermute | solution.py:593
  262.0 8.3 %collective-permute-start.23 = (f32[4,512]{1,0:T(4,128)S(1)}, f32[4,512]{1,0:T(4,128)S(1)}, u32[]{:S(2)}, u32[]{:S(2)}) collective-permute-start(f32[4,512]{1,0:T(4,128)S(1)} %reshape.566), channel_id=1, source_target_pairs={{0,1},{1,0},{2,3},{3,2},{4,5},{5,4},{6,7},{7,6},{8,9},{9,8},{10,11... | collective-permute-start | bytes 24584 | tf_op jit(solution)/shard_map/ppermute | solution.py:593
  322.7 292.9 %reduce-scatter.8.cloned.1.call-start = ((), (), s32[]{:S(2)}) async-start(), calls=%async_computation.5 | async-start | bytes 4718592 | tf_op jit(solution)/shard_map/reduce_scatter | solution.py:1042
  323.0 4.7 collective-permute-start.29
  325.7 3.7 collective-permute-start.28
  326.2 3.7 collective-permute-start.27
  327.6 289.3 %reduce-scatter.6.cloned.1.call-start = ((), (), s32[]{:S(2)}) async-start(), calls=%async_computation.4 | async-start | bytes 10485760 | tf_op jit(solution)/shard_map/reduce_scatter | solution.py:1084
  333.1 41.8 %copy-start.6 = (bf16[2,4,128,1024]{3,2,1,0:T(8,128)(2,1)S(1)}, bf16[2,4,128,1024]{3,2,1,0:T(8,128)(2,1)}, u32[]{:S(2)}) copy-start(bf16[2,4,128,1024]{3,2,1,0:T(8,128)(2,1)} %copy-done.5) | copy-start | bytes 6291460
  424.6 29.4 %collective-permute-start.30 = (bf16[4,320,256]{2,1,0:T(8,128)(2,1)S(1)}, bf16[4,320,256]{2,1,0:T(8,128)(2,1)}, u32[]{:S(2)}, u32[]{:S(2)}) collective-permute-start(bf16[4,320,256]{2,1,0:T(8,128)(2,1)S(1)} %pad_maximum_fusion.9), channel_id=1, source_target_pairs={{0,4},{4,0},{8,12},{12,8},{16,20},{20,16},{24,28},{28,24},{1,5},{5... | collective-permute-start | bytes 1966088 | tf_op jit(solution)/shard_map/ppermute | solution.py:593
  455.4 31.8 %collective-permute-start.33 = (bf16[320,256]{1,0:T(8,128)(2,1)S(1)}, bf16[320,256]{1,0:T(8,128)(2,1)S(1)}, u32[]{:S(2)}, u32[]{:S(2)}) collective-permute-start(bf16[320,256]{1,0:T(8,128)(2,1)S(1)} %get-tuple-element.284), channel_id=1, source_target_pairs={{0,3},{1,2},{2,1},{3,0},{4,7},{5,6},{6,5},{7,4},{8,11},{9,10},{10,... | collective-permute-start | bytes 491528 | tf_op jit(solution)/shard_map/ppermute | solution.py:593
  457.1 30.1 %collective-permute-start.32 = (bf16[320,256]{1,0:T(8,128)(2,1)S(1)}, bf16[320,256]{1,0:T(8,128)(2,1)S(1)}, u32[]{:S(2)}, u32[]{:S(2)}) collective-permute-start(bf16[320,256]{1,0:T(8,128)(2,1)S(1)} %get-tuple-element.285), channel_id=1, source_target_pairs={{0,2},{1,3},{2,0},{3,1},{4,6},{5,7},{6,4},{7,5},{8,10},{9,11},{10,... | collective-permute-start | bytes 491528 | tf_op jit(solution)/shard_map/ppermute | solution.py:593
  457.5 29.7 %collective-permute-start.31 = (bf16[320,256]{1,0:T(8,128)(2,1)S(1)}, bf16[320,256]{1,0:T(8,128)(2,1)S(1)}, u32[]{:S(2)}, u32[]{:S(2)}) collective-permute-start(bf16[320,256]{1,0:T(8,128)(2,1)S(1)} %get-tuple-element.286), channel_id=1, source_target_pairs={{0,1},{1,0},{2,3},{3,2},{4,5},{5,4},{6,7},{7,6},{8,9},{9,8},{10,11... | collective-permute-start | bytes 491528 | tf_op jit(solution)/shard_map/ppermute | solution.py:593
  487.2 7.6 %collective-permute-start.34 = (bf16[2048,1024]{1,0:T(8,128)(2,1)}, bf16[2048,1024]{1,0:T(8,128)(2,1)}, u32[]{:S(2)}, u32[]{:S(2)}) collective-permute-start(bf16[2048,1024]{1,0:T(8,128)(2,1)} %get-tuple-element.178), channel_id=1, source_target_pairs={{0,4},{4,0},{8,12},{12,8},{16,20},{20,16},{24,28},{28,24},{1,5},{5... | collective-permute-start | bytes 12582920 | tf_op jit(solution)/shard_map/ppermute | solution.py:593
  498.6 57.7 %collective-permute-start.35 = (bf16[2,592,512]{2,1,0:T(8,128)(2,1)S(1)}, bf16[2,592,512]{2,1,0:T(8,128)(2,1)}, u32[]{:S(2)}, u32[]{:S(2)}) collective-permute-start(bf16[2,592,512]{2,1,0:T(8,128)(2,1)S(1)} %pad_maximum_fusion.4), channel_id=1, source_target_pairs={{0,8},{4,12},{8,0},{12,4},{16,24},{20,28},{24,16},{28,20},{1,9},{5... | collective-permute-start | bytes 3637256 | tf_op jit(solution)/shard_map/ppermute | solution.py:593
  501.6 55.7 %collective-permute-start.36 = (bf16[2,592,512]{2,1,0:T(8,128)(2,1)}, bf16[2,592,512]{2,1,0:T(8,128)(2,1)}, u32[]{:S(2)}, u32[]{:S(2)}) collective-permute-start(bf16[2,592,512]{2,1,0:T(8,128)(2,1)} %pad_maximum_fusion.5), channel_id=1, source_target_pairs={{0,16},{4,20},{8,24},{12,28},{16,0},{20,4},{24,8},{28,12},{1,17},{... | collective-permute-start | bytes 3637256 | tf_op jit(solution)/shard_map/ppermute | solution.py:593
  503.2 53.1 %collective-permute-start.37 = (bf16[320,256]{1,0:T(8,128)(2,1)S(1)}, bf16[320,256]{1,0:T(8,128)(2,1)S(1)}, u32[]{:S(2)}, u32[]{:S(2)}) collective-permute-start(bf16[320,256]{1,0:T(8,128)(2,1)S(1)} %fusion.36), channel_id=1, source_target_pairs={{0,8},{4,12},{8,0},{12,4},{16,24},{20,28},{24,16},{28,20},{1,9},{5... | collective-permute-start | bytes 491528 | tf_op jit(solution)/shard_map/ppermute | solution.py:593
  560.0 37.1 %collective-permute-start.39 = (bf16[592,512]{1,0:T(8,128)(2,1)S(1)}, bf16[592,512]{1,0:T(8,128)(2,1)S(1)}, u32[]{:S(2)}, u32[]{:S(2)}) collective-permute-start(bf16[592,512]{1,0:T(8,128)(2,1)S(1)} %get-tuple-element.260), channel_id=1, source_target_pairs={{0,8},{4,12},{8,0},{12,4},{16,24},{20,28},{24,16},{28,20},{1,9},{5... | collective-permute-start | bytes 1818632 | tf_op jit(solution)/shard_map/ppermute | solution.py:593
  561.6 35.6 %collective-permute-start.38 = (bf16[592,512]{1,0:T(8,128)(2,1)S(1)}, bf16[592,512]{1,0:T(8,128)(2,1)S(1)}, u32[]{:S(2)}, u32[]{:S(2)}) collective-permute-start(bf16[592,512]{1,0:T(8,128)(2,1)S(1)} %get-tuple-element.261), channel_id=1, source_target_pairs={{0,16},{4,20},{8,24},{12,28},{16,0},{20,4},{24,8},{28,12},{1,17},{... | collective-permute-start | bytes 1818632 | tf_op jit(solution)/shard_map/ppermute | solution.py:593
  562.6 34.5 %collective-permute-start.40 = (bf16[320,256]{1,0:T(8,128)(2,1)S(1)}, bf16[320,256]{1,0:T(8,128)(2,1)S(1)}, u32[]{:S(2)}, u32[]{:S(2)}) collective-permute-start(bf16[320,256]{1,0:T(8,128)(2,1)S(1)} %add_convert_fusion.11), channel_id=1, source_target_pairs={{0,16},{4,20},{8,24},{12,28},{16,0},{20,4},{24,8},{28,12},{1,17},{... | collective-permute-start | bytes 491528 | tf_op jit(solution)/shard_map/ppermute | solution.py:593
  600.2 11.2 %collective-permute-start.43 = (bf16[592,256]{1,0:T(8,128)(2,1)S(1)}, bf16[592,256]{1,0:T(8,128)(2,1)}, u32[]{:S(2)}, u32[]{:S(2)}) collective-permute-start(bf16[592,256]{1,0:T(8,128)(2,1)S(1)} %get-tuple-element.287), channel_id=1, source_target_pairs={{0,3},{1,2},{2,1},{3,0},{4,7},{5,6},{6,5},{7,4},{8,11},{9,10},{10,... | collective-permute-start | bytes 909320 | tf_op jit(solution)/shard_map/ppermute | solution.py:593
  601.6 13.4 %collective-permute-start.42 = (bf16[592,256]{1,0:T(8,128)(2,1)S(1)}, bf16[592,256]{1,0:T(8,128)(2,1)}, u32[]{:S(2)}, u32[]{:S(2)}) collective-permute-start(bf16[592,256]{1,0:T(8,128)(2,1)S(1)} %get-tuple-element.288), channel_id=1, source_target_pairs={{0,2},{1,3},{2,0},{3,1},{4,6},{5,7},{6,4},{7,5},{8,10},{9,11},{10,... | collective-permute-start | bytes 909320 | tf_op jit(solution)/shard_map/ppermute | solution.py:593
  602.1 13.3 %collective-permute-start.41 = (bf16[592,256]{1,0:T(8,128)(2,1)S(1)}, bf16[592,256]{1,0:T(8,128)(2,1)}, u32[]{:S(2)}, u32[]{:S(2)}) collective-permute-start(bf16[592,256]{1,0:T(8,128)(2,1)S(1)} %get-tuple-element.289), channel_id=1, source_target_pairs={{0,1},{1,0},{2,3},{3,2},{4,5},{5,4},{6,7},{7,6},{8,9},{9,8},{10,11... | collective-permute-start | bytes 909320 | tf_op jit(solution)/shard_map/ppermute | solution.py:593
  622.3 15.9 %collective-permute-start.48 = (f32[1,7024]{1,0:T(1,128)S(1)}, f32[1,7024]{1,0:T(1,128)S(1)}, u32[]{:S(2)}, u32[]{:S(2)}) collective-permute-start(f32[1,7024]{1,0:T(1,128)S(1)} %get-tuple-element.311), channel_id=1, source_target_pairs={{0,1},{1,0},{2,3},{3,2},{4,5},{5,4},{6,7},{7,6},{8,9},{9,8},{10,11... | collective-permute-start | bytes 84296 | tf_op jit(solution)/shard_map/ppermute | solution.py:593
  622.6 15.6 %collective-permute-start.50 = (f32[1,7024]{1,0:T(1,128)S(1)}, f32[1,7024]{1,0:T(1,128)S(1)}, u32[]{:S(2)}, u32[]{:S(2)}) collective-permute-start(f32[1,7024]{1,0:T(1,128)S(1)} %get-tuple-element.312), channel_id=1, source_target_pairs={{0,3},{1,2},{2,1},{3,0},{4,7},{5,6},{6,5},{7,4},{8,11},{9,10},{10,... | collective-permute-start | bytes 84296 | tf_op jit(solution)/shard_map/ppermute | solution.py:593
  624.5 13.8 %collective-permute-start.49 = (f32[1,7024]{1,0:T(1,128)S(1)}, f32[1,7024]{1,0:T(1,128)S(1)}, u32[]{:S(2)}, u32[]{:S(2)}) collective-permute-start(f32[1,7024]{1,0:T(1,128)S(1)} %get-tuple-element.313), channel_id=1, source_target_pairs={{0,2},{1,3},{2,0},{3,1},{4,6},{5,7},{6,4},{7,5},{8,10},{9,11},{10,... | collective-permute-start | bytes 84296 | tf_op jit(solution)/shard_map/ppermute | solution.py:593
  626.6 28.8 %collective-permute-start.47 = (bf16[256,256]{1,0:T(8,128)(2,1)}, bf16[256,256]{1,0:T(8,128)(2,1)}, u32[]{:S(2)}, u32[]{:S(2)}) collective-permute-start(bf16[256,256]{1,0:T(8,128)(2,1)} %get-tuple-element.296), channel_id=1, source_target_pairs={{0,3},{1,2},{2,1},{3,0},{4,7},{5,6},{6,5},{7,4},{8,11},{9,10},{10,... | collective-permute-start | bytes 393224 | tf_op jit(solution)/shard_map/ppermute | solution.py:593
  638.3 4.8 collective-permute-start.51
  638.4 17.0 %collective-permute-start.46 = (bf16[256,256]{1,0:T(8,128)(2,1)}, bf16[256,256]{1,0:T(8,128)(2,1)}, u32[]{:S(2)}, u32[]{:S(2)}) collective-permute-start(bf16[256,256]{1,0:T(8,128)(2,1)} %get-tuple-element.297), channel_id=1, source_target_pairs={{0,2},{1,3},{2,0},{3,1},{4,6},{5,7},{6,4},{7,5},{8,10},{9,11},{10,... | collective-permute-start | bytes 393224 | tf_op jit(solution)/shard_map/ppermute | solution.py:593
  639.2 16.2 %collective-permute-start.45 = (bf16[256,256]{1,0:T(8,128)(2,1)}, bf16[256,256]{1,0:T(8,128)(2,1)}, u32[]{:S(2)}, u32[]{:S(2)}) collective-permute-start(bf16[256,256]{1,0:T(8,128)(2,1)} %get-tuple-element.298), channel_id=1, source_target_pairs={{0,1},{1,0},{2,3},{3,2},{4,5},{5,4},{6,7},{7,6},{8,9},{9,8},{10,11... | collective-permute-start | bytes 393224 | tf_op jit(solution)/shard_map/ppermute | solution.py:593
  643.2 3.9 collective-permute-start.52
  644.1 16.4 %collective-permute-start.44 = (bf16[256,1064]{0,1:T(8,128)(2,1)}, bf16[256,1064]{0,1:T(8,128)(2,1)}, u32[]{:S(2)}, u32[]{:S(2)}) collective-permute-start(bf16[256,1064]{0,1:T(8,128)(2,1)} %broadcast_select_fusion.2), channel_id=1, source_target_pairs={{0,4},{4,0},{8,12},{12,8},{16,20},{20,16},{24,28},{28,24},{1,5},{5... | collective-permute-start | bytes 1634312 | tf_op jit(solution)/shard_map/ppermute | solution.py:593
  647.3 3.9 collective-permute-start.53
  (52 other events, 309.6 us)
Sparse Core Ops, SparseCore 0:
  9.9 115.9 all-gather.4
  127.8 87.6 all-gather.6
  322.8 85.9 reduce-scatter.3
  411.1 49.9 reduce-scatter.7
  464.4 84.5 reduce-scatter.5

commit v5 on v4

--- a/solution.py
+++ b/solution.py
@@ -783,7 +783,7 @@
 
 
 def rows_into(buffer, row, rows, length, pieces, gain=None):
-    tile = 128
+    tile = 256
     counts = [p.shape[0] // tile for p in pieces]
     starts = [sum(counts[:i]) for i in range(len(counts) + 1)]
     width = pieces[0].shape[1]

time: 682 us -> 678 us (level)
  no operation moved by 1% of the time
where the time goes in v5:
time: 678 us; the launch traced here: 670 us
  Pallas kernels  291 us (43%)
  waiting for transfers between devices  180 us (27%)
  other arithmetic  66.3 us (10%)
  starting transfers between devices  57.9 us (9%)
  local copies, waits for them, and re-layouts  38.1 us (6%)
  between operations  19.1 us (3%)
  matrix products  17.2 us (3%)
    ppermute x54, waiting for transfers between devices, swap(): return lax.ppermute(value, axis, [(i, i ^ mask) for i in range(size)])  179 us
    pallas_call x5, Pallas kernels, matmul(): pl.pallas_call(kernel, grid=(m // tm, n // tn), in_specs=in_specs, out_sp...  90.4 us
    pallas_call x2, Pallas kernels, mix_backward(): pl.pallas_call(backward_first if before is None else backward_kernel, gri...  84.2 us
    ppermute x54, starting transfers between devices, swap(): return lax.ppermute(value, axis, [(i, i ^ mask) for i in range(size)])  57.5 us
    pallas_call x2, Pallas kernels, mix_forward(): pl.pallas_call(forward_kernel, grid=(rows, channels // BC), in_specs=in_s...  36.2 us
    pallas_call x1, Pallas kernels, matmul_blocks(): pl.pallas_call(kernel, grid_spec=pltpu.PrefetchScalarGridSpec(num_scalar_...  27.6 us
    pallas_call x4, Pallas kernels, place_blocks(): pl.pallas_call(kernel, grid_spec=pltpu.PrefetchScalarGridSpec(num_scalar_...  17.1 us
    unnamed x133, local copies, waits for them, and re-layouts  16.1 us
  transfers between devices with their start and end apart: 59, of which 22 were waited for; matrix products, arithmetic and copies ran while one was open for 15% of the time, Pallas kernels for 37%

profile of v5, /device:TPU:0, one launch (start us, length us, event | category | flops | bytes accessed | tf_op | source)
XLA Modules:
  0.0 669.8 jit_solution(5957496836499436194)
XLA Ops:
  8.1 1.8 convert_element_type.345
  12.2 3.9 collective-permute-start.2
  16.8 4.4 fusion.13
  21.3 2.9 collective-permute-start.7
  25.0 3.0 collective-permute-start.4
  28.2 10.2 %collective-permute-done.7 = bf16[592,256]{1,0:T(8,128)(2,1)S(1)} collective-permute-done((bf16[592,256]{1,0:T(8,128)(2,1)S(1)}, bf16[592,256]{1,0:T(8,128)(2,1)S(1)}, u32[]{:S(2)}, u32[]{:S(2)}) %collective-permute-start.7) | collective-permute-done | bytes 303136 | tf_op jit(solution)/shard_map/ppermute | solution.py:593
  38.3 6.5 collective-permute-done.6
  44.8 6.8 %collective-permute-done.5 = bf16[592,256]{1,0:T(8,128)(2,1)S(1)} collective-permute-done((bf16[592,256]{1,0:T(8,128)(2,1)S(1)}, bf16[592,256]{1,0:T(8,128)(2,1)S(1)}, u32[]{:S(2)}, u32[]{:S(2)}) %collective-permute-start.5) | collective-permute-done | bytes 303136 | tf_op jit(solution)/shard_map/ppermute | solution.py:593
  52.8 2.6 collective-permute-start.8
  60.6 3.1 collective-permute-done.10
  63.7 2.5 collective-permute-done.11
  67.2 26.7 %collective-permute-done.8 = bf16[1,1776,256]{2,1,0:T(8,128)(2,1)} collective-permute-done((bf16[1,1776,256]{2,1,0:T(8,128)(2,1)S(1)}, bf16[1,1776,256]{2,1,0:T(8,128)(2,1)}, u32[]{:S(2)}, u32[]{:S(2)}) %collective-permute-start.8) | collective-permute-done | bytes 909344 | tf_op jit(solution)/shard_map/ppermute | solution.py:593
  93.9 2.6 pad_maximum_fusion.2.refs_0_
  109.5 3.1 place_blocks.4.refs_1_
  113.5 3.1 collective-permute-done.16
  116.6 3.3 collective-permute-done.15
  120.0 2.2 collective-permute-done.14
  123.1 3.3 place_blocks.5.refs_2_
  129.6 10.5 %rows_into.1.refs_0_.b_ref = bf16[2048,2048]{1,0:T(8,128)(2,1)} custom-call(bf16[2048,2048]{1,0:T(8,128)(2,1)} %bitcast.265, f32[1,2048]{1,0:T(1,128)} %bitcast.285), custom_call_target="tpu_custom_call" | custom-call | tf_op jit(solution)/shard_map/rows_into/pallas_call | solution.py:813
  140.9 3.7 place.2.refs_3_
  148.7 8.6 %matmul_nt.2.bc_ref.refs_3_ = f32[2048,384]{1,0:T(8,128)} custom-call(bf16[2048,2048]{1,0:T(8,128)(2,1)} %rows_into.1.refs_0_.b_ref, bf16[384,2048]{1,0:T(8,128)(2,1)} %maximum_maximum_fusion.refs_1_), custom_call_target="tpu_custom_call" | custom-call | flops 3221225472 | bytes 11534336 | tf_op jit(solution)/shard_map/matmul_nt/pallas_call | solution.py:704
  163.4 5.4 place_blocks.6.refs_2_
  169.2 2.2 constant_dynamic-update-slice_fusion.1
  171.4 5.3 place_blocks.7.refs_1_
  176.7 25.3 %matmul_nt.3.gate_ref.xin_ref.refs_1_.refs_2_ = f32[2048,2048]{1,0:T(8,128)} custom-call(bf16[2048,2048]{1,0:T(8,128)(2,1)} %rows_into.1.refs_0_.b_ref, bf16[2048,2048]{1,0:T(8,128)(2,1)} %place_blocks.7.refs_1_), custom_call_target="tpu_custom_call" | custom-call | flops 17179869184 | bytes 25165824 | tf_op jit(solution)/shard_map/matmul_nt/pallas_call | solution.py:704
  202.0 1.9 constant_dynamic-update-slice_fusion
  203.9 3.7 collective-permute-start.22
  207.6 18.0 %mix_forward.2 = (f32[1024,1024]{1,0:T(8,128)}, f32[1024,1024]{1,0:T(8,128)}, bf16[2,4,128,1024]{3,2,1,0:T(8,128)(2,1)S(1)}, f32[1024,1]{1,0:T(8,128)S(1)}) custom-call(s32[2,4]{1,0:T(2,128)S(1)} %get-tuple-element.144.starts_ref.refs_0_, f32[2048,2048]{1,0:T(8,128)} %matmul_nt.3.gate_ref.xin_ref.refs_1_.refs_2_, ...), custom_call_target="tpu_custom_call" | custom-call | flops 18874368000 | bytes 12582912 | tf_op jit(solution)/shard_map/mix_forward/pallas_call | solution.py:434
  227.7 3.4 collective-permute-done.22
  233.4 18.2 %mix_forward.3 = (f32[1024,1024]{1,0:T(8,128)}, f32[1024,1024]{1,0:T(8,128)}, bf16[2,4,128,1024]{3,2,1,0:T(8,128)(2,1)S(1)}, f32[1024,1]{1,0:T(8,128)S(1)}) custom-call(s32[2,4]{1,0:T(2,128)S(1)} %get-tuple-element.147.starts_ref.refs_0_, f32[2048,2048]{1,0:T(8,128)} %matmul_nt.3.gate_ref.xin_ref.refs_1_.refs_2_, ...), custom_call_target="tpu_custom_call" | custom-call | flops 18874368000 | bytes 12582912 | tf_op jit(solution)/shard_map/mix_forward/pallas_call | solution.py:434
  255.0 3.0 collective-permute-start.26
  261.0 5.5 place.3.w_ref.refs_1_
  266.6 4.0 multiply_convert_fusion.1
  270.5 2.5 pad_maximum_fusion.mixed_ref.refs_0_
  273.0 15.8 %mixed_gradient.1 = (bf16[2048,1024]{1,0:T(8,128)(2,1)}, f32[2048,1]{1,0:T(8,128)}) custom-call(bf16[2048,2048]{1,0:T(8,128)(2,1)} %bitcast.263, bf16[1024,2048]{1,0:T(8,128)(2,1)} %place.3.w_ref.refs_1_, f32[2048,1]{1,0:T(8,128)} %copy.192.live_ref, bf16[2048,1024]{1,0:T(8,128)(2,1)} %pad_maximum_fusion.mixed_ref.refs_0_), custom_call_target="tpu_custom_call" | custom-call | tf_op jit(solution)/shard_map/mixed_gradient/pallas_call | solution.py:769
  290.4 13.8 %matmul_tn.1 = bf16[1024,2048]{1,0:T(8,128)(2,1)} custom-call(bf16[2048,1024]{1,0:T(8,128)(2,1)} %pad_maximum_fusion.mixed_ref.refs_0_, bf16[2048,2048]{1,0:T(8,128)(2,1)} %bitcast.264, bf16[2048,1]{1,0:T(8,128)(2,1)} %copy.193.refs_2_), custom_call_target="tpu_custom_call" | custom-call | flops 8589934592 | bytes 16777216 | tf_op jit(solution)/shard_map/matmul_tn/pallas_call | solution.py:704
  304.2 14.8 %matmul_nn.2 = bf16[2048,2048]{1,0:T(8,128)(2,1)} custom-call(bf16[2048,1024]{1,0:T(8,128)(2,1)} %pad_maximum_fusion.mixed_ref.refs_0_, bf16[1024,2048]{1,0:T(8,128)(2,1)} %place.3.w_ref.refs_1_), custom_call_target="tpu_custom_call" | custom-call | flops 8589934592 | bytes 16777216 | tf_op jit(solution)/shard_map/matmul_nn/pallas_call | solution.py:704
  319.3 2.9 collective-permute-start.29
  323.9 1.9 collective-permute-done.28
  329.6 41.8 %mix_backward.2 = (bf16[2048,2048]{1,0:T(8,128)(2,1)}, bf16[1024,256]{1,0:T(8,128)(2,1)S(1)}, f32[16,1024]{1,0:T(8,128)S(1)}, f32[2,1,1024]{2,1,0:T(1,128)S(1)},...) custom-call(s32[2,4]{1,0:T(2,128)S(1)} %get-tuple-element.144.starts, ...), custom_call_target="tpu_custom_call" | custom-call | flops 44040192000 | bytes 12582912 | tf_op jit(solution)/shard_map/mix_backward/pallas_call | solution.py:510
  371.5 42.3 %mix_backward.3 = (bf16[2048,2048]{1,0:T(8,128)(2,1)}, bf16[1024,256]{1,0:T(8,128)(2,1)S(1)}, f32[16,1024]{1,0:T(8,128)S(1)}, f32[2,1,1024]{2,1,0:T(1,128)S(1)},...) custom-call(s32[2,4]{1,0:T(2,128)S(1)} %get-tuple-element.147.starts, ...), custom_call_target="tpu_custom_call", output_to_operand_aliasing={{0}: (18, {})} | custom-call | flops 44040192000 | bytes 12582912 | tf_op jit(solution)/shard_map/mix_backward/pallas_call | solution.py:510
  414.6 6.3 convolution_convert_fusion
  422.6 28.0 %matmul_nn.3 = bf16[2048,2048]{1,0:T(8,128)(2,1)} custom-call(bf16[2048,2048]{1,0:T(8,128)(2,1)} %get-tuple-element.175.refs_0_.a_ref, bf16[2048,2048]{1,0:T(8,128)(2,1)} %place_blocks.7.refs_1_, bf16[2048,320]{1,0:T(8,128)(2,1)} %pad_maximum_fusion.3.refs_2_, bf16[320,2048]{1,0:T(8,128)(2,1)} %place.2.refs_3_), custom_call_target="tpu_custom_call" | custom-call | flops 17179869184 | bytes 25165824 | tf_op jit(solution)/shard_map/matmul_nn/pallas_call | solution.py:704
  456.1 27.6 %matmul_blocks.1 = (bf16[2048,1024]{1,0:T(8,128)(2,1)}, bf16[2048,1024]{1,0:T(8,128)(2,1)}) custom-call(s32[8]{0:T(128)} %stack.256.chosen_ref, bf16[2048,2048]{1,0:T(8,128)(2,1)} %get-tuple-element.175.refs_0_.a_ref, bf16[2048,2048]{1,0:T(8,128)(2,1)} %rows_into.1.refs_0_.b_ref), custom_call_target="tpu_custom_call" | custom-call | tf_op jit(solution)/shard_map/matmul_blocks/pallas_call | solution.py:731
  483.9 7.4 %collective-permute-done.34 = bf16[2048,1024]{1,0:T(8,128)(2,1)} collective-permute-done((bf16[2048,1024]{1,0:T(8,128)(2,1)}, bf16[2048,1024]{1,0:T(8,128)(2,1)}, u32[]{:S(2)}, u32[]{:S(2)}) %collective-permute-start.34) | collective-permute-done | bytes 4194336 | tf_op jit(solution)/shard_map/ppermute | solution.py:593
  491.3 3.7 fusion.31
  495.1 1.9 collective-permute-start.35
  501.2 51.6 %collective-permute-done.37 = bf16[320,256]{1,0:T(8,128)(2,1)S(1)} collective-permute-done((bf16[320,256]{1,0:T(8,128)(2,1)S(1)}, bf16[320,256]{1,0:T(8,128)(2,1)S(1)}, u32[]{:S(2)}, u32[]{:S(2)}) %collective-permute-start.37) | collective-permute-done | bytes 163872 | tf_op jit(solution)/shard_map/ppermute | solution.py:593
  553.9 2.7 fusion.19
  559.2 2.1 collective-permute-start.40
  561.5 32.1 %collective-permute-done.40 = bf16[320,256]{1,0:T(8,128)(2,1)S(1)} collective-permute-done((bf16[320,256]{1,0:T(8,128)(2,1)S(1)}, bf16[320,256]{1,0:T(8,128)(2,1)S(1)}, u32[]{:S(2)}, u32[]{:S(2)}) %collective-permute-start.40) | collective-permute-done | bytes 163872 | tf_op jit(solution)/shard_map/ppermute | solution.py:593
  593.7 3.0 add_convert_fusion
  598.6 1.8 collective-permute-start.41
  600.5 7.5 %collective-permute-done.43 = bf16[592,256]{1,0:T(8,128)(2,1)} collective-permute-done((bf16[592,256]{1,0:T(8,128)(2,1)S(1)}, bf16[592,256]{1,0:T(8,128)(2,1)}, u32[]{:S(2)}, u32[]{:S(2)}) %collective-permute-start.43) | collective-permute-done | bytes 303136 | tf_op jit(solution)/shard_map/ppermute | solution.py:593
  607.9 3.6 collective-permute-done.42
  613.9 4.0 fusion.8
  619.1 1.8 collective-permute-start.50
  628.2 6.5 fusion.12
  635.7 1.8 collective-permute-start.45
  637.5 2.2 collective-permute-done.51
  640.7 3.0 collective-permute-done.52
  643.9 3.7 fusion.7
  653.2 3.9 multiply_subtract_fusion.1
  658.8 4.0 multiply_subtract_fusion
  (435 shorter events, 94.1 us)
Async XLA Ops:
  7.2 122.4 %all-gather.5.cloned.1.call-start = ((), (), s32[]{:S(2)}) async-start(), calls=%async_computation.6 | async-start | bytes 10485760 | tf_op jit(solution)/shard_map/all_gather | solution.py:924
  7.9 265.1 %all-gather.7.cloned.1.call-start = ((), (), s32[]{:S(2)}) async-start(), calls=%async_computation.7 | async-start | bytes 10485760 | tf_op jit(solution)/shard_map/all_gather | solution.py:925
  9.9 2.1 collective-permute-start.3
  12.2 12.6 %collective-permute-start.2 = (bf16[1,7034]{1,0:T(2,128)(2,1)S(1)}, bf16[1,7034]{1,0:T(2,128)(2,1)S(1)}, u32[]{:S(2)}, u32[]{:S(2)}) collective-permute-start(bf16[1,7034]{1,0:T(2,128)(2,1)S(1)} %broadcast_in_dim.74), channel_id=1, source_target_pairs={{0,3},{1,2},{2,1},{3,0},{4,7},{5,6},{6,5},{7,4},{8,11},{9,10},{10,... | collective-permute-start | bytes 42212 | tf_op jit(solution)/shard_map/ppermute | solution.py:593
  16.1 8.9 %collective-permute-start.1 = (bf16[1,7034]{1,0:T(2,128)(2,1)S(1)}, bf16[1,7034]{1,0:T(2,128)(2,1)S(1)}, u32[]{:S(2)}, u32[]{:S(2)}) collective-permute-start(bf16[1,7034]{1,0:T(2,128)(2,1)S(1)} %broadcast_in_dim.74), channel_id=1, source_target_pairs={{0,2},{1,3},{2,0},{3,1},{4,6},{5,7},{6,4},{7,5},{8,10},{9,11},{10,... | collective-permute-start | bytes 42212 | tf_op jit(solution)/shard_map/ppermute | solution.py:593
  16.6 11.4 %collective-permute-start = (bf16[1,7034]{1,0:T(2,128)(2,1)S(1)}, bf16[1,7034]{1,0:T(2,128)(2,1)S(1)}, u32[]{:S(2)}, u32[]{:S(2)}) collective-permute-start(bf16[1,7034]{1,0:T(2,128)(2,1)S(1)} %broadcast_in_dim.74), channel_id=1, source_target_pairs={{0,1},{1,0},{2,3},{3,2},{4,5},{5,4},{6,7},{7,6},{8,9},{9,8},{10,11... | collective-permute-start | bytes 42212 | tf_op jit(solution)/shard_map/ppermute | solution.py:593
  21.3 17.0 %collective-permute-start.7 = (bf16[592,256]{1,0:T(8,128)(2,1)S(1)}, bf16[592,256]{1,0:T(8,128)(2,1)S(1)}, u32[]{:S(2)}, u32[]{:S(2)}) collective-permute-start(bf16[592,256]{1,0:T(8,128)(2,1)S(1)} %get-tuple-element.271), channel_id=1, source_target_pairs={{0,3},{1,2},{2,1},{3,0},{4,7},{5,6},{6,5},{7,4},{8,11},{9,10},{10,... | collective-permute-start | bytes 909320 | tf_op jit(solution)/shard_map/ppermute | solution.py:593
  24.3 20.5 %collective-permute-start.6 = (bf16[592,256]{1,0:T(8,128)(2,1)S(1)}, bf16[592,256]{1,0:T(8,128)(2,1)S(1)}, u32[]{:S(2)}, u32[]{:S(2)}) collective-permute-start(bf16[592,256]{1,0:T(8,128)(2,1)S(1)} %get-tuple-element.272), channel_id=1, source_target_pairs={{0,2},{1,3},{2,0},{3,1},{4,6},{5,7},{6,4},{7,5},{8,10},{9,11},{10,... | collective-permute-start | bytes 909320 | tf_op jit(solution)/shard_map/ppermute | solution.py:593
  24.8 32.1 %copy-start.13 = (f32[1024,256]{1,0:T(8,128)S(1)}, f32[1024,256]{1,0:T(8,128)}, u32[]{:S(2)}) copy-start(f32[1024,256]{1,0:T(8,128)} %param.36) | copy-start | bytes 3145732
  24.8 26.8 %collective-permute-start.5 = (bf16[592,256]{1,0:T(8,128)(2,1)S(1)}, bf16[592,256]{1,0:T(8,128)(2,1)S(1)}, u32[]{:S(2)}, u32[]{:S(2)}) collective-permute-start(bf16[592,256]{1,0:T(8,128)(2,1)S(1)} %get-tuple-element.273), channel_id=1, source_target_pairs={{0,1},{1,0},{2,3},{3,2},{4,5},{5,4},{6,7},{7,6},{8,9},{9,8},{10,11... | collective-permute-start | bytes 909320 | tf_op jit(solution)/shard_map/ppermute | solution.py:593
  25.0 26.7 %collective-permute-start.4 = (bf16[1,912,256]{2,1,0:T(8,128)(2,1)S(1)}, bf16[1,912,256]{2,1,0:T(8,128)(2,1)S(1)}, u32[]{:S(2)}, u32[]{:S(2)}) collective-permute-start(bf16[1,912,256]{2,1,0:T(8,128)(2,1)S(1)} %maximum_bitcast_fusion.1), channel_id=1, source_target_pairs={{0,16},{4,20},{8,24},{12,28},{16,0},{20,4},{24,8},{28,12},{1,17},{... | collective-permute-start | bytes 1400840 | tf_op jit(solution)/shard_map/ppermute | solution.py:593
  52.8 41.1 %collective-permute-start.8 = (bf16[1,1776,256]{2,1,0:T(8,128)(2,1)S(1)}, bf16[1,1776,256]{2,1,0:T(8,128)(2,1)}, u32[]{:S(2)}, u32[]{:S(2)}) collective-permute-start(bf16[1,1776,256]{2,1,0:T(8,128)(2,1)S(1)} %maximum_bitcast_fusion), channel_id=1, source_target_pairs={{0,16},{4,20},{8,24},{12,28},{16,0},{20,4},{24,8},{28,12},{1,17},{... | collective-permute-start | bytes 2727944 | tf_op jit(solution)/shard_map/ppermute | solution.py:593
  55.4 41.0 %collective-permute-start.9 = (bf16[2,912,256]{2,1,0:T(8,128)(2,1)}, bf16[2,912,256]{2,1,0:T(8,128)(2,1)}, u32[]{:S(2)}, u32[]{:S(2)}) collective-permute-start(bf16[2,912,256]{2,1,0:T(8,128)(2,1)} %pad_maximum_fusion.7), channel_id=1, source_target_pairs={{0,8},{4,12},{8,0},{12,4},{16,24},{20,28},{24,16},{28,20},{1,9},{5... | collective-permute-start | bytes 2801672 | tf_op jit(solution)/shard_map/ppermute | solution.py:593
  57.1 6.7 collective-permute-start.10
  58.7 7.5 %collective-permute-start.11 = (bf16[256,256]{1,0:T(8,128)(2,1)S(1)}, bf16[256,256]{1,0:T(8,128)(2,1)S(1)}, u32[]{:S(2)}, u32[]{:S(2)}) collective-permute-start(bf16[256,256]{1,0:T(8,128)(2,1)S(1)} %get-tuple-element.131), channel_id=1, source_target_pairs={{0,2},{1,3},{2,0},{3,1},{4,6},{5,7},{6,4},{7,5},{8,10},{9,11},{10,... | collective-permute-start | bytes 393224 | tf_op jit(solution)/shard_map/ppermute | solution.py:593
  59.1 7.0 %collective-permute-start.12 = (bf16[256,256]{1,0:T(8,128)(2,1)S(1)}, bf16[256,256]{1,0:T(8,128)(2,1)S(1)}, u32[]{:S(2)}, u32[]{:S(2)}) collective-permute-start(bf16[256,256]{1,0:T(8,128)(2,1)S(1)} %get-tuple-element.132), channel_id=1, source_target_pairs={{0,3},{1,2},{2,1},{3,0},{4,7},{5,6},{6,5},{7,4},{8,11},{9,10},{10,... | collective-permute-start | bytes 393224 | tf_op jit(solution)/shard_map/ppermute | solution.py:593
  66.3 30.1 %copy-start.19 = (bf16[1,912,256]{2,1,0:T(8,128)(2,1)S(1)}, bf16[1,912,256]{2,1,0:T(8,128)(2,1)}, u32[]{:S(2)}) copy-start(bf16[1,912,256]{2,1,0:T(8,128)(2,1)} %copy-done.18) | copy-start | bytes 1400836
  97.8 25.3 %collective-permute-start.13 = (bf16[4,912,256]{2,1,0:T(8,128)(2,1)S(1)}, bf16[4,912,256]{2,1,0:T(8,128)(2,1)}, u32[]{:S(2)}, u32[]{:S(2)}) collective-permute-start(bf16[4,912,256]{2,1,0:T(8,128)(2,1)S(1)} %pad_maximum_fusion.1.refs_0_), channel_id=1, source_target_pairs={{0,4},{4,0},{8,12},{12,8},{16,20},{20,16},{24,28},{28,24},{1,5},{5... | collective-permute-start | bytes 5603336 | tf_op jit(solution)/shard_map/ppermute | solution.py:593
  97.9 358.2 %reduce-scatter.4.cloned.1.call-start = ((), (), s32[]{:S(2)}) async-start(), calls=%async_computation.3 | async-start | bytes 10485760 | tf_op jit(solution)/shard_map/reduce_scatter | solution.py:1044
  105.1 11.5 %collective-permute-start.16 = (bf16[320,256]{1,0:T(8,128)(2,1)S(1)}, bf16[320,256]{1,0:T(8,128)(2,1)S(1)}, u32[]{:S(2)}, u32[]{:S(2)}) collective-permute-start(bf16[320,256]{1,0:T(8,128)(2,1)S(1)} %fusion.80), channel_id=1, source_target_pairs={{0,3},{1,2},{2,1},{3,0},{4,7},{5,6},{6,5},{7,4},{8,11},{9,10},{10,... | collective-permute-start | bytes 491528 | tf_op jit(solution)/shard_map/ppermute | solution.py:593
  106.6 13.3 %collective-permute-start.15 = (bf16[320,256]{1,0:T(8,128)(2,1)S(1)}, bf16[320,256]{1,0:T(8,128)(2,1)S(1)}, u32[]{:S(2)}, u32[]{:S(2)}) collective-permute-start(bf16[320,256]{1,0:T(8,128)(2,1)S(1)} %fusion.80), channel_id=1, source_target_pairs={{0,2},{1,3},{2,0},{3,1},{4,6},{5,7},{6,4},{7,5},{8,10},{9,11},{10,... | collective-permute-start | bytes 491528 | tf_op jit(solution)/shard_map/ppermute | solution.py:593
  108.2 13.9 %collective-permute-start.14 = (bf16[320,256]{1,0:T(8,128)(2,1)S(1)}, bf16[320,256]{1,0:T(8,128)(2,1)S(1)}, u32[]{:S(2)}, u32[]{:S(2)}) collective-permute-start(bf16[320,256]{1,0:T(8,128)(2,1)S(1)} %fusion.80), channel_id=1, source_target_pairs={{0,1},{1,0},{2,3},{3,2},{4,5},{5,4},{6,7},{7,6},{8,9},{9,8},{10,11... | collective-permute-start | bytes 491528 | tf_op jit(solution)/shard_map/ppermute | solution.py:593
  109.0 48.3 %collective-permute-start.19 = (bf16[2,1776,256]{2,1,0:T(8,128)(2,1)}, bf16[2,1776,256]{2,1,0:T(8,128)(2,1)}, u32[]{:S(2)}, u32[]{:S(2)}) collective-permute-start(bf16[2,1776,256]{2,1,0:T(8,128)(2,1)} %pad_maximum_fusion.2.refs_0_), channel_id=1, source_target_pairs={{0,8},{4,12},{8,0},{12,4},{16,24},{20,28},{24,16},{28,20},{1,9},{5... | collective-permute-start | bytes 5455880 | tf_op jit(solution)/shard_map/ppermute | solution.py:593
  126.4 13.7 %collective-permute-start.17 = (bf16[4,320,256]{2,1,0:T(8,128)(2,1)}, bf16[4,320,256]{2,1,0:T(8,128)(2,1)S(1)}, u32[]{:S(2)}, u32[]{:S(2)}) collective-permute-start(bf16[4,320,256]{2,1,0:T(8,128)(2,1)} %pad_maximum_fusion.8.refs_0_), channel_id=1, source_target_pairs={{0,4},{4,0},{8,12},{12,8},{16,20},{20,16},{24,28},{28,24},{1,5},{5... | collective-permute-start | bytes 1966088 | tf_op jit(solution)/shard_map/ppermute | solution.py:593
  129.1 42.3 %collective-permute-start.18 = (bf16[2,1776,256]{2,1,0:T(8,128)(2,1)S(1)}, bf16[2,1776,256]{2,1,0:T(8,128)(2,1)}, u32[]{:S(2)}, u32[]{:S(2)}) collective-permute-start(bf16[2,1776,256]{2,1,0:T(8,128)(2,1)S(1)} %copy-done.12), channel_id=1, source_target_pairs={{0,4},{4,0},{8,12},{12,8},{16,20},{20,16},{24,28},{28,24},{1,5},{5... | collective-permute-start | bytes 5455880 | tf_op jit(solution)/shard_map/ppermute | solution.py:593
  157.2 14.2 %collective-permute-start.20 = (bf16[2,1776,256]{2,1,0:T(8,128)(2,1)}, bf16[2,1776,256]{2,1,0:T(8,128)(2,1)}, u32[]{:S(2)}, u32[]{:S(2)}) collective-permute-start(bf16[2,1776,256]{2,1,0:T(8,128)(2,1)} %collective-permute-done.19.refs_1_), channel_id=1, source_target_pairs={{0,4},{4,0},{8,12},{12,8},{16,20},{20,16},{24,28},{28,24},{1,5},{5... | collective-permute-start | bytes 5455880 | tf_op jit(solution)/shard_map/ppermute | solution.py:593
  168.9 33.1 %collective-permute-start.21 = (bf16[1,1024,256]{2,1,0:T(8,128)(2,1)}, bf16[1,1024,256]{2,1,0:T(8,128)(2,1)}, u32[]{:S(2)}, u32[]{:S(2)}) collective-permute-start(bf16[1,1024,256]{2,1,0:T(8,128)(2,1)} %bitcast.54), channel_id=1, source_target_pairs={{0,16},{4,20},{8,24},{12,28},{16,0},{20,4},{24,8},{28,12},{1,17},{... | collective-permute-start | bytes 1572872 | tf_op jit(solution)/shard_map/ppermute | solution.py:593
  176.7 25.3 %copy-start.23 = (bf16[2,1024,256]{2,1,0:T(8,128)(2,1)S(1)}, bf16[2,1024,256]{2,1,0:T(8,128)(2,1)}, u32[]{:S(2)}) copy-start(bf16[2,1024,256]{2,1,0:T(8,128)(2,1)} %get-tuple-element.301) | copy-start | bytes 3145732
  176.7 30.9 %copy-start = (f32[2048,384]{1,0:T(8,128)S(1)}, f32[2048,384]{1,0:T(8,128)}, u32[]{:S(2)}) copy-start(f32[2048,384]{1,0:T(8,128)} %matmul_nt.2.bc_ref.refs_3_) | copy-start | bytes 9437188
  203.9 27.2 %collective-permute-start.22 = (bf16[2,1024,256]{2,1,0:T(8,128)(2,1)S(1)}, bf16[2,1024,256]{2,1,0:T(8,128)(2,1)S(1)}, u32[]{:S(2)}, u32[]{:S(2)}) collective-permute-start(bf16[2,1024,256]{2,1,0:T(8,128)(2,1)S(1)} %get-tuple-element.299), channel_id=1, source_target_pairs={{0,8},{4,12},{8,0},{12,4},{16,24},{20,28},{24,16},{28,20},{1,9},{5... | collective-permute-start | bytes 3145736 | tf_op jit(solution)/shard_map/ppermute | solution.py:593
  232.2 28.9 %collective-permute-start.24 = (bf16[4,1024,256]{2,1,0:T(8,128)(2,1)}, bf16[4,1024,256]{2,1,0:T(8,128)(2,1)}, u32[]{:S(2)}, u32[]{:S(2)}) collective-permute-start(bf16[4,1024,256]{2,1,0:T(8,128)(2,1)} %constant_dynamic-update-slice_fusion.2.refs_0_), channel_id=1, source_target_pairs={{0,4},{4,0},{8,12},{12,8},{16,20},{20,16},{24,28},{28,24},{1,5},{5... | collective-permute-start | bytes 6291464 | tf_op jit(solution)/shard_map/ppermute | solution.py:593
  255.0 11.5 %collective-permute-start.26 = (f32[4,512]{1,0:T(4,128)S(1)}, f32[4,512]{1,0:T(4,128)S(1)}, u32[]{:S(2)}, u32[]{:S(2)}) collective-permute-start(f32[4,512]{1,0:T(4,128)S(1)} %reshape.566), channel_id=1, source_target_pairs={{0,3},{1,2},{2,1},{3,0},{4,7},{5,6},{6,5},{7,4},{8,11},{9,10},{10,... | collective-permute-start | bytes 24584 | tf_op jit(solution)/shard_map/ppermute | solution.py:593
  258.0 8.5 %collective-permute-start.25 = (f32[4,512]{1,0:T(4,128)S(1)}, f32[4,512]{1,0:T(4,128)S(1)}, u32[]{:S(2)}, u32[]{:S(2)}) collective-permute-start(f32[4,512]{1,0:T(4,128)S(1)} %reshape.566), channel_id=1, source_target_pairs={{0,2},{1,3},{2,0},{3,1},{4,6},{5,7},{6,4},{7,5},{8,10},{9,11},{10,... | collective-permute-start | bytes 24584 | tf_op jit(solution)/shard_map/ppermute | solution.py:593
  258.5 8.0 %collective-permute-start.23 = (f32[4,512]{1,0:T(4,128)S(1)}, f32[4,512]{1,0:T(4,128)S(1)}, u32[]{:S(2)}, u32[]{:S(2)}) collective-permute-start(f32[4,512]{1,0:T(4,128)S(1)} %reshape.566), channel_id=1, source_target_pairs={{0,1},{1,0},{2,3},{3,2},{4,5},{5,4},{6,7},{7,6},{8,9},{9,8},{10,11... | collective-permute-start | bytes 24584 | tf_op jit(solution)/shard_map/ppermute | solution.py:593
  319.0 293.1 %reduce-scatter.8.cloned.1.call-start = ((), (), s32[]{:S(2)}) async-start(), calls=%async_computation.5 | async-start | bytes 4718592 | tf_op jit(solution)/shard_map/reduce_scatter | solution.py:1042
  319.3 4.7 collective-permute-start.29
  322.2 3.7 collective-permute-start.28
  322.7 3.7 collective-permute-start.27
  323.9 289.5 %reduce-scatter.6.cloned.1.call-start = ((), (), s32[]{:S(2)}) async-start(), calls=%async_computation.4 | async-start | bytes 10485760 | tf_op jit(solution)/shard_map/reduce_scatter | solution.py:1084
  329.6 41.8 %copy-start.6 = (bf16[2,4,128,1024]{3,2,1,0:T(8,128)(2,1)S(1)}, bf16[2,4,128,1024]{3,2,1,0:T(8,128)(2,1)}, u32[]{:S(2)}) copy-start(bf16[2,4,128,1024]{3,2,1,0:T(8,128)(2,1)} %copy-done.5) | copy-start | bytes 6291460
  421.2 29.4 %collective-permute-start.30 = (bf16[4,320,256]{2,1,0:T(8,128)(2,1)S(1)}, bf16[4,320,256]{2,1,0:T(8,128)(2,1)}, u32[]{:S(2)}, u32[]{:S(2)}) collective-permute-start(bf16[4,320,256]{2,1,0:T(8,128)(2,1)S(1)} %pad_maximum_fusion.9), channel_id=1, source_target_pairs={{0,4},{4,0},{8,12},{12,8},{16,20},{20,16},{24,28},{28,24},{1,5},{5... | collective-permute-start | bytes 1966088 | tf_op jit(solution)/shard_map/ppermute | solution.py:593
  451.9 31.8 %collective-permute-start.33 = (bf16[320,256]{1,0:T(8,128)(2,1)S(1)}, bf16[320,256]{1,0:T(8,128)(2,1)S(1)}, u32[]{:S(2)}, u32[]{:S(2)}) collective-permute-start(bf16[320,256]{1,0:T(8,128)(2,1)S(1)} %get-tuple-element.284), channel_id=1, source_target_pairs={{0,3},{1,2},{2,1},{3,0},{4,7},{5,6},{6,5},{7,4},{8,11},{9,10},{10,... | collective-permute-start | bytes 491528 | tf_op jit(solution)/shard_map/ppermute | solution.py:593
  453.6 30.1 %collective-permute-start.32 = (bf16[320,256]{1,0:T(8,128)(2,1)S(1)}, bf16[320,256]{1,0:T(8,128)(2,1)S(1)}, u32[]{:S(2)}, u32[]{:S(2)}) collective-permute-start(bf16[320,256]{1,0:T(8,128)(2,1)S(1)} %get-tuple-element.285), channel_id=1, source_target_pairs={{0,2},{1,3},{2,0},{3,1},{4,6},{5,7},{6,4},{7,5},{8,10},{9,11},{10,... | collective-permute-start | bytes 491528 | tf_op jit(solution)/shard_map/ppermute | solution.py:593
  453.8 29.9 %collective-permute-start.31 = (bf16[320,256]{1,0:T(8,128)(2,1)S(1)}, bf16[320,256]{1,0:T(8,128)(2,1)S(1)}, u32[]{:S(2)}, u32[]{:S(2)}) collective-permute-start(bf16[320,256]{1,0:T(8,128)(2,1)S(1)} %get-tuple-element.286), channel_id=1, source_target_pairs={{0,1},{1,0},{2,3},{3,2},{4,5},{5,4},{6,7},{7,6},{8,9},{9,8},{10,11... | collective-permute-start | bytes 491528 | tf_op jit(solution)/shard_map/ppermute | solution.py:593
  483.7 7.6 %collective-permute-start.34 = (bf16[2048,1024]{1,0:T(8,128)(2,1)}, bf16[2048,1024]{1,0:T(8,128)(2,1)}, u32[]{:S(2)}, u32[]{:S(2)}) collective-permute-start(bf16[2048,1024]{1,0:T(8,128)(2,1)} %get-tuple-element.178), channel_id=1, source_target_pairs={{0,4},{4,0},{8,12},{12,8},{16,20},{20,16},{24,28},{28,24},{1,5},{5... | collective-permute-start | bytes 12582920 | tf_op jit(solution)/shard_map/ppermute | solution.py:593
  495.1 57.7 %collective-permute-start.35 = (bf16[2,592,512]{2,1,0:T(8,128)(2,1)S(1)}, bf16[2,592,512]{2,1,0:T(8,128)(2,1)}, u32[]{:S(2)}, u32[]{:S(2)}) collective-permute-start(bf16[2,592,512]{2,1,0:T(8,128)(2,1)S(1)} %pad_maximum_fusion.4), channel_id=1, source_target_pairs={{0,8},{4,12},{8,0},{12,4},{16,24},{20,28},{24,16},{28,20},{1,9},{5... | collective-permute-start | bytes 3637256 | tf_op jit(solution)/shard_map/ppermute | solution.py:593
  498.2 55.7 %collective-permute-start.36 = (bf16[2,592,512]{2,1,0:T(8,128)(2,1)}, bf16[2,592,512]{2,1,0:T(8,128)(2,1)}, u32[]{:S(2)}, u32[]{:S(2)}) collective-permute-start(bf16[2,592,512]{2,1,0:T(8,128)(2,1)} %pad_maximum_fusion.5), channel_id=1, source_target_pairs={{0,16},{4,20},{8,24},{12,28},{16,0},{20,4},{24,8},{28,12},{1,17},{... | collective-permute-start | bytes 3637256 | tf_op jit(solution)/shard_map/ppermute | solution.py:593
  499.8 53.0 %collective-permute-start.37 = (bf16[320,256]{1,0:T(8,128)(2,1)S(1)}, bf16[320,256]{1,0:T(8,128)(2,1)S(1)}, u32[]{:S(2)}, u32[]{:S(2)}) collective-permute-start(bf16[320,256]{1,0:T(8,128)(2,1)S(1)} %fusion.36), channel_id=1, source_target_pairs={{0,8},{4,12},{8,0},{12,4},{16,24},{20,28},{24,16},{28,20},{1,9},{5... | collective-permute-start | bytes 491528 | tf_op jit(solution)/shard_map/ppermute | solution.py:593
  556.6 37.1 %collective-permute-start.39 = (bf16[592,512]{1,0:T(8,128)(2,1)S(1)}, bf16[592,512]{1,0:T(8,128)(2,1)S(1)}, u32[]{:S(2)}, u32[]{:S(2)}) collective-permute-start(bf16[592,512]{1,0:T(8,128)(2,1)S(1)} %get-tuple-element.260), channel_id=1, source_target_pairs={{0,8},{4,12},{8,0},{12,4},{16,24},{20,28},{24,16},{28,20},{1,9},{5... | collective-permute-start | bytes 1818632 | tf_op jit(solution)/shard_map/ppermute | solution.py:593
  558.1 35.6 %collective-permute-start.38 = (bf16[592,512]{1,0:T(8,128)(2,1)S(1)}, bf16[592,512]{1,0:T(8,128)(2,1)S(1)}, u32[]{:S(2)}, u32[]{:S(2)}) collective-permute-start(bf16[592,512]{1,0:T(8,128)(2,1)S(1)} %get-tuple-element.261), channel_id=1, source_target_pairs={{0,16},{4,20},{8,24},{12,28},{16,0},{20,4},{24,8},{28,12},{1,17},{... | collective-permute-start | bytes 1818632 | tf_op jit(solution)/shard_map/ppermute | solution.py:593
  559.2 34.4 %collective-permute-start.40 = (bf16[320,256]{1,0:T(8,128)(2,1)S(1)}, bf16[320,256]{1,0:T(8,128)(2,1)S(1)}, u32[]{:S(2)}, u32[]{:S(2)}) collective-permute-start(bf16[320,256]{1,0:T(8,128)(2,1)S(1)} %add_convert_fusion.11), channel_id=1, source_target_pairs={{0,16},{4,20},{8,24},{12,28},{16,0},{20,4},{24,8},{28,12},{1,17},{... | collective-permute-start | bytes 491528 | tf_op jit(solution)/shard_map/ppermute | solution.py:593
  596.7 11.2 %collective-permute-start.43 = (bf16[592,256]{1,0:T(8,128)(2,1)S(1)}, bf16[592,256]{1,0:T(8,128)(2,1)}, u32[]{:S(2)}, u32[]{:S(2)}) collective-permute-start(bf16[592,256]{1,0:T(8,128)(2,1)S(1)} %get-tuple-element.287), channel_id=1, source_target_pairs={{0,3},{1,2},{2,1},{3,0},{4,7},{5,6},{6,5},{7,4},{8,11},{9,10},{10,... | collective-permute-start | bytes 909320 | tf_op jit(solution)/shard_map/ppermute | solution.py:593
  598.2 13.4 %collective-permute-start.42 = (bf16[592,256]{1,0:T(8,128)(2,1)S(1)}, bf16[592,256]{1,0:T(8,128)(2,1)}, u32[]{:S(2)}, u32[]{:S(2)}) collective-permute-start(bf16[592,256]{1,0:T(8,128)(2,1)S(1)} %get-tuple-element.288), channel_id=1, source_target_pairs={{0,2},{1,3},{2,0},{3,1},{4,6},{5,7},{6,4},{7,5},{8,10},{9,11},{10,... | collective-permute-start | bytes 909320 | tf_op jit(solution)/shard_map/ppermute | solution.py:593
  598.6 13.3 %collective-permute-start.41 = (bf16[592,256]{1,0:T(8,128)(2,1)S(1)}, bf16[592,256]{1,0:T(8,128)(2,1)}, u32[]{:S(2)}, u32[]{:S(2)}) collective-permute-start(bf16[592,256]{1,0:T(8,128)(2,1)S(1)} %get-tuple-element.289), channel_id=1, source_target_pairs={{0,1},{1,0},{2,3},{3,2},{4,5},{5,4},{6,7},{7,6},{8,9},{9,8},{10,11... | collective-permute-start | bytes 909320 | tf_op jit(solution)/shard_map/ppermute | solution.py:593
  618.8 16.0 %collective-permute-start.48 = (f32[1,7024]{1,0:T(1,128)S(1)}, f32[1,7024]{1,0:T(1,128)S(1)}, u32[]{:S(2)}, u32[]{:S(2)}) collective-permute-start(f32[1,7024]{1,0:T(1,128)S(1)} %get-tuple-element.311), channel_id=1, source_target_pairs={{0,1},{1,0},{2,3},{3,2},{4,5},{5,4},{6,7},{7,6},{8,9},{9,8},{10,11... | collective-permute-start | bytes 84296 | tf_op jit(solution)/shard_map/ppermute | solution.py:593
  619.1 15.7 %collective-permute-start.50 = (f32[1,7024]{1,0:T(1,128)S(1)}, f32[1,7024]{1,0:T(1,128)S(1)}, u32[]{:S(2)}, u32[]{:S(2)}) collective-permute-start(f32[1,7024]{1,0:T(1,128)S(1)} %get-tuple-element.312), channel_id=1, source_target_pairs={{0,3},{1,2},{2,1},{3,0},{4,7},{5,6},{6,5},{7,4},{8,11},{9,10},{10,... | collective-permute-start | bytes 84296 | tf_op jit(solution)/shard_map/ppermute | solution.py:593
  620.9 13.9 %collective-permute-start.49 = (f32[1,7024]{1,0:T(1,128)S(1)}, f32[1,7024]{1,0:T(1,128)S(1)}, u32[]{:S(2)}, u32[]{:S(2)}) collective-permute-start(f32[1,7024]{1,0:T(1,128)S(1)} %get-tuple-element.313), channel_id=1, source_target_pairs={{0,2},{1,3},{2,0},{3,1},{4,6},{5,7},{6,4},{7,5},{8,10},{9,11},{10,... | collective-permute-start | bytes 84296 | tf_op jit(solution)/shard_map/ppermute | solution.py:593
  623.1 28.9 %collective-permute-start.47 = (bf16[256,256]{1,0:T(8,128)(2,1)}, bf16[256,256]{1,0:T(8,128)(2,1)}, u32[]{:S(2)}, u32[]{:S(2)}) collective-permute-start(bf16[256,256]{1,0:T(8,128)(2,1)} %get-tuple-element.296), channel_id=1, source_target_pairs={{0,3},{1,2},{2,1},{3,0},{4,7},{5,6},{6,5},{7,4},{8,11},{9,10},{10,... | collective-permute-start | bytes 393224 | tf_op jit(solution)/shard_map/ppermute | solution.py:593
  634.8 4.8 collective-permute-start.51
  635.0 17.0 %collective-permute-start.46 = (bf16[256,256]{1,0:T(8,128)(2,1)}, bf16[256,256]{1,0:T(8,128)(2,1)}, u32[]{:S(2)}, u32[]{:S(2)}) collective-permute-start(bf16[256,256]{1,0:T(8,128)(2,1)} %get-tuple-element.297), channel_id=1, source_target_pairs={{0,2},{1,3},{2,0},{3,1},{4,6},{5,7},{6,4},{7,5},{8,10},{9,11},{10,... | collective-permute-start | bytes 393224 | tf_op jit(solution)/shard_map/ppermute | solution.py:593
  635.7 16.3 %collective-permute-start.45 = (bf16[256,256]{1,0:T(8,128)(2,1)}, bf16[256,256]{1,0:T(8,128)(2,1)}, u32[]{:S(2)}, u32[]{:S(2)}) collective-permute-start(bf16[256,256]{1,0:T(8,128)(2,1)} %get-tuple-element.298), channel_id=1, source_target_pairs={{0,1},{1,0},{2,3},{3,2},{4,5},{5,4},{6,7},{7,6},{8,9},{9,8},{10,11... | collective-permute-start | bytes 393224 | tf_op jit(solution)/shard_map/ppermute | solution.py:593
  639.7 3.9 collective-permute-start.52
  640.6 16.4 %collective-permute-start.44 = (bf16[256,1064]{0,1:T(8,128)(2,1)}, bf16[256,1064]{0,1:T(8,128)(2,1)}, u32[]{:S(2)}, u32[]{:S(2)}) collective-permute-start(bf16[256,1064]{0,1:T(8,128)(2,1)} %broadcast_select_fusion.2), channel_id=1, source_target_pairs={{0,4},{4,0},{8,12},{12,8},{16,20},{20,16},{24,28},{28,24},{1,5},{5... | collective-permute-start | bytes 1634312 | tf_op jit(solution)/shard_map/ppermute | solution.py:593
  643.8 3.9 collective-permute-start.53
  (52 other events, 305.8 us)
Sparse Core Ops, SparseCore 0:
  9.9 115.9 all-gather.4
  127.8 87.6 all-gather.6
  319.1 86.1 reduce-scatter.3
  407.6 49.9 reduce-scatter.7
  460.9 84.5 reduce-scatter.5
